TPU v7x, 32 devices: a whole 2x2x4 slice. The times are simulated.
32 devices in a mesh: rows: 8 (over y, x, core), cols: 4 (over z).
Axes of the slice: x: 2, y: 2, z: 4, core: 2. Of those that a mesh axis runs over, the one named last changes fastest.
Arguments:
- affinity: bfloat16 [4, 64, 4, 8, 4096], P(None, 'rows', 'cols'), may hold values from -6 to 6
- block_columns: int32 [4, 64, 4, 8], P(None, 'rows', 'cols'), may hold values from 0 to 63
- block_counts: int32 [4, 64, 4], P(None, 'rows', 'cols'), may hold values from 0 to 8
- inv_degree: float32 [4, 64, 64], P('cols', 'rows'), may hold values from 0.4 to 6.1
- panel: float32 [4, 64, 4096], P('cols', 'rows'), may hold values from -6 to 6
Outputs:
- panel_out: float32 [4, 64, 4096], P('cols', 'rows')
Inputs may be any that keep to these rules, and one draw needn't show every extreme that they name: `block_columns`: slots at or past a block row's count are ignored; listed block columns may repeat, and their blocks then add.
All inputs are finite; a program needn't handle non-finite values.
Results may differ from a plain program's by a relative error of at most 0.019.
Values may be sent and summed in bfloat16 or wider, within the bound.
No kernel may reach another device: no remote copies, remote signals or barrier semaphores. Data moves between devices by JAX's collectives and lax.ppermute only.
A program may use at most 128 MiB of HBM per device.

v0:
```python
import jax
import jax.numpy as jnp
from jax import lax
from jax.sharding import PartitionSpec as P

ITERS = 2


def local_terms(values_slice, columns_slice, counts_slice, panel_blocks, block_size, panel_width):
    groups = values_slice.shape[0]
    block_rows = values_slice.shape[1]
    accum = jnp.zeros((groups, block_rows, block_size, panel_width), jnp.float32)
    for slot_index in range(values_slice.shape[2]):
        picked = jnp.take(panel_blocks, columns_slice[:, :, slot_index], axis=0)
        live = (counts_slice > slot_index)[:, :, None, None]
        picked = jnp.where(live, picked, jnp.zeros_like(picked))
        matrix = values_slice[:, :, slot_index].reshape(groups, block_rows, block_size, block_size)
        accum = accum + jnp.einsum(
            "giab,gibk->giak", matrix, picked, preferred_element_type=jnp.float32
        )
    return accum.reshape(groups, block_rows, block_size * panel_width)


def normalize(rows_out, gram_matrix, panel_width):
    identity = jnp.eye(panel_width, dtype=jnp.float32)
    lower_factor = jnp.linalg.cholesky(gram_matrix)
    inverse = lax.linalg.triangular_solve(lower_factor, identity, left_side=True, lower=True)
    return jnp.dot(rows_out, inverse.T, precision=lax.Precision.HIGHEST)


def body(affinity, block_columns, block_counts, inv_degree, panel):
    groups = affinity.shape[0]
    block_rows = affinity.shape[1]
    block_size = inv_degree.shape[2]
    panel_width = panel.shape[2] // block_size
    trajectories = float(groups * lax.axis_size("rows") * block_rows * block_size)
    values_local = affinity[:, :, 0]
    columns_local = block_columns[:, :, 0]
    counts_local = block_counts[:, :, 0]
    current = panel
    for iteration in range(ITERS):
        scaled = (
            current.reshape(1, block_rows, block_size, panel_width) * inv_degree[..., None]
        ).astype(jnp.bfloat16)
        scaled = scaled.reshape(1, block_rows, block_size * panel_width)
        gathered = lax.all_gather(scaled, "rows", axis=1, tiled=True)
        panel_blocks = gathered[0].reshape(-1, block_size, panel_width)
        owned = lax.psum_scatter(
            local_terms(
                values_local, columns_local, counts_local, panel_blocks, block_size, panel_width
            ).astype(jnp.bfloat16),
            "cols",
            scatter_dimension=0,
            tiled=True,
        ).astype(jnp.float32)
        rows_out = (
            owned.reshape(1, block_rows, block_size, panel_width) * inv_degree[..., None]
        ).reshape(-1, panel_width)
        local_gram = jnp.dot(rows_out.T, rows_out, precision=lax.Precision.HIGHEST)
        gram_matrix = lax.psum(local_gram, ("rows", "cols")) / trajectories
        current = normalize(rows_out, gram_matrix, panel_width).reshape(
            1, block_rows, block_size * panel_width
        )
    return current


def solution(mesh):
    return jax.shard_map(
        body,
        mesh=mesh,
        in_specs=(
            P(None, "rows", "cols", None, None),
            P(None, "rows", "cols", None),
            P(None, "rows", "cols"),
            P("cols", "rows", None),
            P("cols", "rows", None),
        ),
        out_specs=P("cols", "rows", None),
        check_vma=False,
    )
```

profile of v0, /device:TPU:0, one launch (start us, length us, event | category | flops | bytes accessed | tf_op | source)
XLA Modules:
  0.0 298.1 jit_solution(14886765254311913208)
XLA Ops:
  14.3 12.5 %all_gather.6 = bf16[1,64,4096]{2,1,0:T(8,128)(2,1)} all-gather(bf16[1,8,4096]{2,1,0:T(8,128)(2,1)S(1)} %multiply_convert_fusion), channel_id=1, replica_groups=mesh['rows'=8,'cols'=4] {'rows'}, dimensions={1}, use_global_device_ids=true | all-gather | bytes 589824 | tf_op jit(solution)/shard_map/all_gather | solution.py:46
  26.8 2.1 reshape_squeeze.38
  30.2 2.0 copy.20
  32.9 16.8 %slice_reduce_fusion = (bf16[4,8,4096]{2,1,0:T(8,128)(2,1)S(1)}, bf16[4,8,4096]{2,1,0:T(8,128)(2,1)}, bf16[4,8,4096]{2,1,0:T(8,128)(2,1)}, bf16[4,8,4096]{2,1,0:...) fusion(bf16[4,8,8,4096]{3,2,1,0:T(8,128)(2,1)S(1)} %bitcast.89), kind=kLoop, calls=%fused_computation.39 | loop fusion | bytes 4194304 | tf_op jit(solution)/shard_map/slice | solution.py:17
  49.7 2.3 reshape_squeeze.39
  63.0 2.3 reshape_squeeze.43
  68.5 2.3 reshape_squeeze.44
  73.9 2.3 reshape_squeeze.45
  90.5 20.1 %reduce-scatter.3.cloned.1.call-done = bf16[1,8,4096]{2,1,0:T(8,128)(2,1)} async-done(((bf16[4,8,4096]{2,1,0:T(8,128)(2,1)}), bf16[1,8,4096]{2,1,0:T(8,128)(2,1)}) %reduce-scatter.3.cloned.1.call-update) | async-done | bytes 65552 | tf_op jit(solution)/shard_map/reduce_scatter | solution.py:48
  112.1 38.9 %psum.14 = f32[64,64]{0,1:T(8,128)S(1)} all-reduce(f32[64,64]{0,1:T(8,128)S(1)} %convolution_bitcast_fusion.2), channel_id=1, replica_groups=mesh['rows'=8,'cols'=4] {'rows','cols'}, use_global_device_ids=true, to_apply=%region_1.3 | all-reduce | flops 4096 | bytes 32768 | tf_op jit(solution)/shard_map/psum | solution.py:60
  151.0 5.8 %cholesky.44 = f32[64,64]{1,0:T(8,128)S(1)} custom-call(f32[64,64]{1,0:T(8,128)S(1)} %fusion.84), custom_call_target="Cholesky" | custom-call | tf_op jit(solution)/shard_map/jit(cholesky)/cholesky | solution.py:26
  158.2 4.9 %custom-call.6 = f32[1,64,64]{1,2,0:T(8,128)S(1)} custom-call(f32[1,64,64]{2,1,0:T(8,128)S(1)} %fusion.79), custom_call_target="InvertDiagBlocksLowerTriangular" | custom-call | tf_op jit(solution)/shard_map/triangular_solve/custom-call.0 | solution.py:27
  165.0 11.6 %all_gather.7 = bf16[1,64,4096]{2,1,0:T(8,128)(2,1)} all-gather(bf16[1,8,4096]{2,1,0:T(8,128)(2,1)S(1)} %reshape.155), channel_id=1, replica_groups=mesh['rows'=8,'cols'=4] {'rows'}, dimensions={1}, use_global_device_ids=true | all-gather | bytes 589824 | tf_op jit(solution)/shard_map/all_gather | solution.py:46
  176.6 2.1 reshape_squeeze.47
  190.0 2.1 copy.32
  193.7 2.1 copy.33
  195.8 2.1 copy.34
  197.9 2.1 copy.35
  202.0 2.0 copy.37
  204.0 2.1 copy.38
  217.4 18.8 %reduce-scatter.5.cloned.1.call-done = bf16[1,8,4096]{2,1,0:T(8,128)(2,1)} async-done(((bf16[4,8,4096]{2,1,0:T(8,128)(2,1)}), bf16[1,8,4096]{2,1,0:T(8,128)(2,1)}) %reduce-scatter.5.cloned.1.call-update) | async-done | bytes 65552 | tf_op jit(solution)/shard_map/reduce_scatter | solution.py:48
  237.7 38.9 %psum.15 = f32[64,64]{0,1:T(8,128)S(1)} all-reduce(f32[64,64]{0,1:T(8,128)S(1)} %convolution_bitcast_fusion.1), channel_id=1, replica_groups=mesh['rows'=8,'cols'=4] {'rows','cols'}, use_global_device_ids=true, to_apply=%region_5.9 | all-reduce | flops 4096 | bytes 32768 | tf_op jit(solution)/shard_map/psum | solution.py:60
  276.7 5.8 %cholesky.55 = f32[64,64]{1,0:T(8,128)S(1)} custom-call(f32[64,64]{1,0:T(8,128)S(1)} %fusion.82), custom_call_target="Cholesky" | custom-call | tf_op jit(solution)/shard_map/jit(cholesky)/cholesky | solution.py:26
  283.9 4.9 %custom-call.7 = f32[1,64,64]{1,2,0:T(8,128)S(1)} custom-call(f32[1,64,64]{2,1,0:T(8,128)S(1)} %fusion.80), custom_call_target="InvertDiagBlocksLowerTriangular" | custom-call | tf_op jit(solution)/shard_map/triangular_solve/custom-call.0 | solution.py:27
  (185 shorter events, 77.5 us)
Async XLA Ops:
  6.5 104.0 %reduce-scatter.3.cloned.1.call-start = ((), (), s32[]{:S(2)}) async-start(), calls=%async_computation.2 | async-start | bytes 327680 | tf_op jit(solution)/shard_map/reduce_scatter | solution.py:48
  14.3 18.0 %copy-start.35 = (s32[4,8,1]{1,2,0:T(1,128)S(1)}, s32[4,8,1]{1,2,0:T(1,128)}, u32[]{:S(2)}) copy-start(s32[4,8,1]{1,2,0:T(1,128)} %param.12) | copy-start | bytes 388
  14.3 18.7 %copy-start = (bf16[4,8,1,8,4096]{4,3,2,1,0:T(8,128)(2,1)S(1)}, bf16[4,8,1,8,4096]{4,3,2,1,0:T(8,128)(2,1)}, u32[]{:S(2)}) copy-start(bf16[4,8,1,8,4096]{4,3,2,1,0:T(8,128)(2,1)} %param.10) | copy-start | bytes 6291460
  49.7 4.1 %copy-start.21 = (bf16[4,8,4096]{2,1,0:T(8,128)(2,1)S(1)}, bf16[4,8,4096]{2,1,0:T(8,128)(2,1)}, u32[]{:S(2)}) copy-start(bf16[4,8,4096]{2,1,0:T(8,128)(2,1)} %get-tuple-element.14) | copy-start | bytes 786436
  52.8 3.3 %copy-start.20 = (bf16[4,8,4096]{2,1,0:T(8,128)(2,1)S(1)}, bf16[4,8,4096]{2,1,0:T(8,128)(2,1)}, u32[]{:S(2)}) copy-start(bf16[4,8,4096]{2,1,0:T(8,128)(2,1)} %get-tuple-element.13) | copy-start | bytes 786436
  78.3 3.7 %copy-start.8 = (bf16[32,64,64]{1,2,0:T(8,128)(2,1)S(1)}, bf16[32,64,64]{1,2,0:T(8,128)(2,1)}, u32[]{:S(2)}) copy-start(bf16[32,64,64]{1,2,0:T(8,128)(2,1)} %copy.20) | copy-start | bytes 786436
  79.1 4.4 %copy-start.9 = (bf16[32,64,64]{1,2,0:T(8,128)(2,1)S(1)}, bf16[32,64,64]{1,2,0:T(8,128)(2,1)}, u32[]{:S(2)}) copy-start(bf16[32,64,64]{1,2,0:T(8,128)(2,1)} %copy.21) | copy-start | bytes 786436
  79.1 4.4 %copy-start.33 = (pred[4,8]{1,0:T(4,128)(4,1)S(1)}, pred[4,8]{1,0:T(4,128)(4,1)}, u32[]{:S(2)}) copy-start(pred[4,8]{1,0:T(4,128)(4,1)} %get-tuple-element.47) | copy-start | bytes 100
  85.0 1.2 copy-start.12
  85.6 1.3 copy-start.13
  85.6 1.3 copy-start.30
  86.7 1.2 copy-start.14
  86.7 1.2 copy-start.28
  88.9 75.5 %copy-start.22 = (f32[1,8,64]{2,1,0:T(8,128)S(1)}, f32[1,8,64]{2,1,0:T(8,128)}, u32[]{:S(2)}) copy-start(f32[1,8,64]{2,1,0:T(8,128)} %param.13) | copy-start | bytes 6148
  90.4 145.8 %reduce-scatter.5.cloned.1.call-start = ((), (), s32[]{:S(2)}) async-start(), calls=%async_computation.3 | async-start | bytes 327680 | tf_op jit(solution)/shard_map/reduce_scatter | solution.py:48
  178.7 5.7 %copy-start.23 = (s32[1024]{0:T(1024)S(1)}, s32[1024]{0:T(1024)}, u32[]{:S(2)}) copy-start(s32[1024]{0:T(1024)} %pad_clamp_fusion.3) | copy-start | bytes 12292
  180.1 5.7 %copy-start.24 = (s32[1024]{0:T(1024)S(1)}, s32[1024]{0:T(1024)}, u32[]{:S(2)}) copy-start(s32[1024]{0:T(1024)} %pad_clamp_fusion.2) | copy-start | bytes 12292
  181.5 5.7 %copy-start.25 = (s32[1024]{0:T(1024)S(1)}, s32[1024]{0:T(1024)}, u32[]{:S(2)}) copy-start(s32[1024]{0:T(1024)} %pad_clamp_fusion.1) | copy-start | bytes 12292
  182.9 5.7 %copy-start.26 = (s32[1024]{0:T(1024)S(1)}, s32[1024]{0:T(1024)}, u32[]{:S(2)}) copy-start(s32[1024]{0:T(1024)} %pad_clamp_fusion) | copy-start | bytes 12292
  185.8 6.3 %copy-start.34 = (pred[4,8]{1,0:T(4,128)(4,1)S(1)}, pred[4,8]{1,0:T(4,128)(4,1)}, u32[]{:S(2)}) copy-start(pred[4,8]{1,0:T(4,128)(4,1)} %get-tuple-element.40) | copy-start | bytes 100
  208.1 1.6 copy-start.19
  210.7 1.2 copy-start.17
  211.9 1.2 copy-start.16
  213.1 1.2 copy-start.15
  (14 other events, 15.1 us)
Sparse Core Ops, SparseCore 0:
  90.5 19.9 reduce-scatter.2
  217.5 18.6 reduce-scatter.4
where the time goes:
time: 300 us; the launch traced here: 298 us
  blocking collectives  102 us (34%)
  local copies, waits for them, and re-layouts  96.1 us (32%)
  waiting for transfers between devices  38.8 us (13%)
  other arithmetic  33.9 us (11%)
  between operations  14.1 us (5%)
  matrix products  13.3 us (4%)
    psum x2, blocking collectives, body(): gram_matrix = lax.psum(local_gram, ('rows', 'cols')) / trajectories  77.8 us
    gather x32, local copies, waits for them, and re-layouts, local_terms(): picked = jnp.take(panel_blocks, columns_slice[:, :, slot_index], axis=0)  42.6 us
    reduce_scatter x2, waiting for transfers between devices, body(): lax.psum_scatter(local_terms(values_local, columns_local, counts_local, p...  38.8 us
    all_gather x2, blocking collectives, body(): gathered = lax.all_gather(scaled, 'rows', axis=1, tiled=True)  24.1 us
    slice x1, local copies, waits for them, and re-layouts, local_terms(): values_slice[:, :, slot_index]  16.8 us
    another operation x6, other arithmetic, normalize(): lower_factor = jnp.linalg.cholesky(gram_matrix)  13 us
    another operation x8, local copies, waits for them, and re-layouts, local_terms(): values_slice[:, :, slot_index]  12.2 us
    another operation x4, other arithmetic, normalize(): lax.linalg.triangular_solve(lower_factor, identity, left_side=True, lower...  11.1 us
  transfers between devices with their start and end apart: 2, of which 2 were waited for; matrix products, arithmetic and copies ran while one was open for 0% of the time, Pallas kernels for 0%

commit v1 on v0

v1 whole, which is shorter than its diff:
```python
import functools

import jax
import jax.numpy as jnp
from jax import lax
from jax.experimental import pallas as pl
from jax.experimental.pallas import tpu as pltpu
from jax.sharding import PartitionSpec as P

ITERS = 2
BF16 = jnp.bfloat16
F32 = jnp.float32
HIGHEST = lax.Precision.HIGHEST
VMEM_LIMIT = 48 * 1024 * 1024


def params():
    return pltpu.CompilerParams(vmem_limit_bytes=VMEM_LIMIT)


def vmem():
    return pl.BlockSpec(memory_space=pltpu.VMEM)


def smem():
    return pl.BlockSpec(memory_space=pltpu.SMEM)


def iota(shape, dim):
    return lax.broadcasted_iota(jnp.int32, shape, dim)


def start_kernel(panel_ref, inv_ref, scaled_ref, degree_ref, scratch):
    block_rows, block_size = inv_ref.shape[1], inv_ref.shape[2]
    half = block_size // 2
    for t in range(half):
        scratch[t * block_rows : (t + 1) * block_rows, :] = panel_ref[0, :, t * 128 : (t + 1) * 128]
    pair = iota((half, block_size), 1) // 2 == iota((half, block_size), 0)
    spread = (iota((block_size, 128), 0) % 2 == iota((block_size, 128), 1) // 64).astype(F32)
    rows = [
        jnp.where(pair, jnp.broadcast_to(inv_ref[0, i : i + 1, :], (half, block_size)), 0.0)
        for i in range(block_rows)
    ]
    degree = jnp.dot(
        jnp.concatenate(rows, axis=0), spread, precision=HIGHEST, preferred_element_type=F32
    )
    for i in range(block_rows):
        part = degree[i * half : (i + 1) * half]
        degree_ref[i] = part
        scaled_ref[i] = (scratch[pl.ds(i, half, stride=block_rows), :] * part).astype(BF16)


def start(panel, inv_degree):
    block_rows, block_size = inv_degree.shape[1:]
    shape = (block_rows, block_size // 2, 128)
    return pl.pallas_call(
        start_kernel,
        out_shape=(jax.ShapeDtypeStruct(shape, BF16), jax.ShapeDtypeStruct(shape, F32)),
        in_specs=[vmem(), vmem()],
        out_specs=(vmem(), vmem()),
        scratch_shapes=[pltpu.VMEM((block_rows * block_size // 2, 128), F32)],
        compiler_params=params(),
        name="start",
    )(panel, inv_degree)


def prep_kernel(place_ref, counts_ref, affinity_ref, out_ref, scratch):
    block_rows, slots = affinity_ref.shape[1], affinity_ref.shape[3]
    half = affinity_ref.shape[4] // 128
    group = pl.program_id(0) ^ place_ref[1]
    source, target = iota((256, 256), 0), iota((256, 256), 1)
    moved = (source // 64 % 2) * 128 + (source // 128) * 64 + (source % 2) * 32 + source % 64 // 2
    permute = (moved == target).astype(BF16)
    for i in range(block_rows):
        count = counts_ref[group, i, 0]
        block = affinity_ref[0, i, 0].astype(F32)
        live = iota(block.shape, 0) < count
        block = jnp.where(live, block, 0.0)
        for t in range(half):
            scratch[i % 2, t * slots : (t + 1) * slots, :] = block[:, t * 128 : (t + 1) * 128]
        parts = [
            scratch[i % 2, pl.ds(s, half, stride=slots), :].astype(BF16) for s in range(slots)
        ]
        pairs = [
            jnp.concatenate(parts[s : s + 2], axis=1) for s in range(0, slots, 2)
        ]
        moved_pairs = jnp.dot(
            jnp.concatenate(pairs, axis=0), permute, preferred_element_type=F32
        ).astype(BF16)
        for s in range(slots // 2):
            piece = moved_pairs[s * half : (s + 1) * half]
            out_ref[0, i, :half, s * 128 : (s + 1) * 128] = piece[:, :128]
            out_ref[0, i, half:, s * 128 : (s + 1) * 128] = piece[:, 128:]


def prep(place, block_counts, affinity):
    groups, block_rows, _, slots, flat = affinity.shape
    return pl.pallas_call(
        prep_kernel,
        grid_spec=pltpu.PrefetchScalarGridSpec(
            num_scalar_prefetch=2,
            grid=(groups,),
            in_specs=[
                pl.BlockSpec(
                    (1, block_rows, 1, slots, flat),
                    lambda m, place, counts: (m ^ place[1], 0, 0, 0, 0),
                )
            ],
            out_specs=pl.BlockSpec(
                (1, block_rows, 64, slots * 64), lambda m, place, counts: (m, 0, 0, 0)
            ),
            scratch_shapes=[pltpu.VMEM((2, flat // 128 * slots, 128), F32)],
        ),
        out_shape=jax.ShapeDtypeStruct((groups, block_rows, 64, slots * 64), BF16),
        compiler_params=params(),
        name="prep",
    )(place, block_counts, affinity)


def product_kernel(offsets, place_ref, columns_ref, matrix_ref, *refs):
    pieces, outs, table = refs[:2], refs[2:-1], refs[-1]
    groups, block_rows, block_size, _ = matrix_ref.shape
    slots = columns_ref.shape[3]
    half = block_size // 2
    blocks = table.shape[0]
    low = iota((half, 128), 1) < 64
    for index, offset in enumerate(offsets):
        per_piece = len(offsets) // 2
        source = pieces[index // per_piece]
        base = (place_ref[0] ^ offset) * block_rows
        for i in range(block_rows):
            block = source[index % per_piece, i]
            turned = jnp.concatenate([block[:, 64:], block[:, :64]], axis=1)
            table[base + i, :half] = jnp.where(low, block, turned)
            table[base + i, half:] = jnp.where(low, turned, block)
    for m in range(groups):
        group = m ^ place_ref[1]

        def one(i, carry):
            picked = [
                table[columns_ref[group, i, 0, s] & (blocks - 1)] for s in range(slots)
            ]
            result = jnp.dot(
                matrix_ref[m, i], jnp.concatenate(picked, axis=0), preferred_element_type=F32
            )
            outs[m][i] = jnp.where(low, result[:half], result[half:]).astype(BF16)
            return carry

        lax.fori_loop(0, block_rows, one, 0, unroll=True)


def product(offsets, place, block_columns, matrix, near, far):
    groups, block_rows, block_size, _ = matrix.shape
    blocks = 2 * near.shape[0] * block_rows
    shape = jax.ShapeDtypeStruct((block_rows, block_size // 2, 128), BF16)
    return pl.pallas_call(
        functools.partial(product_kernel, offsets),
        out_shape=(shape,) * groups,
        in_specs=[smem(), smem(), vmem(), vmem(), vmem()],
        out_specs=(vmem(),) * groups,
        scratch_shapes=[pltpu.VMEM((blocks, block_size, 128), BF16)],
        compiler_params=params(),
        name="product",
    )(place, block_columns, matrix, near, far)


def collect_kernel(degree_ref, *refs):
    terms, rows_ref, gram_ref = refs[:-2], refs[-2], refs[-1]
    summed = terms[0][...].astype(F32)
    for term in terms[1:]:
        summed = summed + term[...].astype(F32)
    rows = summed * degree_ref[...]
    rows_ref[...] = rows
    flat = rows.reshape(-1, 128)
    both = lax.dot_general(
        flat, flat, (((0,), (0,)), ((), ())), precision=HIGHEST, preferred_element_type=F32
    )
    gram = both[:64, :64] + both[64:, 64:]
    gram_ref[...] = jnp.concatenate([gram[:32], gram[32:]], axis=1)


def collect(degree, terms):
    return pl.pallas_call(
        collect_kernel,
        out_shape=(
            jax.ShapeDtypeStruct(degree.shape, F32),
            jax.ShapeDtypeStruct((32, 128), F32),
        ),
        in_specs=[vmem()] * (1 + len(terms)),
        out_specs=(vmem(), vmem()),
        compiler_params=params(),
        name="collect",
    )(degree, *terms)


def inverse_factor(gram):
    size = gram.shape[0]
    row_at = iota((size, 128), 0)
    unit = (iota((size, 64), 0) == iota((size, 64), 1)).astype(F32)
    work = jnp.concatenate([gram, unit], axis=1)
    for j in range(size):
        column = jnp.broadcast_to(work[:, j : j + 1], (size, 128))
        scale = lax.rsqrt(column[j : j + 1])
        row = work[j : j + 1] * scale
        column = jnp.where(row_at > j, column * scale, 0.0)
        work = jnp.where(row_at == j, row, work) - column * row
    return work[:, 64:]


def unpack_gram(parts, total):
    packed = parts[0][...]
    for part in parts[1:]:
        packed = packed + part[...]
    return jnp.concatenate([packed[:, :64], packed[:, 64:]], axis=0) / total


def apply_factor(rows, inverse):
    zero = jnp.zeros_like(inverse)
    both = jnp.concatenate(
        [jnp.concatenate([inverse, zero], axis=1), jnp.concatenate([zero, inverse], axis=1)], axis=0
    )
    return lax.dot_general(
        rows, both, (((1,), (1,)), ((), ())), precision=HIGHEST, preferred_element_type=F32
    )


def middle_kernel(total, degree_ref, rows_ref, *refs):
    inverse = inverse_factor(unpack_gram(refs[:-1], total))
    current = apply_factor(rows_ref[...].reshape(-1, 128), inverse)
    refs[-1][...] = (current.reshape(degree_ref.shape) * degree_ref[...]).astype(BF16)


def middle(total, degree, rows, grams):
    return pl.pallas_call(
        functools.partial(middle_kernel, total),
        out_shape=jax.ShapeDtypeStruct(degree.shape, BF16),
        in_specs=[vmem()] * (2 + len(grams)),
        out_specs=vmem(),
        compiler_params=params(),
        name="middle",
    )(degree, rows, *grams)


def finish_kernel(total, rows_ref, *refs):
    out_ref, scratch = refs[-2:]
    block_rows, half, _ = rows_ref.shape
    inverse = inverse_factor(unpack_gram(refs[:-2], total))
    current = apply_factor(rows_ref[...].reshape(-1, 128), inverse)
    for i in range(block_rows):
        scratch[pl.ds(i, half, stride=block_rows), :] = current[i * half : (i + 1) * half]
    for t in range(half):
        out_ref[0, :, t * 128 : (t + 1) * 128] = scratch[t * block_rows : (t + 1) * block_rows, :]


def finish(total, rows, grams):
    block_rows, half, _ = rows.shape
    return pl.pallas_call(
        functools.partial(finish_kernel, total),
        out_shape=jax.ShapeDtypeStruct((1, block_rows, half * 128), F32),
        in_specs=[vmem()] * (1 + len(grams)),
        out_specs=vmem(),
        scratch_shapes=[pltpu.VMEM((block_rows * half, 128), F32)],
        compiler_params=params(),
        name="finish",
    )(rows, *grams)


def swap(value, axis, mask):
    size = lax.axis_size(axis)
    return lax.ppermute(value, axis, [(index, index ^ mask) for index in range(size)])


def stages(size):
    if size == 8:
        return [[2, 4, 6], [1]]
    bits, bit = [], 1
    while bit < size:
        bits.append([bit])
        bit *= 2
    return bits


def gather_rows(scaled):
    plan = stages(lax.axis_size("rows"))
    held, offsets = scaled[None], [0]
    for masks in plan[:-1]:
        held = jnp.concatenate([held] + [swap(held, "rows", mask) for mask in masks], axis=0)
        offsets = offsets + [mask ^ offset for mask in masks for offset in offsets]
    (last,) = plan[-1]
    offsets = offsets + [last ^ offset for offset in offsets]
    return held, swap(held, "rows", last), offsets


def add_grams(gram):
    for masks in reversed(stages(lax.axis_size("rows"))):
        gram = sum([swap(gram, "rows", mask) for mask in masks], gram)
    return [gram] + [swap(gram, "cols", mask) for mask in range(1, lax.axis_size("cols"))]


def body(affinity, block_columns, block_counts, inv_degree, panel):
    block_rows, block_size = inv_degree.shape[1:]
    groups = affinity.shape[0]
    total = float(groups * lax.axis_size("rows") * block_rows * block_size)
    place = jnp.stack([lax.axis_index("rows"), lax.axis_index("cols")]).astype(jnp.int32)
    scaled, degree = start(panel, inv_degree)
    matrix = prep(place, block_counts, affinity)
    for iteration in range(ITERS):
        near, far, offsets = gather_rows(scaled)
        terms = product(offsets, place, block_columns, matrix, near, far)
        terms = [terms[0]] + [swap(terms[m], "cols", m) for m in range(1, groups)]
        rows, gram = collect(degree, terms)
        grams = add_grams(gram)
        if iteration < ITERS - 1:
            scaled = middle(total, degree, rows, grams)
    return finish(total, rows, grams)


def solution(mesh):
    return jax.shard_map(
        body,
        mesh=mesh,
        in_specs=(
            P(None, "rows", "cols", None, None),
            P(None, "rows", "cols", None),
            P(None, "rows", "cols"),
            P("cols", "rows", None),
            P("cols", "rows", None),
        ),
        out_specs=P("cols", "rows", None),
        check_vma=False,
    )
```

time: 300 us -> 89.5 us (0.30)
  blocking collectives: 102 us -> 0 us
  local copies, waits for them, and re-layouts: 96.1 us -> 3.96 us
  other arithmetic: 33.9 us -> 0.17 us
  starting transfers between devices: 0.04 us -> 33 us
  Pallas kernels: 0 us -> 19.8 us
  between operations: 14.1 us -> 0.13 us
  matrix products: 13.3 us -> 0 us
  waiting for transfers between devices: 38.8 us -> 32.2 us
    psum x2 -> x0, blocking collectives: 77.8 us -> none  [body(): gram_matrix = lax.psum(local_gram, ('rows', 'cols')) / trajectories]
    gather x32 -> x0, local copies, waits for them, and re-layouts: 42.6 us -> none  [local_terms(): picked = jnp.take(panel_blocks, columns_slice[:, :, slot_index], axis=0)]
    reduce_scatter x2 -> x0, waiting for transfers between devices: 38.8 us -> none  [body(): lax.psum_scatter(local_terms(values_local, columns_local, counts_local, p...]
    ppermute x0 -> x28, starting transfers between devices: none -> 33 us  [swap(): lax.ppermute(value, axis, [(index, index ^ mask) for index in range(size)])]
    ppermute x0 -> x28, waiting for transfers between devices: none -> 32.2 us  [swap(): lax.ppermute(value, axis, [(index, index ^ mask) for index in range(size)])]
    all_gather x2 -> x0, blocking collectives: 24.1 us -> none  [body(): gathered = lax.all_gather(scaled, 'rows', axis=1, tiled=True)]
    another operation x10 -> x1, other arithmetic: 24.1 us -> 0.07 us  [body(): jnp.stack([lax.axis_index('rows'), lax.axis_index('cols')])]
    pallas_call x0 -> x8, Pallas kernels: none -> 19.8 us  [the longest x1 6.39 us: finish(): pl.pallas_call(functools.partial(finish_kernel, total), out_shape=jax.Sha...]
  transfers between devices with their start and end apart: 2 -> 28, of which waited for: 2 -> 23; matrix products, arithmetic and copies ran while one was open for 0% -> 1% of each run, Pallas kernels for 0% -> 3%
where the time goes in v1:
time: 89.5 us; the launch traced here: 89.2 us
  starting transfers between devices  33 us (37%)
  waiting for transfers between devices  32.2 us (36%)
  Pallas kernels  19.8 us (22%)
  local copies, waits for them, and re-layouts  3.96 us (4%)
    ppermute x28, starting transfers between devices, swap(): lax.ppermute(value, axis, [(index, index ^ mask) for index in range(size)])  33 us
    ppermute x28, waiting for transfers between devices, swap(): lax.ppermute(value, axis, [(index, index ^ mask) for index in range(size)])  32.2 us
    pallas_call x1, Pallas kernels, finish(): pl.pallas_call(functools.partial(finish_kernel, total), out_shape=jax.Sha...  6.39 us
    pallas_call x1, Pallas kernels, middle(): pl.pallas_call(functools.partial(middle_kernel, total), out_shape=jax.Sha...  5.72 us
    unnamed x9, local copies, waits for them, and re-layouts  3.96 us
    pallas_call x2, Pallas kernels, product(): pl.pallas_call(functools.partial(product_kernel, offsets), out_shape=(sha...  3.76 us
    pallas_call x1, Pallas kernels, prep(): pl.pallas_call(prep_kernel, grid_spec=pltpu.PrefetchScalarGridSpec(num_sc...  2.73 us
  transfers between devices with their start and end apart: 28, of which 23 were waited for; matrix products, arithmetic and copies ran while one was open for 1% of the time, Pallas kernels for 3%

profile of v1, /device:TPU:0, one launch (start us, length us, event | category | flops | bytes accessed | tf_op | source)
XLA Modules:
  0.0 89.2 jit_solution(2672097036354453927)
XLA Ops:
  1.8 4.0 %collective-permute-start.2 = (bf16[1,8,32,128]{3,2,1,0:T(8,128)(2,1)S(1)}, bf16[1,8,32,128]{3,2,1,0:T(8,128)(2,1)S(1)}, u32[]{:S(2)}, u32[]{:S(2)}) collective-permute-start(bf16[1,8,32,128]{3,2,1,0:T(8,128)(2,1)S(1)} %bitcast.8), channel_id=1, source_target_pairs={{0,24},{4,28},{8,16},{12,20},{16,8},{20,12},{24,0},{28,4},{1,25},{... | collective-permute-start | bytes 196616 | tf_op jit(solution)/shard_map/ppermute | solution.py:270
  6.4 1.6 %collective-permute-done.2 = bf16[1,8,32,128]{3,2,1,0:T(8,128)(2,1)S(1)} collective-permute-done((bf16[1,8,32,128]{3,2,1,0:T(8,128)(2,1)S(1)}, bf16[1,8,32,128]{3,2,1,0:T(8,128)(2,1)S(1)}, u32[]{:S(2)}, u32[]{:S(2)}) %collective-permute-start.2) | collective-permute-done | bytes 65568 | tf_op jit(solution)/shard_map/ppermute | solution.py:270
  8.1 2.0 %collective-permute-done.1 = bf16[1,8,32,128]{3,2,1,0:T(8,128)(2,1)S(1)} collective-permute-done((bf16[1,8,32,128]{3,2,1,0:T(8,128)(2,1)S(1)}, bf16[1,8,32,128]{3,2,1,0:T(8,128)(2,1)S(1)}, u32[]{:S(2)}, u32[]{:S(2)}) %collective-permute-start.1) | collective-permute-done | bytes 65568 | tf_op jit(solution)/shard_map/ppermute | solution.py:270
  11.6 1.6 %copy-done = bf16[4,8,1,8,4096]{4,3,2,1,0:T(8,128)(2,1)S(1)} copy-done((bf16[4,8,1,8,4096]{4,3,2,1,0:T(8,128)(2,1)S(1)}, bf16[4,8,1,8,4096]{4,3,2,1,0:T(8,128)(2,1)}, u32[]{:S(2)}) %copy-start) | copy-done | bytes 2097176
  13.1 2.7 %prep.1.matrix_ref = bf16[4,8,64,512]{3,2,1,0:T(8,128)(2,1)S(1)} custom-call(s32[2]{0:T(128)S(1)} %pad_add_fusion.place_ref, s32[4,8,1]{2,1,0:T(8,128)S(1)} %copy.6.counts_ref, bf16[4,8,1,8,4096]{4,3,2,1,0:T(8,128)(2,1)S(1)} %copy-done), custom_call_target="tpu_custom_call" | custom-call | tf_op jit(solution)/shard_map/prep/pallas_call | solution.py:98
  15.9 1.9 %product.2 = (bf16[8,32,128]{2,1,0:T(8,128)(2,1)S(1)}, bf16[8,32,128]{2,1,0:T(8,128)(2,1)S(1)}, bf16[8,32,128]{2,1,0:T(8,128)(2,1)S(1)}, bf16[8,32,128]{2,1,0:T(8,128)(2,1)S(1)}) custom-call(s32[2]{0:T(128)S(1)} %pad_add_fusion.place_ref, s32[4,8,1,8]{3,2,1,0:T(1,128)S(1)} %copy-done.2, bf16[4,8,64,512]{3,2,1,0:T(8,128)(2,1)S(1)} %prep.1.matrix_ref, ...), custom_call_target="tpu_custom_call" | custom-call | tf_op jit(solution)/shard_map/product/pallas_call | solution.py:156
  17.8 1.6 %collective-permute-start.4 = (bf16[8,32,128]{2,1,0:T(8,128)(2,1)S(1)}, bf16[8,32,128]{2,1,0:T(8,128)(2,1)S(1)}, u32[]{:S(2)}, u32[]{:S(2)}) collective-permute-start(bf16[8,32,128]{2,1,0:T(8,128)(2,1)S(1)} %get-tuple-element.22), channel_id=1, source_target_pairs={{0,1},{1,0},{2,3},{3,2},{4,5},{5,4},{6,7},{7,6},{8,9},{9,8},{10,11... | collective-permute-start | bytes 196616 | tf_op jit(solution)/shard_map/ppermute | solution.py:270
  19.4 2.6 %collective-permute-start.5 = (bf16[8,32,128]{2,1,0:T(8,128)(2,1)S(1)}, bf16[8,32,128]{2,1,0:T(8,128)(2,1)S(1)}, u32[]{:S(2)}, u32[]{:S(2)}) collective-permute-start(bf16[8,32,128]{2,1,0:T(8,128)(2,1)S(1)} %get-tuple-element.23), channel_id=1, source_target_pairs={{0,2},{1,3},{2,0},{3,1},{4,6},{5,7},{6,4},{7,5},{8,10},{9,11},{10,... | collective-permute-start | bytes 196616 | tf_op jit(solution)/shard_map/ppermute | solution.py:270
  22.4 4.1 %collective-permute-done.5.refs_2_ = bf16[8,32,128]{2,1,0:T(8,128)(2,1)S(1)} collective-permute-done((bf16[8,32,128]{2,1,0:T(8,128)(2,1)S(1)}, bf16[8,32,128]{2,1,0:T(8,128)(2,1)S(1)}, u32[]{:S(2)}, u32[]{:S(2)}) %collective-permute-start.5) | collective-permute-done | bytes 65568 | tf_op jit(solution)/shard_map/ppermute | solution.py:270
  26.4 1.7 %collective-permute-done.6.refs_3_ = bf16[8,32,128]{2,1,0:T(8,128)(2,1)S(1)} collective-permute-done((bf16[8,32,128]{2,1,0:T(8,128)(2,1)S(1)}, bf16[8,32,128]{2,1,0:T(8,128)(2,1)S(1)}, u32[]{:S(2)}, u32[]{:S(2)}) %collective-permute-start.6) | collective-permute-done | bytes 65568 | tf_op jit(solution)/shard_map/ppermute | solution.py:270
  29.8 1.5 %collective-permute-start.10 = (f32[32,128]{1,0:T(8,128)S(1)}, f32[32,128]{1,0:T(8,128)S(1)}, u32[]{:S(2)}, u32[]{:S(2)}) collective-permute-start(f32[32,128]{1,0:T(8,128)S(1)} %add.24), channel_id=1, source_target_pairs={{0,24},{4,28},{8,16},{12,20},{16,8},{20,12},{24,0},{28,4},{1,25},{... | collective-permute-start | bytes 49160 | tf_op jit(solution)/shard_map/ppermute | solution.py:270
  35.6 2.4 %collective-permute-start.13 = (f32[32,128]{1,0:T(8,128)S(1)}, f32[32,128]{1,0:T(8,128)S(1)}, u32[]{:S(2)}, u32[]{:S(2)}) collective-permute-start(f32[32,128]{1,0:T(8,128)S(1)} %add_add_fusion.1.refs_0_), channel_id=1, source_target_pairs={{0,3},{1,2},{2,1},{3,0},{4,7},{5,6},{6,5},{7,4},{8,11},{9,10},{10,... | collective-permute-start | bytes 49160 | tf_op jit(solution)/shard_map/ppermute | solution.py:270
  38.3 1.7 %collective-permute-start.11 = (f32[32,128]{1,0:T(8,128)S(1)}, f32[32,128]{1,0:T(8,128)S(1)}, u32[]{:S(2)}, u32[]{:S(2)}) collective-permute-start(f32[32,128]{1,0:T(8,128)S(1)} %add_add_fusion.1.refs_0_), channel_id=1, source_target_pairs={{0,1},{1,0},{2,3},{3,2},{4,5},{5,4},{6,7},{7,6},{8,9},{9,8},{10,11... | collective-permute-start | bytes 49160 | tf_op jit(solution)/shard_map/ppermute | solution.py:270
  42.6 5.7 %middle.1 = bf16[8,32,128]{2,1,0:T(8,128)(2,1)S(1)} custom-call(f32[8,32,128]{2,1,0:T(8,128)S(1)} %get-tuple-element.19.degree_ref, f32[8,32,128]{2,1,0:T(8,128)S(1)} %get-tuple-element.25.rows_ref, f32[32,128]{1,0:T(8,128)S(1)} %add_add_fusion.1.refs_0_, f32[32,128]{1,0:T(8,128)S(1)} %collective-permute-done.11.refs_1_, ...), custom_call_target="tpu_custom_call" | custom-call | tf_op jit(solution)/shard_map/middle/pallas_call | solution.py:234
  48.3 2.5 %collective-permute-start.16 = (bf16[1,8,32,128]{3,2,1,0:T(8,128)(2,1)S(1)}, bf16[1,8,32,128]{3,2,1,0:T(8,128)(2,1)S(1)}, u32[]{:S(2)}, u32[]{:S(2)}) collective-permute-start(bf16[1,8,32,128]{3,2,1,0:T(8,128)(2,1)S(1)} %bitcast.4), channel_id=1, source_target_pairs={{0,24},{4,28},{8,16},{12,20},{16,8},{20,12},{24,0},{28,4},{1,25},{... | collective-permute-start | bytes 196616 | tf_op jit(solution)/shard_map/ppermute | solution.py:270
  51.9 1.7 %collective-permute-done.16 = bf16[1,8,32,128]{3,2,1,0:T(8,128)(2,1)S(1)} collective-permute-done((bf16[1,8,32,128]{3,2,1,0:T(8,128)(2,1)S(1)}, bf16[1,8,32,128]{3,2,1,0:T(8,128)(2,1)S(1)}, u32[]{:S(2)}, u32[]{:S(2)}) %collective-permute-start.16) | collective-permute-done | bytes 65568 | tf_op jit(solution)/shard_map/ppermute | solution.py:270
  53.5 1.6 %collective-permute-done.15 = bf16[1,8,32,128]{3,2,1,0:T(8,128)(2,1)S(1)} collective-permute-done((bf16[1,8,32,128]{3,2,1,0:T(8,128)(2,1)S(1)}, bf16[1,8,32,128]{3,2,1,0:T(8,128)(2,1)S(1)}, u32[]{:S(2)}, u32[]{:S(2)}) %collective-permute-start.15) | collective-permute-done | bytes 65568 | tf_op jit(solution)/shard_map/ppermute | solution.py:270
  55.7 1.5 %collective-permute-done.17.refs_1_ = bf16[4,8,32,128]{3,2,1,0:T(8,128)(2,1)S(1)} collective-permute-done((bf16[4,8,32,128]{3,2,1,0:T(8,128)(2,1)S(1)}, bf16[4,8,32,128]{3,2,1,0:T(8,128)(2,1)S(1)}, u32[]{:S(2)}, u32[]{:S(2)}) %collective-permute-start.17) | collective-permute-done | bytes 262176 | tf_op jit(solution)/shard_map/ppermute | solution.py:270
  57.2 1.9 %product.3 = (bf16[8,32,128]{2,1,0:T(8,128)(2,1)S(1)}, bf16[8,32,128]{2,1,0:T(8,128)(2,1)S(1)}, bf16[8,32,128]{2,1,0:T(8,128)(2,1)S(1)}, bf16[8,32,128]{2,1,0:T(8,128)(2,1)S(1)}) custom-call(s32[2]{0:T(128)S(1)} %pad_add_fusion.place_ref, s32[4,8,1,8]{3,2,1,0:T(1,128)S(1)} %copy-done.2, bf16[4,8,64,512]{3,2,1,0:T(8,128)(2,1)S(1)} %prep.1.matrix_ref, ...), custom_call_target="tpu_custom_call" | custom-call | tf_op jit(solution)/shard_map/product/pallas_call | solution.py:156
  61.6 2.0 %collective-permute-start.20 = (bf16[8,32,128]{2,1,0:T(8,128)(2,1)S(1)}, bf16[8,32,128]{2,1,0:T(8,128)(2,1)S(1)}, u32[]{:S(2)}, u32[]{:S(2)}) collective-permute-start(bf16[8,32,128]{2,1,0:T(8,128)(2,1)S(1)} %get-tuple-element.30), channel_id=1, source_target_pairs={{0,3},{1,2},{2,1},{3,0},{4,7},{5,6},{6,5},{7,4},{8,11},{9,10},{10,... | collective-permute-start | bytes 196616 | tf_op jit(solution)/shard_map/ppermute | solution.py:270
  63.6 5.0 %collective-permute-done.19.refs_2_ = bf16[8,32,128]{2,1,0:T(8,128)(2,1)S(1)} collective-permute-done((bf16[8,32,128]{2,1,0:T(8,128)(2,1)S(1)}, bf16[8,32,128]{2,1,0:T(8,128)(2,1)S(1)}, u32[]{:S(2)}, u32[]{:S(2)}) %collective-permute-start.19) | collective-permute-done | bytes 65568 | tf_op jit(solution)/shard_map/ppermute | solution.py:270
  75.9 2.1 %collective-permute-start.27 = (f32[32,128]{1,0:T(8,128)S(1)}, f32[32,128]{1,0:T(8,128)S(1)}, u32[]{:S(2)}, u32[]{:S(2)}) collective-permute-start(f32[32,128]{1,0:T(8,128)S(1)} %add_add_fusion.refs_0_), channel_id=1, source_target_pairs={{0,3},{1,2},{2,1},{3,0},{4,7},{5,6},{6,5},{7,4},{8,11},{9,10},{10,... | collective-permute-start | bytes 49160 | tf_op jit(solution)/shard_map/ppermute | solution.py:270
  78.7 1.6 %collective-permute-start.25 = (f32[32,128]{1,0:T(8,128)S(1)}, f32[32,128]{1,0:T(8,128)S(1)}, u32[]{:S(2)}, u32[]{:S(2)}) collective-permute-start(f32[32,128]{1,0:T(8,128)S(1)} %add_add_fusion.refs_0_), channel_id=1, source_target_pairs={{0,1},{1,0},{2,3},{3,2},{4,5},{5,4},{6,7},{7,6},{8,9},{9,8},{10,11... | collective-permute-start | bytes 49160 | tf_op jit(solution)/shard_map/ppermute | solution.py:270
  82.9 6.4 %finish.1 = f32[1,8,4096]{2,1,0:T(8,128)} custom-call(f32[8,32,128]{2,1,0:T(8,128)S(1)} %get-tuple-element.31.rows_ref, f32[32,128]{1,0:T(8,128)S(1)} %add_add_fusion.refs_0_, f32[32,128]{1,0:T(8,128)S(1)} %collective-permute-done.25.refs_1_, f32[32,128]{1,0:T(8,128)S(1)} %collective-permute-done.26.refs_2_, f32[32,128]{1,0:T(8,128)S(1)} %collective-permute-done.27.refs_3_), custom_call_target="tpu_custom_call" | custom-call | tf_op jit(solution)/shard_map/finish/pallas_call | solution.py:257
  (56 shorter events, 27.8 us)
Async XLA Ops:
  1.8 6.2 %collective-permute-start.2 = (bf16[1,8,32,128]{3,2,1,0:T(8,128)(2,1)S(1)}, bf16[1,8,32,128]{3,2,1,0:T(8,128)(2,1)S(1)}, u32[]{:S(2)}, u32[]{:S(2)}) collective-permute-start(bf16[1,8,32,128]{3,2,1,0:T(8,128)(2,1)S(1)} %bitcast.8), channel_id=1, source_target_pairs={{0,24},{4,28},{8,16},{12,20},{16,8},{20,12},{24,0},{28,4},{1,25},{... | collective-permute-start | bytes 196616 | tf_op jit(solution)/shard_map/ppermute | solution.py:270
  5.8 4.3 %collective-permute-start.1 = (bf16[1,8,32,128]{3,2,1,0:T(8,128)(2,1)S(1)}, bf16[1,8,32,128]{3,2,1,0:T(8,128)(2,1)S(1)}, u32[]{:S(2)}, u32[]{:S(2)}) collective-permute-start(bf16[1,8,32,128]{3,2,1,0:T(8,128)(2,1)S(1)} %bitcast.9), channel_id=1, source_target_pairs={{0,16},{4,20},{8,24},{12,28},{16,0},{20,4},{24,8},{28,12},{1,17},{... | collective-permute-start | bytes 196616 | tf_op jit(solution)/shard_map/ppermute | solution.py:270
  6.3 4.3 %collective-permute-start = (bf16[1,8,32,128]{3,2,1,0:T(8,128)(2,1)S(1)}, bf16[1,8,32,128]{3,2,1,0:T(8,128)(2,1)S(1)}, u32[]{:S(2)}, u32[]{:S(2)}) collective-permute-start(bf16[1,8,32,128]{3,2,1,0:T(8,128)(2,1)S(1)} %bitcast.10), channel_id=1, source_target_pairs={{0,8},{4,12},{8,0},{12,4},{16,24},{20,28},{24,16},{28,20},{1,9},{5... | collective-permute-start | bytes 196616 | tf_op jit(solution)/shard_map/ppermute | solution.py:270
  10.6 5.3 %collective-permute-start.3 = (bf16[4,8,32,128]{3,2,1,0:T(8,128)(2,1)S(1)}, bf16[4,8,32,128]{3,2,1,0:T(8,128)(2,1)S(1)}, u32[]{:S(2)}, u32[]{:S(2)}) collective-permute-start(bf16[4,8,32,128]{3,2,1,0:T(8,128)(2,1)S(1)} %pad_maximum_fusion.refs_0_), channel_id=1, source_target_pairs={{0,4},{4,0},{8,12},{12,8},{16,20},{20,16},{24,28},{28,24},{1,5},{5... | collective-permute-start | bytes 786440 | tf_op jit(solution)/shard_map/ppermute | solution.py:270
  17.8 4.6 %collective-permute-start.4 = (bf16[8,32,128]{2,1,0:T(8,128)(2,1)S(1)}, bf16[8,32,128]{2,1,0:T(8,128)(2,1)S(1)}, u32[]{:S(2)}, u32[]{:S(2)}) collective-permute-start(bf16[8,32,128]{2,1,0:T(8,128)(2,1)S(1)} %get-tuple-element.22), channel_id=1, source_target_pairs={{0,1},{1,0},{2,3},{3,2},{4,5},{5,4},{6,7},{7,6},{8,9},{9,8},{10,11... | collective-permute-start | bytes 196616 | tf_op jit(solution)/shard_map/ppermute | solution.py:270
  19.4 7.0 %collective-permute-start.5 = (bf16[8,32,128]{2,1,0:T(8,128)(2,1)S(1)}, bf16[8,32,128]{2,1,0:T(8,128)(2,1)S(1)}, u32[]{:S(2)}, u32[]{:S(2)}) collective-permute-start(bf16[8,32,128]{2,1,0:T(8,128)(2,1)S(1)} %get-tuple-element.23), channel_id=1, source_target_pairs={{0,2},{1,3},{2,0},{3,1},{4,6},{5,7},{6,4},{7,5},{8,10},{9,11},{10,... | collective-permute-start | bytes 196616 | tf_op jit(solution)/shard_map/ppermute | solution.py:270
  22.0 6.1 %collective-permute-start.6 = (bf16[8,32,128]{2,1,0:T(8,128)(2,1)S(1)}, bf16[8,32,128]{2,1,0:T(8,128)(2,1)S(1)}, u32[]{:S(2)}, u32[]{:S(2)}) collective-permute-start(bf16[8,32,128]{2,1,0:T(8,128)(2,1)S(1)} %get-tuple-element.24), channel_id=1, source_target_pairs={{0,3},{1,2},{2,1},{3,0},{4,7},{5,6},{6,5},{7,4},{8,11},{9,10},{10,... | collective-permute-start | bytes 196616 | tf_op jit(solution)/shard_map/ppermute | solution.py:270
  29.8 4.6 %collective-permute-start.10 = (f32[32,128]{1,0:T(8,128)S(1)}, f32[32,128]{1,0:T(8,128)S(1)}, u32[]{:S(2)}, u32[]{:S(2)}) collective-permute-start(f32[32,128]{1,0:T(8,128)S(1)} %add.24), channel_id=1, source_target_pairs={{0,24},{4,28},{8,16},{12,20},{16,8},{20,12},{24,0},{28,4},{1,25},{... | collective-permute-start | bytes 49160 | tf_op jit(solution)/shard_map/ppermute | solution.py:270
  31.3 3.7 %collective-permute-start.9 = (f32[32,128]{1,0:T(8,128)S(1)}, f32[32,128]{1,0:T(8,128)S(1)}, u32[]{:S(2)}, u32[]{:S(2)}) collective-permute-start(f32[32,128]{1,0:T(8,128)S(1)} %add.24), channel_id=1, source_target_pairs={{0,16},{4,20},{8,24},{12,28},{16,0},{20,4},{24,8},{28,12},{1,17},{... | collective-permute-start | bytes 49160 | tf_op jit(solution)/shard_map/ppermute | solution.py:270
  31.8 3.7 %collective-permute-start.8 = (f32[32,128]{1,0:T(8,128)S(1)}, f32[32,128]{1,0:T(8,128)S(1)}, u32[]{:S(2)}, u32[]{:S(2)}) collective-permute-start(f32[32,128]{1,0:T(8,128)S(1)} %add.24), channel_id=1, source_target_pairs={{0,8},{4,12},{8,0},{12,4},{16,24},{20,28},{24,16},{28,20},{1,9},{5... | collective-permute-start | bytes 49160 | tf_op jit(solution)/shard_map/ppermute | solution.py:270
  35.6 5.6 %collective-permute-start.13 = (f32[32,128]{1,0:T(8,128)S(1)}, f32[32,128]{1,0:T(8,128)S(1)}, u32[]{:S(2)}, u32[]{:S(2)}) collective-permute-start(f32[32,128]{1,0:T(8,128)S(1)} %add_add_fusion.1.refs_0_), channel_id=1, source_target_pairs={{0,3},{1,2},{2,1},{3,0},{4,7},{5,6},{6,5},{7,4},{8,11},{9,10},{10,... | collective-permute-start | bytes 49160 | tf_op jit(solution)/shard_map/ppermute | solution.py:270
  37.9 4.6 %collective-permute-start.12 = (f32[32,128]{1,0:T(8,128)S(1)}, f32[32,128]{1,0:T(8,128)S(1)}, u32[]{:S(2)}, u32[]{:S(2)}) collective-permute-start(f32[32,128]{1,0:T(8,128)S(1)} %add_add_fusion.1.refs_0_), channel_id=1, source_target_pairs={{0,2},{1,3},{2,0},{3,1},{4,6},{5,7},{6,4},{7,5},{8,10},{9,11},{10,... | collective-permute-start | bytes 49160 | tf_op jit(solution)/shard_map/ppermute | solution.py:270
  38.3 4.3 %collective-permute-start.11 = (f32[32,128]{1,0:T(8,128)S(1)}, f32[32,128]{1,0:T(8,128)S(1)}, u32[]{:S(2)}, u32[]{:S(2)}) collective-permute-start(f32[32,128]{1,0:T(8,128)S(1)} %add_add_fusion.1.refs_0_), channel_id=1, source_target_pairs={{0,1},{1,0},{2,3},{3,2},{4,5},{5,4},{6,7},{7,6},{8,9},{9,8},{10,11... | collective-permute-start | bytes 49160 | tf_op jit(solution)/shard_map/ppermute | solution.py:270
  48.3 5.2 %collective-permute-start.16 = (bf16[1,8,32,128]{3,2,1,0:T(8,128)(2,1)S(1)}, bf16[1,8,32,128]{3,2,1,0:T(8,128)(2,1)S(1)}, u32[]{:S(2)}, u32[]{:S(2)}) collective-permute-start(bf16[1,8,32,128]{3,2,1,0:T(8,128)(2,1)S(1)} %bitcast.4), channel_id=1, source_target_pairs={{0,24},{4,28},{8,16},{12,20},{16,8},{20,12},{24,0},{28,4},{1,25},{... | collective-permute-start | bytes 196616 | tf_op jit(solution)/shard_map/ppermute | solution.py:270
  50.8 4.3 %collective-permute-start.15 = (bf16[1,8,32,128]{3,2,1,0:T(8,128)(2,1)S(1)}, bf16[1,8,32,128]{3,2,1,0:T(8,128)(2,1)S(1)}, u32[]{:S(2)}, u32[]{:S(2)}) collective-permute-start(bf16[1,8,32,128]{3,2,1,0:T(8,128)(2,1)S(1)} %bitcast.5), channel_id=1, source_target_pairs={{0,16},{4,20},{8,24},{12,28},{16,0},{20,4},{24,8},{28,12},{1,17},{... | collective-permute-start | bytes 196616 | tf_op jit(solution)/shard_map/ppermute | solution.py:270
  51.3 4.3 %collective-permute-start.14 = (bf16[1,8,32,128]{3,2,1,0:T(8,128)(2,1)S(1)}, bf16[1,8,32,128]{3,2,1,0:T(8,128)(2,1)S(1)}, u32[]{:S(2)}, u32[]{:S(2)}) collective-permute-start(bf16[1,8,32,128]{3,2,1,0:T(8,128)(2,1)S(1)} %bitcast.6), channel_id=1, source_target_pairs={{0,8},{4,12},{8,0},{12,4},{16,24},{20,28},{24,16},{28,20},{1,9},{5... | collective-permute-start | bytes 196616 | tf_op jit(solution)/shard_map/ppermute | solution.py:270
  59.1 4.5 %collective-permute-start.18 = (bf16[8,32,128]{2,1,0:T(8,128)(2,1)S(1)}, bf16[8,32,128]{2,1,0:T(8,128)(2,1)S(1)}, u32[]{:S(2)}, u32[]{:S(2)}) collective-permute-start(bf16[8,32,128]{2,1,0:T(8,128)(2,1)S(1)} %get-tuple-element.28), channel_id=1, source_target_pairs={{0,1},{1,0},{2,3},{3,2},{4,5},{5,4},{6,7},{7,6},{8,9},{9,8},{10,11... | collective-permute-start | bytes 196616 | tf_op jit(solution)/shard_map/ppermute | solution.py:270
  60.3 8.2 %collective-permute-start.19 = (bf16[8,32,128]{2,1,0:T(8,128)(2,1)S(1)}, bf16[8,32,128]{2,1,0:T(8,128)(2,1)S(1)}, u32[]{:S(2)}, u32[]{:S(2)}) collective-permute-start(bf16[8,32,128]{2,1,0:T(8,128)(2,1)S(1)} %get-tuple-element.29), channel_id=1, source_target_pairs={{0,2},{1,3},{2,0},{3,1},{4,6},{5,7},{6,4},{7,5},{8,10},{9,11},{10,... | collective-permute-start | bytes 196616 | tf_op jit(solution)/shard_map/ppermute | solution.py:270
  61.6 7.0 %collective-permute-start.20 = (bf16[8,32,128]{2,1,0:T(8,128)(2,1)S(1)}, bf16[8,32,128]{2,1,0:T(8,128)(2,1)S(1)}, u32[]{:S(2)}, u32[]{:S(2)}) collective-permute-start(bf16[8,32,128]{2,1,0:T(8,128)(2,1)S(1)} %get-tuple-element.30), channel_id=1, source_target_pairs={{0,3},{1,2},{2,1},{3,0},{4,7},{5,6},{6,5},{7,4},{8,11},{9,10},{10,... | collective-permute-start | bytes 196616 | tf_op jit(solution)/shard_map/ppermute | solution.py:270
  70.2 4.6 %collective-permute-start.24 = (f32[32,128]{1,0:T(8,128)S(1)}, f32[32,128]{1,0:T(8,128)S(1)}, u32[]{:S(2)}, u32[]{:S(2)}) collective-permute-start(f32[32,128]{1,0:T(8,128)S(1)} %add.28), channel_id=1, source_target_pairs={{0,24},{4,28},{8,16},{12,20},{16,8},{20,12},{24,0},{28,4},{1,25},{... | collective-permute-start | bytes 49160 | tf_op jit(solution)/shard_map/ppermute | solution.py:270
  71.7 3.7 %collective-permute-start.23 = (f32[32,128]{1,0:T(8,128)S(1)}, f32[32,128]{1,0:T(8,128)S(1)}, u32[]{:S(2)}, u32[]{:S(2)}) collective-permute-start(f32[32,128]{1,0:T(8,128)S(1)} %add.28), channel_id=1, source_target_pairs={{0,16},{4,20},{8,24},{12,28},{16,0},{20,4},{24,8},{28,12},{1,17},{... | collective-permute-start | bytes 49160 | tf_op jit(solution)/shard_map/ppermute | solution.py:270
  75.9 5.6 %collective-permute-start.27 = (f32[32,128]{1,0:T(8,128)S(1)}, f32[32,128]{1,0:T(8,128)S(1)}, u32[]{:S(2)}, u32[]{:S(2)}) collective-permute-start(f32[32,128]{1,0:T(8,128)S(1)} %add_add_fusion.refs_0_), channel_id=1, source_target_pairs={{0,3},{1,2},{2,1},{3,0},{4,7},{5,6},{6,5},{7,4},{8,11},{9,10},{10,... | collective-permute-start | bytes 49160 | tf_op jit(solution)/shard_map/ppermute | solution.py:270
  78.1 4.8 %collective-permute-start.26 = (f32[32,128]{1,0:T(8,128)S(1)}, f32[32,128]{1,0:T(8,128)S(1)}, u32[]{:S(2)}, u32[]{:S(2)}) collective-permute-start(f32[32,128]{1,0:T(8,128)S(1)} %add_add_fusion.refs_0_), channel_id=1, source_target_pairs={{0,2},{1,3},{2,0},{3,1},{4,6},{5,7},{6,4},{7,5},{8,10},{9,11},{10,... | collective-permute-start | bytes 49160 | tf_op jit(solution)/shard_map/ppermute | solution.py:270
  78.7 4.1 %collective-permute-start.25 = (f32[32,128]{1,0:T(8,128)S(1)}, f32[32,128]{1,0:T(8,128)S(1)}, u32[]{:S(2)}, u32[]{:S(2)}) collective-permute-start(f32[32,128]{1,0:T(8,128)S(1)} %add_add_fusion.refs_0_), channel_id=1, source_target_pairs={{0,1},{1,0},{2,3},{3,2},{4,5},{5,4},{6,7},{7,6},{8,9},{9,8},{10,11... | collective-permute-start | bytes 49160 | tf_op jit(solution)/shard_map/ppermute | solution.py:270
  (8 other events, 13.7 us)

commit v2 on v1

--- a/solution.py
+++ b/solution.py
@@ -7,7 +7,6 @@
 from jax.experimental.pallas import tpu as pltpu
 from jax.sharding import PartitionSpec as P
 
-ITERS = 2
 BF16 = jnp.bfloat16
 F32 = jnp.float32
 HIGHEST = lax.Precision.HIGHEST
@@ -30,9 +29,17 @@
     return lax.broadcasted_iota(jnp.int32, shape, dim)
 
 
-def start_kernel(panel_ref, inv_ref, scaled_ref, degree_ref, scratch):
+def start_kernel(panel_hbm, inv_hbm, scaled_ref, degree_ref, panel_ref, inv_ref, scratch, sems):
     block_rows, block_size = inv_ref.shape[1], inv_ref.shape[2]
     half = block_size // 2
+    copies = [
+        pltpu.make_async_copy(inv_hbm, inv_ref, sems.at[0]),
+        pltpu.make_async_copy(panel_hbm, panel_ref, sems.at[1]),
+    ]
+    for copy in copies:
+        copy.start()
+    for copy in copies:
+        copy.wait()
     for t in range(half):
         scratch[t * block_rows : (t + 1) * block_rows, :] = panel_ref[0, :, t * 128 : (t + 1) * 128]
     pair = iota((half, block_size), 1) // 2 == iota((half, block_size), 0)
@@ -56,15 +63,21 @@
     return pl.pallas_call(
         start_kernel,
         out_shape=(jax.ShapeDtypeStruct(shape, BF16), jax.ShapeDtypeStruct(shape, F32)),
-        in_specs=[vmem(), vmem()],
+        in_specs=[pl.BlockSpec(memory_space=pl.ANY)] * 2,
         out_specs=(vmem(), vmem()),
-        scratch_shapes=[pltpu.VMEM((block_rows * block_size // 2, 128), F32)],
+        scratch_shapes=[
+            pltpu.VMEM(panel.shape, F32),
+            pltpu.VMEM(inv_degree.shape, F32),
+            pltpu.VMEM((block_rows * block_size // 2, 128), F32),
+            pltpu.SemaphoreType.DMA((2,)),
+        ],
         compiler_params=params(),
         name="start",
     )(panel, inv_degree)
 
 
-def prep_kernel(place_ref, counts_ref, affinity_ref, out_ref, scratch):
+def prep_kernel(place_ref, counts_ref, affinity_ref, out_ref, done_ref, scratch):
+    done_ref[...] = jnp.zeros_like(done_ref)
     block_rows, slots = affinity_ref.shape[1], affinity_ref.shape[3]
     half = affinity_ref.shape[4] // 128
     group = pl.program_id(0) ^ place_ref[1]
@@ -106,26 +119,69 @@
                     lambda m, place, counts: (m ^ place[1], 0, 0, 0, 0),
                 )
             ],
-            out_specs=pl.BlockSpec(
-                (1, block_rows, 64, slots * 64), lambda m, place, counts: (m, 0, 0, 0)
-            ),
+            out_specs=[
+                pl.BlockSpec(
+                    (1, block_rows, 64, slots * 64), lambda m, place, counts: (m, 0, 0, 0)
+                ),
+                pl.BlockSpec((8, 128), lambda m, place, counts: (0, 0)),
+            ],
             scratch_shapes=[pltpu.VMEM((2, flat // 128 * slots, 128), F32)],
         ),
-        out_shape=jax.ShapeDtypeStruct((groups, block_rows, 64, slots * 64), BF16),
+        out_shape=[
+            jax.ShapeDtypeStruct((groups, block_rows, 64, slots * 64), BF16),
+            jax.ShapeDtypeStruct((8, 128), F32),
+        ],
         compiler_params=params(),
         name="prep",
     )(place, block_counts, affinity)
 
 
-def product_kernel(offsets, place_ref, columns_ref, matrix_ref, *refs):
+def stack_kernel(count, *refs):
+    for index in range(count):
+        refs[-1][index] = refs[index][...]
+
+
+def stack(pieces, after):
+    shape = pieces[0].shape
+    return pl.pallas_call(
+        functools.partial(stack_kernel, len(pieces)),
+        out_shape=jax.ShapeDtypeStruct((len(pieces),) + shape, BF16),
+        in_specs=[vmem()] * (len(pieces) + len(after)),
+        out_specs=vmem(),
+        compiler_params=params(),
+        name="stack",
+    )(*pieces, *after)
+
+
+def split(value):
+    high = value.astype(BF16)
+    rest = value - high.astype(F32)
+    middle = rest.astype(BF16)
+    return high, middle, (rest - middle.astype(F32)).astype(BF16)
+
+
+def joined(ref, where, first):
+    high, middle, low = (ref[(*where, first + part)].astype(F32) for part in range(3))
+    return high + (middle + low)
+
+
+def product_kernel(offsets, with_gram, place_ref, columns_ref, matrix_ref, *refs):
     pieces, outs, table = refs[:2], refs[2:-1], refs[-1]
     groups, block_rows, block_size, _ = matrix_ref.shape
     slots = columns_ref.shape[3]
     half = block_size // 2
     blocks = table.shape[0]
+    per_piece = len(offsets) // 2
     low = iota((half, 128), 1) < 64
+    if with_gram:
+        gram = joined(pieces[0], (0,), block_rows)
+        for index in range(1, len(offsets)):
+            gram = gram + joined(pieces[index // per_piece], (index % per_piece,), block_rows)
+        outs[-1][...] = gram
+        for part, value in enumerate(split(gram)):
+            for m in range(1, groups):
+                outs[m][block_rows + part] = value
     for index, offset in enumerate(offsets):
-        per_piece = len(offsets) // 2
         source = pieces[index // per_piece]
         base = (place_ref[0] ^ offset) * block_rows
         for i in range(block_rows):
@@ -151,53 +207,95 @@
 
 def product(offsets, place, block_columns, matrix, near, far):
     groups, block_rows, block_size, _ = matrix.shape
+    with_gram = near.shape[1] > block_rows
+    half = block_size // 2
     blocks = 2 * near.shape[0] * block_rows
-    shape = jax.ShapeDtypeStruct((block_rows, block_size // 2, 128), BF16)
-    return pl.pallas_call(
-        functools.partial(product_kernel, offsets),
-        out_shape=(shape,) * groups,
+    shapes = [jax.ShapeDtypeStruct((block_rows, half, 128), BF16)]
+    shapes += [jax.ShapeDtypeStruct(near.shape[1:], BF16)] * (groups - 1)
+    if with_gram:
+        shapes.append(jax.ShapeDtypeStruct((32, 128), F32))
+    return pl.pallas_call(
+        functools.partial(product_kernel, offsets, with_gram),
+        out_shape=shapes,
         in_specs=[smem(), smem(), vmem(), vmem(), vmem()],
-        out_specs=(vmem(),) * groups,
+        out_specs=[vmem()] * len(shapes),
         scratch_shapes=[pltpu.VMEM((blocks, block_size, 128), BF16)],
         compiler_params=params(),
         name="product",
     )(place, block_columns, matrix, near, far)
 
 
-def collect_kernel(degree_ref, *refs):
-    terms, rows_ref, gram_ref = refs[:-2], refs[-2], refs[-1]
+def add_terms(terms, block_rows):
     summed = terms[0][...].astype(F32)
     for term in terms[1:]:
-        summed = summed + term[...].astype(F32)
-    rows = summed * degree_ref[...]
-    rows_ref[...] = rows
+        summed = summed + term[:block_rows].astype(F32)
+    return summed
+
+
+def local_gram(rows):
     flat = rows.reshape(-1, 128)
     both = lax.dot_general(
         flat, flat, (((0,), (0,)), ((), ())), precision=HIGHEST, preferred_element_type=F32
     )
     gram = both[:64, :64] + both[64:, 64:]
-    gram_ref[...] = jnp.concatenate([gram[:32], gram[32:]], axis=1)
-
-
-def collect(degree, terms):
-    return pl.pallas_call(
-        collect_kernel,
-        out_shape=(
-            jax.ShapeDtypeStruct(degree.shape, F32),
-            jax.ShapeDtypeStruct((32, 128), F32),
-        ),
+    return jnp.concatenate([gram[:32], gram[32:]], axis=1)
+
+
+def middle_kernel(degree_ref, *refs):
+    terms, out_ref = refs[:-1], refs[-1]
+    block_rows = degree_ref.shape[0]
+    degree = degree_ref[...]
+    rows = add_terms(terms, block_rows) * degree
+    out_ref[:block_rows] = (rows * degree).astype(BF16)
+    for part, value in enumerate(split(local_gram(rows))):
+        out_ref[block_rows + part] = value
+
+
+def middle(degree, terms):
+    block_rows, half, width = degree.shape
+    return pl.pallas_call(
+        middle_kernel,
+        out_shape=jax.ShapeDtypeStruct((block_rows + 3, half, width), BF16),
         in_specs=[vmem()] * (1 + len(terms)),
-        out_specs=(vmem(), vmem()),
+        out_specs=vmem(),
+        compiler_params=params(),
+        name="middle",
+    )(degree, *terms)
+
+
+def collect_kernel(total, degree_ref, first_ref, *refs):
+    terms, (rows_ref, gram_ref, first_out_ref) = refs[:-3], refs[-3:]
+    block_rows = degree_ref.shape[0]
+    first = first_ref[...]
+    for term in terms[1:]:
+        first = first + joined(term, (), block_rows)
+    first = first / total
+    row, lane = iota(first.shape, 0), iota(first.shape, 1)
+    diagonal = lane % 64 == row + lane // 64 * 32
+    trace = jnp.sum(jnp.where(diagonal, first, 0.0), axis=(0, 1), keepdims=True)
+    scale = lax.rsqrt(trace / 64.0)
+    first_out_ref[...] = first * (scale * scale)
+    rows = add_terms(terms, block_rows) * degree_ref[...] * scale[None]
+    rows_ref[...] = rows
+    gram_ref[...] = local_gram(rows)
+
+
+def collect(total, degree, first, terms):
+    small = jax.ShapeDtypeStruct((32, 128), F32)
+    return pl.pallas_call(
+        functools.partial(collect_kernel, total),
+        out_shape=(jax.ShapeDtypeStruct(degree.shape, F32), small, small),
+        in_specs=[vmem()] * (2 + len(terms)),
+        out_specs=(vmem(),) * 3,
         compiler_params=params(),
         name="collect",
-    )(degree, *terms)
-
-
-def inverse_factor(gram):
+    )(degree, first, *terms)
+
+
+def factor_and_solve(gram, right):
     size = gram.shape[0]
     row_at = iota((size, 128), 0)
-    unit = (iota((size, 64), 0) == iota((size, 64), 1)).astype(F32)
-    work = jnp.concatenate([gram, unit], axis=1)
+    work = jnp.concatenate([gram, right], axis=1)
     for j in range(size):
         column = jnp.broadcast_to(work[:, j : j + 1], (size, 128))
         scale = lax.rsqrt(column[j : j + 1])
@@ -207,62 +305,65 @@
     return work[:, 64:]
 
 
-def unpack_gram(parts, total):
-    packed = parts[0][...]
-    for part in parts[1:]:
+def unpacked(packed):
+    return jnp.concatenate([packed[:, :64], packed[:, 64:]], axis=0)
+
+
+def first_factor_kernel(gram_ref, out_ref):
+    unit = (iota((64, 64), 0) == iota((64, 64), 1)).astype(F32)
+    out_ref[...] = factor_and_solve(unpacked(gram_ref[...]), unit)
+
+
+def first_factor(gram):
+    return pl.pallas_call(
+        first_factor_kernel,
+        out_shape=jax.ShapeDtypeStruct((64, 64), F32),
+        in_specs=[vmem()],
+        out_specs=vmem(),
+        compiler_params=params(),
+        name="first_factor",
+    )(gram)
+
+
+def dot_turned(left, right):
+    return lax.dot_general(
+        left, right, (((1,), (1,)), ((), ())), precision=HIGHEST, preferred_element_type=F32
+    )
+
+
+def finish_kernel(total, rows_ref, inverse_ref, *refs):
+    out_ref, scratch = refs[-2:]
+    block_rows, half, _ = rows_ref.shape
+    packed = refs[0][...]
+    for part in refs[1:-2]:
         packed = packed + part[...]
-    return jnp.concatenate([packed[:, :64], packed[:, 64:]], axis=0) / total
-
-
-def apply_factor(rows, inverse):
+    first = inverse_ref[...]
+    gram = dot_turned(
+        jnp.dot(first, unpacked(packed), precision=HIGHEST, preferred_element_type=F32), first
+    )
+    inverse = factor_and_solve(gram / total, first)
     zero = jnp.zeros_like(inverse)
     both = jnp.concatenate(
         [jnp.concatenate([inverse, zero], axis=1), jnp.concatenate([zero, inverse], axis=1)], axis=0
     )
-    return lax.dot_general(
-        rows, both, (((1,), (1,)), ((), ())), precision=HIGHEST, preferred_element_type=F32
-    )
-
-
-def middle_kernel(total, degree_ref, rows_ref, *refs):
-    inverse = inverse_factor(unpack_gram(refs[:-1], total))
-    current = apply_factor(rows_ref[...].reshape(-1, 128), inverse)
-    refs[-1][...] = (current.reshape(degree_ref.shape) * degree_ref[...]).astype(BF16)
-
-
-def middle(total, degree, rows, grams):
-    return pl.pallas_call(
-        functools.partial(middle_kernel, total),
-        out_shape=jax.ShapeDtypeStruct(degree.shape, BF16),
-        in_specs=[vmem()] * (2 + len(grams)),
-        out_specs=vmem(),
-        compiler_params=params(),
-        name="middle",
-    )(degree, rows, *grams)
-
-
-def finish_kernel(total, rows_ref, *refs):
-    out_ref, scratch = refs[-2:]
-    block_rows, half, _ = rows_ref.shape
-    inverse = inverse_factor(unpack_gram(refs[:-2], total))
-    current = apply_factor(rows_ref[...].reshape(-1, 128), inverse)
+    current = dot_turned(rows_ref[...].reshape(-1, 128), both)
     for i in range(block_rows):
         scratch[pl.ds(i, half, stride=block_rows), :] = current[i * half : (i + 1) * half]
     for t in range(half):
         out_ref[0, :, t * 128 : (t + 1) * 128] = scratch[t * block_rows : (t + 1) * block_rows, :]
 
 
-def finish(total, rows, grams):
+def finish(total, rows, inverse, grams):
     block_rows, half, _ = rows.shape
     return pl.pallas_call(
         functools.partial(finish_kernel, total),
         out_shape=jax.ShapeDtypeStruct((1, block_rows, half * 128), F32),
-        in_specs=[vmem()] * (1 + len(grams)),
+        in_specs=[vmem()] * (2 + len(grams)),
         out_specs=vmem(),
         scratch_shapes=[pltpu.VMEM((block_rows * half, 128), F32)],
         compiler_params=params(),
         name="finish",
-    )(rows, *grams)
+    )(rows, inverse, *grams)
 
 
 def swap(value, axis, mask):
@@ -280,15 +381,16 @@
     return bits
 
 
-def gather_rows(scaled):
+def gather_rows(message, after):
     plan = stages(lax.axis_size("rows"))
-    held, offsets = scaled[None], [0]
+    held, offsets = [message], [0]
     for masks in plan[:-1]:
-        held = jnp.concatenate([held] + [swap(held, "rows", mask) for mask in masks], axis=0)
+        held = held + [swap(piece, "rows", mask) for mask in masks for piece in held]
         offsets = offsets + [mask ^ offset for mask in masks for offset in offsets]
+    near = stack(held, after)
     (last,) = plan[-1]
     offsets = offsets + [last ^ offset for offset in offsets]
-    return held, swap(held, "rows", last), offsets
+    return near, swap(near, "rows", last), offsets
 
 
 def add_grams(gram):
@@ -303,16 +405,17 @@
     total = float(groups * lax.axis_size("rows") * block_rows * block_size)
     place = jnp.stack([lax.axis_index("rows"), lax.axis_index("cols")]).astype(jnp.int32)
     scaled, degree = start(panel, inv_degree)
-    matrix = prep(place, block_counts, affinity)
-    for iteration in range(ITERS):
-        near, far, offsets = gather_rows(scaled)
-        terms = product(offsets, place, block_columns, matrix, near, far)
-        terms = [terms[0]] + [swap(terms[m], "cols", m) for m in range(1, groups)]
-        rows, gram = collect(degree, terms)
-        grams = add_grams(gram)
-        if iteration < ITERS - 1:
-            scaled = middle(total, degree, rows, grams)
-    return finish(total, rows, grams)
+    matrix, done = prep(place, block_counts, affinity)
+    near, far, offsets = gather_rows(scaled, [done])
+    terms = product(offsets, place, block_columns, matrix, near, far)
+    terms = [terms[0]] + [swap(terms[m], "cols", m) for m in range(1, groups)]
+    message = middle(degree, terms)
+    near, far, offsets = gather_rows(message, [])
+    *terms, first = product(offsets, place, block_columns, matrix, near, far)
+    terms = [terms[0]] + [swap(terms[m], "cols", m) for m in range(1, groups)]
+    rows, gram, first = collect(total, degree, first, terms)
+    inverse = first_factor(first)
+    return finish(total, rows, inverse, add_grams(gram))
 
 
 def solution(mesh):

time: 89.5 us -> 73.2 us (0.82)
  waiting for transfers between devices: 32.2 us -> 23.5 us
  starting transfers between devices: 33 us -> 25.3 us
    ppermute x28 -> x21, waiting for transfers between devices: 32.2 us -> 23.5 us  [swap(): lax.ppermute(value, axis, [(index, index ^ mask) for index in range(size)])]
    ppermute x28 -> x21, starting transfers between devices: 33 us -> 25.3 us  [swap(): lax.ppermute(value, axis, [(index, index ^ mask) for index in range(size)])]
    pallas_call x5 -> x7, Pallas kernels: 10.4 us -> 10.1 us  [the longest x1 5.39 us: first_factor(): pl.pallas_call(first_factor_kernel, out_shape=jax.ShapeDtypeStruct((64, 6...]
  transfers between devices with their start and end apart: 28 -> 21, of which waited for: 23 -> 14; matrix products, arithmetic and copies ran while one was open for 1% -> 1% of each run, Pallas kernels for 3% -> 11%
where the time goes in v2:
time: 73.2 us; the launch traced here: 73 us
  starting transfers between devices  25.3 us (35%)
  waiting for transfers between devices  23.5 us (32%)
  Pallas kernels  20 us (27%)
  local copies, waits for them, and re-layouts  3.96 us (5%)
    ppermute x21, starting transfers between devices, swap(): lax.ppermute(value, axis, [(index, index ^ mask) for index in range(size)])  25.3 us
    ppermute x21, waiting for transfers between devices, swap(): lax.ppermute(value, axis, [(index, index ^ mask) for index in range(size)])  23.5 us
    pallas_call x1, Pallas kernels, finish(): pl.pallas_call(functools.partial(finish_kernel, total), out_shape=jax.Sha...  6.77 us
    pallas_call x1, Pallas kernels, first_factor(): pl.pallas_call(first_factor_kernel, out_shape=jax.ShapeDtypeStruct((64, 6...  5.39 us
    unnamed x9, local copies, waits for them, and re-layouts  3.96 us
    pallas_call x2, Pallas kernels, product(): pl.pallas_call(functools.partial(product_kernel, offsets, with_gram), out...  3.63 us
    pallas_call x1, Pallas kernels, prep(): pl.pallas_call(prep_kernel, grid_spec=pltpu.PrefetchScalarGridSpec(num_sc...  2.73 us
  transfers between devices with their start and end apart: 21, of which 14 were waited for; matrix products, arithmetic and copies ran while one was open for 1% of the time, Pallas kernels for 11%

profile of v2, /device:TPU:0, one launch (start us, length us, event | category | flops | bytes accessed | tf_op | source)
XLA Modules:
  0.0 73.0 jit_solution(6066411969347709120)
XLA Ops:
  2.0 4.0 %collective-permute-start.2 = (bf16[8,32,128]{2,1,0:T(8,128)(2,1)S(1)}, bf16[8,32,128]{2,1,0:T(8,128)(2,1)S(1)}, u32[]{:S(2)}, u32[]{:S(2)}) collective-permute-start(bf16[8,32,128]{2,1,0:T(8,128)(2,1)S(1)} %get-tuple-element.23.refs_0_), channel_id=1, source_target_pairs={{0,24},{4,28},{8,16},{12,20},{16,8},{20,12},{24,0},{28,4},{1,25},{... | collective-permute-start | bytes 196616 | tf_op jit(solution)/shard_map/ppermute | solution.py:371
  7.5 1.6 %copy-done = bf16[4,8,1,8,4096]{4,3,2,1,0:T(8,128)(2,1)S(1)} copy-done((bf16[4,8,1,8,4096]{4,3,2,1,0:T(8,128)(2,1)S(1)}, bf16[4,8,1,8,4096]{4,3,2,1,0:T(8,128)(2,1)}, u32[]{:S(2)}) %copy-start) | copy-done | bytes 2097176
  9.1 2.7 %prep.1 = (bf16[4,8,64,512]{3,2,1,0:T(8,128)(2,1)S(1)}, f32[8,128]{1,0:T(8,128)S(1)}) custom-call(s32[2]{0:T(128)S(1)} %pad_add_fusion.place_ref, s32[4,8,1]{2,1,0:T(8,128)S(1)} %copy.6.counts_ref, bf16[4,8,1,8,4096]{4,3,2,1,0:T(8,128)(2,1)S(1)} %copy-done), custom_call_target="tpu_custom_call" | custom-call | tf_op jit(solution)/shard_map/prep/pallas_call | solution.py:111
  12.0 1.5 %collective-permute-done.3.refs_1_ = bf16[4,8,32,128]{3,2,1,0:T(8,128)(2,1)S(1)} collective-permute-done((bf16[4,8,32,128]{3,2,1,0:T(8,128)(2,1)S(1)}, bf16[4,8,32,128]{3,2,1,0:T(8,128)(2,1)S(1)}, u32[]{:S(2)}, u32[]{:S(2)}) %collective-permute-start.3) | collective-permute-done | bytes 262176 | tf_op jit(solution)/shard_map/ppermute | solution.py:371
  13.5 1.8 %product.2 = (bf16[8,32,128]{2,1,0:T(8,128)(2,1)S(1)}, bf16[8,32,128]{2,1,0:T(8,128)(2,1)S(1)}, bf16[8,32,128]{2,1,0:T(8,128)(2,1)S(1)}, bf16[8,32,128]{2,1,0:T(8,128)(2,1)S(1)}) custom-call(s32[2]{0:T(128)S(1)} %pad_add_fusion.place_ref, s32[4,8,1,8]{3,2,1,0:T(1,128)S(1)} %copy-done.2, bf16[4,8,64,512]{3,2,1,0:T(8,128)(2,1)S(1)} %get-tuple-element.22.matrix_ref, ...), custom_call_target="tpu_custom_call" | custom-call | tf_op jit(solution)/shard_map/product/pallas_call | solution.py:217
  15.3 2.0 %collective-permute-start.4 = (bf16[8,32,128]{2,1,0:T(8,128)(2,1)S(1)}, bf16[8,32,128]{2,1,0:T(8,128)(2,1)S(1)}, u32[]{:S(2)}, u32[]{:S(2)}) collective-permute-start(bf16[8,32,128]{2,1,0:T(8,128)(2,1)S(1)} %get-tuple-element.26), channel_id=1, source_target_pairs={{0,1},{1,0},{2,3},{3,2},{4,5},{5,4},{6,7},{7,6},{8,9},{9,8},{10,11... | collective-permute-start | bytes 196616 | tf_op jit(solution)/shard_map/ppermute | solution.py:371
  17.3 2.6 %collective-permute-start.5 = (bf16[8,32,128]{2,1,0:T(8,128)(2,1)S(1)}, bf16[8,32,128]{2,1,0:T(8,128)(2,1)S(1)}, u32[]{:S(2)}, u32[]{:S(2)}) collective-permute-start(bf16[8,32,128]{2,1,0:T(8,128)(2,1)S(1)} %get-tuple-element.27), channel_id=1, source_target_pairs={{0,2},{1,3},{2,0},{3,1},{4,6},{5,7},{6,4},{7,5},{8,10},{9,11},{10,... | collective-permute-start | bytes 196616 | tf_op jit(solution)/shard_map/ppermute | solution.py:371
  19.9 4.9 %collective-permute-done.5.refs_2_ = bf16[8,32,128]{2,1,0:T(8,128)(2,1)S(1)} collective-permute-done((bf16[8,32,128]{2,1,0:T(8,128)(2,1)S(1)}, bf16[8,32,128]{2,1,0:T(8,128)(2,1)S(1)}, u32[]{:S(2)}, u32[]{:S(2)}) %collective-permute-start.5) | collective-permute-done | bytes 65568 | tf_op jit(solution)/shard_map/ppermute | solution.py:371
  24.9 1.2 %collective-permute-done.6.refs_3_ = bf16[8,32,128]{2,1,0:T(8,128)(2,1)S(1)} collective-permute-done((bf16[8,32,128]{2,1,0:T(8,128)(2,1)S(1)}, bf16[8,32,128]{2,1,0:T(8,128)(2,1)S(1)}, u32[]{:S(2)}, u32[]{:S(2)}) %collective-permute-start.6) | collective-permute-done | bytes 65568 | tf_op jit(solution)/shard_map/ppermute | solution.py:371
  26.6 2.5 %collective-permute-start.9 = (bf16[11,32,128]{2,1,0:T(8,128)(2,1)S(1)}, bf16[11,32,128]{2,1,0:T(8,128)(2,1)S(1)}, u32[]{:S(2)}, u32[]{:S(2)}) collective-permute-start(bf16[11,32,128]{2,1,0:T(8,128)(2,1)S(1)} %middle.1.refs_0_), channel_id=1, source_target_pairs={{0,24},{4,28},{8,16},{12,20},{16,8},{20,12},{24,0},{28,4},{1,25},{... | collective-permute-start | bytes 270344 | tf_op jit(solution)/shard_map/ppermute | solution.py:371
  30.1 2.9 %collective-permute-done.9.refs_3_ = bf16[11,32,128]{2,1,0:T(8,128)(2,1)S(1)} collective-permute-done((bf16[11,32,128]{2,1,0:T(8,128)(2,1)S(1)}, bf16[11,32,128]{2,1,0:T(8,128)(2,1)S(1)}, u32[]{:S(2)}, u32[]{:S(2)}) %collective-permute-start.9) | collective-permute-done | bytes 90144 | tf_op jit(solution)/shard_map/ppermute | solution.py:371
  34.2 1.7 %collective-permute-done.10.refs_1_ = bf16[4,11,32,128]{3,2,1,0:T(8,128)(2,1)S(1)} collective-permute-done((bf16[4,11,32,128]{3,2,1,0:T(8,128)(2,1)S(1)}, bf16[4,11,32,128]{3,2,1,0:T(8,128)(2,1)S(1)}, u32[]{:S(2)}, u32[]{:S(2)}) %collective-permute-start.10) | collective-permute-done | bytes 360480 | tf_op jit(solution)/shard_map/ppermute | solution.py:371
  35.9 1.8 %product.3 = (bf16[8,32,128]{2,1,0:T(8,128)(2,1)S(1)}, bf16[11,32,128]{2,1,0:T(8,128)(2,1)S(1)}, bf16[11,32,128]{2,1,0:T(8,128)(2,1)S(1)}, bf16[11,32,128]{2,1,0:T(8,128)(2,1)S(1)}, f32[32,128]{1,0:T(8,128)S(1)}) custom-call(s32[2]{0:T(128)S(1)} %pad_add_fusion.place_ref, s32[4,8,1,8]{3,2,1,0:T(1,128)S(1)} %copy-done.2, ...), custom_call_target="tpu_custom_call" | custom-call | tf_op jit(solution)/shard_map/product/pallas_call | solution.py:217
  38.6 1.7 %collective-permute-start.12 = (bf16[11,32,128]{2,1,0:T(8,128)(2,1)S(1)}, bf16[11,32,128]{2,1,0:T(8,128)(2,1)S(1)}, u32[]{:S(2)}, u32[]{:S(2)}) collective-permute-start(bf16[11,32,128]{2,1,0:T(8,128)(2,1)S(1)} %get-tuple-element.32), channel_id=1, source_target_pairs={{0,2},{1,3},{2,0},{3,1},{4,6},{5,7},{6,4},{7,5},{8,10},{9,11},{10,... | collective-permute-start | bytes 270344 | tf_op jit(solution)/shard_map/ppermute | solution.py:371
  40.3 1.8 %collective-permute-start.13 = (bf16[11,32,128]{2,1,0:T(8,128)(2,1)S(1)}, bf16[11,32,128]{2,1,0:T(8,128)(2,1)S(1)}, u32[]{:S(2)}, u32[]{:S(2)}) collective-permute-start(bf16[11,32,128]{2,1,0:T(8,128)(2,1)S(1)} %get-tuple-element.33), channel_id=1, source_target_pairs={{0,3},{1,2},{2,1},{3,0},{4,7},{5,6},{6,5},{7,4},{8,11},{9,10},{10,... | collective-permute-start | bytes 270344 | tf_op jit(solution)/shard_map/ppermute | solution.py:371
  42.2 1.4 %collective-permute-done.11.refs_1_ = bf16[11,32,128]{2,1,0:T(8,128)(2,1)S(1)} collective-permute-done((bf16[11,32,128]{2,1,0:T(8,128)(2,1)S(1)}, bf16[11,32,128]{2,1,0:T(8,128)(2,1)S(1)}, u32[]{:S(2)}, u32[]{:S(2)}) %collective-permute-start.11) | collective-permute-done | bytes 90144 | tf_op jit(solution)/shard_map/ppermute | solution.py:371
  43.5 5.2 %collective-permute-done.12.refs_2_ = bf16[11,32,128]{2,1,0:T(8,128)(2,1)S(1)} collective-permute-done((bf16[11,32,128]{2,1,0:T(8,128)(2,1)S(1)}, bf16[11,32,128]{2,1,0:T(8,128)(2,1)S(1)}, u32[]{:S(2)}, u32[]{:S(2)}) %collective-permute-start.12) | collective-permute-done | bytes 90144 | tf_op jit(solution)/shard_map/ppermute | solution.py:371
  49.3 1.2 %collective-permute-done.14 = f32[32,128]{1,0:T(8,128)S(1)} collective-permute-done((f32[32,128]{1,0:T(8,128)S(1)}, f32[32,128]{1,0:T(8,128)S(1)}, u32[]{:S(2)}, u32[]{:S(2)}) %collective-permute-start.14) | collective-permute-done | bytes 16416 | tf_op jit(solution)/shard_map/ppermute | solution.py:371
  50.5 1.5 %collective-permute-start.17 = (f32[32,128]{1,0:T(8,128)S(1)}, f32[32,128]{1,0:T(8,128)S(1)}, u32[]{:S(2)}, u32[]{:S(2)}) collective-permute-start(f32[32,128]{1,0:T(8,128)S(1)} %add.12), channel_id=1, source_target_pairs={{0,24},{4,28},{8,16},{12,20},{16,8},{20,12},{24,0},{28,4},{1,25},{... | collective-permute-start | bytes 49160 | tf_op jit(solution)/shard_map/ppermute | solution.py:371
  52.6 1.3 %collective-permute-start.15 = (f32[32,128]{1,0:T(8,128)S(1)}, f32[32,128]{1,0:T(8,128)S(1)}, u32[]{:S(2)}, u32[]{:S(2)}) collective-permute-start(f32[32,128]{1,0:T(8,128)S(1)} %add.12), channel_id=1, source_target_pairs={{0,8},{4,12},{8,0},{12,4},{16,24},{20,28},{24,16},{28,20},{1,9},{5... | collective-permute-start | bytes 49160 | tf_op jit(solution)/shard_map/ppermute | solution.py:371
  56.4 2.0 %collective-permute-start.20 = (f32[32,128]{1,0:T(8,128)S(1)}, f32[32,128]{1,0:T(8,128)S(1)}, u32[]{:S(2)}, u32[]{:S(2)}) collective-permute-start(f32[32,128]{1,0:T(8,128)S(1)} %add_add_fusion.refs_0_), channel_id=1, source_target_pairs={{0,3},{1,2},{2,1},{3,0},{4,7},{5,6},{6,5},{7,4},{8,11},{9,10},{10,... | collective-permute-start | bytes 49160 | tf_op jit(solution)/shard_map/ppermute | solution.py:371
  59.4 1.4 %collective-permute-start.18 = (f32[32,128]{1,0:T(8,128)S(1)}, f32[32,128]{1,0:T(8,128)S(1)}, u32[]{:S(2)}, u32[]{:S(2)}) collective-permute-start(f32[32,128]{1,0:T(8,128)S(1)} %add_add_fusion.refs_0_), channel_id=1, source_target_pairs={{0,1},{1,0},{2,3},{3,2},{4,5},{5,4},{6,7},{7,6},{8,9},{9,8},{10,11... | collective-permute-start | bytes 49160 | tf_op jit(solution)/shard_map/ppermute | solution.py:371
  60.8 5.4 %first_factor.1.inverse_ref = f32[64,64]{1,0:T(8,128)S(1)} custom-call(f32[32,128]{1,0:T(8,128)S(1)} %get-tuple-element.35.gram_ref), custom_call_target="tpu_custom_call" | custom-call | tf_op jit(solution)/shard_map/first_factor/pallas_call | solution.py:318
  66.2 6.8 %finish.1 = f32[1,8,4096]{2,1,0:T(8,128)} custom-call(f32[8,32,128]{2,1,0:T(8,128)S(1)} %get-tuple-element.34.rows_ref, f32[64,64]{1,0:T(8,128)S(1)} %first_factor.1.inverse_ref, f32[32,128]{1,0:T(8,128)S(1)} %add_add_fusion.refs_0_, f32[32,128]{1,0:T(8,128)S(1)} %collective-permute-done.18.refs_1_, f32[32,128]{1,0:T(8,128)S(1)} %collective-permute-done.19.refs_2_, ...), custom_call_target="tpu_custom_call" | custom-call | tf_op jit(solution)/shard_map/finish/pallas_call | solution.py:358
  (40 shorter events, 12.0 us)
Async XLA Ops:
  0.0 0.9 %copy-start.1 = (f32[1,8,4096]{2,1,0:T(8,128)S(1)}, f32[1,8,4096]{2,1,0:T(8,128)}, u32[]{:S(2)}) copy-start(f32[1,8,4096]{2,1,0:T(8,128)} %panel_hbm.1) | copy-start | bytes 393220
  1.6 11.9 %copy-start.2 = (s32[4,8,1,8]{3,2,1,0:T(1,128)S(1)}, s32[4,8,1,8]{3,2,1,0:T(1,128)}, u32[]{:S(2)}) copy-start(s32[4,8,1,8]{3,2,1,0:T(1,128)} %columns_ref.3) | copy-start | bytes 3076
  2.0 9.8 %collective-permute-start.2 = (bf16[8,32,128]{2,1,0:T(8,128)(2,1)S(1)}, bf16[8,32,128]{2,1,0:T(8,128)(2,1)S(1)}, u32[]{:S(2)}, u32[]{:S(2)}) collective-permute-start(bf16[8,32,128]{2,1,0:T(8,128)(2,1)S(1)} %get-tuple-element.23.refs_0_), channel_id=1, source_target_pairs={{0,24},{4,28},{8,16},{12,20},{16,8},{20,12},{24,0},{28,4},{1,25},{... | collective-permute-start | bytes 196616 | tf_op jit(solution)/shard_map/ppermute | solution.py:371
  6.0 5.8 %collective-permute-start.1 = (bf16[8,32,128]{2,1,0:T(8,128)(2,1)S(1)}, bf16[8,32,128]{2,1,0:T(8,128)(2,1)S(1)}, u32[]{:S(2)}, u32[]{:S(2)}) collective-permute-start(bf16[8,32,128]{2,1,0:T(8,128)(2,1)S(1)} %get-tuple-element.23.refs_0_), channel_id=1, source_target_pairs={{0,16},{4,20},{8,24},{12,28},{16,0},{20,4},{24,8},{28,12},{1,17},{... | collective-permute-start | bytes 196616 | tf_op jit(solution)/shard_map/ppermute | solution.py:371
  6.5 5.3 %collective-permute-start = (bf16[8,32,128]{2,1,0:T(8,128)(2,1)S(1)}, bf16[8,32,128]{2,1,0:T(8,128)(2,1)S(1)}, u32[]{:S(2)}, u32[]{:S(2)}) collective-permute-start(bf16[8,32,128]{2,1,0:T(8,128)(2,1)S(1)} %get-tuple-element.23.refs_0_), channel_id=1, source_target_pairs={{0,8},{4,12},{8,0},{12,4},{16,24},{20,28},{24,16},{28,20},{1,9},{5... | collective-permute-start | bytes 196616 | tf_op jit(solution)/shard_map/ppermute | solution.py:371
  7.5 1.6 %copy-start = (bf16[4,8,1,8,4096]{4,3,2,1,0:T(8,128)(2,1)S(1)}, bf16[4,8,1,8,4096]{4,3,2,1,0:T(8,128)(2,1)}, u32[]{:S(2)}) copy-start(bf16[4,8,1,8,4096]{4,3,2,1,0:T(8,128)(2,1)} %affinity_ref.1) | copy-start | bytes 6291460
  11.9 1.6 %collective-permute-start.3 = (bf16[4,8,32,128]{3,2,1,0:T(8,128)(2,1)S(1)}, bf16[4,8,32,128]{3,2,1,0:T(8,128)(2,1)S(1)}, u32[]{:S(2)}, u32[]{:S(2)}) collective-permute-start(bf16[4,8,32,128]{3,2,1,0:T(8,128)(2,1)S(1)} %stack.14.refs_0_), channel_id=1, source_target_pairs={{0,4},{4,0},{8,12},{12,8},{16,20},{20,16},{24,28},{28,24},{1,5},{5... | collective-permute-start | bytes 786440 | tf_op jit(solution)/shard_map/ppermute | solution.py:371
  15.3 4.6 %collective-permute-start.4 = (bf16[8,32,128]{2,1,0:T(8,128)(2,1)S(1)}, bf16[8,32,128]{2,1,0:T(8,128)(2,1)S(1)}, u32[]{:S(2)}, u32[]{:S(2)}) collective-permute-start(bf16[8,32,128]{2,1,0:T(8,128)(2,1)S(1)} %get-tuple-element.26), channel_id=1, source_target_pairs={{0,1},{1,0},{2,3},{3,2},{4,5},{5,4},{6,7},{7,6},{8,9},{9,8},{10,11... | collective-permute-start | bytes 196616 | tf_op jit(solution)/shard_map/ppermute | solution.py:371
  17.3 7.5 %collective-permute-start.5 = (bf16[8,32,128]{2,1,0:T(8,128)(2,1)S(1)}, bf16[8,32,128]{2,1,0:T(8,128)(2,1)S(1)}, u32[]{:S(2)}, u32[]{:S(2)}) collective-permute-start(bf16[8,32,128]{2,1,0:T(8,128)(2,1)S(1)} %get-tuple-element.27), channel_id=1, source_target_pairs={{0,2},{1,3},{2,0},{3,1},{4,6},{5,7},{6,4},{7,5},{8,10},{9,11},{10,... | collective-permute-start | bytes 196616 | tf_op jit(solution)/shard_map/ppermute | solution.py:371
  19.9 6.2 %collective-permute-start.6 = (bf16[8,32,128]{2,1,0:T(8,128)(2,1)S(1)}, bf16[8,32,128]{2,1,0:T(8,128)(2,1)S(1)}, u32[]{:S(2)}, u32[]{:S(2)}) collective-permute-start(bf16[8,32,128]{2,1,0:T(8,128)(2,1)S(1)} %get-tuple-element.28), channel_id=1, source_target_pairs={{0,3},{1,2},{2,1},{3,0},{4,7},{5,6},{6,5},{7,4},{8,11},{9,10},{10,... | collective-permute-start | bytes 196616 | tf_op jit(solution)/shard_map/ppermute | solution.py:371
  26.6 6.5 %collective-permute-start.9 = (bf16[11,32,128]{2,1,0:T(8,128)(2,1)S(1)}, bf16[11,32,128]{2,1,0:T(8,128)(2,1)S(1)}, u32[]{:S(2)}, u32[]{:S(2)}) collective-permute-start(bf16[11,32,128]{2,1,0:T(8,128)(2,1)S(1)} %middle.1.refs_0_), channel_id=1, source_target_pairs={{0,24},{4,28},{8,16},{12,20},{16,8},{20,12},{24,0},{28,4},{1,25},{... | collective-permute-start | bytes 270344 | tf_op jit(solution)/shard_map/ppermute | solution.py:371
  29.1 4.7 %collective-permute-start.8 = (bf16[11,32,128]{2,1,0:T(8,128)(2,1)S(1)}, bf16[11,32,128]{2,1,0:T(8,128)(2,1)S(1)}, u32[]{:S(2)}, u32[]{:S(2)}) collective-permute-start(bf16[11,32,128]{2,1,0:T(8,128)(2,1)S(1)} %middle.1.refs_0_), channel_id=1, source_target_pairs={{0,16},{4,20},{8,24},{12,28},{16,0},{20,4},{24,8},{28,12},{1,17},{... | collective-permute-start | bytes 270344 | tf_op jit(solution)/shard_map/ppermute | solution.py:371
  29.6 4.5 %collective-permute-start.7 = (bf16[11,32,128]{2,1,0:T(8,128)(2,1)S(1)}, bf16[11,32,128]{2,1,0:T(8,128)(2,1)S(1)}, u32[]{:S(2)}, u32[]{:S(2)}) collective-permute-start(bf16[11,32,128]{2,1,0:T(8,128)(2,1)S(1)} %middle.1.refs_0_), channel_id=1, source_target_pairs={{0,8},{4,12},{8,0},{12,4},{16,24},{20,28},{24,16},{28,20},{1,9},{5... | collective-permute-start | bytes 270344 | tf_op jit(solution)/shard_map/ppermute | solution.py:371
  34.1 1.7 %collective-permute-start.10 = (bf16[4,11,32,128]{3,2,1,0:T(8,128)(2,1)S(1)}, bf16[4,11,32,128]{3,2,1,0:T(8,128)(2,1)S(1)}, u32[]{:S(2)}, u32[]{:S(2)}) collective-permute-start(bf16[4,11,32,128]{3,2,1,0:T(8,128)(2,1)S(1)} %stack.15.refs_0_), channel_id=1, source_target_pairs={{0,4},{4,0},{8,12},{12,8},{16,20},{20,16},{24,28},{28,24},{1,5},{5... | collective-permute-start | bytes 1081352 | tf_op jit(solution)/shard_map/ppermute | solution.py:371
  37.7 5.8 %collective-permute-start.11 = (bf16[11,32,128]{2,1,0:T(8,128)(2,1)S(1)}, bf16[11,32,128]{2,1,0:T(8,128)(2,1)S(1)}, u32[]{:S(2)}, u32[]{:S(2)}) collective-permute-start(bf16[11,32,128]{2,1,0:T(8,128)(2,1)S(1)} %get-tuple-element.31), channel_id=1, source_target_pairs={{0,1},{1,0},{2,3},{3,2},{4,5},{5,4},{6,7},{7,6},{8,9},{9,8},{10,11... | collective-permute-start | bytes 270344 | tf_op jit(solution)/shard_map/ppermute | solution.py:371
  38.6 10.1 %collective-permute-start.12 = (bf16[11,32,128]{2,1,0:T(8,128)(2,1)S(1)}, bf16[11,32,128]{2,1,0:T(8,128)(2,1)S(1)}, u32[]{:S(2)}, u32[]{:S(2)}) collective-permute-start(bf16[11,32,128]{2,1,0:T(8,128)(2,1)S(1)} %get-tuple-element.32), channel_id=1, source_target_pairs={{0,2},{1,3},{2,0},{3,1},{4,6},{5,7},{6,4},{7,5},{8,10},{9,11},{10,... | collective-permute-start | bytes 270344 | tf_op jit(solution)/shard_map/ppermute | solution.py:371
  40.3 8.4 %collective-permute-start.13 = (bf16[11,32,128]{2,1,0:T(8,128)(2,1)S(1)}, bf16[11,32,128]{2,1,0:T(8,128)(2,1)S(1)}, u32[]{:S(2)}, u32[]{:S(2)}) collective-permute-start(bf16[11,32,128]{2,1,0:T(8,128)(2,1)S(1)} %get-tuple-element.33), channel_id=1, source_target_pairs={{0,3},{1,2},{2,1},{3,0},{4,7},{5,6},{6,5},{7,4},{8,11},{9,10},{10,... | collective-permute-start | bytes 270344 | tf_op jit(solution)/shard_map/ppermute | solution.py:371
  49.3 1.2 %collective-permute-start.14 = (f32[32,128]{1,0:T(8,128)S(1)}, f32[32,128]{1,0:T(8,128)S(1)}, u32[]{:S(2)}, u32[]{:S(2)}) collective-permute-start(f32[32,128]{1,0:T(8,128)S(1)} %get-tuple-element.36), channel_id=1, source_target_pairs={{0,4},{4,0},{8,12},{12,8},{16,20},{20,16},{24,28},{28,24},{1,5},{5... | collective-permute-start | bytes 49160 | tf_op jit(solution)/shard_map/ppermute | solution.py:371
  50.5 4.6 %collective-permute-start.17 = (f32[32,128]{1,0:T(8,128)S(1)}, f32[32,128]{1,0:T(8,128)S(1)}, u32[]{:S(2)}, u32[]{:S(2)}) collective-permute-start(f32[32,128]{1,0:T(8,128)S(1)} %add.12), channel_id=1, source_target_pairs={{0,24},{4,28},{8,16},{12,20},{16,8},{20,12},{24,0},{28,4},{1,25},{... | collective-permute-start | bytes 49160 | tf_op jit(solution)/shard_map/ppermute | solution.py:371
  52.0 3.7 %collective-permute-start.16 = (f32[32,128]{1,0:T(8,128)S(1)}, f32[32,128]{1,0:T(8,128)S(1)}, u32[]{:S(2)}, u32[]{:S(2)}) collective-permute-start(f32[32,128]{1,0:T(8,128)S(1)} %add.12), channel_id=1, source_target_pairs={{0,16},{4,20},{8,24},{12,28},{16,0},{20,4},{24,8},{28,12},{1,17},{... | collective-permute-start | bytes 49160 | tf_op jit(solution)/shard_map/ppermute | solution.py:371
  52.6 3.7 %collective-permute-start.15 = (f32[32,128]{1,0:T(8,128)S(1)}, f32[32,128]{1,0:T(8,128)S(1)}, u32[]{:S(2)}, u32[]{:S(2)}) collective-permute-start(f32[32,128]{1,0:T(8,128)S(1)} %add.12), channel_id=1, source_target_pairs={{0,8},{4,12},{8,0},{12,4},{16,24},{20,28},{24,16},{28,20},{1,9},{5... | collective-permute-start | bytes 49160 | tf_op jit(solution)/shard_map/ppermute | solution.py:371
  56.4 9.8 %collective-permute-start.20 = (f32[32,128]{1,0:T(8,128)S(1)}, f32[32,128]{1,0:T(8,128)S(1)}, u32[]{:S(2)}, u32[]{:S(2)}) collective-permute-start(f32[32,128]{1,0:T(8,128)S(1)} %add_add_fusion.refs_0_), channel_id=1, source_target_pairs={{0,3},{1,2},{2,1},{3,0},{4,7},{5,6},{6,5},{7,4},{8,11},{9,10},{10,... | collective-permute-start | bytes 49160 | tf_op jit(solution)/shard_map/ppermute | solution.py:371
  58.4 7.8 %collective-permute-start.19 = (f32[32,128]{1,0:T(8,128)S(1)}, f32[32,128]{1,0:T(8,128)S(1)}, u32[]{:S(2)}, u32[]{:S(2)}) collective-permute-start(f32[32,128]{1,0:T(8,128)S(1)} %add_add_fusion.refs_0_), channel_id=1, source_target_pairs={{0,2},{1,3},{2,0},{3,1},{4,6},{5,7},{6,4},{7,5},{8,10},{9,11},{10,... | collective-permute-start | bytes 49160 | tf_op jit(solution)/shard_map/ppermute | solution.py:371
  59.4 6.8 %collective-permute-start.18 = (f32[32,128]{1,0:T(8,128)S(1)}, f32[32,128]{1,0:T(8,128)S(1)}, u32[]{:S(2)}, u32[]{:S(2)}) collective-permute-start(f32[32,128]{1,0:T(8,128)S(1)} %add_add_fusion.refs_0_), channel_id=1, source_target_pairs={{0,1},{1,0},{2,3},{3,2},{4,5},{5,4},{6,7},{7,6},{8,9},{9,8},{10,11... | collective-permute-start | bytes 49160 | tf_op jit(solution)/shard_map/ppermute | solution.py:371
  (1 other events, 0.7 us)

commit v3 on v0

v3 whole, which is shorter than its diff:
```python
import functools

import jax
import jax.numpy as jnp
from jax import lax
from jax.experimental import pallas as pl
from jax.experimental.pallas import tpu as pltpu
from jax.sharding import PartitionSpec as P

BF16 = jnp.bfloat16
F32 = jnp.float32
HIGHEST = lax.Precision.HIGHEST
MIB = 1024 * 1024


def params(limit=48 * MIB):
    return pltpu.CompilerParams(vmem_limit_bytes=limit)


def vmem():
    return pl.BlockSpec(memory_space=pltpu.VMEM)


def hbm():
    return pl.BlockSpec(memory_space=pltpu.HBM)


def smem():
    return pl.BlockSpec(memory_space=pltpu.SMEM)


def shaped(shape, dtype):
    return jax.ShapeDtypeStruct(shape, dtype)


def iota(shape, dim):
    return lax.broadcasted_iota(jnp.int32, shape, dim)


def call(kernel, name, ins, outs, operands, scratch=(), limit=48 * MIB, **kwargs):
    return pl.pallas_call(
        kernel,
        out_shape=outs,
        in_specs=ins,
        out_specs=jax.tree.map(lambda _: vmem(), outs),
        scratch_shapes=list(scratch),
        compiler_params=params(limit),
        name=name,
        **kwargs,
    )(*operands)


def start_kernel(panel_hbm, inv_hbm, scaled_ref, degree_ref, panel_ref, inv_ref, scratch, sems):
    block_rows, block_size = inv_ref.shape[1], inv_ref.shape[2]
    half = block_size // 2
    copies = [
        pltpu.make_async_copy(inv_hbm, inv_ref, sems.at[0]),
        pltpu.make_async_copy(panel_hbm, panel_ref, sems.at[1]),
    ]
    for copy in copies:
        copy.start()
    copies[0].wait()
    pair = iota((half, block_size), 1) // 2 == iota((half, block_size), 0)
    spread = (iota((block_size, 128), 0) % 2 == iota((block_size, 128), 1) // 64).astype(F32)
    rows = [
        jnp.where(pair, jnp.broadcast_to(inv_ref[0, i : i + 1, :], (half, block_size)), 0.0)
        for i in range(block_rows)
    ]
    degree_ref[...] = jnp.dot(
        jnp.concatenate(rows, axis=0), spread, precision=HIGHEST, preferred_element_type=F32
    )
    copies[1].wait()
    for t in range(half):
        scratch[t * block_rows : (t + 1) * block_rows, :] = panel_ref[0, :, t * 128 : (t + 1) * 128]
    for i in range(block_rows):
        where = slice(i * half, (i + 1) * half)
        part = scratch[pl.ds(i, half, stride=block_rows), :] * degree_ref[where, :]
        scaled_ref[where, :] = part.astype(BF16)


def start(panel, inv_degree):
    block_rows, block_size = inv_degree.shape[1:]
    shape = (block_rows * block_size // 2, 128)
    return call(
        start_kernel,
        "start",
        [hbm(), hbm()],
        (shaped(shape, BF16), shaped(shape, F32)),
        (panel, inv_degree),
        [
            pltpu.VMEM(panel.shape, F32),
            pltpu.VMEM(inv_degree.shape, F32),
            pltpu.VMEM(shape, F32),
            pltpu.SemaphoreType.DMA((2,)),
        ],
    )


def prep_kernel(place_ref, affinity_hbm, out_ref, done_ref, affinity_ref, scratch, sems):
    done_ref[...] = jnp.zeros_like(done_ref)
    groups, block_rows, _, slots, flat = affinity_ref.shape
    half = flat // 128
    copies = [
        pltpu.make_async_copy(affinity_hbm.at[m ^ place_ref[1]], affinity_ref.at[m], sems.at[m])
        for m in range(groups)
    ]
    for copy in copies:
        copy.start()
    source, target = iota((256, 256), 0), iota((256, 256), 1)
    moved = (source // 64 % 2) * 128 + (source // 128) * 64 + (source % 2) * 32 + source % 64 // 2
    permute = (moved == target).astype(BF16)
    for m in range(groups):
        copies[m].wait()
        for i in range(block_rows):
            block = affinity_ref[m, i, 0].astype(F32)
            for t in range(half):
                scratch[i % 2, t * slots : (t + 1) * slots, :] = block[:, t * 128 : (t + 1) * 128]
            parts = [
                scratch[i % 2, pl.ds(s, half, stride=slots), :].astype(BF16) for s in range(slots)
            ]
            pairs = [jnp.concatenate(parts[s : s + 2], axis=1) for s in range(0, slots, 2)]
            moved_pairs = jnp.dot(
                jnp.concatenate(pairs, axis=0), permute, preferred_element_type=F32
            ).astype(BF16)
            for s in range(slots // 2):
                piece = moved_pairs[s * half : (s + 1) * half]
                out_ref[m, i, :half, s * 128 : (s + 1) * 128] = piece[:, :128]
                out_ref[m, i, half:, s * 128 : (s + 1) * 128] = piece[:, 128:]


def prep(place, affinity):
    groups, block_rows, _, slots, flat = affinity.shape
    return call(
        prep_kernel,
        "prep",
        [smem(), hbm()],
        (shaped((groups, block_rows, 64, slots * 64), BF16), shaped((8, 128), F32)),
        (place, affinity),
        [
            pltpu.VMEM(affinity.shape, BF16),
            pltpu.VMEM((2, flat // 128 * slots, 128), F32),
            pltpu.SemaphoreType.DMA((groups,)),
        ],
    )


def split(value):
    high = value.astype(BF16)
    rest = value - high.astype(F32)
    middle = rest.astype(BF16)
    return high, middle, (rest - middle.astype(F32)).astype(BF16)


def joined(ref, index, first):
    high, middle, low = (
        ref[index, first + 32 * part : first + 32 * (part + 1)].astype(F32) for part in range(3)
    )
    return high + (middle + low)


def stack_kernel(count, *refs):
    for index in range(count):
        refs[-1][index] = refs[index][...]


def stack(pieces, after):
    return call(
        functools.partial(stack_kernel, len(pieces)),
        "stack",
        [vmem()] * (len(pieces) + len(after)),
        shaped((len(pieces),) + pieces[0].shape, BF16),
        (*pieces, *after),
    )


def fill_table(place_ref, pieces_ref, offsets, table):
    block_rows = (table.shape[0] - 1) // (2 * len(offsets))
    low = iota((32, 128), 1) < 64
    for index, offset in enumerate(offsets):
        base = (place_ref[0] ^ offset) * block_rows
        for i in range(block_rows):
            block = pieces_ref[index, i * 32 : (i + 1) * 32, :]
            turned = jnp.concatenate([block[:, 64:], block[:, :64]], axis=1)
            table[base + i, :32] = jnp.where(low, block, turned)
            table[base + i, 32:] = jnp.where(low, turned, block)


def near_kernel(offsets, place_ref, near_ref, table):
    table[table.shape[0] - 1] = jnp.zeros(table.shape[1:], BF16)
    fill_table(place_ref, near_ref, offsets, table)


def far_kernel(offsets, place_ref, far_ref, near_ref, old_table, table, *grams):
    del old_table
    fill_table(place_ref, far_ref, offsets, table)
    if grams:
        gram_ref, trace_ref = grams
        first = (table.shape[0] - 1) // (2 * len(offsets)) * 32
        gram = joined(near_ref, 0, first) + joined(far_ref, 0, first)
        for index in range(1, len(offsets)):
            gram = gram + joined(near_ref, index, first) + joined(far_ref, index, first)
        gram_ref[...] = gram
        row, lane = iota(gram.shape, 0), iota(gram.shape, 1)
        diagonal = lane % 64 == row + lane // 64 * 32
        trace = jnp.sum(jnp.where(diagonal, gram, 0.0), axis=(0, 1), keepdims=True)
        trace_ref[...] = jnp.broadcast_to(trace, trace_ref.shape).astype(BF16)


def tables(offsets, place, near, far, block_rows):
    count = near.shape[0]
    table_shape = shaped((2 * count * block_rows + 1, 64, 128), BF16)
    table = call(
        functools.partial(near_kernel, offsets[:count]),
        "near",
        [smem(), vmem()],
        table_shape,
        (place, near),
    )
    outs = [table_shape]
    if near.shape[1] > block_rows * 32:
        outs += [shaped((32, 128), F32), shaped((16, 128), BF16)]
    return call(
        functools.partial(far_kernel, offsets[count:]),
        "far",
        [smem(), vmem(), vmem(), vmem()],
        outs,
        (place, far, near, table),
        input_output_aliases={3: 0},
    )


def product_kernel(m, place_ref, columns_ref, matrix_ref, table, *refs):
    out_ref = refs[-1]
    block_rows, slots = columns_ref.shape[1], columns_ref.shape[3]
    group = m ^ place_ref[1]
    low = iota((32, 128), 1) < 64
    for i in range(block_rows):
        picked = [table[columns_ref[group, i, 0, s]] for s in range(slots)]
        result = jnp.dot(
            matrix_ref[m, i], jnp.concatenate(picked, axis=0), preferred_element_type=F32
        )
        out_ref[i * 32 : (i + 1) * 32, :] = jnp.where(low, result[:32], result[32:]).astype(BF16)
    if len(refs) > 1:
        out_ref[block_rows * 32 :, :] = refs[0][...]


def product(m, place, columns, matrix, table, trace):
    rows = matrix.shape[1] * 32 + sum(extra.shape[0] for extra in trace)
    return call(
        functools.partial(product_kernel, m),
        "product",
        [smem(), smem()] + [vmem()] * (2 + len(trace)),
        shaped((rows, 128), BF16),
        (place, columns, matrix, table, *trace),
    )


def products(place, columns, matrix, table, trace):
    groups = matrix.shape[0]
    terms = []
    for m in range(groups - 1, 0, -1):
        terms.append(swap(product(m, place, columns, matrix, table, trace), "cols", m))
    return [product(0, place, columns, matrix, table, trace)] + terms


def add_terms(terms, rows):
    summed = terms[0][:rows].astype(F32)
    for term in terms[1:]:
        summed = summed + term[:rows].astype(F32)
    return summed


def local_gram(rows):
    both = lax.dot_general(
        rows, rows, (((0,), (0,)), ((), ())), precision=HIGHEST, preferred_element_type=F32
    )
    gram = both[:64, :64] + both[64:, 64:]
    return jnp.concatenate([gram[:32], gram[32:]], axis=1)


def middle_kernel(degree_ref, *refs):
    terms, out_ref = refs[:-1], refs[-1]
    count = degree_ref.shape[0]
    degree = degree_ref[...]
    rows = add_terms(terms, count) * degree
    out_ref[:count] = (rows * degree).astype(BF16)
    for part, value in enumerate(split(local_gram(rows))):
        out_ref[count + part * 32 : count + (part + 1) * 32] = value


def middle(degree, terms):
    return call(
        middle_kernel,
        "middle",
        [vmem()] * (1 + len(terms)),
        shaped((degree.shape[0] + 96, 128), BF16),
        (degree, *terms),
    )


def collect_kernel(total, degree_ref, first_ref, *refs):
    terms, (rows_ref, grams_ref) = refs[:-2], refs[-2:]
    count = degree_ref.shape[0]
    largest = terms[0][count:].astype(F32)
    for term in terms[1:]:
        largest = jnp.maximum(largest, term[count:].astype(F32))
    scale = lax.rsqrt(largest[:1] / total)
    rows = add_terms(terms, count) * degree_ref[...] * scale
    rows_ref[...] = rows
    grams_ref[32:] = first_ref[...] * (scale * scale)
    grams_ref[:32] = local_gram(rows)


def collect(total, degree, first, terms):
    return call(
        functools.partial(collect_kernel, total),
        "collect",
        [vmem()] * (2 + len(terms)),
        (shaped(degree.shape, F32), shaped((64, 128), F32)),
        (degree, first, *terms),
    )


def lower_solve(gram, right):
    work = jnp.concatenate([gram, right], axis=1)
    blocks = gram.shape[0] // 8
    rows = [work[8 * i : 8 * i + 8] for i in range(blocks)]
    at = iota((8, 128), 0)

    def columns(first, column):
        return [
            jnp.broadcast_to(rows[i][:, column : column + 1], (8, 128))
            for i in range(first, blocks)
        ]

    def spread(block, row):
        return jnp.broadcast_to(block[row : row + 1], (8, 128))

    current = [columns(0, q) for q in range(8)]
    for b in range(blocks):
        count = blocks - b
        later = []
        if count > 1:
            later = [columns(b + 1, 8 * (b + 1) + q) for q in range(8)]
        for q in range(8):
            root = lax.rsqrt(spread(current[q][0], q))
            inverse = root * root
            raw = spread(rows[b], q)
            scaled = raw * inverse
            for p in range(q + 1, 8):
                weight = spread(current[q][0], p) * inverse
                current[p] = [x - y * weight for x, y in zip(current[p], current[q])]
            below = rows[b] - current[q][0] * scaled
            rows[b] = jnp.where(at == q, raw * root, jnp.where(at > q, below, rows[b]))
            for i in range(1, count):
                rows[b + i] = rows[b + i] - current[q][i] * scaled
            for p in range(len(later)):
                weight = spread(current[q][1], p) * inverse
                later[p] = [x - y * weight for x, y in zip(later[p], current[q][1:])]
        current = later
    return jnp.concatenate(rows, axis=0)[:, 64:]


def unpacked(packed):
    return jnp.concatenate([packed[:, :64], packed[:, 64:]], axis=0)


def add_columns_kernel(total, *refs):
    parts, (gram_ref, first_ref) = refs[:-2], refs[-2:]
    summed = parts[0][...]
    for part in parts[1:]:
        summed = summed + part[...]
    gram_ref[...] = summed[:32]
    first_ref[...] = summed[32:] / total


def add_columns(total, parts):
    return call(
        functools.partial(add_columns_kernel, total),
        "add_columns",
        [vmem()] * len(parts),
        (shaped((32, 128), F32), shaped((32, 128), F32)),
        parts,
    )


def first_factor_kernel(gram_ref, out_ref):
    unit = (iota((64, 64), 0) == iota((64, 64), 1)).astype(F32)
    out_ref[...] = lower_solve(unpacked(gram_ref[...]), unit)


def first_factor(gram):
    return call(first_factor_kernel, "first_factor", [vmem()], shaped((64, 64), F32), (gram,))


def dot_turned(left, right):
    return lax.dot_general(
        left, right, (((1,), (1,)), ((), ())), precision=HIGHEST, preferred_element_type=F32
    )


def finish_kernel(total, rows_ref, inverse_ref, *refs):
    out_ref, scratch = refs[-2:]
    block_rows = out_ref.shape[1]
    packed = refs[0][...]
    for part in refs[1:-2]:
        packed = packed + part[...]
    first = inverse_ref[...]
    gram = dot_turned(
        jnp.dot(first, unpacked(packed), precision=HIGHEST, preferred_element_type=F32), first
    )
    inverse = lower_solve(gram / total, first)
    zero = jnp.zeros_like(inverse)
    both = jnp.concatenate(
        [jnp.concatenate([inverse, zero], axis=1), jnp.concatenate([zero, inverse], axis=1)], axis=0
    )
    current = dot_turned(rows_ref[...], both)
    for i in range(block_rows):
        scratch[pl.ds(i, 32, stride=block_rows), :] = current[i * 32 : (i + 1) * 32]
    for t in range(32):
        out_ref[0, :, t * 128 : (t + 1) * 128] = scratch[t * block_rows : (t + 1) * block_rows, :]


def finish(total, block_rows, rows, inverse, grams):
    return call(
        functools.partial(finish_kernel, total),
        "finish",
        [vmem()] * (2 + len(grams)),
        shaped((1, block_rows, 32 * 128), F32),
        (rows, inverse, *grams),
        [pltpu.VMEM(rows.shape, F32)],
    )


def swap(value, axis, mask):
    size = lax.axis_size(axis)
    return lax.ppermute(value, axis, [(index, index ^ mask) for index in range(size)])


def stages(size):
    if size == 8:
        return [[6, 4, 2], [1]]
    bits, bit = [], 1
    while bit < size:
        bits.append([bit])
        bit *= 2
    return bits


def gather_rows(message, after):
    plan = stages(lax.axis_size("rows"))
    held, offsets = [message], [0]
    for masks in plan[:-1]:
        held = held + [swap(piece, "rows", mask) for mask in masks for piece in held]
        offsets = offsets + [mask ^ offset for mask in masks for offset in offsets]
    near = stack(held, after)
    (last,) = plan[-1]
    offsets = offsets + [last ^ offset for offset in offsets]
    return near, swap(near, "rows", last), offsets


def add_rows(gram):
    *plan, (last,) = stages(lax.axis_size("rows"))
    for masks in plan:
        gram = sum([swap(gram, "rows", mask) for mask in masks], gram)
    return [gram, swap(gram, "rows", last)]


def body(affinity, block_columns, block_counts, inv_degree, panel):
    block_rows, block_size = inv_degree.shape[1:]
    groups, _, _, slots, _ = affinity.shape
    ranks = lax.axis_size("rows")
    total = float(groups * ranks * block_rows * block_size)
    blocks = ranks * block_rows
    place = jnp.stack([lax.axis_index("rows"), lax.axis_index("cols")]).astype(jnp.int32)
    live = iota(block_columns.shape, 3) < block_counts[..., None]
    columns = jnp.where(live, jnp.clip(block_columns, 0, blocks - 1), blocks)

    panel, inv_degree, affinity = (
        pltpu.with_memory_space_constraint(value, pltpu.HBM) for value in (panel, inv_degree, affinity)
    )
    scaled, degree = start(panel, inv_degree)
    matrix, done = prep(place, affinity)
    near, far, offsets = gather_rows(scaled, [done])
    (table,) = tables(offsets, place, near, far, block_rows)
    terms = products(place, columns, matrix, table, [])
    near, far, offsets = gather_rows(middle(degree, terms), [])
    table, first, trace = tables(offsets, place, near, far, block_rows)
    terms = products(place, columns, matrix, table, [trace])
    rows, grams = collect(total, degree, first, terms)
    parts = [grams] + [swap(grams, "cols", m) for m in range(groups - 1, 0, -1)]
    gram, first = add_columns(total, parts)
    return finish(total, block_rows, rows, first_factor(first), add_rows(gram))


def solution(mesh):
    return jax.shard_map(
        body,
        mesh=mesh,
        in_specs=(
            P(None, "rows", "cols", None, None),
            P(None, "rows", "cols", None),
            P(None, "rows", "cols"),
            P("cols", "rows", None),
            P("cols", "rows", None),
        ),
        out_specs=P("cols", "rows", None),
        check_vma=False,
    )
```

time: 300 us -> 69.5 us (0.23)
  blocking collectives: 102 us -> 0 us
  local copies, waits for them, and re-layouts: 96.1 us -> 0.01 us
  other arithmetic: 33.9 us -> 0.18 us
  starting transfers between devices: 0.04 us -> 25.1 us
  Pallas kernels: 0 us -> 21.2 us
  waiting for transfers between devices: 38.8 us -> 22.6 us
  between operations: 14.1 us -> 0.19 us
  matrix products: 13.3 us -> 0 us
    psum x2 -> x0, blocking collectives: 77.8 us -> none  [body(): gram_matrix = lax.psum(local_gram, ('rows', 'cols')) / trajectories]
    gather x32 -> x0, local copies, waits for them, and re-layouts: 42.6 us -> none  [local_terms(): picked = jnp.take(panel_blocks, columns_slice[:, :, slot_index], axis=0)]
    reduce_scatter x2 -> x0, waiting for transfers between devices: 38.8 us -> none  [body(): lax.psum_scatter(local_terms(values_local, columns_local, counts_local, p...]
    ppermute x0 -> x21, starting transfers between devices: none -> 25.1 us  [swap(): lax.ppermute(value, axis, [(index, index ^ mask) for index in range(size)])]
    all_gather x2 -> x0, blocking collectives: 24.1 us -> none  [body(): gathered = lax.all_gather(scaled, 'rows', axis=1, tiled=True)]
    another operation x10 -> x1, other arithmetic: 24.1 us -> 0.07 us  [body(): jnp.stack([lax.axis_index('rows'), lax.axis_index('cols')])]
    ppermute x0 -> x21, waiting for transfers between devices: none -> 22.6 us  [swap(): lax.ppermute(value, axis, [(index, index ^ mask) for index in range(size)])]
    pallas_call x0 -> x21, Pallas kernels: none -> 21.2 us  [call(): pl.pallas_call(kernel, out_shape=outs, in_specs=ins, out_specs=jax.tree.m...]
  transfers between devices with their start and end apart: 2 -> 21, of which waited for: 2 -> 15; matrix products, arithmetic and copies ran while one was open for 0% -> 0% of each run, Pallas kernels for 0% -> 12%
where the time goes in v3:
time: 69.5 us; the launch traced here: 69.3 us
  starting transfers between devices  25.1 us (36%)
  waiting for transfers between devices  22.6 us (33%)
  Pallas kernels  21.2 us (31%)
    ppermute x21, starting transfers between devices, swap(): lax.ppermute(value, axis, [(index, index ^ mask) for index in range(size)])  25.1 us
    ppermute x21, waiting for transfers between devices, swap(): lax.ppermute(value, axis, [(index, index ^ mask) for index in range(size)])  22.6 us
    pallas_call x21, Pallas kernels, call(): pl.pallas_call(kernel, out_shape=outs, in_specs=ins, out_specs=jax.tree.m...  21.2 us
  transfers between devices with their start and end apart: 21, of which 15 were waited for; matrix products, arithmetic and copies ran while one was open for 0% of the time, Pallas kernels for 12%

profile of v3, /device:TPU:0, one launch (start us, length us, event | category | flops | bytes accessed | tf_op | source)
XLA Modules:
  0.0 69.3 jit_solution(17820361459699012909)
XLA Ops:
  1.0 3.0 %collective-permute-start.2 = (bf16[256,128]{1,0:T(8,128)(2,1)S(1)}, bf16[256,128]{1,0:T(8,128)(2,1)S(1)}, u32[]{:S(2)}, u32[]{:S(2)}) collective-permute-start(bf16[256,128]{1,0:T(8,128)(2,1)S(1)} %get-tuple-element.18.refs_0_), channel_id=1, source_target_pairs={{0,8},{4,12},{8,0},{12,4},{16,24},{20,28},{24,16},{28,20},{1,9},{5... | collective-permute-start | bytes 196616 | tf_op jit(solution)/shard_map/ppermute | solution.py:437
  4.0 1.5 %collective-permute-start.1 = (bf16[256,128]{1,0:T(8,128)(2,1)S(1)}, bf16[256,128]{1,0:T(8,128)(2,1)S(1)}, u32[]{:S(2)}, u32[]{:S(2)}) collective-permute-start(bf16[256,128]{1,0:T(8,128)(2,1)S(1)} %get-tuple-element.18.refs_0_), channel_id=1, source_target_pairs={{0,16},{4,20},{8,24},{12,28},{16,0},{20,4},{24,8},{28,12},{1,17},{... | collective-permute-start | bytes 196616 | tf_op jit(solution)/shard_map/ppermute | solution.py:437
  5.6 3.1 %prep.1 = (bf16[4,8,64,512]{3,2,1,0:T(8,128)(2,1)S(1)}, f32[8,128]{1,0:T(8,128)S(1)}) custom-call(s32[2]{0:T(128)S(1)} %pad_add_fusion.place_ref, bf16[4,8,1,8,4096]{4,3,2,1,0:T(8,128)(2,1)} %affinity_hbm.1), custom_call_target="tpu_custom_call" | custom-call | tf_op jit(solution)/shard_map/prep/pallas_call | solution.py:41
  8.7 2.0 %collective-permute-done.refs_1_ = bf16[256,128]{1,0:T(8,128)(2,1)S(1)} collective-permute-done((bf16[256,128]{1,0:T(8,128)(2,1)S(1)}, bf16[256,128]{1,0:T(8,128)(2,1)S(1)}, u32[]{:S(2)}, u32[]{:S(2)}) %collective-permute-start) | collective-permute-done | bytes 65568 | tf_op jit(solution)/shard_map/ppermute | solution.py:437
  13.0 1.1 %product.11 = bf16[256,128]{1,0:T(8,128)(2,1)S(1)} custom-call(s32[2]{0:T(128)S(1)} %pad_add_fusion.place_ref, s32[4,8,1,8]{3,2,1,0:T(1,128)S(1)} %compare_select_fusion.columns_ref, bf16[4,8,64,512]{3,2,1,0:T(8,128)(2,1)S(1)} %get-tuple-element.17.matrix_ref, bf16[65,64,128]{2,1,0:T(8,128)(2,1)S(1)} %far.2.table), custom_call_target="tpu_custom_call" | custom-call | tf_op jit(solution)/shard_map/product/pallas_call | solution.py:41
  15.3 1.1 %product.9 = bf16[256,128]{1,0:T(8,128)(2,1)S(1)} custom-call(s32[2]{0:T(128)S(1)} %pad_add_fusion.place_ref, s32[4,8,1,8]{3,2,1,0:T(1,128)S(1)} %compare_select_fusion.columns_ref, bf16[4,8,64,512]{3,2,1,0:T(8,128)(2,1)S(1)} %get-tuple-element.17.matrix_ref, bf16[65,64,128]{2,1,0:T(8,128)(2,1)S(1)} %far.2.table), custom_call_target="tpu_custom_call" | custom-call | tf_op jit(solution)/shard_map/product/pallas_call | solution.py:41
  16.4 3.7 %collective-permute-start.4 = (bf16[256,128]{1,0:T(8,128)(2,1)S(1)}, bf16[256,128]{1,0:T(8,128)(2,1)S(1)}, u32[]{:S(2)}, u32[]{:S(2)}) collective-permute-start(bf16[256,128]{1,0:T(8,128)(2,1)S(1)} %product.9), channel_id=1, source_target_pairs={{0,3},{1,2},{2,1},{3,0},{4,7},{5,6},{6,5},{7,4},{8,11},{9,10},{10,... | collective-permute-start | bytes 196616 | tf_op jit(solution)/shard_map/ppermute | solution.py:437
  22.8 3.2 %collective-permute-done.5.refs_2_ = bf16[256,128]{1,0:T(8,128)(2,1)S(1)} collective-permute-done((bf16[256,128]{1,0:T(8,128)(2,1)S(1)}, bf16[256,128]{1,0:T(8,128)(2,1)S(1)}, u32[]{:S(2)}, u32[]{:S(2)}) %collective-permute-start.5) | collective-permute-done | bytes 65568 | tf_op jit(solution)/shard_map/ppermute | solution.py:437
  28.0 2.0 %collective-permute-start.7 = (bf16[352,128]{1,0:T(8,128)(2,1)S(1)}, bf16[352,128]{1,0:T(8,128)(2,1)S(1)}, u32[]{:S(2)}, u32[]{:S(2)}) collective-permute-start(bf16[352,128]{1,0:T(8,128)(2,1)S(1)} %middle.1.refs_0_), channel_id=1, source_target_pairs={{0,24},{4,28},{8,16},{12,20},{16,8},{20,12},{24,0},{28,4},{1,25},{... | collective-permute-start | bytes 270344 | tf_op jit(solution)/shard_map/ppermute | solution.py:437
  30.0 1.8 %collective-permute-done.9.refs_3_ = bf16[352,128]{1,0:T(8,128)(2,1)S(1)} collective-permute-done((bf16[352,128]{1,0:T(8,128)(2,1)S(1)}, bf16[352,128]{1,0:T(8,128)(2,1)S(1)}, u32[]{:S(2)}, u32[]{:S(2)}) %collective-permute-start.9) | collective-permute-done | bytes 90144 | tf_op jit(solution)/shard_map/ppermute | solution.py:437
  39.4 2.5 %collective-permute-start.11 = (bf16[272,128]{1,0:T(8,128)(2,1)S(1)}, bf16[272,128]{1,0:T(8,128)(2,1)S(1)}, u32[]{:S(2)}, u32[]{:S(2)}) collective-permute-start(bf16[272,128]{1,0:T(8,128)(2,1)S(1)} %product.13), channel_id=1, source_target_pairs={{0,3},{1,2},{2,1},{3,0},{4,7},{5,6},{6,5},{7,4},{8,11},{9,10},{10,... | collective-permute-start | bytes 208904 | tf_op jit(solution)/shard_map/ppermute | solution.py:437
  42.0 1.9 %collective-permute-start.13 = (bf16[272,128]{1,0:T(8,128)(2,1)S(1)}, bf16[272,128]{1,0:T(8,128)(2,1)S(1)}, u32[]{:S(2)}, u32[]{:S(2)}) collective-permute-start(bf16[272,128]{1,0:T(8,128)(2,1)S(1)} %product.15), channel_id=1, source_target_pairs={{0,1},{1,0},{2,3},{3,2},{4,5},{5,4},{6,7},{7,6},{8,9},{9,8},{10,11... | collective-permute-start | bytes 208904 | tf_op jit(solution)/shard_map/ppermute | solution.py:437
  45.0 1.4 %collective-permute-done.11.refs_1_ = bf16[272,128]{1,0:T(8,128)(2,1)S(1)} collective-permute-done((bf16[272,128]{1,0:T(8,128)(2,1)S(1)}, bf16[272,128]{1,0:T(8,128)(2,1)S(1)}, u32[]{:S(2)}, u32[]{:S(2)}) %collective-permute-start.11) | collective-permute-done | bytes 69664 | tf_op jit(solution)/shard_map/ppermute | solution.py:437
  46.3 2.4 %collective-permute-done.12.refs_2_ = bf16[272,128]{1,0:T(8,128)(2,1)S(1)} collective-permute-done((bf16[272,128]{1,0:T(8,128)(2,1)S(1)}, bf16[272,128]{1,0:T(8,128)(2,1)S(1)}, u32[]{:S(2)}, u32[]{:S(2)}) %collective-permute-start.12) | collective-permute-done | bytes 69664 | tf_op jit(solution)/shard_map/ppermute | solution.py:437
  49.6 2.3 %collective-permute-start.15 = (f32[64,128]{1,0:T(8,128)S(1)}, f32[64,128]{1,0:T(8,128)S(1)}, u32[]{:S(2)}, u32[]{:S(2)}) collective-permute-start(f32[64,128]{1,0:T(8,128)S(1)} %get-tuple-element.24.refs_0_), channel_id=1, source_target_pairs={{0,2},{1,3},{2,0},{3,1},{4,6},{5,7},{6,4},{7,5},{8,10},{9,11},{10,... | collective-permute-start | bytes 98312 | tf_op jit(solution)/shard_map/ppermute | solution.py:437
  52.0 1.7 %collective-permute-start.14 = (f32[64,128]{1,0:T(8,128)S(1)}, f32[64,128]{1,0:T(8,128)S(1)}, u32[]{:S(2)}, u32[]{:S(2)}) collective-permute-start(f32[64,128]{1,0:T(8,128)S(1)} %get-tuple-element.24.refs_0_), channel_id=1, source_target_pairs={{0,3},{1,2},{2,1},{3,0},{4,7},{5,6},{6,5},{7,4},{8,11},{9,10},{10,... | collective-permute-start | bytes 98312 | tf_op jit(solution)/shard_map/ppermute | solution.py:437
  53.6 1.2 %collective-permute-done.15.refs_2_ = f32[64,128]{1,0:T(8,128)S(1)} collective-permute-done((f32[64,128]{1,0:T(8,128)S(1)}, f32[64,128]{1,0:T(8,128)S(1)}, u32[]{:S(2)}, u32[]{:S(2)}) %collective-permute-start.15) | collective-permute-done | bytes 32800 | tf_op jit(solution)/shard_map/ppermute | solution.py:437
  54.9 2.8 %collective-permute-done.14.refs_1_ = f32[64,128]{1,0:T(8,128)S(1)} collective-permute-done((f32[64,128]{1,0:T(8,128)S(1)}, f32[64,128]{1,0:T(8,128)S(1)}, u32[]{:S(2)}, u32[]{:S(2)}) %collective-permute-start.14) | collective-permute-done | bytes 32800 | tf_op jit(solution)/shard_map/ppermute | solution.py:437
  57.7 1.2 %collective-permute-start.19 = (f32[32,128]{1,0:T(8,128)S(1)}, f32[32,128]{1,0:T(8,128)S(1)}, u32[]{:S(2)}, u32[]{:S(2)}) collective-permute-start(f32[32,128]{1,0:T(8,128)S(1)} %get-tuple-element.26), channel_id=1, source_target_pairs={{0,8},{4,12},{8,0},{12,4},{16,24},{20,28},{24,16},{28,20},{1,9},{5... | collective-permute-start | bytes 49160 | tf_op jit(solution)/shard_map/ppermute | solution.py:437
  58.9 1.4 %collective-permute-start.18 = (f32[32,128]{1,0:T(8,128)S(1)}, f32[32,128]{1,0:T(8,128)S(1)}, u32[]{:S(2)}, u32[]{:S(2)}) collective-permute-start(f32[32,128]{1,0:T(8,128)S(1)} %get-tuple-element.26), channel_id=1, source_target_pairs={{0,16},{4,20},{8,24},{12,28},{16,0},{20,4},{24,8},{28,12},{1,17},{... | collective-permute-start | bytes 49160 | tf_op jit(solution)/shard_map/ppermute | solution.py:437
  61.5 1.1 %collective-permute-done.18 = f32[32,128]{1,0:T(8,128)S(1)} collective-permute-done((f32[32,128]{1,0:T(8,128)S(1)}, f32[32,128]{1,0:T(8,128)S(1)}, u32[]{:S(2)}, u32[]{:S(2)}) %collective-permute-start.18) | collective-permute-done | bytes 16416 | tf_op jit(solution)/shard_map/ppermute | solution.py:437
  62.6 2.3 %collective-permute-done.17 = f32[32,128]{1,0:T(8,128)S(1)} collective-permute-done((f32[32,128]{1,0:T(8,128)S(1)}, f32[32,128]{1,0:T(8,128)S(1)}, u32[]{:S(2)}, u32[]{:S(2)}) %collective-permute-start.17) | collective-permute-done | bytes 16416 | tf_op jit(solution)/shard_map/ppermute | solution.py:437
  64.9 1.5 %first_factor.1.inverse_ref = f32[64,64]{1,0:T(8,128)S(1)} custom-call(f32[32,128]{1,0:T(8,128)S(1)} %get-tuple-element.25.gram_ref), custom_call_target="tpu_custom_call" | custom-call | tf_op jit(solution)/shard_map/first_factor/pallas_call | solution.py:41
  66.4 2.9 %finish.1 = f32[1,8,4096]{2,1,0:T(8,128)} custom-call(f32[256,128]{1,0:T(8,128)S(1)} %get-tuple-element.23.rows_ref, f32[64,64]{1,0:T(8,128)S(1)} %first_factor.1.inverse_ref, f32[32,128]{1,0:T(8,128)S(1)} %add_add_fusion.refs_0_, f32[32,128]{1,0:T(8,128)S(1)} %collective-permute-done.20.refs_1_), custom_call_target="tpu_custom_call" | custom-call | tf_op jit(solution)/shard_map/finish/pallas_call | solution.py:41
  (46 shorter events, 20.1 us)
Async XLA Ops:
  1.0 7.7 %collective-permute-start.2 = (bf16[256,128]{1,0:T(8,128)(2,1)S(1)}, bf16[256,128]{1,0:T(8,128)(2,1)S(1)}, u32[]{:S(2)}, u32[]{:S(2)}) collective-permute-start(bf16[256,128]{1,0:T(8,128)(2,1)S(1)} %get-tuple-element.18.refs_0_), channel_id=1, source_target_pairs={{0,8},{4,12},{8,0},{12,4},{16,24},{20,28},{24,16},{28,20},{1,9},{5... | collective-permute-start | bytes 196616 | tf_op jit(solution)/shard_map/ppermute | solution.py:437
  4.0 4.7 %collective-permute-start.1 = (bf16[256,128]{1,0:T(8,128)(2,1)S(1)}, bf16[256,128]{1,0:T(8,128)(2,1)S(1)}, u32[]{:S(2)}, u32[]{:S(2)}) collective-permute-start(bf16[256,128]{1,0:T(8,128)(2,1)S(1)} %get-tuple-element.18.refs_0_), channel_id=1, source_target_pairs={{0,16},{4,20},{8,24},{12,28},{16,0},{20,4},{24,8},{28,12},{1,17},{... | collective-permute-start | bytes 196616 | tf_op jit(solution)/shard_map/ppermute | solution.py:437
  5.5 5.2 %collective-permute-start = (bf16[256,128]{1,0:T(8,128)(2,1)S(1)}, bf16[256,128]{1,0:T(8,128)(2,1)S(1)}, u32[]{:S(2)}, u32[]{:S(2)}) collective-permute-start(bf16[256,128]{1,0:T(8,128)(2,1)S(1)} %get-tuple-element.18.refs_0_), channel_id=1, source_target_pairs={{0,24},{4,28},{8,16},{12,20},{16,8},{20,12},{24,0},{28,4},{1,25},{... | collective-permute-start | bytes 196616 | tf_op jit(solution)/shard_map/ppermute | solution.py:437
  5.6 5.2 %copy-start = (s32[4,8,1,8]{3,2,1,0:T(1,128)S(1)}, s32[4,8,1,8]{3,2,1,0:T(1,128)}, u32[]{:S(2)}) copy-start(s32[4,8,1,8]{3,2,1,0:T(1,128)} %param.6) | copy-start | bytes 3076
  5.6 5.2 %copy-start.1 = (s32[4,8,1]{1,2,0:T(1,128)S(1)}, s32[4,8,1]{1,2,0:T(1,128)}, u32[]{:S(2)}) copy-start(s32[4,8,1]{1,2,0:T(1,128)} %param.7) | copy-start | bytes 388
  10.7 1.6 %collective-permute-start.3 = (bf16[4,256,128]{2,1,0:T(8,128)(2,1)S(1)}, bf16[4,256,128]{2,1,0:T(8,128)(2,1)S(1)}, u32[]{:S(2)}, u32[]{:S(2)}) collective-permute-start(bf16[4,256,128]{2,1,0:T(8,128)(2,1)S(1)} %stack.14.near_ref), channel_id=1, source_target_pairs={{0,4},{4,0},{8,12},{12,8},{16,20},{20,16},{24,28},{28,24},{1,5},{5... | collective-permute-start | bytes 786440 | tf_op jit(solution)/shard_map/ppermute | solution.py:437
  16.4 6.4 %collective-permute-start.4 = (bf16[256,128]{1,0:T(8,128)(2,1)S(1)}, bf16[256,128]{1,0:T(8,128)(2,1)S(1)}, u32[]{:S(2)}, u32[]{:S(2)}) collective-permute-start(bf16[256,128]{1,0:T(8,128)(2,1)S(1)} %product.9), channel_id=1, source_target_pairs={{0,3},{1,2},{2,1},{3,0},{4,7},{5,6},{6,5},{7,4},{8,11},{9,10},{10,... | collective-permute-start | bytes 196616 | tf_op jit(solution)/shard_map/ppermute | solution.py:437
  20.1 5.9 %collective-permute-start.5 = (bf16[256,128]{1,0:T(8,128)(2,1)S(1)}, bf16[256,128]{1,0:T(8,128)(2,1)S(1)}, u32[]{:S(2)}, u32[]{:S(2)}) collective-permute-start(bf16[256,128]{1,0:T(8,128)(2,1)S(1)} %product.10), channel_id=1, source_target_pairs={{0,2},{1,3},{2,0},{3,1},{4,6},{5,7},{6,4},{7,5},{8,10},{9,11},{10,... | collective-permute-start | bytes 196616 | tf_op jit(solution)/shard_map/ppermute | solution.py:437
  20.1 5.9 %collective-permute-start.6 = (bf16[256,128]{1,0:T(8,128)(2,1)S(1)}, bf16[256,128]{1,0:T(8,128)(2,1)S(1)}, u32[]{:S(2)}, u32[]{:S(2)}) collective-permute-start(bf16[256,128]{1,0:T(8,128)(2,1)S(1)} %product.11), channel_id=1, source_target_pairs={{0,1},{1,0},{2,3},{3,2},{4,5},{5,4},{6,7},{7,6},{8,9},{9,8},{10,11... | collective-permute-start | bytes 196616 | tf_op jit(solution)/shard_map/ppermute | solution.py:437
  26.4 5.4 %collective-permute-start.9 = (bf16[352,128]{1,0:T(8,128)(2,1)S(1)}, bf16[352,128]{1,0:T(8,128)(2,1)S(1)}, u32[]{:S(2)}, u32[]{:S(2)}) collective-permute-start(bf16[352,128]{1,0:T(8,128)(2,1)S(1)} %middle.1.refs_0_), channel_id=1, source_target_pairs={{0,8},{4,12},{8,0},{12,4},{16,24},{20,28},{24,16},{28,20},{1,9},{5... | collective-permute-start | bytes 270344 | tf_op jit(solution)/shard_map/ppermute | solution.py:437
  27.0 5.5 %collective-permute-start.8 = (bf16[352,128]{1,0:T(8,128)(2,1)S(1)}, bf16[352,128]{1,0:T(8,128)(2,1)S(1)}, u32[]{:S(2)}, u32[]{:S(2)}) collective-permute-start(bf16[352,128]{1,0:T(8,128)(2,1)S(1)} %middle.1.refs_0_), channel_id=1, source_target_pairs={{0,16},{4,20},{8,24},{12,28},{16,0},{20,4},{24,8},{28,12},{1,17},{... | collective-permute-start | bytes 270344 | tf_op jit(solution)/shard_map/ppermute | solution.py:437
  28.0 5.5 %collective-permute-start.7 = (bf16[352,128]{1,0:T(8,128)(2,1)S(1)}, bf16[352,128]{1,0:T(8,128)(2,1)S(1)}, u32[]{:S(2)}, u32[]{:S(2)}) collective-permute-start(bf16[352,128]{1,0:T(8,128)(2,1)S(1)} %middle.1.refs_0_), channel_id=1, source_target_pairs={{0,24},{4,28},{8,16},{12,20},{16,8},{20,12},{24,0},{28,4},{1,25},{... | collective-permute-start | bytes 270344 | tf_op jit(solution)/shard_map/ppermute | solution.py:437
  33.5 1.7 %collective-permute-start.10 = (bf16[4,352,128]{2,1,0:T(8,128)(2,1)S(1)}, bf16[4,352,128]{2,1,0:T(8,128)(2,1)S(1)}, u32[]{:S(2)}, u32[]{:S(2)}) collective-permute-start(bf16[4,352,128]{2,1,0:T(8,128)(2,1)S(1)} %stack.15.near_ref), channel_id=1, source_target_pairs={{0,4},{4,0},{8,12},{12,8},{16,20},{20,16},{24,28},{28,24},{1,5},{5... | collective-permute-start | bytes 1081352 | tf_op jit(solution)/shard_map/ppermute | solution.py:437
  39.4 6.9 %collective-permute-start.11 = (bf16[272,128]{1,0:T(8,128)(2,1)S(1)}, bf16[272,128]{1,0:T(8,128)(2,1)S(1)}, u32[]{:S(2)}, u32[]{:S(2)}) collective-permute-start(bf16[272,128]{1,0:T(8,128)(2,1)S(1)} %product.13), channel_id=1, source_target_pairs={{0,3},{1,2},{2,1},{3,0},{4,7},{5,6},{6,5},{7,4},{8,11},{9,10},{10,... | collective-permute-start | bytes 208904 | tf_op jit(solution)/shard_map/ppermute | solution.py:437
  41.9 6.8 %collective-permute-start.12 = (bf16[272,128]{1,0:T(8,128)(2,1)S(1)}, bf16[272,128]{1,0:T(8,128)(2,1)S(1)}, u32[]{:S(2)}, u32[]{:S(2)}) collective-permute-start(bf16[272,128]{1,0:T(8,128)(2,1)S(1)} %product.14), channel_id=1, source_target_pairs={{0,2},{1,3},{2,0},{3,1},{4,6},{5,7},{6,4},{7,5},{8,10},{9,11},{10,... | collective-permute-start | bytes 208904 | tf_op jit(solution)/shard_map/ppermute | solution.py:437
  42.0 6.8 %collective-permute-start.13 = (bf16[272,128]{1,0:T(8,128)(2,1)S(1)}, bf16[272,128]{1,0:T(8,128)(2,1)S(1)}, u32[]{:S(2)}, u32[]{:S(2)}) collective-permute-start(bf16[272,128]{1,0:T(8,128)(2,1)S(1)} %product.15), channel_id=1, source_target_pairs={{0,1},{1,0},{2,3},{3,2},{4,5},{5,4},{6,7},{7,6},{8,9},{9,8},{10,11... | collective-permute-start | bytes 208904 | tf_op jit(solution)/shard_map/ppermute | solution.py:437
  49.2 4.4 %collective-permute-start.16 = (f32[64,128]{1,0:T(8,128)S(1)}, f32[64,128]{1,0:T(8,128)S(1)}, u32[]{:S(2)}, u32[]{:S(2)}) collective-permute-start(f32[64,128]{1,0:T(8,128)S(1)} %get-tuple-element.24.refs_0_), channel_id=1, source_target_pairs={{0,1},{1,0},{2,3},{3,2},{4,5},{5,4},{6,7},{7,6},{8,9},{9,8},{10,11... | collective-permute-start | bytes 98312 | tf_op jit(solution)/shard_map/ppermute | solution.py:437
  49.6 5.2 %collective-permute-start.15 = (f32[64,128]{1,0:T(8,128)S(1)}, f32[64,128]{1,0:T(8,128)S(1)}, u32[]{:S(2)}, u32[]{:S(2)}) collective-permute-start(f32[64,128]{1,0:T(8,128)S(1)} %get-tuple-element.24.refs_0_), channel_id=1, source_target_pairs={{0,2},{1,3},{2,0},{3,1},{4,6},{5,7},{6,4},{7,5},{8,10},{9,11},{10,... | collective-permute-start | bytes 98312 | tf_op jit(solution)/shard_map/ppermute | solution.py:437
  52.0 5.7 %collective-permute-start.14 = (f32[64,128]{1,0:T(8,128)S(1)}, f32[64,128]{1,0:T(8,128)S(1)}, u32[]{:S(2)}, u32[]{:S(2)}) collective-permute-start(f32[64,128]{1,0:T(8,128)S(1)} %get-tuple-element.24.refs_0_), channel_id=1, source_target_pairs={{0,3},{1,2},{2,1},{3,0},{4,7},{5,6},{6,5},{7,4},{8,11},{9,10},{10,... | collective-permute-start | bytes 98312 | tf_op jit(solution)/shard_map/ppermute | solution.py:437
  57.7 3.8 %collective-permute-start.19 = (f32[32,128]{1,0:T(8,128)S(1)}, f32[32,128]{1,0:T(8,128)S(1)}, u32[]{:S(2)}, u32[]{:S(2)}) collective-permute-start(f32[32,128]{1,0:T(8,128)S(1)} %get-tuple-element.26), channel_id=1, source_target_pairs={{0,8},{4,12},{8,0},{12,4},{16,24},{20,28},{24,16},{28,20},{1,9},{5... | collective-permute-start | bytes 49160 | tf_op jit(solution)/shard_map/ppermute | solution.py:437
  58.9 3.7 %collective-permute-start.18 = (f32[32,128]{1,0:T(8,128)S(1)}, f32[32,128]{1,0:T(8,128)S(1)}, u32[]{:S(2)}, u32[]{:S(2)}) collective-permute-start(f32[32,128]{1,0:T(8,128)S(1)} %get-tuple-element.26), channel_id=1, source_target_pairs={{0,16},{4,20},{8,24},{12,28},{16,0},{20,4},{24,8},{28,12},{1,17},{... | collective-permute-start | bytes 49160 | tf_op jit(solution)/shard_map/ppermute | solution.py:437
  60.3 4.6 %collective-permute-start.17 = (f32[32,128]{1,0:T(8,128)S(1)}, f32[32,128]{1,0:T(8,128)S(1)}, u32[]{:S(2)}, u32[]{:S(2)}) collective-permute-start(f32[32,128]{1,0:T(8,128)S(1)} %get-tuple-element.26), channel_id=1, source_target_pairs={{0,24},{4,28},{8,16},{12,20},{16,8},{20,12},{24,0},{28,4},{1,25},{... | collective-permute-start | bytes 49160 | tf_op jit(solution)/shard_map/ppermute | solution.py:437
  64.9 1.5 %collective-permute-start.20 = (f32[32,128]{1,0:T(8,128)S(1)}, f32[32,128]{1,0:T(8,128)S(1)}, u32[]{:S(2)}, u32[]{:S(2)}) collective-permute-start(f32[32,128]{1,0:T(8,128)S(1)} %add_add_fusion.refs_0_), channel_id=1, source_target_pairs={{0,4},{4,0},{8,12},{12,8},{16,20},{20,16},{24,28},{28,24},{1,5},{5... | collective-permute-start | bytes 49160 | tf_op jit(solution)/shard_map/ppermute | solution.py:437

commit v4 on v3

--- a/solution.py
+++ b/solution.py
@@ -96,20 +96,21 @@
     )
 
 
-def prep_kernel(place_ref, affinity_hbm, out_ref, done_ref, affinity_ref, scratch, sems):
+def prep_kernel(ranges, affinity_hbm, out_ref, done_ref, affinity_ref, scratch, sems):
     done_ref[...] = jnp.zeros_like(done_ref)
-    groups, block_rows, _, slots, flat = affinity_ref.shape
+    count, block_rows, _, slots, flat = affinity_ref.shape
     half = flat // 128
+    own = lax.axis_index("cols")
     copies = [
-        pltpu.make_async_copy(affinity_hbm.at[m ^ place_ref[1]], affinity_ref.at[m], sems.at[m])
-        for m in range(groups)
+        pltpu.make_async_copy(affinity_hbm.at[m ^ own], affinity_ref.at[place], sems.at[place])
+        for place, m in enumerate(ranges)
     ]
     for copy in copies:
         copy.start()
     source, target = iota((256, 256), 0), iota((256, 256), 1)
     moved = (source // 64 % 2) * 128 + (source // 128) * 64 + (source % 2) * 32 + source % 64 // 2
     permute = (moved == target).astype(BF16)
-    for m in range(groups):
+    for m in range(count):
         copies[m].wait()
         for i in range(block_rows):
             block = affinity_ref[m, i, 0].astype(F32)
@@ -128,18 +129,19 @@
                 out_ref[m, i, half:, s * 128 : (s + 1) * 128] = piece[:, 128:]
 
 
-def prep(place, affinity):
-    groups, block_rows, _, slots, flat = affinity.shape
-    return call(
-        prep_kernel,
+def prep(ranges, affinity):
+    _, block_rows, _, slots, flat = affinity.shape
+    count = len(ranges)
+    return call(
+        functools.partial(prep_kernel, ranges),
         "prep",
-        [smem(), hbm()],
-        (shaped((groups, block_rows, 64, slots * 64), BF16), shaped((8, 128), F32)),
-        (place, affinity),
+        [hbm()],
+        (shaped((count, block_rows, 64, slots * 64), BF16), shaped((8, 128), F32)),
+        (affinity,),
         [
-            pltpu.VMEM(affinity.shape, BF16),
+            pltpu.VMEM((count,) + affinity.shape[1:], BF16),
             pltpu.VMEM((2, flat // 128 * slots, 128), F32),
-            pltpu.SemaphoreType.DMA((groups,)),
+            pltpu.SemaphoreType.DMA((count,)),
         ],
     )
 
@@ -173,11 +175,11 @@
     )
 
 
-def fill_table(place_ref, pieces_ref, offsets, table):
+def fill_table(pieces_ref, offsets, table):
     block_rows = (table.shape[0] - 1) // (2 * len(offsets))
     low = iota((32, 128), 1) < 64
     for index, offset in enumerate(offsets):
-        base = (place_ref[0] ^ offset) * block_rows
+        base = (lax.axis_index("rows") ^ offset) * block_rows
         for i in range(block_rows):
             block = pieces_ref[index, i * 32 : (i + 1) * 32, :]
             turned = jnp.concatenate([block[:, 64:], block[:, :64]], axis=1)
@@ -185,17 +187,41 @@
             table[base + i, 32:] = jnp.where(low, turned, block)
 
 
-def near_kernel(offsets, place_ref, near_ref, table):
+def near_kernel(offsets, near_ref, table):
     table[table.shape[0] - 1] = jnp.zeros(table.shape[1:], BF16)
-    fill_table(place_ref, near_ref, offsets, table)
-
-
-def far_kernel(offsets, place_ref, far_ref, near_ref, old_table, table, *grams):
+    fill_table(near_ref, offsets, table)
+
+
+def near_table(offsets, near, block_rows):
+    count = near.shape[0]
+    return call(
+        functools.partial(near_kernel, offsets[:count]),
+        "near",
+        [vmem()],
+        shaped((2 * count * block_rows + 1, 64, 128), BF16),
+        (near,),
+    )
+
+
+def one_product(group, columns, matrix, table, out_ref):
+    block_rows, slots = columns.shape[1], columns.shape[3]
+    low = iota((32, 128), 1) < 64
+    for i in range(block_rows):
+        picked = [table[columns[group, i, 0, s]] for s in range(slots)]
+        result = jnp.dot(matrix[i], jnp.concatenate(picked, axis=0), preferred_element_type=F32)
+        out_ref[i * 32 : (i + 1) * 32, :] = jnp.where(low, result[:32], result[32:]).astype(BF16)
+
+
+def others_kernel(offsets, ranges, columns_any, matrix_ref, far_ref, near_ref, old_table, table, *refs):
     del old_table
-    fill_table(place_ref, far_ref, offsets, table)
+    *outs, columns, sem = refs
+    copy = pltpu.make_async_copy(columns_any, columns, sem)
+    copy.start()
+    fill_table(far_ref, offsets, table)
+    terms, grams = outs[: len(ranges)], outs[len(ranges) :]
+    first = matrix_ref.shape[1] * 32
     if grams:
         gram_ref, trace_ref = grams
-        first = (table.shape[0] - 1) // (2 * len(offsets)) * 32
         gram = joined(near_ref, 0, first) + joined(far_ref, 0, first)
         for index in range(1, len(offsets)):
             gram = gram + joined(near_ref, index, first) + joined(far_ref, index, first)
@@ -203,64 +229,45 @@
         row, lane = iota(gram.shape, 0), iota(gram.shape, 1)
         diagonal = lane % 64 == row + lane // 64 * 32
         trace = jnp.sum(jnp.where(diagonal, gram, 0.0), axis=(0, 1), keepdims=True)
-        trace_ref[...] = jnp.broadcast_to(trace, trace_ref.shape).astype(BF16)
-
-
-def tables(offsets, place, near, far, block_rows):
-    count = near.shape[0]
-    table_shape = shaped((2 * count * block_rows + 1, 64, 128), BF16)
-    table = call(
-        functools.partial(near_kernel, offsets[:count]),
-        "near",
-        [smem(), vmem()],
-        table_shape,
-        (place, near),
-    )
-    outs = [table_shape]
-    if near.shape[1] > block_rows * 32:
+        trace = jnp.broadcast_to(trace, trace_ref.shape).astype(BF16)
+        trace_ref[...] = trace
+        for term in terms:
+            term[first:, :] = trace
+    copy.wait()
+    for place, m in enumerate(ranges):
+        group = m ^ lax.axis_index("cols")
+        one_product(group, columns, matrix_ref.at[place], table, terms[place])
+
+
+def own_kernel(columns, matrix_ref, table, out_ref):
+    one_product(lax.axis_index("cols"), columns, matrix_ref.at[0], table, out_ref)
+
+
+def products(offsets, ranges, columns, matrix, own_matrix, near, far, table):
+    block_rows, count = matrix.shape[1], near.shape[0]
+    extra = near.shape[1] > block_rows * 32
+    rows = block_rows * 32
+    outs = [shaped(table.shape, BF16)] + [shaped((rows + 16 * extra, 128), BF16)] * len(ranges)
+    if extra:
         outs += [shaped((32, 128), F32), shaped((16, 128), BF16)]
-    return call(
-        functools.partial(far_kernel, offsets[count:]),
-        "far",
-        [smem(), vmem(), vmem(), vmem()],
+    table, *outs = call(
+        functools.partial(others_kernel, offsets[count:], ranges),
+        "others",
+        [pl.BlockSpec(memory_space=pl.ANY)] + [vmem()] * 4,
         outs,
-        (place, far, near, table),
-        input_output_aliases={3: 0},
-    )
-
-
-def product_kernel(m, place_ref, columns_ref, matrix_ref, table, *refs):
-    out_ref = refs[-1]
-    block_rows, slots = columns_ref.shape[1], columns_ref.shape[3]
-    group = m ^ place_ref[1]
-    low = iota((32, 128), 1) < 64
-    for i in range(block_rows):
-        picked = [table[columns_ref[group, i, 0, s]] for s in range(slots)]
-        result = jnp.dot(
-            matrix_ref[m, i], jnp.concatenate(picked, axis=0), preferred_element_type=F32
-        )
-        out_ref[i * 32 : (i + 1) * 32, :] = jnp.where(low, result[:32], result[32:]).astype(BF16)
-    if len(refs) > 1:
-        out_ref[block_rows * 32 :, :] = refs[0][...]
-
-
-def product(m, place, columns, matrix, table, trace):
-    rows = matrix.shape[1] * 32 + sum(extra.shape[0] for extra in trace)
-    return call(
-        functools.partial(product_kernel, m),
-        "product",
-        [smem(), smem()] + [vmem()] * (2 + len(trace)),
+        (columns, matrix, far, near, table),
+        [pltpu.SMEM(columns.shape, jnp.int32), pltpu.SemaphoreType.DMA],
+        input_output_aliases={4: 0},
+    )
+    terms = [swap(term, "cols", m) for m, term in zip(ranges, outs)]
+    own = call(
+        own_kernel,
+        "own",
+        [smem(), vmem(), vmem()],
         shaped((rows, 128), BF16),
-        (place, columns, matrix, table, *trace),
-    )
-
-
-def products(place, columns, matrix, table, trace):
-    groups = matrix.shape[0]
-    terms = []
-    for m in range(groups - 1, 0, -1):
-        terms.append(swap(product(m, place, columns, matrix, table, trace), "cols", m))
-    return [product(0, place, columns, matrix, table, trace)] + terms
+        (columns, own_matrix, table),
+    )
+    return [own] + terms, outs[len(ranges) :]
 
 
 def add_terms(terms, rows):
@@ -298,10 +305,10 @@
     )
 
 
-def collect_kernel(total, degree_ref, first_ref, *refs):
+def collect_kernel(total, degree_ref, first_ref, trace_ref, *refs):
     terms, (rows_ref, grams_ref) = refs[:-2], refs[-2:]
     count = degree_ref.shape[0]
-    largest = terms[0][count:].astype(F32)
+    largest = trace_ref[...].astype(F32)
     for term in terms[1:]:
         largest = jnp.maximum(largest, term[count:].astype(F32))
     scale = lax.rsqrt(largest[:1] / total)
@@ -311,13 +318,13 @@
     grams_ref[:32] = local_gram(rows)
 
 
-def collect(total, degree, first, terms):
+def collect(total, degree, first, trace, terms):
     return call(
         functools.partial(collect_kernel, total),
         "collect",
-        [vmem()] * (2 + len(terms)),
+        [vmem()] * (3 + len(terms)),
         (shaped(degree.shape, F32), shaped((64, 128), F32)),
-        (degree, first, *terms),
+        (degree, first, trace, *terms),
     )
 
 
@@ -384,6 +391,23 @@
     )
 
 
+def add_parts_kernel(count, *refs):
+    summed = refs[0][...]
+    for part in refs[1:count]:
+        summed = summed + part[...]
+    refs[-1][...] = summed
+
+
+def add_parts(parts, after):
+    return call(
+        functools.partial(add_parts_kernel, len(parts)),
+        "add_parts",
+        [vmem()] * (len(parts) + len(after)),
+        shaped(parts[0].shape, F32),
+        (*parts, *after),
+    )
+
+
 def first_factor_kernel(gram_ref, out_ref):
     unit = (iota((64, 64), 0) == iota((64, 64), 1)).astype(F32)
     out_ref[...] = lower_solve(unpacked(gram_ref[...]), unit)
@@ -459,10 +483,10 @@
     return near, swap(near, "rows", last), offsets
 
 
-def add_rows(gram):
+def add_rows(gram, after):
     *plan, (last,) = stages(lax.axis_size("rows"))
     for masks in plan:
-        gram = sum([swap(gram, "rows", mask) for mask in masks], gram)
+        gram = add_parts([gram] + [swap(gram, "rows", mask) for mask in masks], after)
     return [gram, swap(gram, "rows", last)]
 
 
@@ -472,25 +496,26 @@
     ranks = lax.axis_size("rows")
     total = float(groups * ranks * block_rows * block_size)
     blocks = ranks * block_rows
-    place = jnp.stack([lax.axis_index("rows"), lax.axis_index("cols")]).astype(jnp.int32)
     live = iota(block_columns.shape, 3) < block_counts[..., None]
     columns = jnp.where(live, jnp.clip(block_columns, 0, blocks - 1), blocks)
-
     panel, inv_degree, affinity = (
         pltpu.with_memory_space_constraint(value, pltpu.HBM) for value in (panel, inv_degree, affinity)
     )
+    ranges = list(range(groups - 1, 0, -1))
+
     scaled, degree = start(panel, inv_degree)
-    matrix, done = prep(place, affinity)
+    matrix, done = prep(ranges, affinity)
+    own_matrix, _ = prep([0], affinity)
     near, far, offsets = gather_rows(scaled, [done])
-    (table,) = tables(offsets, place, near, far, block_rows)
-    terms = products(place, columns, matrix, table, [])
+    table = near_table(offsets, near, block_rows)
+    terms, _ = products(offsets, ranges, columns, matrix, own_matrix, near, far, table)
     near, far, offsets = gather_rows(middle(degree, terms), [])
-    table, first, trace = tables(offsets, place, near, far, block_rows)
-    terms = products(place, columns, matrix, table, [trace])
-    rows, grams = collect(total, degree, first, terms)
-    parts = [grams] + [swap(grams, "cols", m) for m in range(groups - 1, 0, -1)]
-    gram, first = add_columns(total, parts)
-    return finish(total, block_rows, rows, first_factor(first), add_rows(gram))
+    table = near_table(offsets, near, block_rows)
+    terms, (first, trace) = products(offsets, ranges, columns, matrix, own_matrix, near, far, table)
+    rows, grams = collect(total, degree, first, trace, terms)
+    gram, first = add_columns(total, [grams] + [swap(grams, "cols", m) for m in ranges])
+    inverse = first_factor(first)
+    return finish(total, block_rows, rows, inverse, add_rows(gram, [inverse]))
 
 
 def solution(mesh):

time: 69.5 us -> 64.1 us (0.922)
  Pallas kernels: 21.2 us -> 15.8 us
    pallas_call x21 -> x17, Pallas kernels: 21.2 us -> 15.8 us  [call(): pl.pallas_call(kernel, out_shape=outs, in_specs=ins, out_specs=jax.tree.m...]
  transfers between devices with their start and end apart: 21 -> 21, of which waited for: 15 -> 14; matrix products, arithmetic and copies ran while one was open for 0% -> 0% of each run, Pallas kernels for 12% -> 12%
where the time goes in v4:
time: 64.1 us; the launch traced here: 63.9 us
  starting transfers between devices  25.1 us (39%)
  waiting for transfers between devices  22.7 us (35%)
  Pallas kernels  15.8 us (25%)
    ppermute x21, starting transfers between devices, swap(): lax.ppermute(value, axis, [(index, index ^ mask) for index in range(size)])  25.1 us
    ppermute x21, waiting for transfers between devices, swap(): lax.ppermute(value, axis, [(index, index ^ mask) for index in range(size)])  22.7 us
    pallas_call x17, Pallas kernels, call(): pl.pallas_call(kernel, out_shape=outs, in_specs=ins, out_specs=jax.tree.m...  15.8 us
  transfers between devices with their start and end apart: 21, of which 14 were waited for; matrix products, arithmetic and copies ran while one was open for 0% of the time, Pallas kernels for 12%

profile of v4, /device:TPU:0, one launch (start us, length us, event | category | flops | bytes accessed | tf_op | source)
XLA Modules:
  0.0 63.9 jit_solution(17794629099850967010)
XLA Ops:
  1.0 3.0 %collective-permute-start.2 = (bf16[256,128]{1,0:T(8,128)(2,1)S(1)}, bf16[256,128]{1,0:T(8,128)(2,1)S(1)}, u32[]{:S(2)}, u32[]{:S(2)}) collective-permute-start(bf16[256,128]{1,0:T(8,128)(2,1)S(1)} %get-tuple-element.27.refs_0_), channel_id=1, source_target_pairs={{0,8},{4,12},{8,0},{12,4},{16,24},{20,28},{24,16},{28,20},{1,9},{5... | collective-permute-start | bytes 196616 | tf_op jit(solution)/shard_map/ppermute | solution.py:461
  4.0 1.5 %collective-permute-start.1 = (bf16[256,128]{1,0:T(8,128)(2,1)S(1)}, bf16[256,128]{1,0:T(8,128)(2,1)S(1)}, u32[]{:S(2)}, u32[]{:S(2)}) collective-permute-start(bf16[256,128]{1,0:T(8,128)(2,1)S(1)} %get-tuple-element.27.refs_0_), channel_id=1, source_target_pairs={{0,16},{4,20},{8,24},{12,28},{16,0},{20,4},{24,8},{28,12},{1,17},{... | collective-permute-start | bytes 196616 | tf_op jit(solution)/shard_map/ppermute | solution.py:461
  5.6 2.2 %prep.2 = (bf16[3,8,64,512]{3,2,1,0:T(8,128)(2,1)S(1)}, f32[8,128]{1,0:T(8,128)S(1)}) custom-call(bf16[4,8,1,8,4096]{4,3,2,1,0:T(8,128)(2,1)} %affinity_hbm.3), custom_call_target="tpu_custom_call" | custom-call | tf_op jit(solution)/shard_map/prep/pallas_call | solution.py:41
  8.3 2.4 %collective-permute-done.refs_1_ = bf16[256,128]{1,0:T(8,128)(2,1)S(1)} collective-permute-done((bf16[256,128]{1,0:T(8,128)(2,1)S(1)}, bf16[256,128]{1,0:T(8,128)(2,1)S(1)}, u32[]{:S(2)}, u32[]{:S(2)}) %collective-permute-start) | collective-permute-done | bytes 65568 | tf_op jit(solution)/shard_map/ppermute | solution.py:461
  12.3 1.6 %others.2 = (bf16[65,64,128]{2,1,0:T(8,128)(2,1)S(1)}, bf16[256,128]{1,0:T(8,128)(2,1)S(1)}, bf16[256,128]{1,0:T(8,128)(2,1)S(1)}, bf16[256,128]{1,0:T(8,128)(2,1)S(1)}) custom-call(s32[4,8,1,8]{3,2,1,0:T(1,128)S(1)} %compare_select_fusion.columns_any.columns, ...), custom_call_target="tpu_custom_call", output_to_operand_aliasing={{0}: (4, {})} | custom-call | tf_op jit(solution)/shard_map/others/pallas_call | solution.py:41
  13.9 3.7 %collective-permute-start.4 = (bf16[256,128]{1,0:T(8,128)(2,1)S(1)}, bf16[256,128]{1,0:T(8,128)(2,1)S(1)}, u32[]{:S(2)}, u32[]{:S(2)}) collective-permute-start(bf16[256,128]{1,0:T(8,128)(2,1)S(1)} %get-tuple-element.30), channel_id=1, source_target_pairs={{0,3},{1,2},{2,1},{3,0},{4,7},{5,6},{6,5},{7,4},{8,11},{9,10},{10,... | collective-permute-start | bytes 196616 | tf_op jit(solution)/shard_map/ppermute | solution.py:461
  18.4 1.6 %prep.3 = (bf16[1,8,64,512]{3,2,1,0:T(8,128)(2,1)S(1)}, f32[8,128]{1,0:T(8,128)}) custom-call(bf16[4,8,1,8,4096]{4,3,2,1,0:T(8,128)(2,1)} %affinity_hbm.3), custom_call_target="tpu_custom_call" | custom-call | tf_op jit(solution)/shard_map/prep/pallas_call | solution.py:41
  21.2 2.3 %collective-permute-done.5.refs_2_ = bf16[256,128]{1,0:T(8,128)(2,1)S(1)} collective-permute-done((bf16[256,128]{1,0:T(8,128)(2,1)S(1)}, bf16[256,128]{1,0:T(8,128)(2,1)S(1)}, u32[]{:S(2)}, u32[]{:S(2)}) %collective-permute-start.5) | collective-permute-done | bytes 65568 | tf_op jit(solution)/shard_map/ppermute | solution.py:461
  25.1 2.4 %collective-permute-start.7 = (bf16[352,128]{1,0:T(8,128)(2,1)S(1)}, bf16[352,128]{1,0:T(8,128)(2,1)S(1)}, u32[]{:S(2)}, u32[]{:S(2)}) collective-permute-start(bf16[352,128]{1,0:T(8,128)(2,1)S(1)} %middle.1.refs_0_), channel_id=1, source_target_pairs={{0,24},{4,28},{8,16},{12,20},{16,8},{20,12},{24,0},{28,4},{1,25},{... | collective-permute-start | bytes 270344 | tf_op jit(solution)/shard_map/ppermute | solution.py:461
  27.5 1.9 %collective-permute-done.9.refs_3_ = bf16[352,128]{1,0:T(8,128)(2,1)S(1)} collective-permute-done((bf16[352,128]{1,0:T(8,128)(2,1)S(1)}, bf16[352,128]{1,0:T(8,128)(2,1)S(1)}, u32[]{:S(2)}, u32[]{:S(2)}) %collective-permute-start.9) | collective-permute-done | bytes 90144 | tf_op jit(solution)/shard_map/ppermute | solution.py:461
  29.4 1.4 %collective-permute-done.8.refs_2_ = bf16[352,128]{1,0:T(8,128)(2,1)S(1)} collective-permute-done((bf16[352,128]{1,0:T(8,128)(2,1)S(1)}, bf16[352,128]{1,0:T(8,128)(2,1)S(1)}, u32[]{:S(2)}, u32[]{:S(2)}) %collective-permute-start.8) | collective-permute-done | bytes 90144 | tf_op jit(solution)/shard_map/ppermute | solution.py:461
  31.1 1.5 %collective-permute-done.10.far_ref = bf16[4,352,128]{2,1,0:T(8,128)(2,1)S(1)} collective-permute-done((bf16[4,352,128]{2,1,0:T(8,128)(2,1)S(1)}, bf16[4,352,128]{2,1,0:T(8,128)(2,1)S(1)}, u32[]{:S(2)}, u32[]{:S(2)}) %collective-permute-start.10) | collective-permute-done | bytes 360480 | tf_op jit(solution)/shard_map/ppermute | solution.py:461
  32.6 1.6 %others.3 = (bf16[65,64,128]{2,1,0:T(8,128)(2,1)S(1)}, bf16[272,128]{1,0:T(8,128)(2,1)S(1)}, bf16[272,128]{1,0:T(8,128)(2,1)S(1)}, bf16[272,128]{1,0:T(8,128)(2,...) custom-call(s32[4,8,1,8]{3,2,1,0:T(1,128)S(1)} %compare_select_fusion.columns_any.colu, ...), custom_call_target="tpu_custom_call", output_to_operand_aliasing={{0}: (4, {})} | custom-call | tf_op jit(solution)/shard_map/others/pallas_call | solution.py:41
  34.2 2.3 %collective-permute-start.11 = (bf16[272,128]{1,0:T(8,128)(2,1)S(1)}, bf16[272,128]{1,0:T(8,128)(2,1)S(1)}, u32[]{:S(2)}, u32[]{:S(2)}) collective-permute-start(bf16[272,128]{1,0:T(8,128)(2,1)S(1)} %get-tuple-element.36), channel_id=1, source_target_pairs={{0,3},{1,2},{2,1},{3,0},{4,7},{5,6},{6,5},{7,4},{8,11},{9,10},{10,... | collective-permute-start | bytes 208904 | tf_op jit(solution)/shard_map/ppermute | solution.py:461
  36.5 2.1 %collective-permute-start.13 = (bf16[272,128]{1,0:T(8,128)(2,1)S(1)}, bf16[272,128]{1,0:T(8,128)(2,1)S(1)}, u32[]{:S(2)}, u32[]{:S(2)}) collective-permute-start(bf16[272,128]{1,0:T(8,128)(2,1)S(1)} %get-tuple-element.38), channel_id=1, source_target_pairs={{0,1},{1,0},{2,3},{3,2},{4,5},{5,4},{6,7},{7,6},{8,9},{9,8},{10,11... | collective-permute-start | bytes 208904 | tf_op jit(solution)/shard_map/ppermute | solution.py:461
  41.1 2.1 %collective-permute-done.12.refs_2_ = bf16[272,128]{1,0:T(8,128)(2,1)S(1)} collective-permute-done((bf16[272,128]{1,0:T(8,128)(2,1)S(1)}, bf16[272,128]{1,0:T(8,128)(2,1)S(1)}, u32[]{:S(2)}, u32[]{:S(2)}) %collective-permute-start.12) | collective-permute-done | bytes 69664 | tf_op jit(solution)/shard_map/ppermute | solution.py:461
  44.2 2.3 %collective-permute-start.15 = (f32[64,128]{1,0:T(8,128)S(1)}, f32[64,128]{1,0:T(8,128)S(1)}, u32[]{:S(2)}, u32[]{:S(2)}) collective-permute-start(f32[64,128]{1,0:T(8,128)S(1)} %get-tuple-element.40.refs_0_), channel_id=1, source_target_pairs={{0,2},{1,3},{2,0},{3,1},{4,6},{5,7},{6,4},{7,5},{8,10},{9,11},{10,... | collective-permute-start | bytes 98312 | tf_op jit(solution)/shard_map/ppermute | solution.py:461
  46.6 1.6 %collective-permute-start.14 = (f32[64,128]{1,0:T(8,128)S(1)}, f32[64,128]{1,0:T(8,128)S(1)}, u32[]{:S(2)}, u32[]{:S(2)}) collective-permute-start(f32[64,128]{1,0:T(8,128)S(1)} %get-tuple-element.40.refs_0_), channel_id=1, source_target_pairs={{0,3},{1,2},{2,1},{3,0},{4,7},{5,6},{6,5},{7,4},{8,11},{9,10},{10,... | collective-permute-start | bytes 98312 | tf_op jit(solution)/shard_map/ppermute | solution.py:461
  49.5 2.8 %collective-permute-done.14.refs_1_ = f32[64,128]{1,0:T(8,128)S(1)} collective-permute-done((f32[64,128]{1,0:T(8,128)S(1)}, f32[64,128]{1,0:T(8,128)S(1)}, u32[]{:S(2)}, u32[]{:S(2)}) %collective-permute-start.14) | collective-permute-done | bytes 32800 | tf_op jit(solution)/shard_map/ppermute | solution.py:461
  52.3 1.5 %collective-permute-start.19 = (f32[32,128]{1,0:T(8,128)S(1)}, f32[32,128]{1,0:T(8,128)S(1)}, u32[]{:S(2)}, u32[]{:S(2)}) collective-permute-start(f32[32,128]{1,0:T(8,128)S(1)} %get-tuple-element.42.refs_0_), channel_id=1, source_target_pairs={{0,8},{4,12},{8,0},{12,4},{16,24},{20,28},{24,16},{28,20},{1,9},{5... | collective-permute-start | bytes 49160 | tf_op jit(solution)/shard_map/ppermute | solution.py:461
  53.8 1.5 %collective-permute-start.18 = (f32[32,128]{1,0:T(8,128)S(1)}, f32[32,128]{1,0:T(8,128)S(1)}, u32[]{:S(2)}, u32[]{:S(2)}) collective-permute-start(f32[32,128]{1,0:T(8,128)S(1)} %get-tuple-element.42.refs_0_), channel_id=1, source_target_pairs={{0,16},{4,20},{8,24},{12,28},{16,0},{20,4},{24,8},{28,12},{1,17},{... | collective-permute-start | bytes 49160 | tf_op jit(solution)/shard_map/ppermute | solution.py:461
  55.8 1.5 %first_factor.1.refs_4_.inverse_ref = f32[64,64]{1,0:T(8,128)S(1)} custom-call(f32[32,128]{1,0:T(8,128)S(1)} %get-tuple-element.41.gram_ref), custom_call_target="tpu_custom_call" | custom-call | tf_op jit(solution)/shard_map/first_factor/pallas_call | solution.py:41
  57.5 2.4 %collective-permute-done.17.refs_1_ = f32[32,128]{1,0:T(8,128)S(1)} collective-permute-done((f32[32,128]{1,0:T(8,128)S(1)}, f32[32,128]{1,0:T(8,128)S(1)}, u32[]{:S(2)}, u32[]{:S(2)}) %collective-permute-start.17) | collective-permute-done | bytes 16416 | tf_op jit(solution)/shard_map/ppermute | solution.py:461
  61.1 2.8 %finish.1 = f32[1,8,4096]{2,1,0:T(8,128)} custom-call(f32[256,128]{1,0:T(8,128)S(1)} %get-tuple-element.39.rows_ref, f32[64,64]{1,0:T(8,128)S(1)} %first_factor.1.refs_4_.inverse_ref, f32[32,128]{1,0:T(8,128)S(1)} %add_parts.1.refs_0_, f32[32,128]{1,0:T(8,128)S(1)} %collective-permute-done.20.refs_1_), custom_call_target="tpu_custom_call" | custom-call | tf_op jit(solution)/shard_map/finish/pallas_call | solution.py:41
  (40 shorter events, 13.6 us)
Async XLA Ops:
  1.0 9.8 %copy-start = (s32[4,8,1,8]{3,2,1,0:T(1,128)S(1)}, s32[4,8,1,8]{3,2,1,0:T(1,128)}, u32[]{:S(2)}) copy-start(s32[4,8,1,8]{3,2,1,0:T(1,128)} %param.6) | copy-start | bytes 3076
  1.0 9.8 %copy-start.1 = (s32[4,8,1]{1,2,0:T(1,128)S(1)}, s32[4,8,1]{1,2,0:T(1,128)}, u32[]{:S(2)}) copy-start(s32[4,8,1]{1,2,0:T(1,128)} %param.7) | copy-start | bytes 388
  1.0 6.7 %collective-permute-start.2 = (bf16[256,128]{1,0:T(8,128)(2,1)S(1)}, bf16[256,128]{1,0:T(8,128)(2,1)S(1)}, u32[]{:S(2)}, u32[]{:S(2)}) collective-permute-start(bf16[256,128]{1,0:T(8,128)(2,1)S(1)} %get-tuple-element.27.refs_0_), channel_id=1, source_target_pairs={{0,8},{4,12},{8,0},{12,4},{16,24},{20,28},{24,16},{28,20},{1,9},{5... | collective-permute-start | bytes 196616 | tf_op jit(solution)/shard_map/ppermute | solution.py:461
  4.0 4.3 %collective-permute-start.1 = (bf16[256,128]{1,0:T(8,128)(2,1)S(1)}, bf16[256,128]{1,0:T(8,128)(2,1)S(1)}, u32[]{:S(2)}, u32[]{:S(2)}) collective-permute-start(bf16[256,128]{1,0:T(8,128)(2,1)S(1)} %get-tuple-element.27.refs_0_), channel_id=1, source_target_pairs={{0,16},{4,20},{8,24},{12,28},{16,0},{20,4},{24,8},{28,12},{1,17},{... | collective-permute-start | bytes 196616 | tf_op jit(solution)/shard_map/ppermute | solution.py:461
  5.6 5.2 %collective-permute-start = (bf16[256,128]{1,0:T(8,128)(2,1)S(1)}, bf16[256,128]{1,0:T(8,128)(2,1)S(1)}, u32[]{:S(2)}, u32[]{:S(2)}) collective-permute-start(bf16[256,128]{1,0:T(8,128)(2,1)S(1)} %get-tuple-element.27.refs_0_), channel_id=1, source_target_pairs={{0,24},{4,28},{8,16},{12,20},{16,8},{20,12},{24,0},{28,4},{1,25},{... | collective-permute-start | bytes 196616 | tf_op jit(solution)/shard_map/ppermute | solution.py:461
  10.7 1.6 %collective-permute-start.3 = (bf16[4,256,128]{2,1,0:T(8,128)(2,1)S(1)}, bf16[4,256,128]{2,1,0:T(8,128)(2,1)S(1)}, u32[]{:S(2)}, u32[]{:S(2)}) collective-permute-start(bf16[4,256,128]{2,1,0:T(8,128)(2,1)S(1)} %stack.2.near_ref), channel_id=1, source_target_pairs={{0,4},{4,0},{8,12},{12,8},{16,20},{20,16},{24,28},{28,24},{1,5},{5... | collective-permute-start | bytes 786440 | tf_op jit(solution)/shard_map/ppermute | solution.py:461
  13.9 7.2 %collective-permute-start.4 = (bf16[256,128]{1,0:T(8,128)(2,1)S(1)}, bf16[256,128]{1,0:T(8,128)(2,1)S(1)}, u32[]{:S(2)}, u32[]{:S(2)}) collective-permute-start(bf16[256,128]{1,0:T(8,128)(2,1)S(1)} %get-tuple-element.30), channel_id=1, source_target_pairs={{0,3},{1,2},{2,1},{3,0},{4,7},{5,6},{6,5},{7,4},{8,11},{9,10},{10,... | collective-permute-start | bytes 196616 | tf_op jit(solution)/shard_map/ppermute | solution.py:461
  17.6 5.9 %collective-permute-start.5 = (bf16[256,128]{1,0:T(8,128)(2,1)S(1)}, bf16[256,128]{1,0:T(8,128)(2,1)S(1)}, u32[]{:S(2)}, u32[]{:S(2)}) collective-permute-start(bf16[256,128]{1,0:T(8,128)(2,1)S(1)} %get-tuple-element.31), channel_id=1, source_target_pairs={{0,2},{1,3},{2,0},{3,1},{4,6},{5,7},{6,4},{7,5},{8,10},{9,11},{10,... | collective-permute-start | bytes 196616 | tf_op jit(solution)/shard_map/ppermute | solution.py:461
  17.6 5.9 %collective-permute-start.6 = (bf16[256,128]{1,0:T(8,128)(2,1)S(1)}, bf16[256,128]{1,0:T(8,128)(2,1)S(1)}, u32[]{:S(2)}, u32[]{:S(2)}) collective-permute-start(bf16[256,128]{1,0:T(8,128)(2,1)S(1)} %get-tuple-element.32), channel_id=1, source_target_pairs={{0,1},{1,0},{2,3},{3,2},{4,5},{5,4},{6,7},{7,6},{8,9},{9,8},{10,11... | collective-permute-start | bytes 196616 | tf_op jit(solution)/shard_map/ppermute | solution.py:461
  24.0 5.4 %collective-permute-start.9 = (bf16[352,128]{1,0:T(8,128)(2,1)S(1)}, bf16[352,128]{1,0:T(8,128)(2,1)S(1)}, u32[]{:S(2)}, u32[]{:S(2)}) collective-permute-start(bf16[352,128]{1,0:T(8,128)(2,1)S(1)} %middle.1.refs_0_), channel_id=1, source_target_pairs={{0,8},{4,12},{8,0},{12,4},{16,24},{20,28},{24,16},{28,20},{1,9},{5... | collective-permute-start | bytes 270344 | tf_op jit(solution)/shard_map/ppermute | solution.py:461
  24.6 6.2 %collective-permute-start.8 = (bf16[352,128]{1,0:T(8,128)(2,1)S(1)}, bf16[352,128]{1,0:T(8,128)(2,1)S(1)}, u32[]{:S(2)}, u32[]{:S(2)}) collective-permute-start(bf16[352,128]{1,0:T(8,128)(2,1)S(1)} %middle.1.refs_0_), channel_id=1, source_target_pairs={{0,16},{4,20},{8,24},{12,28},{16,0},{20,4},{24,8},{28,12},{1,17},{... | collective-permute-start | bytes 270344 | tf_op jit(solution)/shard_map/ppermute | solution.py:461
  25.1 5.7 %collective-permute-start.7 = (bf16[352,128]{1,0:T(8,128)(2,1)S(1)}, bf16[352,128]{1,0:T(8,128)(2,1)S(1)}, u32[]{:S(2)}, u32[]{:S(2)}) collective-permute-start(bf16[352,128]{1,0:T(8,128)(2,1)S(1)} %middle.1.refs_0_), channel_id=1, source_target_pairs={{0,24},{4,28},{8,16},{12,20},{16,8},{20,12},{24,0},{28,4},{1,25},{... | collective-permute-start | bytes 270344 | tf_op jit(solution)/shard_map/ppermute | solution.py:461
  30.8 1.7 %collective-permute-start.10 = (bf16[4,352,128]{2,1,0:T(8,128)(2,1)S(1)}, bf16[4,352,128]{2,1,0:T(8,128)(2,1)S(1)}, u32[]{:S(2)}, u32[]{:S(2)}) collective-permute-start(bf16[4,352,128]{2,1,0:T(8,128)(2,1)S(1)} %stack.3.near_ref), channel_id=1, source_target_pairs={{0,4},{4,0},{8,12},{12,8},{16,20},{20,16},{24,28},{28,24},{1,5},{5... | collective-permute-start | bytes 1081352 | tf_op jit(solution)/shard_map/ppermute | solution.py:461
  34.2 6.9 %collective-permute-start.11 = (bf16[272,128]{1,0:T(8,128)(2,1)S(1)}, bf16[272,128]{1,0:T(8,128)(2,1)S(1)}, u32[]{:S(2)}, u32[]{:S(2)}) collective-permute-start(bf16[272,128]{1,0:T(8,128)(2,1)S(1)} %get-tuple-element.36), channel_id=1, source_target_pairs={{0,3},{1,2},{2,1},{3,0},{4,7},{5,6},{6,5},{7,4},{8,11},{9,10},{10,... | collective-permute-start | bytes 208904 | tf_op jit(solution)/shard_map/ppermute | solution.py:461
  36.5 6.8 %collective-permute-start.12 = (bf16[272,128]{1,0:T(8,128)(2,1)S(1)}, bf16[272,128]{1,0:T(8,128)(2,1)S(1)}, u32[]{:S(2)}, u32[]{:S(2)}) collective-permute-start(bf16[272,128]{1,0:T(8,128)(2,1)S(1)} %get-tuple-element.37), channel_id=1, source_target_pairs={{0,2},{1,3},{2,0},{3,1},{4,6},{5,7},{6,4},{7,5},{8,10},{9,11},{10,... | collective-permute-start | bytes 208904 | tf_op jit(solution)/shard_map/ppermute | solution.py:461
  36.5 6.8 %collective-permute-start.13 = (bf16[272,128]{1,0:T(8,128)(2,1)S(1)}, bf16[272,128]{1,0:T(8,128)(2,1)S(1)}, u32[]{:S(2)}, u32[]{:S(2)}) collective-permute-start(bf16[272,128]{1,0:T(8,128)(2,1)S(1)} %get-tuple-element.38), channel_id=1, source_target_pairs={{0,1},{1,0},{2,3},{3,2},{4,5},{5,4},{6,7},{7,6},{8,9},{9,8},{10,11... | collective-permute-start | bytes 208904 | tf_op jit(solution)/shard_map/ppermute | solution.py:461
  43.7 4.4 %collective-permute-start.16 = (f32[64,128]{1,0:T(8,128)S(1)}, f32[64,128]{1,0:T(8,128)S(1)}, u32[]{:S(2)}, u32[]{:S(2)}) collective-permute-start(f32[64,128]{1,0:T(8,128)S(1)} %get-tuple-element.40.refs_0_), channel_id=1, source_target_pairs={{0,1},{1,0},{2,3},{3,2},{4,5},{5,4},{6,7},{7,6},{8,9},{9,8},{10,11... | collective-permute-start | bytes 98312 | tf_op jit(solution)/shard_map/ppermute | solution.py:461
  44.2 5.2 %collective-permute-start.15 = (f32[64,128]{1,0:T(8,128)S(1)}, f32[64,128]{1,0:T(8,128)S(1)}, u32[]{:S(2)}, u32[]{:S(2)}) collective-permute-start(f32[64,128]{1,0:T(8,128)S(1)} %get-tuple-element.40.refs_0_), channel_id=1, source_target_pairs={{0,2},{1,3},{2,0},{3,1},{4,6},{5,7},{6,4},{7,5},{8,10},{9,11},{10,... | collective-permute-start | bytes 98312 | tf_op jit(solution)/shard_map/ppermute | solution.py:461
  46.6 5.7 %collective-permute-start.14 = (f32[64,128]{1,0:T(8,128)S(1)}, f32[64,128]{1,0:T(8,128)S(1)}, u32[]{:S(2)}, u32[]{:S(2)}) collective-permute-start(f32[64,128]{1,0:T(8,128)S(1)} %get-tuple-element.40.refs_0_), channel_id=1, source_target_pairs={{0,3},{1,2},{2,1},{3,0},{4,7},{5,6},{6,5},{7,4},{8,11},{9,10},{10,... | collective-permute-start | bytes 98312 | tf_op jit(solution)/shard_map/ppermute | solution.py:461
  52.3 5.0 %collective-permute-start.19 = (f32[32,128]{1,0:T(8,128)S(1)}, f32[32,128]{1,0:T(8,128)S(1)}, u32[]{:S(2)}, u32[]{:S(2)}) collective-permute-start(f32[32,128]{1,0:T(8,128)S(1)} %get-tuple-element.42.refs_0_), channel_id=1, source_target_pairs={{0,8},{4,12},{8,0},{12,4},{16,24},{20,28},{24,16},{28,20},{1,9},{5... | collective-permute-start | bytes 49160 | tf_op jit(solution)/shard_map/ppermute | solution.py:461
  53.8 3.7 %collective-permute-start.18 = (f32[32,128]{1,0:T(8,128)S(1)}, f32[32,128]{1,0:T(8,128)S(1)}, u32[]{:S(2)}, u32[]{:S(2)}) collective-permute-start(f32[32,128]{1,0:T(8,128)S(1)} %get-tuple-element.42.refs_0_), channel_id=1, source_target_pairs={{0,16},{4,20},{8,24},{12,28},{16,0},{20,4},{24,8},{28,12},{1,17},{... | collective-permute-start | bytes 49160 | tf_op jit(solution)/shard_map/ppermute | solution.py:461
  55.3 4.6 %collective-permute-start.17 = (f32[32,128]{1,0:T(8,128)S(1)}, f32[32,128]{1,0:T(8,128)S(1)}, u32[]{:S(2)}, u32[]{:S(2)}) collective-permute-start(f32[32,128]{1,0:T(8,128)S(1)} %get-tuple-element.42.refs_0_), channel_id=1, source_target_pairs={{0,24},{4,28},{8,16},{12,20},{16,8},{20,12},{24,0},{28,4},{1,25},{... | collective-permute-start | bytes 49160 | tf_op jit(solution)/shard_map/ppermute | solution.py:461
  59.9 1.2 %collective-permute-start.20 = (f32[32,128]{1,0:T(8,128)S(1)}, f32[32,128]{1,0:T(8,128)S(1)}, u32[]{:S(2)}, u32[]{:S(2)}) collective-permute-start(f32[32,128]{1,0:T(8,128)S(1)} %add_parts.1.refs_0_), channel_id=1, source_target_pairs={{0,4},{4,0},{8,12},{12,8},{16,20},{20,16},{24,28},{28,24},{1,5},{5... | collective-permute-start | bytes 49160 | tf_op jit(solution)/shard_map/ppermute | solution.py:461

commit v5 on v4

--- a/solution.py
+++ b/solution.py
@@ -463,7 +463,7 @@
 
 def stages(size):
     if size == 8:
-        return [[6, 4, 2], [1]]
+        return [[2, 4, 6], [1]]
     bits, bit = [], 1
     while bit < size:
         bits.append([bit])
@@ -513,7 +513,7 @@
     table = near_table(offsets, near, block_rows)
     terms, (first, trace) = products(offsets, ranges, columns, matrix, own_matrix, near, far, table)
     rows, grams = collect(total, degree, first, trace, terms)
-    gram, first = add_columns(total, [grams] + [swap(grams, "cols", m) for m in ranges])
+    gram, first = add_columns(total, [grams] + [swap(grams, "cols", m) for m in reversed(ranges)])
     inverse = first_factor(first)
     return finish(total, block_rows, rows, inverse, add_rows(gram, [inverse]))
 

time: 64.1 us -> 60.8 us (0.949)
  waiting for transfers between devices: 22.7 us -> 19.3 us
    ppermute x21, waiting for transfers between devices: 22.7 us -> 19.3 us  [swap(): lax.ppermute(value, axis, [(index, index ^ mask) for index in range(size)])]
  transfers between devices with their start and end apart: 21 -> 21, of which waited for: 14 -> 15; matrix products, arithmetic and copies ran while one was open for 0% -> 0% of each run, Pallas kernels for 12% -> 13%
where the time goes in v5:
time: 60.8 us; the launch traced here: 60.6 us
  starting transfers between devices  25.2 us (41%)
  waiting for transfers between devices  19.3 us (32%)
  Pallas kernels  15.9 us (26%)
    ppermute x21, starting transfers between devices, swap(): lax.ppermute(value, axis, [(index, index ^ mask) for index in range(size)])  25.2 us
    ppermute x21, waiting for transfers between devices, swap(): lax.ppermute(value, axis, [(index, index ^ mask) for index in range(size)])  19.3 us
    pallas_call x17, Pallas kernels, call(): pl.pallas_call(kernel, out_shape=outs, in_specs=ins, out_specs=jax.tree.m...  15.9 us
  transfers between devices with their start and end apart: 21, of which 15 were waited for; matrix products, arithmetic and copies ran while one was open for 0% of the time, Pallas kernels for 13%

profile of v5, /device:TPU:0, one launch (start us, length us, event | category | flops | bytes accessed | tf_op | source)
XLA Modules:
  0.0 60.6 jit_solution(9182647735681294923)
XLA Ops:
  1.0 4.0 %collective-permute-start.2 = (bf16[256,128]{1,0:T(8,128)(2,1)S(1)}, bf16[256,128]{1,0:T(8,128)(2,1)S(1)}, u32[]{:S(2)}, u32[]{:S(2)}) collective-permute-start(bf16[256,128]{1,0:T(8,128)(2,1)S(1)} %get-tuple-element.27.refs_0_), channel_id=1, source_target_pairs={{0,24},{4,28},{8,16},{12,20},{16,8},{20,12},{24,0},{28,4},{1,25},{... | collective-permute-start | bytes 196616 | tf_op jit(solution)/shard_map/ppermute | solution.py:461
  5.6 2.2 %prep.2 = (bf16[3,8,64,512]{3,2,1,0:T(8,128)(2,1)S(1)}, f32[8,128]{1,0:T(8,128)S(1)}) custom-call(bf16[4,8,1,8,4096]{4,3,2,1,0:T(8,128)(2,1)} %affinity_hbm.3), custom_call_target="tpu_custom_call" | custom-call | tf_op jit(solution)/shard_map/prep/pallas_call | solution.py:41
  7.8 1.4 %collective-permute-done.1.refs_2_ = bf16[256,128]{1,0:T(8,128)(2,1)S(1)} collective-permute-done((bf16[256,128]{1,0:T(8,128)(2,1)S(1)}, bf16[256,128]{1,0:T(8,128)(2,1)S(1)}, u32[]{:S(2)}, u32[]{:S(2)}) %collective-permute-start.1) | collective-permute-done | bytes 65568 | tf_op jit(solution)/shard_map/ppermute | solution.py:461
  10.1 1.2 %collective-permute-done.3.far_ref = bf16[4,256,128]{2,1,0:T(8,128)(2,1)S(1)} collective-permute-done((bf16[4,256,128]{2,1,0:T(8,128)(2,1)S(1)}, bf16[4,256,128]{2,1,0:T(8,128)(2,1)S(1)}, u32[]{:S(2)}, u32[]{:S(2)}) %collective-permute-start.3) | collective-permute-done | bytes 262176 | tf_op jit(solution)/shard_map/ppermute | solution.py:461
  11.4 1.6 %others.2 = (bf16[65,64,128]{2,1,0:T(8,128)(2,1)S(1)}, bf16[256,128]{1,0:T(8,128)(2,1)S(1)}, bf16[256,128]{1,0:T(8,128)(2,1)S(1)}, bf16[256,128]{1,0:T(8,128)(2,1)S(1)}) custom-call(s32[4,8,1,8]{3,2,1,0:T(1,128)S(1)} %compare_select_fusion.columns_any.columns, ...), custom_call_target="tpu_custom_call", output_to_operand_aliasing={{0}: (4, {})} | custom-call | tf_op jit(solution)/shard_map/others/pallas_call | solution.py:41
  13.0 3.7 %collective-permute-start.4 = (bf16[256,128]{1,0:T(8,128)(2,1)S(1)}, bf16[256,128]{1,0:T(8,128)(2,1)S(1)}, u32[]{:S(2)}, u32[]{:S(2)}) collective-permute-start(bf16[256,128]{1,0:T(8,128)(2,1)S(1)} %get-tuple-element.30), channel_id=1, source_target_pairs={{0,3},{1,2},{2,1},{3,0},{4,7},{5,6},{6,5},{7,4},{8,11},{9,10},{10,... | collective-permute-start | bytes 196616 | tf_op jit(solution)/shard_map/ppermute | solution.py:461
  17.4 1.6 %prep.3 = (bf16[1,8,64,512]{3,2,1,0:T(8,128)(2,1)S(1)}, f32[8,128]{1,0:T(8,128)}) custom-call(bf16[4,8,1,8,4096]{4,3,2,1,0:T(8,128)(2,1)} %affinity_hbm.3), custom_call_target="tpu_custom_call" | custom-call | tf_op jit(solution)/shard_map/prep/pallas_call | solution.py:41
  20.2 2.3 %collective-permute-done.5.refs_2_ = bf16[256,128]{1,0:T(8,128)(2,1)S(1)} collective-permute-done((bf16[256,128]{1,0:T(8,128)(2,1)S(1)}, bf16[256,128]{1,0:T(8,128)(2,1)S(1)}, u32[]{:S(2)}, u32[]{:S(2)}) %collective-permute-start.5) | collective-permute-done | bytes 65568 | tf_op jit(solution)/shard_map/ppermute | solution.py:461
  23.0 1.6 %collective-permute-start.9 = (bf16[352,128]{1,0:T(8,128)(2,1)S(1)}, bf16[352,128]{1,0:T(8,128)(2,1)S(1)}, u32[]{:S(2)}, u32[]{:S(2)}) collective-permute-start(bf16[352,128]{1,0:T(8,128)(2,1)S(1)} %middle.1.refs_0_), channel_id=1, source_target_pairs={{0,24},{4,28},{8,16},{12,20},{16,8},{20,12},{24,0},{28,4},{1,25},{... | collective-permute-start | bytes 270344 | tf_op jit(solution)/shard_map/ppermute | solution.py:461
  25.1 1.5 %collective-permute-start.7 = (bf16[352,128]{1,0:T(8,128)(2,1)S(1)}, bf16[352,128]{1,0:T(8,128)(2,1)S(1)}, u32[]{:S(2)}, u32[]{:S(2)}) collective-permute-start(bf16[352,128]{1,0:T(8,128)(2,1)S(1)} %middle.1.refs_0_), channel_id=1, source_target_pairs={{0,8},{4,12},{8,0},{12,4},{16,24},{20,28},{24,16},{28,20},{1,9},{5... | collective-permute-start | bytes 270344 | tf_op jit(solution)/shard_map/ppermute | solution.py:461
  26.5 2.7 %collective-permute-done.9.refs_3_ = bf16[352,128]{1,0:T(8,128)(2,1)S(1)} collective-permute-done((bf16[352,128]{1,0:T(8,128)(2,1)S(1)}, bf16[352,128]{1,0:T(8,128)(2,1)S(1)}, u32[]{:S(2)}, u32[]{:S(2)}) %collective-permute-start.9) | collective-permute-done | bytes 90144 | tf_op jit(solution)/shard_map/ppermute | solution.py:461
  30.4 1.5 %collective-permute-done.10.far_ref = bf16[4,352,128]{2,1,0:T(8,128)(2,1)S(1)} collective-permute-done((bf16[4,352,128]{2,1,0:T(8,128)(2,1)S(1)}, bf16[4,352,128]{2,1,0:T(8,128)(2,1)S(1)}, u32[]{:S(2)}, u32[]{:S(2)}) %collective-permute-start.10) | collective-permute-done | bytes 360480 | tf_op jit(solution)/shard_map/ppermute | solution.py:461
  31.9 1.6 %others.3 = (bf16[65,64,128]{2,1,0:T(8,128)(2,1)S(1)}, bf16[272,128]{1,0:T(8,128)(2,1)S(1)}, bf16[272,128]{1,0:T(8,128)(2,1)S(1)}, bf16[272,128]{1,0:T(8,128)(2,...) custom-call(s32[4,8,1,8]{3,2,1,0:T(1,128)S(1)} %compare_select_fusion.columns_any.colu, ...), custom_call_target="tpu_custom_call", output_to_operand_aliasing={{0}: (4, {})} | custom-call | tf_op jit(solution)/shard_map/others/pallas_call | solution.py:41
  33.5 2.2 %collective-permute-start.11 = (bf16[272,128]{1,0:T(8,128)(2,1)S(1)}, bf16[272,128]{1,0:T(8,128)(2,1)S(1)}, u32[]{:S(2)}, u32[]{:S(2)}) collective-permute-start(bf16[272,128]{1,0:T(8,128)(2,1)S(1)} %get-tuple-element.36), channel_id=1, source_target_pairs={{0,3},{1,2},{2,1},{3,0},{4,7},{5,6},{6,5},{7,4},{8,11},{9,10},{10,... | collective-permute-start | bytes 208904 | tf_op jit(solution)/shard_map/ppermute | solution.py:461
  35.7 2.3 %collective-permute-start.13 = (bf16[272,128]{1,0:T(8,128)(2,1)S(1)}, bf16[272,128]{1,0:T(8,128)(2,1)S(1)}, u32[]{:S(2)}, u32[]{:S(2)}) collective-permute-start(bf16[272,128]{1,0:T(8,128)(2,1)S(1)} %get-tuple-element.38), channel_id=1, source_target_pairs={{0,1},{1,0},{2,3},{3,2},{4,5},{5,4},{6,7},{7,6},{8,9},{9,8},{10,11... | collective-permute-start | bytes 208904 | tf_op jit(solution)/shard_map/ppermute | solution.py:461
  39.1 1.4 %collective-permute-done.11.refs_1_ = bf16[272,128]{1,0:T(8,128)(2,1)S(1)} collective-permute-done((bf16[272,128]{1,0:T(8,128)(2,1)S(1)}, bf16[272,128]{1,0:T(8,128)(2,1)S(1)}, u32[]{:S(2)}, u32[]{:S(2)}) %collective-permute-start.11) | collective-permute-done | bytes 69664 | tf_op jit(solution)/shard_map/ppermute | solution.py:461
  40.5 2.1 %collective-permute-done.12.refs_2_ = bf16[272,128]{1,0:T(8,128)(2,1)S(1)} collective-permute-done((bf16[272,128]{1,0:T(8,128)(2,1)S(1)}, bf16[272,128]{1,0:T(8,128)(2,1)S(1)}, u32[]{:S(2)}, u32[]{:S(2)}) %collective-permute-start.12) | collective-permute-done | bytes 69664 | tf_op jit(solution)/shard_map/ppermute | solution.py:461
  43.1 2.1 %collective-permute-start.16 = (f32[64,128]{1,0:T(8,128)S(1)}, f32[64,128]{1,0:T(8,128)S(1)}, u32[]{:S(2)}, u32[]{:S(2)}) collective-permute-start(f32[64,128]{1,0:T(8,128)S(1)} %get-tuple-element.40.refs_0_), channel_id=1, source_target_pairs={{0,3},{1,2},{2,1},{3,0},{4,7},{5,6},{6,5},{7,4},{8,11},{9,10},{10,... | collective-permute-start | bytes 98312 | tf_op jit(solution)/shard_map/ppermute | solution.py:461
  45.2 2.3 %collective-permute-start.14 = (f32[64,128]{1,0:T(8,128)S(1)}, f32[64,128]{1,0:T(8,128)S(1)}, u32[]{:S(2)}, u32[]{:S(2)}) collective-permute-start(f32[64,128]{1,0:T(8,128)S(1)} %get-tuple-element.40.refs_0_), channel_id=1, source_target_pairs={{0,1},{1,0},{2,3},{3,2},{4,5},{5,4},{6,7},{7,6},{8,9},{9,8},{10,11... | collective-permute-start | bytes 98312 | tf_op jit(solution)/shard_map/ppermute | solution.py:461
  47.5 1.4 %collective-permute-done.16.refs_3_ = f32[64,128]{1,0:T(8,128)S(1)} collective-permute-done((f32[64,128]{1,0:T(8,128)S(1)}, f32[64,128]{1,0:T(8,128)S(1)}, u32[]{:S(2)}, u32[]{:S(2)}) %collective-permute-start.16) | collective-permute-done | bytes 32800 | tf_op jit(solution)/shard_map/ppermute | solution.py:461
  50.0 2.3 %collective-permute-start.19 = (f32[32,128]{1,0:T(8,128)S(1)}, f32[32,128]{1,0:T(8,128)S(1)}, u32[]{:S(2)}, u32[]{:S(2)}) collective-permute-start(f32[32,128]{1,0:T(8,128)S(1)} %get-tuple-element.42.refs_0_), channel_id=1, source_target_pairs={{0,24},{4,28},{8,16},{12,20},{16,8},{20,12},{24,0},{28,4},{1,25},{... | collective-permute-start | bytes 49160 | tf_op jit(solution)/shard_map/ppermute | solution.py:461
  53.6 1.5 %first_factor.1.refs_4_.inverse_ref = f32[64,64]{1,0:T(8,128)S(1)} custom-call(f32[32,128]{1,0:T(8,128)S(1)} %get-tuple-element.41.gram_ref), custom_call_target="tpu_custom_call" | custom-call | tf_op jit(solution)/shard_map/first_factor/pallas_call | solution.py:41
  56.6 1.2 %collective-permute-done.20.refs_1_ = f32[32,128]{1,0:T(8,128)S(1)} collective-permute-done((f32[32,128]{1,0:T(8,128)S(1)}, f32[32,128]{1,0:T(8,128)S(1)}, u32[]{:S(2)}, u32[]{:S(2)}) %collective-permute-start.20) | collective-permute-done | bytes 16416 | tf_op jit(solution)/shard_map/ppermute | solution.py:461
  57.8 2.9 %finish.1 = f32[1,8,4096]{2,1,0:T(8,128)} custom-call(f32[256,128]{1,0:T(8,128)S(1)} %get-tuple-element.39.rows_ref, f32[64,64]{1,0:T(8,128)S(1)} %first_factor.1.refs_4_.inverse_ref, f32[32,128]{1,0:T(8,128)S(1)} %add_parts.1.refs_0_, f32[32,128]{1,0:T(8,128)S(1)} %collective-permute-done.20.refs_1_), custom_call_target="tpu_custom_call" | custom-call | tf_op jit(solution)/shard_map/finish/pallas_call | solution.py:41
  (40 shorter events, 12.0 us)
Async XLA Ops:
  1.0 8.9 %copy-start = (s32[4,8,1,8]{3,2,1,0:T(1,128)S(1)}, s32[4,8,1,8]{3,2,1,0:T(1,128)}, u32[]{:S(2)}) copy-start(s32[4,8,1,8]{3,2,1,0:T(1,128)} %param.6) | copy-start | bytes 3076
  1.0 8.9 %copy-start.1 = (s32[4,8,1]{1,2,0:T(1,128)S(1)}, s32[4,8,1]{1,2,0:T(1,128)}, u32[]{:S(2)}) copy-start(s32[4,8,1]{1,2,0:T(1,128)} %param.7) | copy-start | bytes 388
  1.0 6.8 %collective-permute-start.2 = (bf16[256,128]{1,0:T(8,128)(2,1)S(1)}, bf16[256,128]{1,0:T(8,128)(2,1)S(1)}, u32[]{:S(2)}, u32[]{:S(2)}) collective-permute-start(bf16[256,128]{1,0:T(8,128)(2,1)S(1)} %get-tuple-element.27.refs_0_), channel_id=1, source_target_pairs={{0,24},{4,28},{8,16},{12,20},{16,8},{20,12},{24,0},{28,4},{1,25},{... | collective-permute-start | bytes 196616 | tf_op jit(solution)/shard_map/ppermute | solution.py:461
  5.0 4.3 %collective-permute-start.1 = (bf16[256,128]{1,0:T(8,128)(2,1)S(1)}, bf16[256,128]{1,0:T(8,128)(2,1)S(1)}, u32[]{:S(2)}, u32[]{:S(2)}) collective-permute-start(bf16[256,128]{1,0:T(8,128)(2,1)S(1)} %get-tuple-element.27.refs_0_), channel_id=1, source_target_pairs={{0,16},{4,20},{8,24},{12,28},{16,0},{20,4},{24,8},{28,12},{1,17},{... | collective-permute-start | bytes 196616 | tf_op jit(solution)/shard_map/ppermute | solution.py:461
  5.5 4.3 %collective-permute-start = (bf16[256,128]{1,0:T(8,128)(2,1)S(1)}, bf16[256,128]{1,0:T(8,128)(2,1)S(1)}, u32[]{:S(2)}, u32[]{:S(2)}) collective-permute-start(bf16[256,128]{1,0:T(8,128)(2,1)S(1)} %get-tuple-element.27.refs_0_), channel_id=1, source_target_pairs={{0,8},{4,12},{8,0},{12,4},{16,24},{20,28},{24,16},{28,20},{1,9},{5... | collective-permute-start | bytes 196616 | tf_op jit(solution)/shard_map/ppermute | solution.py:461
  9.8 1.6 %collective-permute-start.3 = (bf16[4,256,128]{2,1,0:T(8,128)(2,1)S(1)}, bf16[4,256,128]{2,1,0:T(8,128)(2,1)S(1)}, u32[]{:S(2)}, u32[]{:S(2)}) collective-permute-start(bf16[4,256,128]{2,1,0:T(8,128)(2,1)S(1)} %stack.2.near_ref), channel_id=1, source_target_pairs={{0,4},{4,0},{8,12},{12,8},{16,20},{20,16},{24,28},{28,24},{1,5},{5... | collective-permute-start | bytes 786440 | tf_op jit(solution)/shard_map/ppermute | solution.py:461
  13.0 7.2 %collective-permute-start.4 = (bf16[256,128]{1,0:T(8,128)(2,1)S(1)}, bf16[256,128]{1,0:T(8,128)(2,1)S(1)}, u32[]{:S(2)}, u32[]{:S(2)}) collective-permute-start(bf16[256,128]{1,0:T(8,128)(2,1)S(1)} %get-tuple-element.30), channel_id=1, source_target_pairs={{0,3},{1,2},{2,1},{3,0},{4,7},{5,6},{6,5},{7,4},{8,11},{9,10},{10,... | collective-permute-start | bytes 196616 | tf_op jit(solution)/shard_map/ppermute | solution.py:461
  16.6 5.9 %collective-permute-start.5 = (bf16[256,128]{1,0:T(8,128)(2,1)S(1)}, bf16[256,128]{1,0:T(8,128)(2,1)S(1)}, u32[]{:S(2)}, u32[]{:S(2)}) collective-permute-start(bf16[256,128]{1,0:T(8,128)(2,1)S(1)} %get-tuple-element.31), channel_id=1, source_target_pairs={{0,2},{1,3},{2,0},{3,1},{4,6},{5,7},{6,4},{7,5},{8,10},{9,11},{10,... | collective-permute-start | bytes 196616 | tf_op jit(solution)/shard_map/ppermute | solution.py:461
  16.6 5.9 %collective-permute-start.6 = (bf16[256,128]{1,0:T(8,128)(2,1)S(1)}, bf16[256,128]{1,0:T(8,128)(2,1)S(1)}, u32[]{:S(2)}, u32[]{:S(2)}) collective-permute-start(bf16[256,128]{1,0:T(8,128)(2,1)S(1)} %get-tuple-element.32), channel_id=1, source_target_pairs={{0,1},{1,0},{2,3},{3,2},{4,5},{5,4},{6,7},{7,6},{8,9},{9,8},{10,11... | collective-permute-start | bytes 196616 | tf_op jit(solution)/shard_map/ppermute | solution.py:461
  23.0 6.2 %collective-permute-start.9 = (bf16[352,128]{1,0:T(8,128)(2,1)S(1)}, bf16[352,128]{1,0:T(8,128)(2,1)S(1)}, u32[]{:S(2)}, u32[]{:S(2)}) collective-permute-start(bf16[352,128]{1,0:T(8,128)(2,1)S(1)} %middle.1.refs_0_), channel_id=1, source_target_pairs={{0,24},{4,28},{8,16},{12,20},{16,8},{20,12},{24,0},{28,4},{1,25},{... | collective-permute-start | bytes 270344 | tf_op jit(solution)/shard_map/ppermute | solution.py:461
  24.6 5.5 %collective-permute-start.8 = (bf16[352,128]{1,0:T(8,128)(2,1)S(1)}, bf16[352,128]{1,0:T(8,128)(2,1)S(1)}, u32[]{:S(2)}, u32[]{:S(2)}) collective-permute-start(bf16[352,128]{1,0:T(8,128)(2,1)S(1)} %middle.1.refs_0_), channel_id=1, source_target_pairs={{0,16},{4,20},{8,24},{12,28},{16,0},{20,4},{24,8},{28,12},{1,17},{... | collective-permute-start | bytes 270344 | tf_op jit(solution)/shard_map/ppermute | solution.py:461
  25.1 5.1 %collective-permute-start.7 = (bf16[352,128]{1,0:T(8,128)(2,1)S(1)}, bf16[352,128]{1,0:T(8,128)(2,1)S(1)}, u32[]{:S(2)}, u32[]{:S(2)}) collective-permute-start(bf16[352,128]{1,0:T(8,128)(2,1)S(1)} %middle.1.refs_0_), channel_id=1, source_target_pairs={{0,8},{4,12},{8,0},{12,4},{16,24},{20,28},{24,16},{28,20},{1,9},{5... | collective-permute-start | bytes 270344 | tf_op jit(solution)/shard_map/ppermute | solution.py:461
  30.2 1.7 %collective-permute-start.10 = (bf16[4,352,128]{2,1,0:T(8,128)(2,1)S(1)}, bf16[4,352,128]{2,1,0:T(8,128)(2,1)S(1)}, u32[]{:S(2)}, u32[]{:S(2)}) collective-permute-start(bf16[4,352,128]{2,1,0:T(8,128)(2,1)S(1)} %stack.3.near_ref), channel_id=1, source_target_pairs={{0,4},{4,0},{8,12},{12,8},{16,20},{20,16},{24,28},{28,24},{1,5},{5... | collective-permute-start | bytes 1081352 | tf_op jit(solution)/shard_map/ppermute | solution.py:461
  33.5 6.9 %collective-permute-start.11 = (bf16[272,128]{1,0:T(8,128)(2,1)S(1)}, bf16[272,128]{1,0:T(8,128)(2,1)S(1)}, u32[]{:S(2)}, u32[]{:S(2)}) collective-permute-start(bf16[272,128]{1,0:T(8,128)(2,1)S(1)} %get-tuple-element.36), channel_id=1, source_target_pairs={{0,3},{1,2},{2,1},{3,0},{4,7},{5,6},{6,5},{7,4},{8,11},{9,10},{10,... | collective-permute-start | bytes 208904 | tf_op jit(solution)/shard_map/ppermute | solution.py:461
  35.7 6.9 %collective-permute-start.12 = (bf16[272,128]{1,0:T(8,128)(2,1)S(1)}, bf16[272,128]{1,0:T(8,128)(2,1)S(1)}, u32[]{:S(2)}, u32[]{:S(2)}) collective-permute-start(bf16[272,128]{1,0:T(8,128)(2,1)S(1)} %get-tuple-element.37), channel_id=1, source_target_pairs={{0,2},{1,3},{2,0},{3,1},{4,6},{5,7},{6,4},{7,5},{8,10},{9,11},{10,... | collective-permute-start | bytes 208904 | tf_op jit(solution)/shard_map/ppermute | solution.py:461
  35.7 6.9 %collective-permute-start.13 = (bf16[272,128]{1,0:T(8,128)(2,1)S(1)}, bf16[272,128]{1,0:T(8,128)(2,1)S(1)}, u32[]{:S(2)}, u32[]{:S(2)}) collective-permute-start(bf16[272,128]{1,0:T(8,128)(2,1)S(1)} %get-tuple-element.38), channel_id=1, source_target_pairs={{0,1},{1,0},{2,3},{3,2},{4,5},{5,4},{6,7},{7,6},{8,9},{9,8},{10,11... | collective-permute-start | bytes 208904 | tf_op jit(solution)/shard_map/ppermute | solution.py:461
  43.1 5.8 %collective-permute-start.16 = (f32[64,128]{1,0:T(8,128)S(1)}, f32[64,128]{1,0:T(8,128)S(1)}, u32[]{:S(2)}, u32[]{:S(2)}) collective-permute-start(f32[64,128]{1,0:T(8,128)S(1)} %get-tuple-element.40.refs_0_), channel_id=1, source_target_pairs={{0,3},{1,2},{2,1},{3,0},{4,7},{5,6},{6,5},{7,4},{8,11},{9,10},{10,... | collective-permute-start | bytes 98312 | tf_op jit(solution)/shard_map/ppermute | solution.py:461
  45.2 4.8 %collective-permute-start.15 = (f32[64,128]{1,0:T(8,128)S(1)}, f32[64,128]{1,0:T(8,128)S(1)}, u32[]{:S(2)}, u32[]{:S(2)}) collective-permute-start(f32[64,128]{1,0:T(8,128)S(1)} %get-tuple-element.40.refs_0_), channel_id=1, source_target_pairs={{0,2},{1,3},{2,0},{3,1},{4,6},{5,7},{6,4},{7,5},{8,10},{9,11},{10,... | collective-permute-start | bytes 98312 | tf_op jit(solution)/shard_map/ppermute | solution.py:461
  45.2 4.8 %collective-permute-start.14 = (f32[64,128]{1,0:T(8,128)S(1)}, f32[64,128]{1,0:T(8,128)S(1)}, u32[]{:S(2)}, u32[]{:S(2)}) collective-permute-start(f32[64,128]{1,0:T(8,128)S(1)} %get-tuple-element.40.refs_0_), channel_id=1, source_target_pairs={{0,1},{1,0},{2,3},{3,2},{4,5},{5,4},{6,7},{7,6},{8,9},{9,8},{10,11... | collective-permute-start | bytes 98312 | tf_op jit(solution)/shard_map/ppermute | solution.py:461
  50.0 5.0 %collective-permute-start.19 = (f32[32,128]{1,0:T(8,128)S(1)}, f32[32,128]{1,0:T(8,128)S(1)}, u32[]{:S(2)}, u32[]{:S(2)}) collective-permute-start(f32[32,128]{1,0:T(8,128)S(1)} %get-tuple-element.42.refs_0_), channel_id=1, source_target_pairs={{0,24},{4,28},{8,16},{12,20},{16,8},{20,12},{24,0},{28,4},{1,25},{... | collective-permute-start | bytes 49160 | tf_op jit(solution)/shard_map/ppermute | solution.py:461
  52.3 3.7 %collective-permute-start.18 = (f32[32,128]{1,0:T(8,128)S(1)}, f32[32,128]{1,0:T(8,128)S(1)}, u32[]{:S(2)}, u32[]{:S(2)}) collective-permute-start(f32[32,128]{1,0:T(8,128)S(1)} %get-tuple-element.42.refs_0_), channel_id=1, source_target_pairs={{0,16},{4,20},{8,24},{12,28},{16,0},{20,4},{24,8},{28,12},{1,17},{... | collective-permute-start | bytes 49160 | tf_op jit(solution)/shard_map/ppermute | solution.py:461
  52.8 3.7 %collective-permute-start.17 = (f32[32,128]{1,0:T(8,128)S(1)}, f32[32,128]{1,0:T(8,128)S(1)}, u32[]{:S(2)}, u32[]{:S(2)}) collective-permute-start(f32[32,128]{1,0:T(8,128)S(1)} %get-tuple-element.42.refs_0_), channel_id=1, source_target_pairs={{0,8},{4,12},{8,0},{12,4},{16,24},{20,28},{24,16},{28,20},{1,9},{5... | collective-permute-start | bytes 49160 | tf_op jit(solution)/shard_map/ppermute | solution.py:461
  56.6 1.2 %collective-permute-start.20 = (f32[32,128]{1,0:T(8,128)S(1)}, f32[32,128]{1,0:T(8,128)S(1)}, u32[]{:S(2)}, u32[]{:S(2)}) collective-permute-start(f32[32,128]{1,0:T(8,128)S(1)} %add_parts.1.refs_0_), channel_id=1, source_target_pairs={{0,4},{4,0},{8,12},{12,8},{16,20},{20,16},{24,28},{28,24},{1,5},{5... | collective-permute-start | bytes 49160 | tf_op jit(solution)/shard_map/ppermute | solution.py:461

commit v6 on v5

--- a/solution.py
+++ b/solution.py
@@ -461,9 +461,19 @@
     return lax.ppermute(value, axis, [(index, index ^ mask) for index in range(size)])
 
 
+def swap_both(value, row_mask, column_mask):
+    rows, columns = lax.axis_size("rows"), lax.axis_size("cols")
+    pairs = [
+        (row * columns + column, (row ^ row_mask) * columns + (column ^ column_mask))
+        for row in range(rows)
+        for column in range(columns)
+    ]
+    return lax.ppermute(value, ("rows", "cols"), pairs)
+
+
 def stages(size):
     if size == 8:
-        return [[2, 4, 6], [1]]
+        return [[3, 5, 7], [1]]
     bits, bit = [], 1
     while bit < size:
         bits.append([bit])
@@ -513,7 +523,8 @@
     table = near_table(offsets, near, block_rows)
     terms, (first, trace) = products(offsets, ranges, columns, matrix, own_matrix, near, far, table)
     rows, grams = collect(total, degree, first, trace, terms)
-    gram, first = add_columns(total, [grams] + [swap(grams, "cols", m) for m in reversed(ranges)])
+    flip = 1 if ranks == 8 else 0
+    gram, first = add_columns(total, [grams] + [swap_both(grams, flip, m) for m in reversed(ranges)])
     inverse = first_factor(first)
     return finish(total, block_rows, rows, inverse, add_rows(gram, [inverse]))
 

time: 60.8 us -> 60 us (0.987)
  starting transfers between devices: 25.2 us -> 23.2 us
  waiting for transfers between devices: 19.3 us -> 20.6 us
    ppermute x21 -> x18, starting transfers between devices: 25.2 us -> 19.4 us  [swap(): lax.ppermute(value, axis, [(index, index ^ mask) for index in range(size)])]
    ppermute x0 -> x3, starting transfers between devices: none -> 3.74 us  [swap_both(): return lax.ppermute(value, ('rows', 'cols'), pairs)]
    ppermute x0 -> x3, waiting for transfers between devices: none -> 3.08 us  [swap_both(): return lax.ppermute(value, ('rows', 'cols'), pairs)]
    ppermute x21 -> x18, waiting for transfers between devices: 19.3 us -> 17.5 us  [swap(): lax.ppermute(value, axis, [(index, index ^ mask) for index in range(size)])]
  transfers between devices with their start and end apart: 21 -> 21, of which waited for: 15 -> 14; matrix products, arithmetic and copies ran while one was open for 0% -> 0% of each run, Pallas kernels for 13% -> 13%
where the time goes in v6:
time: 60 us; the launch traced here: 59.8 us
  starting transfers between devices  23.2 us (39%)
  waiting for transfers between devices  20.6 us (34%)
  Pallas kernels  15.8 us (26%)
    ppermute x18, starting transfers between devices, swap(): lax.ppermute(value, axis, [(index, index ^ mask) for index in range(size)])  19.4 us
    ppermute x18, waiting for transfers between devices, swap(): lax.ppermute(value, axis, [(index, index ^ mask) for index in range(size)])  17.5 us
    pallas_call x17, Pallas kernels, call(): pl.pallas_call(kernel, out_shape=outs, in_specs=ins, out_specs=jax.tree.m...  15.8 us
    ppermute x3, starting transfers between devices, swap_both(): return lax.ppermute(value, ('rows', 'cols'), pairs)  3.74 us
    ppermute x3, waiting for transfers between devices, swap_both(): return lax.ppermute(value, ('rows', 'cols'), pairs)  3.08 us
  transfers between devices with their start and end apart: 21, of which 14 were waited for; matrix products, arithmetic and copies ran while one was open for 0% of the time, Pallas kernels for 13%

profile of v6, /device:TPU:0, one launch (start us, length us, event | category | flops | bytes accessed | tf_op | source)
XLA Modules:
  0.0 59.8 jit_solution(10452753031934548721)
XLA Ops:
  1.0 3.4 %collective-permute-start.2 = (bf16[256,128]{1,0:T(8,128)(2,1)S(1)}, bf16[256,128]{1,0:T(8,128)(2,1)S(1)}, u32[]{:S(2)}, u32[]{:S(2)}) collective-permute-start(bf16[256,128]{1,0:T(8,128)(2,1)S(1)} %get-tuple-element.27.refs_0_), channel_id=1, source_target_pairs={{0,28},{4,24},{8,20},{12,16},{16,12},{20,8},{24,4},{28,0},{1,29},{... | collective-permute-start | bytes 196616 | tf_op jit(solution)/shard_map/ppermute | solution.py:461
  5.4 2.2 %prep.2 = (bf16[3,8,64,512]{3,2,1,0:T(8,128)(2,1)S(1)}, f32[8,128]{1,0:T(8,128)S(1)}) custom-call(bf16[4,8,1,8,4096]{4,3,2,1,0:T(8,128)(2,1)} %affinity_hbm.3), custom_call_target="tpu_custom_call" | custom-call | tf_op jit(solution)/shard_map/prep/pallas_call | solution.py:41
  8.3 1.2 %collective-permute-done.refs_1_ = bf16[256,128]{1,0:T(8,128)(2,1)S(1)} collective-permute-done((bf16[256,128]{1,0:T(8,128)(2,1)S(1)}, bf16[256,128]{1,0:T(8,128)(2,1)S(1)}, u32[]{:S(2)}, u32[]{:S(2)}) %collective-permute-start) | collective-permute-done | bytes 65568 | tf_op jit(solution)/shard_map/ppermute | solution.py:461
  10.0 1.2 %collective-permute-done.3.far_ref = bf16[4,256,128]{2,1,0:T(8,128)(2,1)S(1)} collective-permute-done((bf16[4,256,128]{2,1,0:T(8,128)(2,1)S(1)}, bf16[4,256,128]{2,1,0:T(8,128)(2,1)S(1)}, u32[]{:S(2)}, u32[]{:S(2)}) %collective-permute-start.3) | collective-permute-done | bytes 262176 | tf_op jit(solution)/shard_map/ppermute | solution.py:461
  11.2 1.6 %others.2 = (bf16[65,64,128]{2,1,0:T(8,128)(2,1)S(1)}, bf16[256,128]{1,0:T(8,128)(2,1)S(1)}, bf16[256,128]{1,0:T(8,128)(2,1)S(1)}, bf16[256,128]{1,0:T(8,128)(2,1)S(1)}) custom-call(s32[4,8,1,8]{3,2,1,0:T(1,128)S(1)} %compare_select_fusion.columns_any.columns, ...), custom_call_target="tpu_custom_call", output_to_operand_aliasing={{0}: (4, {})} | custom-call | tf_op jit(solution)/shard_map/others/pallas_call | solution.py:41
  12.7 3.7 %collective-permute-start.4 = (bf16[256,128]{1,0:T(8,128)(2,1)S(1)}, bf16[256,128]{1,0:T(8,128)(2,1)S(1)}, u32[]{:S(2)}, u32[]{:S(2)}) collective-permute-start(bf16[256,128]{1,0:T(8,128)(2,1)S(1)} %get-tuple-element.30), channel_id=1, source_target_pairs={{0,3},{1,2},{2,1},{3,0},{4,7},{5,6},{6,5},{7,4},{8,11},{9,10},{10,... | collective-permute-start | bytes 196616 | tf_op jit(solution)/shard_map/ppermute | solution.py:461
  17.2 1.6 %prep.3 = (bf16[1,8,64,512]{3,2,1,0:T(8,128)(2,1)S(1)}, f32[8,128]{1,0:T(8,128)}) custom-call(bf16[4,8,1,8,4096]{4,3,2,1,0:T(8,128)(2,1)} %affinity_hbm.3), custom_call_target="tpu_custom_call" | custom-call | tf_op jit(solution)/shard_map/prep/pallas_call | solution.py:41
  20.0 2.3 %collective-permute-done.5.refs_2_ = bf16[256,128]{1,0:T(8,128)(2,1)S(1)} collective-permute-done((bf16[256,128]{1,0:T(8,128)(2,1)S(1)}, bf16[256,128]{1,0:T(8,128)(2,1)S(1)}, u32[]{:S(2)}, u32[]{:S(2)}) %collective-permute-start.5) | collective-permute-done | bytes 65568 | tf_op jit(solution)/shard_map/ppermute | solution.py:461
  23.6 1.6 %collective-permute-start.8 = (bf16[352,128]{1,0:T(8,128)(2,1)S(1)}, bf16[352,128]{1,0:T(8,128)(2,1)S(1)}, u32[]{:S(2)}, u32[]{:S(2)}) collective-permute-start(bf16[352,128]{1,0:T(8,128)(2,1)S(1)} %middle.1.refs_0_), channel_id=1, source_target_pairs={{0,20},{4,16},{8,28},{12,24},{16,4},{20,0},{24,12},{28,8},{1,21},{... | collective-permute-start | bytes 270344 | tf_op jit(solution)/shard_map/ppermute | solution.py:461
  25.6 3.0 %collective-permute-done.9.refs_3_ = bf16[352,128]{1,0:T(8,128)(2,1)S(1)} collective-permute-done((bf16[352,128]{1,0:T(8,128)(2,1)S(1)}, bf16[352,128]{1,0:T(8,128)(2,1)S(1)}, u32[]{:S(2)}, u32[]{:S(2)}) %collective-permute-start.9) | collective-permute-done | bytes 90144 | tf_op jit(solution)/shard_map/ppermute | solution.py:461
  28.6 1.7 %collective-permute-done.8.refs_2_ = bf16[352,128]{1,0:T(8,128)(2,1)S(1)} collective-permute-done((bf16[352,128]{1,0:T(8,128)(2,1)S(1)}, bf16[352,128]{1,0:T(8,128)(2,1)S(1)}, u32[]{:S(2)}, u32[]{:S(2)}) %collective-permute-start.8) | collective-permute-done | bytes 90144 | tf_op jit(solution)/shard_map/ppermute | solution.py:461
  30.9 1.5 %collective-permute-done.10.far_ref = bf16[4,352,128]{2,1,0:T(8,128)(2,1)S(1)} collective-permute-done((bf16[4,352,128]{2,1,0:T(8,128)(2,1)S(1)}, bf16[4,352,128]{2,1,0:T(8,128)(2,1)S(1)}, u32[]{:S(2)}, u32[]{:S(2)}) %collective-permute-start.10) | collective-permute-done | bytes 360480 | tf_op jit(solution)/shard_map/ppermute | solution.py:461
  32.4 1.6 %others.3 = (bf16[65,64,128]{2,1,0:T(8,128)(2,1)S(1)}, bf16[272,128]{1,0:T(8,128)(2,1)S(1)}, bf16[272,128]{1,0:T(8,128)(2,1)S(1)}, bf16[272,128]{1,0:T(8,128)(2,...) custom-call(s32[4,8,1,8]{3,2,1,0:T(1,128)S(1)} %compare_select_fusion.columns_any.colu, ...), custom_call_target="tpu_custom_call", output_to_operand_aliasing={{0}: (4, {})} | custom-call | tf_op jit(solution)/shard_map/others/pallas_call | solution.py:41
  34.0 2.2 %collective-permute-start.11 = (bf16[272,128]{1,0:T(8,128)(2,1)S(1)}, bf16[272,128]{1,0:T(8,128)(2,1)S(1)}, u32[]{:S(2)}, u32[]{:S(2)}) collective-permute-start(bf16[272,128]{1,0:T(8,128)(2,1)S(1)} %get-tuple-element.36), channel_id=1, source_target_pairs={{0,3},{1,2},{2,1},{3,0},{4,7},{5,6},{6,5},{7,4},{8,11},{9,10},{10,... | collective-permute-start | bytes 208904 | tf_op jit(solution)/shard_map/ppermute | solution.py:461
  36.2 2.3 %collective-permute-start.13 = (bf16[272,128]{1,0:T(8,128)(2,1)S(1)}, bf16[272,128]{1,0:T(8,128)(2,1)S(1)}, u32[]{:S(2)}, u32[]{:S(2)}) collective-permute-start(bf16[272,128]{1,0:T(8,128)(2,1)S(1)} %get-tuple-element.38), channel_id=1, source_target_pairs={{0,1},{1,0},{2,3},{3,2},{4,5},{5,4},{6,7},{7,6},{8,9},{9,8},{10,11... | collective-permute-start | bytes 208904 | tf_op jit(solution)/shard_map/ppermute | solution.py:461
  39.6 1.4 %collective-permute-done.11.refs_1_ = bf16[272,128]{1,0:T(8,128)(2,1)S(1)} collective-permute-done((bf16[272,128]{1,0:T(8,128)(2,1)S(1)}, bf16[272,128]{1,0:T(8,128)(2,1)S(1)}, u32[]{:S(2)}, u32[]{:S(2)}) %collective-permute-start.11) | collective-permute-done | bytes 69664 | tf_op jit(solution)/shard_map/ppermute | solution.py:461
  40.9 2.1 %collective-permute-done.12.refs_2_ = bf16[272,128]{1,0:T(8,128)(2,1)S(1)} collective-permute-done((bf16[272,128]{1,0:T(8,128)(2,1)S(1)}, bf16[272,128]{1,0:T(8,128)(2,1)S(1)}, u32[]{:S(2)}, u32[]{:S(2)}) %collective-permute-start.12) | collective-permute-done | bytes 69664 | tf_op jit(solution)/shard_map/ppermute | solution.py:461
  43.5 1.7 %collective-permute-start.16 = (f32[64,128]{1,0:T(8,128)S(1)}, f32[64,128]{1,0:T(8,128)S(1)}, u32[]{:S(2)}, u32[]{:S(2)}) collective-permute-start(f32[64,128]{1,0:T(8,128)S(1)} %get-tuple-element.40.refs_0_), channel_id=1, source_target_pairs={{0,7},{1,6},{2,5},{3,4},{4,3},{5,2},{6,1},{7,0},{8,15},{9,14},{10,... | collective-permute-start | bytes 98312 | tf_op jit(solution)/shard_map/ppermute | solution.py:471
  45.3 2.0 %collective-permute-start.14 = (f32[64,128]{1,0:T(8,128)S(1)}, f32[64,128]{1,0:T(8,128)S(1)}, u32[]{:S(2)}, u32[]{:S(2)}) collective-permute-start(f32[64,128]{1,0:T(8,128)S(1)} %get-tuple-element.40.refs_0_), channel_id=1, source_target_pairs={{0,5},{1,4},{2,7},{3,6},{4,1},{5,0},{6,3},{7,2},{8,13},{9,12},{10,... | collective-permute-start | bytes 98312 | tf_op jit(solution)/shard_map/ppermute | solution.py:471
  47.3 1.6 %collective-permute-done.16.refs_3_ = f32[64,128]{1,0:T(8,128)S(1)} collective-permute-done((f32[64,128]{1,0:T(8,128)S(1)}, f32[64,128]{1,0:T(8,128)S(1)}, u32[]{:S(2)}, u32[]{:S(2)}) %collective-permute-start.16) | collective-permute-done | bytes 32800 | tf_op jit(solution)/shard_map/ppermute | solution.py:471
  48.9 1.5 %collective-permute-done.15.refs_2_ = f32[64,128]{1,0:T(8,128)S(1)} collective-permute-done((f32[64,128]{1,0:T(8,128)S(1)}, f32[64,128]{1,0:T(8,128)S(1)}, u32[]{:S(2)}, u32[]{:S(2)}) %collective-permute-start.15) | collective-permute-done | bytes 32800 | tf_op jit(solution)/shard_map/ppermute | solution.py:471
  51.4 1.3 %collective-permute-start.18 = (f32[32,128]{1,0:T(8,128)S(1)}, f32[32,128]{1,0:T(8,128)S(1)}, u32[]{:S(2)}, u32[]{:S(2)}) collective-permute-start(f32[32,128]{1,0:T(8,128)S(1)} %get-tuple-element.42.refs_0_), channel_id=1, source_target_pairs={{0,20},{4,16},{8,28},{12,24},{16,4},{20,0},{24,12},{28,8},{1,21},{... | collective-permute-start | bytes 49160 | tf_op jit(solution)/shard_map/ppermute | solution.py:461
  53.4 1.5 %first_factor.1.refs_4_.inverse_ref = f32[64,64]{1,0:T(8,128)S(1)} custom-call(f32[32,128]{1,0:T(8,128)S(1)} %get-tuple-element.41.gram_ref), custom_call_target="tpu_custom_call" | custom-call | tf_op jit(solution)/shard_map/first_factor/pallas_call | solution.py:41
  57.0 2.9 %finish.1 = f32[1,8,4096]{2,1,0:T(8,128)} custom-call(f32[256,128]{1,0:T(8,128)S(1)} %get-tuple-element.39.rows_ref, f32[64,64]{1,0:T(8,128)S(1)} %first_factor.1.refs_4_.inverse_ref, f32[32,128]{1,0:T(8,128)S(1)} %add_parts.1.refs_0_, f32[32,128]{1,0:T(8,128)S(1)} %collective-permute-done.20.refs_1_), custom_call_target="tpu_custom_call" | custom-call | tf_op jit(solution)/shard_map/finish/pallas_call | solution.py:41
  (40 shorter events, 12.6 us)
Async XLA Ops:
  1.0 8.7 %copy-start = (s32[4,8,1,8]{3,2,1,0:T(1,128)S(1)}, s32[4,8,1,8]{3,2,1,0:T(1,128)}, u32[]{:S(2)}) copy-start(s32[4,8,1,8]{3,2,1,0:T(1,128)} %param.6) | copy-start | bytes 3076
  1.0 8.7 %copy-start.1 = (s32[4,8,1]{1,2,0:T(1,128)S(1)}, s32[4,8,1]{1,2,0:T(1,128)}, u32[]{:S(2)}) copy-start(s32[4,8,1]{1,2,0:T(1,128)} %param.7) | copy-start | bytes 388
  1.0 6.5 %collective-permute-start.2 = (bf16[256,128]{1,0:T(8,128)(2,1)S(1)}, bf16[256,128]{1,0:T(8,128)(2,1)S(1)}, u32[]{:S(2)}, u32[]{:S(2)}) collective-permute-start(bf16[256,128]{1,0:T(8,128)(2,1)S(1)} %get-tuple-element.27.refs_0_), channel_id=1, source_target_pairs={{0,28},{4,24},{8,20},{12,16},{16,12},{20,8},{24,4},{28,0},{1,29},{... | collective-permute-start | bytes 196616 | tf_op jit(solution)/shard_map/ppermute | solution.py:461
  4.4 3.9 %collective-permute-start.1 = (bf16[256,128]{1,0:T(8,128)(2,1)S(1)}, bf16[256,128]{1,0:T(8,128)(2,1)S(1)}, u32[]{:S(2)}, u32[]{:S(2)}) collective-permute-start(bf16[256,128]{1,0:T(8,128)(2,1)S(1)} %get-tuple-element.27.refs_0_), channel_id=1, source_target_pairs={{0,20},{4,16},{8,28},{12,24},{16,4},{20,0},{24,12},{28,8},{1,21},{... | collective-permute-start | bytes 196616 | tf_op jit(solution)/shard_map/ppermute | solution.py:461
  5.2 4.3 %collective-permute-start = (bf16[256,128]{1,0:T(8,128)(2,1)S(1)}, bf16[256,128]{1,0:T(8,128)(2,1)S(1)}, u32[]{:S(2)}, u32[]{:S(2)}) collective-permute-start(bf16[256,128]{1,0:T(8,128)(2,1)S(1)} %get-tuple-element.27.refs_0_), channel_id=1, source_target_pairs={{0,12},{4,8},{8,4},{12,0},{16,28},{20,24},{24,20},{28,16},{1,13},{... | collective-permute-start | bytes 196616 | tf_op jit(solution)/shard_map/ppermute | solution.py:461
  9.6 1.6 %collective-permute-start.3 = (bf16[4,256,128]{2,1,0:T(8,128)(2,1)S(1)}, bf16[4,256,128]{2,1,0:T(8,128)(2,1)S(1)}, u32[]{:S(2)}, u32[]{:S(2)}) collective-permute-start(bf16[4,256,128]{2,1,0:T(8,128)(2,1)S(1)} %stack.2.near_ref), channel_id=1, source_target_pairs={{0,4},{4,0},{8,12},{12,8},{16,20},{20,16},{24,28},{28,24},{1,5},{5... | collective-permute-start | bytes 786440 | tf_op jit(solution)/shard_map/ppermute | solution.py:461
  12.7 7.2 %collective-permute-start.4 = (bf16[256,128]{1,0:T(8,128)(2,1)S(1)}, bf16[256,128]{1,0:T(8,128)(2,1)S(1)}, u32[]{:S(2)}, u32[]{:S(2)}) collective-permute-start(bf16[256,128]{1,0:T(8,128)(2,1)S(1)} %get-tuple-element.30), channel_id=1, source_target_pairs={{0,3},{1,2},{2,1},{3,0},{4,7},{5,6},{6,5},{7,4},{8,11},{9,10},{10,... | collective-permute-start | bytes 196616 | tf_op jit(solution)/shard_map/ppermute | solution.py:461
  16.4 5.9 %collective-permute-start.5 = (bf16[256,128]{1,0:T(8,128)(2,1)S(1)}, bf16[256,128]{1,0:T(8,128)(2,1)S(1)}, u32[]{:S(2)}, u32[]{:S(2)}) collective-permute-start(bf16[256,128]{1,0:T(8,128)(2,1)S(1)} %get-tuple-element.31), channel_id=1, source_target_pairs={{0,2},{1,3},{2,0},{3,1},{4,6},{5,7},{6,4},{7,5},{8,10},{9,11},{10,... | collective-permute-start | bytes 196616 | tf_op jit(solution)/shard_map/ppermute | solution.py:461
  16.4 5.9 %collective-permute-start.6 = (bf16[256,128]{1,0:T(8,128)(2,1)S(1)}, bf16[256,128]{1,0:T(8,128)(2,1)S(1)}, u32[]{:S(2)}, u32[]{:S(2)}) collective-permute-start(bf16[256,128]{1,0:T(8,128)(2,1)S(1)} %get-tuple-element.32), channel_id=1, source_target_pairs={{0,1},{1,0},{2,3},{3,2},{4,5},{5,4},{6,7},{7,6},{8,9},{9,8},{10,11... | collective-permute-start | bytes 196616 | tf_op jit(solution)/shard_map/ppermute | solution.py:461
  22.8 5.8 %collective-permute-start.9 = (bf16[352,128]{1,0:T(8,128)(2,1)S(1)}, bf16[352,128]{1,0:T(8,128)(2,1)S(1)}, u32[]{:S(2)}, u32[]{:S(2)}) collective-permute-start(bf16[352,128]{1,0:T(8,128)(2,1)S(1)} %middle.1.refs_0_), channel_id=1, source_target_pairs={{0,28},{4,24},{8,20},{12,16},{16,12},{20,8},{24,4},{28,0},{1,29},{... | collective-permute-start | bytes 270344 | tf_op jit(solution)/shard_map/ppermute | solution.py:461
  23.6 6.7 %collective-permute-start.8 = (bf16[352,128]{1,0:T(8,128)(2,1)S(1)}, bf16[352,128]{1,0:T(8,128)(2,1)S(1)}, u32[]{:S(2)}, u32[]{:S(2)}) collective-permute-start(bf16[352,128]{1,0:T(8,128)(2,1)S(1)} %middle.1.refs_0_), channel_id=1, source_target_pairs={{0,20},{4,16},{8,28},{12,24},{16,4},{20,0},{24,12},{28,8},{1,21},{... | collective-permute-start | bytes 270344 | tf_op jit(solution)/shard_map/ppermute | solution.py:461
  25.3 5.3 %collective-permute-start.7 = (bf16[352,128]{1,0:T(8,128)(2,1)S(1)}, bf16[352,128]{1,0:T(8,128)(2,1)S(1)}, u32[]{:S(2)}, u32[]{:S(2)}) collective-permute-start(bf16[352,128]{1,0:T(8,128)(2,1)S(1)} %middle.1.refs_0_), channel_id=1, source_target_pairs={{0,12},{4,8},{8,4},{12,0},{16,28},{20,24},{24,20},{28,16},{1,13},{... | collective-permute-start | bytes 270344 | tf_op jit(solution)/shard_map/ppermute | solution.py:461
  30.6 1.7 %collective-permute-start.10 = (bf16[4,352,128]{2,1,0:T(8,128)(2,1)S(1)}, bf16[4,352,128]{2,1,0:T(8,128)(2,1)S(1)}, u32[]{:S(2)}, u32[]{:S(2)}) collective-permute-start(bf16[4,352,128]{2,1,0:T(8,128)(2,1)S(1)} %stack.3.near_ref), channel_id=1, source_target_pairs={{0,4},{4,0},{8,12},{12,8},{16,20},{20,16},{24,28},{28,24},{1,5},{5... | collective-permute-start | bytes 1081352 | tf_op jit(solution)/shard_map/ppermute | solution.py:461
  34.0 6.9 %collective-permute-start.11 = (bf16[272,128]{1,0:T(8,128)(2,1)S(1)}, bf16[272,128]{1,0:T(8,128)(2,1)S(1)}, u32[]{:S(2)}, u32[]{:S(2)}) collective-permute-start(bf16[272,128]{1,0:T(8,128)(2,1)S(1)} %get-tuple-element.36), channel_id=1, source_target_pairs={{0,3},{1,2},{2,1},{3,0},{4,7},{5,6},{6,5},{7,4},{8,11},{9,10},{10,... | collective-permute-start | bytes 208904 | tf_op jit(solution)/shard_map/ppermute | solution.py:461
  36.2 6.9 %collective-permute-start.12 = (bf16[272,128]{1,0:T(8,128)(2,1)S(1)}, bf16[272,128]{1,0:T(8,128)(2,1)S(1)}, u32[]{:S(2)}, u32[]{:S(2)}) collective-permute-start(bf16[272,128]{1,0:T(8,128)(2,1)S(1)} %get-tuple-element.37), channel_id=1, source_target_pairs={{0,2},{1,3},{2,0},{3,1},{4,6},{5,7},{6,4},{7,5},{8,10},{9,11},{10,... | collective-permute-start | bytes 208904 | tf_op jit(solution)/shard_map/ppermute | solution.py:461
  36.2 6.9 %collective-permute-start.13 = (bf16[272,128]{1,0:T(8,128)(2,1)S(1)}, bf16[272,128]{1,0:T(8,128)(2,1)S(1)}, u32[]{:S(2)}, u32[]{:S(2)}) collective-permute-start(bf16[272,128]{1,0:T(8,128)(2,1)S(1)} %get-tuple-element.38), channel_id=1, source_target_pairs={{0,1},{1,0},{2,3},{3,2},{4,5},{5,4},{6,7},{7,6},{8,9},{9,8},{10,11... | collective-permute-start | bytes 208904 | tf_op jit(solution)/shard_map/ppermute | solution.py:461
  43.5 5.3 %collective-permute-start.16 = (f32[64,128]{1,0:T(8,128)S(1)}, f32[64,128]{1,0:T(8,128)S(1)}, u32[]{:S(2)}, u32[]{:S(2)}) collective-permute-start(f32[64,128]{1,0:T(8,128)S(1)} %get-tuple-element.40.refs_0_), channel_id=1, source_target_pairs={{0,7},{1,6},{2,5},{3,4},{4,3},{5,2},{6,1},{7,0},{8,15},{9,14},{10,... | collective-permute-start | bytes 98312 | tf_op jit(solution)/shard_map/ppermute | solution.py:471
  45.3 5.1 %collective-permute-start.15 = (f32[64,128]{1,0:T(8,128)S(1)}, f32[64,128]{1,0:T(8,128)S(1)}, u32[]{:S(2)}, u32[]{:S(2)}) collective-permute-start(f32[64,128]{1,0:T(8,128)S(1)} %get-tuple-element.40.refs_0_), channel_id=1, source_target_pairs={{0,6},{1,7},{2,4},{3,5},{4,2},{5,3},{6,0},{7,1},{8,14},{9,15},{10,... | collective-permute-start | bytes 98312 | tf_op jit(solution)/shard_map/ppermute | solution.py:471
  45.3 5.1 %collective-permute-start.14 = (f32[64,128]{1,0:T(8,128)S(1)}, f32[64,128]{1,0:T(8,128)S(1)}, u32[]{:S(2)}, u32[]{:S(2)}) collective-permute-start(f32[64,128]{1,0:T(8,128)S(1)} %get-tuple-element.40.refs_0_), channel_id=1, source_target_pairs={{0,5},{1,4},{2,7},{3,6},{4,1},{5,0},{6,3},{7,2},{8,13},{9,12},{10,... | collective-permute-start | bytes 98312 | tf_op jit(solution)/shard_map/ppermute | solution.py:471
  50.4 4.5 %collective-permute-start.19 = (f32[32,128]{1,0:T(8,128)S(1)}, f32[32,128]{1,0:T(8,128)S(1)}, u32[]{:S(2)}, u32[]{:S(2)}) collective-permute-start(f32[32,128]{1,0:T(8,128)S(1)} %get-tuple-element.42.refs_0_), channel_id=1, source_target_pairs={{0,28},{4,24},{8,20},{12,16},{16,12},{20,8},{24,4},{28,0},{1,29},{... | collective-permute-start | bytes 49160 | tf_op jit(solution)/shard_map/ppermute | solution.py:461
  51.4 3.5 %collective-permute-start.18 = (f32[32,128]{1,0:T(8,128)S(1)}, f32[32,128]{1,0:T(8,128)S(1)}, u32[]{:S(2)}, u32[]{:S(2)}) collective-permute-start(f32[32,128]{1,0:T(8,128)S(1)} %get-tuple-element.42.refs_0_), channel_id=1, source_target_pairs={{0,20},{4,16},{8,28},{12,24},{16,4},{20,0},{24,12},{28,8},{1,21},{... | collective-permute-start | bytes 49160 | tf_op jit(solution)/shard_map/ppermute | solution.py:461
  52.6 3.2 %collective-permute-start.17 = (f32[32,128]{1,0:T(8,128)S(1)}, f32[32,128]{1,0:T(8,128)S(1)}, u32[]{:S(2)}, u32[]{:S(2)}) collective-permute-start(f32[32,128]{1,0:T(8,128)S(1)} %get-tuple-element.42.refs_0_), channel_id=1, source_target_pairs={{0,12},{4,8},{8,4},{12,0},{16,28},{20,24},{24,20},{28,16},{1,13},{... | collective-permute-start | bytes 49160 | tf_op jit(solution)/shard_map/ppermute | solution.py:461
  55.8 1.2 %collective-permute-start.20 = (f32[32,128]{1,0:T(8,128)S(1)}, f32[32,128]{1,0:T(8,128)S(1)}, u32[]{:S(2)}, u32[]{:S(2)}) collective-permute-start(f32[32,128]{1,0:T(8,128)S(1)} %add_parts.1.refs_0_), channel_id=1, source_target_pairs={{0,4},{4,0},{8,12},{12,8},{16,20},{20,16},{24,28},{28,24},{1,5},{5... | collective-permute-start | bytes 49160 | tf_op jit(solution)/shard_map/ppermute | solution.py:461

commit v7 on v6

--- a/solution.py
+++ b/solution.py
@@ -96,8 +96,9 @@
     )
 
 
-def prep_kernel(ranges, affinity_hbm, out_ref, done_ref, affinity_ref, scratch, sems):
-    done_ref[...] = jnp.zeros_like(done_ref)
+def prep_kernel(
+    ranges, affinity_hbm, inv_hbm, out_ref, inverse_ref, affinity_ref, inv_ref, scratch, sems, inv_sem
+):
     count, block_rows, _, slots, flat = affinity_ref.shape
     half = flat // 128
     own = lax.axis_index("cols")
@@ -105,11 +106,17 @@
         pltpu.make_async_copy(affinity_hbm.at[m ^ own], affinity_ref.at[place], sems.at[place])
         for place, m in enumerate(ranges)
     ]
+    inv_copy = pltpu.make_async_copy(inv_hbm, inv_ref, inv_sem)
+    inv_copy.start()
     for copy in copies:
         copy.start()
     source, target = iota((256, 256), 0), iota((256, 256), 1)
     moved = (source // 64 % 2) * 128 + (source // 128) * 64 + (source % 2) * 32 + source % 64 // 2
     permute = (moved == target).astype(BF16)
+    inv_copy.wait()
+    inverse = 1.0 / inv_ref[0]
+    high = inverse.astype(BF16).astype(F32)
+    inverse_ref[...] = jnp.concatenate([high, inverse - high], axis=1)
     for m in range(count):
         copies[m].wait()
         for i in range(block_rows):
@@ -129,35 +136,23 @@
                 out_ref[m, i, half:, s * 128 : (s + 1) * 128] = piece[:, 128:]
 
 
-def prep(ranges, affinity):
+def prep(ranges, affinity, inv_degree):
     _, block_rows, _, slots, flat = affinity.shape
     count = len(ranges)
     return call(
         functools.partial(prep_kernel, ranges),
         "prep",
-        [hbm()],
-        (shaped((count, block_rows, 64, slots * 64), BF16), shaped((8, 128), F32)),
-        (affinity,),
+        [hbm(), hbm()],
+        (shaped((count, block_rows, 64, slots * 64), BF16), shaped((block_rows, 128), F32)),
+        (affinity, inv_degree),
         [
             pltpu.VMEM((count,) + affinity.shape[1:], BF16),
+            pltpu.VMEM(inv_degree.shape, F32),
             pltpu.VMEM((2, flat // 128 * slots, 128), F32),
             pltpu.SemaphoreType.DMA((count,)),
+            pltpu.SemaphoreType.DMA,
         ],
     )
-
-
-def split(value):
-    high = value.astype(BF16)
-    rest = value - high.astype(F32)
-    middle = rest.astype(BF16)
-    return high, middle, (rest - middle.astype(F32)).astype(BF16)
-
-
-def joined(ref, index, first):
-    high, middle, low = (
-        ref[index, first + 32 * part : first + 32 * (part + 1)].astype(F32) for part in range(3)
-    )
-    return high + (middle + low)
 
 
 def stack_kernel(count, *refs):
@@ -212,27 +207,28 @@
         out_ref[i * 32 : (i + 1) * 32, :] = jnp.where(low, result[:32], result[32:]).astype(BF16)
 
 
+def largest_notes(notes):
+    largest = notes[0].astype(F32)
+    for note in notes[1:]:
+        largest = jnp.maximum(largest, note.astype(F32))
+    return largest
+
+
 def others_kernel(offsets, ranges, columns_any, matrix_ref, far_ref, near_ref, old_table, table, *refs):
     del old_table
     *outs, columns, sem = refs
     copy = pltpu.make_async_copy(columns_any, columns, sem)
     copy.start()
     fill_table(far_ref, offsets, table)
-    terms, grams = outs[: len(ranges)], outs[len(ranges) :]
-    first = matrix_ref.shape[1] * 32
-    if grams:
-        gram_ref, trace_ref = grams
-        gram = joined(near_ref, 0, first) + joined(far_ref, 0, first)
-        for index in range(1, len(offsets)):
-            gram = gram + joined(near_ref, index, first) + joined(far_ref, index, first)
-        gram_ref[...] = gram
-        row, lane = iota(gram.shape, 0), iota(gram.shape, 1)
-        diagonal = lane % 64 == row + lane // 64 * 32
-        trace = jnp.sum(jnp.where(diagonal, gram, 0.0), axis=(0, 1), keepdims=True)
-        trace = jnp.broadcast_to(trace, trace_ref.shape).astype(BF16)
-        trace_ref[...] = trace
+    terms, first = outs[: len(ranges)], matrix_ref.shape[1] * 32
+    if len(outs) > len(ranges):
+        notes = largest_notes(
+            [ref[index, first:] for ref in (near_ref, far_ref) for index in range(len(offsets))]
+        ).astype(BF16)
+        for ref in outs[len(ranges) :]:
+            ref[...] = notes
         for term in terms:
-            term[first:, :] = trace
+            term[first:, :] = notes
     copy.wait()
     for place, m in enumerate(ranges):
         group = m ^ lax.axis_index("cols")
@@ -249,7 +245,7 @@
     rows = block_rows * 32
     outs = [shaped(table.shape, BF16)] + [shaped((rows + 16 * extra, 128), BF16)] * len(ranges)
     if extra:
-        outs += [shaped((32, 128), F32), shaped((16, 128), BF16)]
+        outs.append(shaped((16, 128), BF16))
     table, *outs = call(
         functools.partial(others_kernel, offsets[count:], ranges),
         "others",
@@ -277,54 +273,92 @@
     return summed
 
 
+def folded(both):
+    gram = both[:64, :64] + both[64:, 64:]
+    return jnp.concatenate([gram[:32], gram[32:]], axis=1)
+
+
 def local_gram(rows):
     both = lax.dot_general(
         rows, rows, (((0,), (0,)), ((), ())), precision=HIGHEST, preferred_element_type=F32
     )
-    gram = both[:64, :64] + both[64:, 64:]
-    return jnp.concatenate([gram[:32], gram[32:]], axis=1)
-
-
-def middle_kernel(degree_ref, *refs):
+    return folded(both)
+
+
+def middle_kernel(degree_ref, inverse_ref, *refs):
     terms, out_ref = refs[:-1], refs[-1]
     count = degree_ref.shape[0]
     degree = degree_ref[...]
     rows = add_terms(terms, count) * degree
     out_ref[:count] = (rows * degree).astype(BF16)
-    for part, value in enumerate(split(local_gram(rows))):
-        out_ref[count + part * 32 : count + (part + 1) * 32] = value
-
-
-def middle(degree, terms):
+    squares = jnp.sum(rows * rows, axis=(0, 1), keepdims=True)
+    out_ref[count:] = jnp.concatenate(
+        [inverse_ref[...], jnp.broadcast_to(squares, (8, 128))], axis=0
+    ).astype(BF16)
+
+
+def middle(degree, inverse, terms):
     return call(
         middle_kernel,
         "middle",
-        [vmem()] * (1 + len(terms)),
-        shaped((degree.shape[0] + 96, 128), BF16),
-        (degree, *terms),
-    )
-
-
-def collect_kernel(total, degree_ref, first_ref, trace_ref, *refs):
+        [vmem()] * (2 + len(terms)),
+        shaped((degree.shape[0] + 16, 128), BF16),
+        (degree, inverse, *terms),
+    )
+
+
+def row_gram_kernel(near_ref, far_ref, gram_ref, rows):
+    lane = iota((32, 128), 1)
+    pair = lane % 64 // 2 == iota((32, 128), 0)
+    spread = (iota((128, 128), 0) % 2 == iota((128, 128), 1) // 64).astype(BF16)
+    count = near_ref.shape[1] - 16
+    size = near_ref.shape[0]
+    for index in range(2 * size):
+        ref = (near_ref, far_ref)[index // size]
+        notes = ref[index % size, count:].astype(F32)
+        masked = [
+            jnp.where(pair, jnp.broadcast_to(notes[i : i + 1], (32, 128)), 0.0).astype(BF16)
+            for i in range(count // 32)
+        ]
+        inverse = jnp.dot(jnp.concatenate(masked, axis=0), spread, preferred_element_type=F32)
+        block = ref[index % size, :count].astype(F32) * inverse
+        rows[index * count : (index + 1) * count, :] = block.astype(BF16)
+    both = lax.dot_general(
+        rows[...], rows[...], (((0,), (0,)), ((), ())), preferred_element_type=F32
+    )
+    gram_ref[...] = folded(both)
+
+
+def row_gram(near, far):
+    count = 2 * near.shape[0] * (near.shape[1] - 16)
+    return call(
+        row_gram_kernel,
+        "row_gram",
+        [vmem(), vmem()],
+        shaped((32, 128), F32),
+        (near, far),
+        [pltpu.VMEM((count, 128), BF16)],
+    )
+
+
+def collect_kernel(devices, total, degree_ref, first_ref, notes_ref, *refs):
     terms, (rows_ref, grams_ref) = refs[:-2], refs[-2:]
     count = degree_ref.shape[0]
-    largest = trace_ref[...].astype(F32)
-    for term in terms[1:]:
-        largest = jnp.maximum(largest, term[count:].astype(F32))
-    scale = lax.rsqrt(largest[:1] / total)
+    largest = largest_notes([notes_ref[...]] + [term[count:] for term in terms[1:]])
+    scale = lax.rsqrt(largest[8:9] * (devices / total))
     rows = add_terms(terms, count) * degree_ref[...] * scale
     rows_ref[...] = rows
     grams_ref[32:] = first_ref[...] * (scale * scale)
     grams_ref[:32] = local_gram(rows)
 
 
-def collect(total, degree, first, trace, terms):
-    return call(
-        functools.partial(collect_kernel, total),
+def collect(devices, total, degree, first, notes, terms):
+    return call(
+        functools.partial(collect_kernel, devices, total),
         "collect",
         [vmem()] * (3 + len(terms)),
         (shaped(degree.shape, F32), shaped((64, 128), F32)),
-        (degree, first, trace, *terms),
+        (degree, first, notes, *terms),
     )
 
 
@@ -514,15 +548,16 @@
     ranges = list(range(groups - 1, 0, -1))
 
     scaled, degree = start(panel, inv_degree)
-    matrix, done = prep(ranges, affinity)
-    own_matrix, _ = prep([0], affinity)
-    near, far, offsets = gather_rows(scaled, [done])
+    matrix, inverse = prep(ranges, affinity, inv_degree)
+    own_matrix, _ = prep([0], affinity, inv_degree)
+    near, far, offsets = gather_rows(scaled, [inverse])
     table = near_table(offsets, near, block_rows)
     terms, _ = products(offsets, ranges, columns, matrix, own_matrix, near, far, table)
-    near, far, offsets = gather_rows(middle(degree, terms), [])
+    near, far, offsets = gather_rows(middle(degree, inverse, terms), [])
     table = near_table(offsets, near, block_rows)
-    terms, (first, trace) = products(offsets, ranges, columns, matrix, own_matrix, near, far, table)
-    rows, grams = collect(total, degree, first, trace, terms)
+    terms, (notes,) = products(offsets, ranges, columns, matrix, own_matrix, near, far, table)
+    devices = float(groups * ranks)
+    rows, grams = collect(devices, total, degree, row_gram(near, far), notes, terms)
     flip = 1 if ranks == 8 else 0
     gram, first = add_columns(total, [grams] + [swap_both(grams, flip, m) for m in reversed(ranges)])
     inverse = first_factor(first)

time: 60 us -> 61.2 us (1.020)
  waiting for transfers between devices: 20.6 us -> 21.6 us
    ppermute x3, waiting for transfers between devices: 3.08 us -> 4.06 us  [swap_both(): return lax.ppermute(value, ('rows', 'cols'), pairs)]
    pallas_call x17 -> x18, Pallas kernels: 15.8 us -> 16.3 us  [call(): pl.pallas_call(kernel, out_shape=outs, in_specs=ins, out_specs=jax.tree.m...]
  transfers between devices with their start and end apart: 21 -> 21, of which waited for: 14 -> 13; matrix products, arithmetic and copies ran while one was open for 0% -> 0% of each run, Pallas kernels for 13% -> 14%
where the time goes in v7:
time: 61.2 us; the launch traced here: 61 us
  starting transfers between devices  22.9 us (37%)
  waiting for transfers between devices  21.6 us (35%)
  Pallas kernels  16.3 us (27%)
    ppermute x18, starting transfers between devices, swap(): lax.ppermute(value, axis, [(index, index ^ mask) for index in range(size)])  19.2 us
    ppermute x18, waiting for transfers between devices, swap(): lax.ppermute(value, axis, [(index, index ^ mask) for index in range(size)])  17.6 us
    pallas_call x18, Pallas kernels, call(): pl.pallas_call(kernel, out_shape=outs, in_specs=ins, out_specs=jax.tree.m...  16.3 us
    ppermute x3, waiting for transfers between devices, swap_both(): return lax.ppermute(value, ('rows', 'cols'), pairs)  4.06 us
    ppermute x3, starting transfers between devices, swap_both(): return lax.ppermute(value, ('rows', 'cols'), pairs)  3.69 us
  transfers between devices with their start and end apart: 21, of which 13 were waited for; matrix products, arithmetic and copies ran while one was open for 0% of the time, Pallas kernels for 14%

profile of v7, /device:TPU:0, one launch (start us, length us, event | category | flops | bytes accessed | tf_op | source)
XLA Modules:
  0.0 61.0 jit_solution(6769137195400864816)
XLA Ops:
  1.0 2.4 %collective-permute-start = (bf16[256,128]{1,0:T(8,128)(2,1)S(1)}, bf16[256,128]{1,0:T(8,128)(2,1)S(1)}, u32[]{:S(2)}, u32[]{:S(2)}) collective-permute-start(bf16[256,128]{1,0:T(8,128)(2,1)S(1)} %get-tuple-element.27.refs_0_), channel_id=1, source_target_pairs={{0,12},{4,8},{8,4},{12,0},{16,28},{20,24},{24,20},{28,16},{1,13},{... | collective-permute-start | bytes 196616 | tf_op jit(solution)/shard_map/ppermute | solution.py:495
  3.5 1.8 %collective-permute-start.1 = (bf16[256,128]{1,0:T(8,128)(2,1)S(1)}, bf16[256,128]{1,0:T(8,128)(2,1)S(1)}, u32[]{:S(2)}, u32[]{:S(2)}) collective-permute-start(bf16[256,128]{1,0:T(8,128)(2,1)S(1)} %get-tuple-element.27.refs_0_), channel_id=1, source_target_pairs={{0,20},{4,16},{8,28},{12,24},{16,4},{20,0},{24,12},{28,8},{1,21},{... | collective-permute-start | bytes 196616 | tf_op jit(solution)/shard_map/ppermute | solution.py:495
  5.3 2.2 %prep.2 = (bf16[3,8,64,512]{3,2,1,0:T(8,128)(2,1)S(1)}, f32[8,128]{1,0:T(8,128)S(1)}) custom-call(bf16[4,8,1,8,4096]{4,3,2,1,0:T(8,128)(2,1)} %affinity_hbm.3, f32[1,8,64]{2,1,0:T(8,128)} %inv_hbm.5), custom_call_target="tpu_custom_call" | custom-call | tf_op jit(solution)/shard_map/prep/pallas_call | solution.py:41
  7.5 3.0 %collective-permute-done.2.refs_3_ = bf16[256,128]{1,0:T(8,128)(2,1)S(1)} collective-permute-done((bf16[256,128]{1,0:T(8,128)(2,1)S(1)}, bf16[256,128]{1,0:T(8,128)(2,1)S(1)}, u32[]{:S(2)}, u32[]{:S(2)}) %collective-permute-start.2) | collective-permute-done | bytes 65568 | tf_op jit(solution)/shard_map/ppermute | solution.py:495
  12.2 1.6 %others.2 = (bf16[65,64,128]{2,1,0:T(8,128)(2,1)S(1)}, bf16[256,128]{1,0:T(8,128)(2,1)S(1)}, bf16[256,128]{1,0:T(8,128)(2,1)S(1)}, bf16[256,128]{1,0:T(8,128)(2,1)S(1)}) custom-call(s32[4,8,1,8]{3,2,1,0:T(1,128)S(1)} %compare_select_fusion.columns_any.columns, ...), custom_call_target="tpu_custom_call", output_to_operand_aliasing={{0}: (4, {})} | custom-call | tf_op jit(solution)/shard_map/others/pallas_call | solution.py:41
  13.8 3.7 %collective-permute-start.4 = (bf16[256,128]{1,0:T(8,128)(2,1)S(1)}, bf16[256,128]{1,0:T(8,128)(2,1)S(1)}, u32[]{:S(2)}, u32[]{:S(2)}) collective-permute-start(bf16[256,128]{1,0:T(8,128)(2,1)S(1)} %get-tuple-element.29), channel_id=1, source_target_pairs={{0,3},{1,2},{2,1},{3,0},{4,7},{5,6},{6,5},{7,4},{8,11},{9,10},{10,... | collective-permute-start | bytes 196616 | tf_op jit(solution)/shard_map/ppermute | solution.py:495
  18.2 1.7 %prep.3 = (bf16[1,8,64,512]{3,2,1,0:T(8,128)(2,1)S(1)}, f32[8,128]{1,0:T(8,128)}) custom-call(bf16[4,8,1,8,4096]{4,3,2,1,0:T(8,128)(2,1)} %affinity_hbm.3, f32[1,8,64]{2,1,0:T(8,128)} %inv_hbm.5), custom_call_target="tpu_custom_call" | custom-call | tf_op jit(solution)/shard_map/prep/pallas_call | solution.py:41
  21.0 2.3 %collective-permute-done.5.refs_2_ = bf16[256,128]{1,0:T(8,128)(2,1)S(1)} collective-permute-done((bf16[256,128]{1,0:T(8,128)(2,1)S(1)}, bf16[256,128]{1,0:T(8,128)(2,1)S(1)}, u32[]{:S(2)}, u32[]{:S(2)}) %collective-permute-start.5) | collective-permute-done | bytes 65568 | tf_op jit(solution)/shard_map/ppermute | solution.py:495
  24.3 1.8 %collective-permute-start.9 = (bf16[272,128]{1,0:T(8,128)(2,1)S(1)}, bf16[272,128]{1,0:T(8,128)(2,1)S(1)}, u32[]{:S(2)}, u32[]{:S(2)}) collective-permute-start(bf16[272,128]{1,0:T(8,128)(2,1)S(1)} %middle.1.refs_0_), channel_id=1, source_target_pairs={{0,28},{4,24},{8,20},{12,16},{16,12},{20,8},{24,4},{28,0},{1,29},{... | collective-permute-start | bytes 208904 | tf_op jit(solution)/shard_map/ppermute | solution.py:495
  26.1 1.8 %collective-permute-done.7.refs_1_ = bf16[272,128]{1,0:T(8,128)(2,1)S(1)} collective-permute-done((bf16[272,128]{1,0:T(8,128)(2,1)S(1)}, bf16[272,128]{1,0:T(8,128)(2,1)S(1)}, u32[]{:S(2)}, u32[]{:S(2)}) %collective-permute-start.7) | collective-permute-done | bytes 69664 | tf_op jit(solution)/shard_map/ppermute | solution.py:495
  27.9 1.5 %collective-permute-done.9.refs_3_ = bf16[272,128]{1,0:T(8,128)(2,1)S(1)} collective-permute-done((bf16[272,128]{1,0:T(8,128)(2,1)S(1)}, bf16[272,128]{1,0:T(8,128)(2,1)S(1)}, u32[]{:S(2)}, u32[]{:S(2)}) %collective-permute-start.9) | collective-permute-done | bytes 69664 | tf_op jit(solution)/shard_map/ppermute | solution.py:495
  29.8 1.3 %collective-permute-done.10.far_ref = bf16[4,272,128]{2,1,0:T(8,128)(2,1)S(1)} collective-permute-done((bf16[4,272,128]{2,1,0:T(8,128)(2,1)S(1)}, bf16[4,272,128]{2,1,0:T(8,128)(2,1)S(1)}, u32[]{:S(2)}, u32[]{:S(2)}) %collective-permute-start.10) | collective-permute-done | bytes 278560 | tf_op jit(solution)/shard_map/ppermute | solution.py:495
  31.1 1.6 %others.3 = (bf16[65,64,128]{2,1,0:T(8,128)(2,1)S(1)}, bf16[272,128]{1,0:T(8,128)(2,1)S(1)}, bf16[272,128]{1,0:T(8,128)(2,1)S(1)}, bf16[272,128]{1,0:T(8,128)(2,1)S(1)}, bf16[16,128]{1,0:T(8,128)(2,1)S(1)}) custom-call(s32[4,8,1,8]{3,2,1,0:T(1,128)S(1)} %compare_select_fusion.columns_any.columns, ...), custom_call_target="tpu_custom_call", output_to_operand_aliasing={{0}: (4, {})} | custom-call | tf_op jit(solution)/shard_map/others/pallas_call | solution.py:41
  32.7 2.5 %collective-permute-start.11 = (bf16[272,128]{1,0:T(8,128)(2,1)S(1)}, bf16[272,128]{1,0:T(8,128)(2,1)S(1)}, u32[]{:S(2)}, u32[]{:S(2)}) collective-permute-start(bf16[272,128]{1,0:T(8,128)(2,1)S(1)} %get-tuple-element.34), channel_id=1, source_target_pairs={{0,3},{1,2},{2,1},{3,0},{4,7},{5,6},{6,5},{7,4},{8,11},{9,10},{10,... | collective-permute-start | bytes 208904 | tf_op jit(solution)/shard_map/ppermute | solution.py:495
  35.3 1.8 %collective-permute-start.13 = (bf16[272,128]{1,0:T(8,128)(2,1)S(1)}, bf16[272,128]{1,0:T(8,128)(2,1)S(1)}, u32[]{:S(2)}, u32[]{:S(2)}) collective-permute-start(bf16[272,128]{1,0:T(8,128)(2,1)S(1)} %get-tuple-element.36), channel_id=1, source_target_pairs={{0,1},{1,0},{2,3},{3,2},{4,5},{5,4},{6,7},{7,6},{8,9},{9,8},{10,11... | collective-permute-start | bytes 208904 | tf_op jit(solution)/shard_map/ppermute | solution.py:495
  39.6 2.4 %collective-permute-done.12.refs_2_ = bf16[272,128]{1,0:T(8,128)(2,1)S(1)} collective-permute-done((bf16[272,128]{1,0:T(8,128)(2,1)S(1)}, bf16[272,128]{1,0:T(8,128)(2,1)S(1)}, u32[]{:S(2)}, u32[]{:S(2)}) %collective-permute-start.12) | collective-permute-done | bytes 69664 | tf_op jit(solution)/shard_map/ppermute | solution.py:495
  42.6 2.4 %collective-permute-start.15 = (f32[64,128]{1,0:T(8,128)S(1)}, f32[64,128]{1,0:T(8,128)S(1)}, u32[]{:S(2)}, u32[]{:S(2)}) collective-permute-start(f32[64,128]{1,0:T(8,128)S(1)} %get-tuple-element.38.refs_0_), channel_id=1, source_target_pairs={{0,6},{1,7},{2,4},{3,5},{4,2},{5,3},{6,0},{7,1},{8,14},{9,15},{10,... | collective-permute-start | bytes 98312 | tf_op jit(solution)/shard_map/ppermute | solution.py:505
  45.0 1.2 %collective-permute-start.16 = (f32[64,128]{1,0:T(8,128)S(1)}, f32[64,128]{1,0:T(8,128)S(1)}, u32[]{:S(2)}, u32[]{:S(2)}) collective-permute-start(f32[64,128]{1,0:T(8,128)S(1)} %get-tuple-element.38.refs_0_), channel_id=1, source_target_pairs={{0,7},{1,6},{2,5},{3,4},{4,3},{5,2},{6,1},{7,0},{8,15},{9,14},{10,... | collective-permute-start | bytes 98312 | tf_op jit(solution)/shard_map/ppermute | solution.py:505
  46.9 3.4 %collective-permute-done.16.refs_3_ = f32[64,128]{1,0:T(8,128)S(1)} collective-permute-done((f32[64,128]{1,0:T(8,128)S(1)}, f32[64,128]{1,0:T(8,128)S(1)}, u32[]{:S(2)}, u32[]{:S(2)}) %collective-permute-start.16) | collective-permute-done | bytes 32800 | tf_op jit(solution)/shard_map/ppermute | solution.py:505
  50.3 1.4 %collective-permute-start.17 = (f32[32,128]{1,0:T(8,128)S(1)}, f32[32,128]{1,0:T(8,128)S(1)}, u32[]{:S(2)}, u32[]{:S(2)}) collective-permute-start(f32[32,128]{1,0:T(8,128)S(1)} %get-tuple-element.40.refs_0_), channel_id=1, source_target_pairs={{0,12},{4,8},{8,4},{12,0},{16,28},{20,24},{24,20},{28,16},{1,13},{... | collective-permute-start | bytes 49160 | tf_op jit(solution)/shard_map/ppermute | solution.py:495
  51.7 1.3 %collective-permute-start.18 = (f32[32,128]{1,0:T(8,128)S(1)}, f32[32,128]{1,0:T(8,128)S(1)}, u32[]{:S(2)}, u32[]{:S(2)}) collective-permute-start(f32[32,128]{1,0:T(8,128)S(1)} %get-tuple-element.40.refs_0_), channel_id=1, source_target_pairs={{0,20},{4,16},{8,28},{12,24},{16,4},{20,0},{24,12},{28,8},{1,21},{... | collective-permute-start | bytes 49160 | tf_op jit(solution)/shard_map/ppermute | solution.py:495
  53.3 1.5 %first_factor.1.refs_4_.inverse_ref = f32[64,64]{1,0:T(8,128)S(1)} custom-call(f32[32,128]{1,0:T(8,128)S(1)} %get-tuple-element.39.gram_ref), custom_call_target="tpu_custom_call" | custom-call | tf_op jit(solution)/shard_map/first_factor/pallas_call | solution.py:41
  54.8 2.2 %collective-permute-done.19.refs_3_ = f32[32,128]{1,0:T(8,128)S(1)} collective-permute-done((f32[32,128]{1,0:T(8,128)S(1)}, f32[32,128]{1,0:T(8,128)S(1)}, u32[]{:S(2)}, u32[]{:S(2)}) %collective-permute-start.19) | collective-permute-done | bytes 16416 | tf_op jit(solution)/shard_map/ppermute | solution.py:495
  58.2 2.8 %finish.1 = f32[1,8,4096]{2,1,0:T(8,128)} custom-call(f32[256,128]{1,0:T(8,128)S(1)} %get-tuple-element.37.rows_ref, f32[64,64]{1,0:T(8,128)S(1)} %first_factor.1.refs_4_.inverse_ref, f32[32,128]{1,0:T(8,128)S(1)} %add_parts.1.refs_0_, f32[32,128]{1,0:T(8,128)S(1)} %collective-permute-done.20.refs_1_), custom_call_target="tpu_custom_call" | custom-call | tf_op jit(solution)/shard_map/finish/pallas_call | solution.py:41
  (41 shorter events, 11.1 us)
Async XLA Ops:
  1.0 9.8 %copy-start = (s32[4,8,1,8]{3,2,1,0:T(1,128)S(1)}, s32[4,8,1,8]{3,2,1,0:T(1,128)}, u32[]{:S(2)}) copy-start(s32[4,8,1,8]{3,2,1,0:T(1,128)} %param.6) | copy-start | bytes 3076
  1.0 9.8 %copy-start.1 = (s32[4,8,1]{1,2,0:T(1,128)S(1)}, s32[4,8,1]{1,2,0:T(1,128)}, u32[]{:S(2)}) copy-start(s32[4,8,1]{1,2,0:T(1,128)} %param.7) | copy-start | bytes 388
  1.0 6.5 %collective-permute-start = (bf16[256,128]{1,0:T(8,128)(2,1)S(1)}, bf16[256,128]{1,0:T(8,128)(2,1)S(1)}, u32[]{:S(2)}, u32[]{:S(2)}) collective-permute-start(bf16[256,128]{1,0:T(8,128)(2,1)S(1)} %get-tuple-element.27.refs_0_), channel_id=1, source_target_pairs={{0,12},{4,8},{8,4},{12,0},{16,28},{20,24},{24,20},{28,16},{1,13},{... | collective-permute-start | bytes 196616 | tf_op jit(solution)/shard_map/ppermute | solution.py:495
  3.5 4.0 %collective-permute-start.1 = (bf16[256,128]{1,0:T(8,128)(2,1)S(1)}, bf16[256,128]{1,0:T(8,128)(2,1)S(1)}, u32[]{:S(2)}, u32[]{:S(2)}) collective-permute-start(bf16[256,128]{1,0:T(8,128)(2,1)S(1)} %get-tuple-element.27.refs_0_), channel_id=1, source_target_pairs={{0,20},{4,16},{8,28},{12,24},{16,4},{20,0},{24,12},{28,8},{1,21},{... | collective-permute-start | bytes 196616 | tf_op jit(solution)/shard_map/ppermute | solution.py:495
  5.3 5.3 %collective-permute-start.2 = (bf16[256,128]{1,0:T(8,128)(2,1)S(1)}, bf16[256,128]{1,0:T(8,128)(2,1)S(1)}, u32[]{:S(2)}, u32[]{:S(2)}) collective-permute-start(bf16[256,128]{1,0:T(8,128)(2,1)S(1)} %get-tuple-element.27.refs_0_), channel_id=1, source_target_pairs={{0,28},{4,24},{8,20},{12,16},{16,12},{20,8},{24,4},{28,0},{1,29},{... | collective-permute-start | bytes 196616 | tf_op jit(solution)/shard_map/ppermute | solution.py:495
  10.6 1.6 %collective-permute-start.3 = (bf16[4,256,128]{2,1,0:T(8,128)(2,1)S(1)}, bf16[4,256,128]{2,1,0:T(8,128)(2,1)S(1)}, u32[]{:S(2)}, u32[]{:S(2)}) collective-permute-start(bf16[4,256,128]{2,1,0:T(8,128)(2,1)S(1)} %stack.2.near_ref), channel_id=1, source_target_pairs={{0,4},{4,0},{8,12},{12,8},{16,20},{20,16},{24,28},{28,24},{1,5},{5... | collective-permute-start | bytes 786440 | tf_op jit(solution)/shard_map/ppermute | solution.py:495
  13.8 7.3 %collective-permute-start.4 = (bf16[256,128]{1,0:T(8,128)(2,1)S(1)}, bf16[256,128]{1,0:T(8,128)(2,1)S(1)}, u32[]{:S(2)}, u32[]{:S(2)}) collective-permute-start(bf16[256,128]{1,0:T(8,128)(2,1)S(1)} %get-tuple-element.29), channel_id=1, source_target_pairs={{0,3},{1,2},{2,1},{3,0},{4,7},{5,6},{6,5},{7,4},{8,11},{9,10},{10,... | collective-permute-start | bytes 196616 | tf_op jit(solution)/shard_map/ppermute | solution.py:495
  17.4 5.9 %collective-permute-start.5 = (bf16[256,128]{1,0:T(8,128)(2,1)S(1)}, bf16[256,128]{1,0:T(8,128)(2,1)S(1)}, u32[]{:S(2)}, u32[]{:S(2)}) collective-permute-start(bf16[256,128]{1,0:T(8,128)(2,1)S(1)} %get-tuple-element.30), channel_id=1, source_target_pairs={{0,2},{1,3},{2,0},{3,1},{4,6},{5,7},{6,4},{7,5},{8,10},{9,11},{10,... | collective-permute-start | bytes 196616 | tf_op jit(solution)/shard_map/ppermute | solution.py:495
  17.4 5.9 %collective-permute-start.6 = (bf16[256,128]{1,0:T(8,128)(2,1)S(1)}, bf16[256,128]{1,0:T(8,128)(2,1)S(1)}, u32[]{:S(2)}, u32[]{:S(2)}) collective-permute-start(bf16[256,128]{1,0:T(8,128)(2,1)S(1)} %get-tuple-element.31), channel_id=1, source_target_pairs={{0,1},{1,0},{2,3},{3,2},{4,5},{5,4},{6,7},{7,6},{8,9},{9,8},{10,11... | collective-permute-start | bytes 196616 | tf_op jit(solution)/shard_map/ppermute | solution.py:495
  23.5 4.4 %collective-permute-start.7 = (bf16[272,128]{1,0:T(8,128)(2,1)S(1)}, bf16[272,128]{1,0:T(8,128)(2,1)S(1)}, u32[]{:S(2)}, u32[]{:S(2)}) collective-permute-start(bf16[272,128]{1,0:T(8,128)(2,1)S(1)} %middle.1.refs_0_), channel_id=1, source_target_pairs={{0,12},{4,8},{8,4},{12,0},{16,28},{20,24},{24,20},{28,16},{1,13},{... | collective-permute-start | bytes 208904 | tf_op jit(solution)/shard_map/ppermute | solution.py:495
  23.6 4.3 %collective-permute-start.8 = (bf16[272,128]{1,0:T(8,128)(2,1)S(1)}, bf16[272,128]{1,0:T(8,128)(2,1)S(1)}, u32[]{:S(2)}, u32[]{:S(2)}) collective-permute-start(bf16[272,128]{1,0:T(8,128)(2,1)S(1)} %middle.1.refs_0_), channel_id=1, source_target_pairs={{0,20},{4,16},{8,28},{12,24},{16,4},{20,0},{24,12},{28,8},{1,21},{... | collective-permute-start | bytes 208904 | tf_op jit(solution)/shard_map/ppermute | solution.py:495
  24.3 5.2 %collective-permute-start.9 = (bf16[272,128]{1,0:T(8,128)(2,1)S(1)}, bf16[272,128]{1,0:T(8,128)(2,1)S(1)}, u32[]{:S(2)}, u32[]{:S(2)}) collective-permute-start(bf16[272,128]{1,0:T(8,128)(2,1)S(1)} %middle.1.refs_0_), channel_id=1, source_target_pairs={{0,28},{4,24},{8,20},{12,16},{16,12},{20,8},{24,4},{28,0},{1,29},{... | collective-permute-start | bytes 208904 | tf_op jit(solution)/shard_map/ppermute | solution.py:495
  29.5 1.6 %collective-permute-start.10 = (bf16[4,272,128]{2,1,0:T(8,128)(2,1)S(1)}, bf16[4,272,128]{2,1,0:T(8,128)(2,1)S(1)}, u32[]{:S(2)}, u32[]{:S(2)}) collective-permute-start(bf16[4,272,128]{2,1,0:T(8,128)(2,1)S(1)} %stack.3.near_ref), channel_id=1, source_target_pairs={{0,4},{4,0},{8,12},{12,8},{16,20},{20,16},{24,28},{28,24},{1,5},{5... | collective-permute-start | bytes 835592 | tf_op jit(solution)/shard_map/ppermute | solution.py:495
  32.7 6.9 %collective-permute-start.11 = (bf16[272,128]{1,0:T(8,128)(2,1)S(1)}, bf16[272,128]{1,0:T(8,128)(2,1)S(1)}, u32[]{:S(2)}, u32[]{:S(2)}) collective-permute-start(bf16[272,128]{1,0:T(8,128)(2,1)S(1)} %get-tuple-element.34), channel_id=1, source_target_pairs={{0,3},{1,2},{2,1},{3,0},{4,7},{5,6},{6,5},{7,4},{8,11},{9,10},{10,... | collective-permute-start | bytes 208904 | tf_op jit(solution)/shard_map/ppermute | solution.py:495
  35.2 6.8 %collective-permute-start.12 = (bf16[272,128]{1,0:T(8,128)(2,1)S(1)}, bf16[272,128]{1,0:T(8,128)(2,1)S(1)}, u32[]{:S(2)}, u32[]{:S(2)}) collective-permute-start(bf16[272,128]{1,0:T(8,128)(2,1)S(1)} %get-tuple-element.35), channel_id=1, source_target_pairs={{0,2},{1,3},{2,0},{3,1},{4,6},{5,7},{6,4},{7,5},{8,10},{9,11},{10,... | collective-permute-start | bytes 208904 | tf_op jit(solution)/shard_map/ppermute | solution.py:495
  35.3 6.8 %collective-permute-start.13 = (bf16[272,128]{1,0:T(8,128)(2,1)S(1)}, bf16[272,128]{1,0:T(8,128)(2,1)S(1)}, u32[]{:S(2)}, u32[]{:S(2)}) collective-permute-start(bf16[272,128]{1,0:T(8,128)(2,1)S(1)} %get-tuple-element.36), channel_id=1, source_target_pairs={{0,1},{1,0},{2,3},{3,2},{4,5},{5,4},{6,7},{7,6},{8,9},{9,8},{10,11... | collective-permute-start | bytes 208904 | tf_op jit(solution)/shard_map/ppermute | solution.py:495
  42.5 3.7 %collective-permute-start.14 = (f32[64,128]{1,0:T(8,128)S(1)}, f32[64,128]{1,0:T(8,128)S(1)}, u32[]{:S(2)}, u32[]{:S(2)}) collective-permute-start(f32[64,128]{1,0:T(8,128)S(1)} %get-tuple-element.38.refs_0_), channel_id=1, source_target_pairs={{0,5},{1,4},{2,7},{3,6},{4,1},{5,0},{6,3},{7,2},{8,13},{9,12},{10,... | collective-permute-start | bytes 98312 | tf_op jit(solution)/shard_map/ppermute | solution.py:505
  42.6 4.3 %collective-permute-start.15 = (f32[64,128]{1,0:T(8,128)S(1)}, f32[64,128]{1,0:T(8,128)S(1)}, u32[]{:S(2)}, u32[]{:S(2)}) collective-permute-start(f32[64,128]{1,0:T(8,128)S(1)} %get-tuple-element.38.refs_0_), channel_id=1, source_target_pairs={{0,6},{1,7},{2,4},{3,5},{4,2},{5,3},{6,0},{7,1},{8,14},{9,15},{10,... | collective-permute-start | bytes 98312 | tf_op jit(solution)/shard_map/ppermute | solution.py:505
  45.0 5.3 %collective-permute-start.16 = (f32[64,128]{1,0:T(8,128)S(1)}, f32[64,128]{1,0:T(8,128)S(1)}, u32[]{:S(2)}, u32[]{:S(2)}) collective-permute-start(f32[64,128]{1,0:T(8,128)S(1)} %get-tuple-element.38.refs_0_), channel_id=1, source_target_pairs={{0,7},{1,6},{2,5},{3,4},{4,3},{5,2},{6,1},{7,0},{8,15},{9,14},{10,... | collective-permute-start | bytes 98312 | tf_op jit(solution)/shard_map/ppermute | solution.py:505
  50.3 4.5 %collective-permute-start.17 = (f32[32,128]{1,0:T(8,128)S(1)}, f32[32,128]{1,0:T(8,128)S(1)}, u32[]{:S(2)}, u32[]{:S(2)}) collective-permute-start(f32[32,128]{1,0:T(8,128)S(1)} %get-tuple-element.40.refs_0_), channel_id=1, source_target_pairs={{0,12},{4,8},{8,4},{12,0},{16,28},{20,24},{24,20},{28,16},{1,13},{... | collective-permute-start | bytes 49160 | tf_op jit(solution)/shard_map/ppermute | solution.py:495
  51.7 3.2 %collective-permute-start.18 = (f32[32,128]{1,0:T(8,128)S(1)}, f32[32,128]{1,0:T(8,128)S(1)}, u32[]{:S(2)}, u32[]{:S(2)}) collective-permute-start(f32[32,128]{1,0:T(8,128)S(1)} %get-tuple-element.40.refs_0_), channel_id=1, source_target_pairs={{0,20},{4,16},{8,28},{12,24},{16,4},{20,0},{24,12},{28,8},{1,21},{... | collective-permute-start | bytes 49160 | tf_op jit(solution)/shard_map/ppermute | solution.py:495
  52.9 4.1 %collective-permute-start.19 = (f32[32,128]{1,0:T(8,128)S(1)}, f32[32,128]{1,0:T(8,128)S(1)}, u32[]{:S(2)}, u32[]{:S(2)}) collective-permute-start(f32[32,128]{1,0:T(8,128)S(1)} %get-tuple-element.40.refs_0_), channel_id=1, source_target_pairs={{0,28},{4,24},{8,20},{12,16},{16,12},{20,8},{24,4},{28,0},{1,29},{... | collective-permute-start | bytes 49160 | tf_op jit(solution)/shard_map/ppermute | solution.py:495
  57.0 1.2 %collective-permute-start.20 = (f32[32,128]{1,0:T(8,128)S(1)}, f32[32,128]{1,0:T(8,128)S(1)}, u32[]{:S(2)}, u32[]{:S(2)}) collective-permute-start(f32[32,128]{1,0:T(8,128)S(1)} %add_parts.1.refs_0_), channel_id=1, source_target_pairs={{0,4},{4,0},{8,12},{12,8},{16,20},{20,16},{24,28},{28,24},{1,5},{5... | collective-permute-start | bytes 49160 | tf_op jit(solution)/shard_map/ppermute | solution.py:495

commit v8 on v7

--- a/solution.py
+++ b/solution.py
@@ -507,7 +507,7 @@
 
 def stages(size):
     if size == 8:
-        return [[3, 5, 7], [1]]
+        return [[7, 5, 3], [1]]
     bits, bit = [], 1
     while bit < size:
         bits.append([bit])
@@ -559,7 +559,7 @@
     devices = float(groups * ranks)
     rows, grams = collect(devices, total, degree, row_gram(near, far), notes, terms)
     flip = 1 if ranks == 8 else 0
-    gram, first = add_columns(total, [grams] + [swap_both(grams, flip, m) for m in reversed(ranges)])
+    gram, first = add_columns(total, [grams] + [swap_both(grams, flip, m) for m in ranges])
     inverse = first_factor(first)
     return finish(total, block_rows, rows, inverse, add_rows(gram, [inverse]))
 

time: 61.2 us -> 58.7 us (0.959)
  waiting for transfers between devices: 21.6 us -> 18.8 us
    ppermute x18, waiting for transfers between devices: 17.6 us -> 15.7 us  [swap(): lax.ppermute(value, axis, [(index, index ^ mask) for index in range(size)])]
    ppermute x3, waiting for transfers between devices: 4.06 us -> 3.08 us  [swap_both(): return lax.ppermute(value, ('rows', 'cols'), pairs)]
  transfers between devices with their start and end apart: 21 -> 21, of which waited for: 13 -> 15; matrix products, arithmetic and copies ran while one was open for 0% -> 0% of each run, Pallas kernels for 14% -> 15%
where the time goes in v8:
time: 58.7 us; the launch traced here: 58.5 us
  starting transfers between devices  23.2 us (40%)
  waiting for transfers between devices  18.8 us (32%)
  Pallas kernels  16.3 us (28%)
    ppermute x18, starting transfers between devices, swap(): lax.ppermute(value, axis, [(index, index ^ mask) for index in range(size)])  19.5 us
    pallas_call x18, Pallas kernels, call(): pl.pallas_call(kernel, out_shape=outs, in_specs=ins, out_specs=jax.tree.m...  16.3 us
    ppermute x18, waiting for transfers between devices, swap(): lax.ppermute(value, axis, [(index, index ^ mask) for index in range(size)])  15.7 us
    ppermute x3, starting transfers between devices, swap_both(): return lax.ppermute(value, ('rows', 'cols'), pairs)  3.74 us
    ppermute x3, waiting for transfers between devices, swap_both(): return lax.ppermute(value, ('rows', 'cols'), pairs)  3.08 us
  transfers between devices with their start and end apart: 21, of which 15 were waited for; matrix products, arithmetic and copies ran while one was open for 0% of the time, Pallas kernels for 15%

profile of v8, /device:TPU:0, one launch (start us, length us, event | category | flops | bytes accessed | tf_op | source)
XLA Modules:
  0.0 58.5 jit_solution(2632591320281432937)
XLA Ops:
  1.0 3.4 %collective-permute-start = (bf16[256,128]{1,0:T(8,128)(2,1)S(1)}, bf16[256,128]{1,0:T(8,128)(2,1)S(1)}, u32[]{:S(2)}, u32[]{:S(2)}) collective-permute-start(bf16[256,128]{1,0:T(8,128)(2,1)S(1)} %get-tuple-element.27.refs_0_), channel_id=1, source_target_pairs={{0,28},{4,24},{8,20},{12,16},{16,12},{20,8},{24,4},{28,0},{1,29},{... | collective-permute-start | bytes 196616 | tf_op jit(solution)/shard_map/ppermute | solution.py:495
  5.4 2.2 %prep.2 = (bf16[3,8,64,512]{3,2,1,0:T(8,128)(2,1)S(1)}, f32[8,128]{1,0:T(8,128)S(1)}) custom-call(bf16[4,8,1,8,4096]{4,3,2,1,0:T(8,128)(2,1)} %affinity_hbm.3, f32[1,8,64]{2,1,0:T(8,128)} %inv_hbm.5), custom_call_target="tpu_custom_call" | custom-call | tf_op jit(solution)/shard_map/prep/pallas_call | solution.py:41
  8.3 1.2 %collective-permute-done.2.refs_3_ = bf16[256,128]{1,0:T(8,128)(2,1)S(1)} collective-permute-done((bf16[256,128]{1,0:T(8,128)(2,1)S(1)}, bf16[256,128]{1,0:T(8,128)(2,1)S(1)}, u32[]{:S(2)}, u32[]{:S(2)}) %collective-permute-start.2) | collective-permute-done | bytes 65568 | tf_op jit(solution)/shard_map/ppermute | solution.py:495
  10.0 1.2 %collective-permute-done.3.far_ref = bf16[4,256,128]{2,1,0:T(8,128)(2,1)S(1)} collective-permute-done((bf16[4,256,128]{2,1,0:T(8,128)(2,1)S(1)}, bf16[4,256,128]{2,1,0:T(8,128)(2,1)S(1)}, u32[]{:S(2)}, u32[]{:S(2)}) %collective-permute-start.3) | collective-permute-done | bytes 262176 | tf_op jit(solution)/shard_map/ppermute | solution.py:495
  11.2 1.6 %others.2 = (bf16[65,64,128]{2,1,0:T(8,128)(2,1)S(1)}, bf16[256,128]{1,0:T(8,128)(2,1)S(1)}, bf16[256,128]{1,0:T(8,128)(2,1)S(1)}, bf16[256,128]{1,0:T(8,128)(2,1)S(1)}) custom-call(s32[4,8,1,8]{3,2,1,0:T(1,128)S(1)} %compare_select_fusion.columns_any.columns, ...), custom_call_target="tpu_custom_call", output_to_operand_aliasing={{0}: (4, {})} | custom-call | tf_op jit(solution)/shard_map/others/pallas_call | solution.py:41
  12.7 3.7 %collective-permute-start.4 = (bf16[256,128]{1,0:T(8,128)(2,1)S(1)}, bf16[256,128]{1,0:T(8,128)(2,1)S(1)}, u32[]{:S(2)}, u32[]{:S(2)}) collective-permute-start(bf16[256,128]{1,0:T(8,128)(2,1)S(1)} %get-tuple-element.29), channel_id=1, source_target_pairs={{0,3},{1,2},{2,1},{3,0},{4,7},{5,6},{6,5},{7,4},{8,11},{9,10},{10,... | collective-permute-start | bytes 196616 | tf_op jit(solution)/shard_map/ppermute | solution.py:495
  17.2 1.7 %prep.3 = (bf16[1,8,64,512]{3,2,1,0:T(8,128)(2,1)S(1)}, f32[8,128]{1,0:T(8,128)}) custom-call(bf16[4,8,1,8,4096]{4,3,2,1,0:T(8,128)(2,1)} %affinity_hbm.3, f32[1,8,64]{2,1,0:T(8,128)} %inv_hbm.5), custom_call_target="tpu_custom_call" | custom-call | tf_op jit(solution)/shard_map/prep/pallas_call | solution.py:41
  18.9 1.1 %own.2.refs_0_ = bf16[256,128]{1,0:T(8,128)(2,1)S(1)} custom-call(s32[4,8,1,8]{3,2,1,0:T(1,128)S(1)} %compare_select_fusion.columns_any.columns, bf16[1,8,64,512]{3,2,1,0:T(8,128)(2,1)S(1)} %get-tuple-element.25.matrix_ref, bf16[65,64,128]{2,1,0:T(8,128)(2,1)S(1)} %get-tuple-element.28.table), custom_call_target="tpu_custom_call" | custom-call | tf_op jit(solution)/shard_map/own/pallas_call | solution.py:41
  20.0 2.3 %collective-permute-done.5.refs_2_ = bf16[256,128]{1,0:T(8,128)(2,1)S(1)} collective-permute-done((bf16[256,128]{1,0:T(8,128)(2,1)S(1)}, bf16[256,128]{1,0:T(8,128)(2,1)S(1)}, u32[]{:S(2)}, u32[]{:S(2)}) %collective-permute-start.5) | collective-permute-done | bytes 65568 | tf_op jit(solution)/shard_map/ppermute | solution.py:495
  23.4 1.6 %collective-permute-start.8 = (bf16[272,128]{1,0:T(8,128)(2,1)S(1)}, bf16[272,128]{1,0:T(8,128)(2,1)S(1)}, u32[]{:S(2)}, u32[]{:S(2)}) collective-permute-start(bf16[272,128]{1,0:T(8,128)(2,1)S(1)} %middle.1.refs_0_), channel_id=1, source_target_pairs={{0,20},{4,16},{8,28},{12,24},{16,4},{20,0},{24,12},{28,8},{1,21},{... | collective-permute-start | bytes 208904 | tf_op jit(solution)/shard_map/ppermute | solution.py:495
  25.3 2.6 %collective-permute-done.7.refs_1_ = bf16[272,128]{1,0:T(8,128)(2,1)S(1)} collective-permute-done((bf16[272,128]{1,0:T(8,128)(2,1)S(1)}, bf16[272,128]{1,0:T(8,128)(2,1)S(1)}, u32[]{:S(2)}, u32[]{:S(2)}) %collective-permute-start.7) | collective-permute-done | bytes 69664 | tf_op jit(solution)/shard_map/ppermute | solution.py:495
  27.9 1.3 %collective-permute-done.8.refs_2_ = bf16[272,128]{1,0:T(8,128)(2,1)S(1)} collective-permute-done((bf16[272,128]{1,0:T(8,128)(2,1)S(1)}, bf16[272,128]{1,0:T(8,128)(2,1)S(1)}, u32[]{:S(2)}, u32[]{:S(2)}) %collective-permute-start.8) | collective-permute-done | bytes 69664 | tf_op jit(solution)/shard_map/ppermute | solution.py:495
  29.8 1.3 %collective-permute-done.10.far_ref = bf16[4,272,128]{2,1,0:T(8,128)(2,1)S(1)} collective-permute-done((bf16[4,272,128]{2,1,0:T(8,128)(2,1)S(1)}, bf16[4,272,128]{2,1,0:T(8,128)(2,1)S(1)}, u32[]{:S(2)}, u32[]{:S(2)}) %collective-permute-start.10) | collective-permute-done | bytes 278560 | tf_op jit(solution)/shard_map/ppermute | solution.py:495
  31.1 1.6 %others.3 = (bf16[65,64,128]{2,1,0:T(8,128)(2,1)S(1)}, bf16[272,128]{1,0:T(8,128)(2,1)S(1)}, bf16[272,128]{1,0:T(8,128)(2,1)S(1)}, bf16[272,128]{1,0:T(8,128)(2,1)S(1)}, bf16[16,128]{1,0:T(8,128)(2,1)S(1)}) custom-call(s32[4,8,1,8]{3,2,1,0:T(1,128)S(1)} %compare_select_fusion.columns_any.columns, ...), custom_call_target="tpu_custom_call", output_to_operand_aliasing={{0}: (4, {})} | custom-call | tf_op jit(solution)/shard_map/others/pallas_call | solution.py:41
  32.7 2.2 %collective-permute-start.11 = (bf16[272,128]{1,0:T(8,128)(2,1)S(1)}, bf16[272,128]{1,0:T(8,128)(2,1)S(1)}, u32[]{:S(2)}, u32[]{:S(2)}) collective-permute-start(bf16[272,128]{1,0:T(8,128)(2,1)S(1)} %get-tuple-element.34), channel_id=1, source_target_pairs={{0,3},{1,2},{2,1},{3,0},{4,7},{5,6},{6,5},{7,4},{8,11},{9,10},{10,... | collective-permute-start | bytes 208904 | tf_op jit(solution)/shard_map/ppermute | solution.py:495
  34.9 2.3 %collective-permute-start.13 = (bf16[272,128]{1,0:T(8,128)(2,1)S(1)}, bf16[272,128]{1,0:T(8,128)(2,1)S(1)}, u32[]{:S(2)}, u32[]{:S(2)}) collective-permute-start(bf16[272,128]{1,0:T(8,128)(2,1)S(1)} %get-tuple-element.36), channel_id=1, source_target_pairs={{0,1},{1,0},{2,3},{3,2},{4,5},{5,4},{6,7},{7,6},{8,9},{9,8},{10,11... | collective-permute-start | bytes 208904 | tf_op jit(solution)/shard_map/ppermute | solution.py:495
  39.6 2.1 %collective-permute-done.12.refs_2_ = bf16[272,128]{1,0:T(8,128)(2,1)S(1)} collective-permute-done((bf16[272,128]{1,0:T(8,128)(2,1)S(1)}, bf16[272,128]{1,0:T(8,128)(2,1)S(1)}, u32[]{:S(2)}, u32[]{:S(2)}) %collective-permute-start.12) | collective-permute-done | bytes 69664 | tf_op jit(solution)/shard_map/ppermute | solution.py:495
  42.2 1.7 %collective-permute-start.14 = (f32[64,128]{1,0:T(8,128)S(1)}, f32[64,128]{1,0:T(8,128)S(1)}, u32[]{:S(2)}, u32[]{:S(2)}) collective-permute-start(f32[64,128]{1,0:T(8,128)S(1)} %get-tuple-element.38.refs_0_), channel_id=1, source_target_pairs={{0,7},{1,6},{2,5},{3,4},{4,3},{5,2},{6,1},{7,0},{8,15},{9,14},{10,... | collective-permute-start | bytes 98312 | tf_op jit(solution)/shard_map/ppermute | solution.py:505
  44.0 2.0 %collective-permute-start.16 = (f32[64,128]{1,0:T(8,128)S(1)}, f32[64,128]{1,0:T(8,128)S(1)}, u32[]{:S(2)}, u32[]{:S(2)}) collective-permute-start(f32[64,128]{1,0:T(8,128)S(1)} %get-tuple-element.38.refs_0_), channel_id=1, source_target_pairs={{0,5},{1,4},{2,7},{3,6},{4,1},{5,0},{6,3},{7,2},{8,13},{9,12},{10,... | collective-permute-start | bytes 98312 | tf_op jit(solution)/shard_map/ppermute | solution.py:505
  46.0 1.6 %collective-permute-done.14.refs_1_ = f32[64,128]{1,0:T(8,128)S(1)} collective-permute-done((f32[64,128]{1,0:T(8,128)S(1)}, f32[64,128]{1,0:T(8,128)S(1)}, u32[]{:S(2)}, u32[]{:S(2)}) %collective-permute-start.14) | collective-permute-done | bytes 32800 | tf_op jit(solution)/shard_map/ppermute | solution.py:505
  47.6 1.5 %collective-permute-done.15.refs_2_ = f32[64,128]{1,0:T(8,128)S(1)} collective-permute-done((f32[64,128]{1,0:T(8,128)S(1)}, f32[64,128]{1,0:T(8,128)S(1)}, u32[]{:S(2)}, u32[]{:S(2)}) %collective-permute-start.15) | collective-permute-done | bytes 32800 | tf_op jit(solution)/shard_map/ppermute | solution.py:505
  49.1 1.4 %collective-permute-start.17 = (f32[32,128]{1,0:T(8,128)S(1)}, f32[32,128]{1,0:T(8,128)S(1)}, u32[]{:S(2)}, u32[]{:S(2)}) collective-permute-start(f32[32,128]{1,0:T(8,128)S(1)} %get-tuple-element.40.refs_0_), channel_id=1, source_target_pairs={{0,28},{4,24},{8,20},{12,16},{16,12},{20,8},{24,4},{28,0},{1,29},{... | collective-permute-start | bytes 49160 | tf_op jit(solution)/shard_map/ppermute | solution.py:495
  52.1 1.5 %first_factor.1.refs_4_.inverse_ref = f32[64,64]{1,0:T(8,128)S(1)} custom-call(f32[32,128]{1,0:T(8,128)S(1)} %get-tuple-element.39.gram_ref), custom_call_target="tpu_custom_call" | custom-call | tf_op jit(solution)/shard_map/first_factor/pallas_call | solution.py:41
  55.7 2.9 %finish.1 = f32[1,8,4096]{2,1,0:T(8,128)} custom-call(f32[256,128]{1,0:T(8,128)S(1)} %get-tuple-element.37.rows_ref, f32[64,64]{1,0:T(8,128)S(1)} %first_factor.1.refs_4_.inverse_ref, f32[32,128]{1,0:T(8,128)S(1)} %add_parts.1.refs_0_, f32[32,128]{1,0:T(8,128)S(1)} %collective-permute-done.20.refs_1_), custom_call_target="tpu_custom_call" | custom-call | tf_op jit(solution)/shard_map/finish/pallas_call | solution.py:41
  (41 shorter events, 12.4 us)
Async XLA Ops:
  1.0 8.7 %copy-start = (s32[4,8,1,8]{3,2,1,0:T(1,128)S(1)}, s32[4,8,1,8]{3,2,1,0:T(1,128)}, u32[]{:S(2)}) copy-start(s32[4,8,1,8]{3,2,1,0:T(1,128)} %param.6) | copy-start | bytes 3076
  1.0 8.7 %copy-start.1 = (s32[4,8,1]{1,2,0:T(1,128)S(1)}, s32[4,8,1]{1,2,0:T(1,128)}, u32[]{:S(2)}) copy-start(s32[4,8,1]{1,2,0:T(1,128)} %param.7) | copy-start | bytes 388
  1.0 6.5 %collective-permute-start = (bf16[256,128]{1,0:T(8,128)(2,1)S(1)}, bf16[256,128]{1,0:T(8,128)(2,1)S(1)}, u32[]{:S(2)}, u32[]{:S(2)}) collective-permute-start(bf16[256,128]{1,0:T(8,128)(2,1)S(1)} %get-tuple-element.27.refs_0_), channel_id=1, source_target_pairs={{0,28},{4,24},{8,20},{12,16},{16,12},{20,8},{24,4},{28,0},{1,29},{... | collective-permute-start | bytes 196616 | tf_op jit(solution)/shard_map/ppermute | solution.py:495
  4.4 3.9 %collective-permute-start.1 = (bf16[256,128]{1,0:T(8,128)(2,1)S(1)}, bf16[256,128]{1,0:T(8,128)(2,1)S(1)}, u32[]{:S(2)}, u32[]{:S(2)}) collective-permute-start(bf16[256,128]{1,0:T(8,128)(2,1)S(1)} %get-tuple-element.27.refs_0_), channel_id=1, source_target_pairs={{0,20},{4,16},{8,28},{12,24},{16,4},{20,0},{24,12},{28,8},{1,21},{... | collective-permute-start | bytes 196616 | tf_op jit(solution)/shard_map/ppermute | solution.py:495
  5.2 4.3 %collective-permute-start.2 = (bf16[256,128]{1,0:T(8,128)(2,1)S(1)}, bf16[256,128]{1,0:T(8,128)(2,1)S(1)}, u32[]{:S(2)}, u32[]{:S(2)}) collective-permute-start(bf16[256,128]{1,0:T(8,128)(2,1)S(1)} %get-tuple-element.27.refs_0_), channel_id=1, source_target_pairs={{0,12},{4,8},{8,4},{12,0},{16,28},{20,24},{24,20},{28,16},{1,13},{... | collective-permute-start | bytes 196616 | tf_op jit(solution)/shard_map/ppermute | solution.py:495
  9.6 1.6 %collective-permute-start.3 = (bf16[4,256,128]{2,1,0:T(8,128)(2,1)S(1)}, bf16[4,256,128]{2,1,0:T(8,128)(2,1)S(1)}, u32[]{:S(2)}, u32[]{:S(2)}) collective-permute-start(bf16[4,256,128]{2,1,0:T(8,128)(2,1)S(1)} %stack.2.near_ref), channel_id=1, source_target_pairs={{0,4},{4,0},{8,12},{12,8},{16,20},{20,16},{24,28},{28,24},{1,5},{5... | collective-permute-start | bytes 786440 | tf_op jit(solution)/shard_map/ppermute | solution.py:495
  12.7 7.3 %collective-permute-start.4 = (bf16[256,128]{1,0:T(8,128)(2,1)S(1)}, bf16[256,128]{1,0:T(8,128)(2,1)S(1)}, u32[]{:S(2)}, u32[]{:S(2)}) collective-permute-start(bf16[256,128]{1,0:T(8,128)(2,1)S(1)} %get-tuple-element.29), channel_id=1, source_target_pairs={{0,3},{1,2},{2,1},{3,0},{4,7},{5,6},{6,5},{7,4},{8,11},{9,10},{10,... | collective-permute-start | bytes 196616 | tf_op jit(solution)/shard_map/ppermute | solution.py:495
  16.4 5.9 %collective-permute-start.5 = (bf16[256,128]{1,0:T(8,128)(2,1)S(1)}, bf16[256,128]{1,0:T(8,128)(2,1)S(1)}, u32[]{:S(2)}, u32[]{:S(2)}) collective-permute-start(bf16[256,128]{1,0:T(8,128)(2,1)S(1)} %get-tuple-element.30), channel_id=1, source_target_pairs={{0,2},{1,3},{2,0},{3,1},{4,6},{5,7},{6,4},{7,5},{8,10},{9,11},{10,... | collective-permute-start | bytes 196616 | tf_op jit(solution)/shard_map/ppermute | solution.py:495
  16.4 5.9 %collective-permute-start.6 = (bf16[256,128]{1,0:T(8,128)(2,1)S(1)}, bf16[256,128]{1,0:T(8,128)(2,1)S(1)}, u32[]{:S(2)}, u32[]{:S(2)}) collective-permute-start(bf16[256,128]{1,0:T(8,128)(2,1)S(1)} %get-tuple-element.31), channel_id=1, source_target_pairs={{0,1},{1,0},{2,3},{3,2},{4,5},{5,4},{6,7},{7,6},{8,9},{9,8},{10,11... | collective-permute-start | bytes 196616 | tf_op jit(solution)/shard_map/ppermute | solution.py:495
  22.5 5.4 %collective-permute-start.7 = (bf16[272,128]{1,0:T(8,128)(2,1)S(1)}, bf16[272,128]{1,0:T(8,128)(2,1)S(1)}, u32[]{:S(2)}, u32[]{:S(2)}) collective-permute-start(bf16[272,128]{1,0:T(8,128)(2,1)S(1)} %middle.1.refs_0_), channel_id=1, source_target_pairs={{0,28},{4,24},{8,20},{12,16},{16,12},{20,8},{24,4},{28,0},{1,29},{... | collective-permute-start | bytes 208904 | tf_op jit(solution)/shard_map/ppermute | solution.py:495
  23.4 5.8 %collective-permute-start.8 = (bf16[272,128]{1,0:T(8,128)(2,1)S(1)}, bf16[272,128]{1,0:T(8,128)(2,1)S(1)}, u32[]{:S(2)}, u32[]{:S(2)}) collective-permute-start(bf16[272,128]{1,0:T(8,128)(2,1)S(1)} %middle.1.refs_0_), channel_id=1, source_target_pairs={{0,20},{4,16},{8,28},{12,24},{16,4},{20,0},{24,12},{28,8},{1,21},{... | collective-permute-start | bytes 208904 | tf_op jit(solution)/shard_map/ppermute | solution.py:495
  25.0 4.4 %collective-permute-start.9 = (bf16[272,128]{1,0:T(8,128)(2,1)S(1)}, bf16[272,128]{1,0:T(8,128)(2,1)S(1)}, u32[]{:S(2)}, u32[]{:S(2)}) collective-permute-start(bf16[272,128]{1,0:T(8,128)(2,1)S(1)} %middle.1.refs_0_), channel_id=1, source_target_pairs={{0,12},{4,8},{8,4},{12,0},{16,28},{20,24},{24,20},{28,16},{1,13},{... | collective-permute-start | bytes 208904 | tf_op jit(solution)/shard_map/ppermute | solution.py:495
  29.5 1.6 %collective-permute-start.10 = (bf16[4,272,128]{2,1,0:T(8,128)(2,1)S(1)}, bf16[4,272,128]{2,1,0:T(8,128)(2,1)S(1)}, u32[]{:S(2)}, u32[]{:S(2)}) collective-permute-start(bf16[4,272,128]{2,1,0:T(8,128)(2,1)S(1)} %stack.3.near_ref), channel_id=1, source_target_pairs={{0,4},{4,0},{8,12},{12,8},{16,20},{20,16},{24,28},{28,24},{1,5},{5... | collective-permute-start | bytes 835592 | tf_op jit(solution)/shard_map/ppermute | solution.py:495
  32.7 6.9 %collective-permute-start.11 = (bf16[272,128]{1,0:T(8,128)(2,1)S(1)}, bf16[272,128]{1,0:T(8,128)(2,1)S(1)}, u32[]{:S(2)}, u32[]{:S(2)}) collective-permute-start(bf16[272,128]{1,0:T(8,128)(2,1)S(1)} %get-tuple-element.34), channel_id=1, source_target_pairs={{0,3},{1,2},{2,1},{3,0},{4,7},{5,6},{6,5},{7,4},{8,11},{9,10},{10,... | collective-permute-start | bytes 208904 | tf_op jit(solution)/shard_map/ppermute | solution.py:495
  34.9 6.9 %collective-permute-start.12 = (bf16[272,128]{1,0:T(8,128)(2,1)S(1)}, bf16[272,128]{1,0:T(8,128)(2,1)S(1)}, u32[]{:S(2)}, u32[]{:S(2)}) collective-permute-start(bf16[272,128]{1,0:T(8,128)(2,1)S(1)} %get-tuple-element.35), channel_id=1, source_target_pairs={{0,2},{1,3},{2,0},{3,1},{4,6},{5,7},{6,4},{7,5},{8,10},{9,11},{10,... | collective-permute-start | bytes 208904 | tf_op jit(solution)/shard_map/ppermute | solution.py:495
  34.9 6.9 %collective-permute-start.13 = (bf16[272,128]{1,0:T(8,128)(2,1)S(1)}, bf16[272,128]{1,0:T(8,128)(2,1)S(1)}, u32[]{:S(2)}, u32[]{:S(2)}) collective-permute-start(bf16[272,128]{1,0:T(8,128)(2,1)S(1)} %get-tuple-element.36), channel_id=1, source_target_pairs={{0,1},{1,0},{2,3},{3,2},{4,5},{5,4},{6,7},{7,6},{8,9},{9,8},{10,11... | collective-permute-start | bytes 208904 | tf_op jit(solution)/shard_map/ppermute | solution.py:495
  42.2 5.3 %collective-permute-start.14 = (f32[64,128]{1,0:T(8,128)S(1)}, f32[64,128]{1,0:T(8,128)S(1)}, u32[]{:S(2)}, u32[]{:S(2)}) collective-permute-start(f32[64,128]{1,0:T(8,128)S(1)} %get-tuple-element.38.refs_0_), channel_id=1, source_target_pairs={{0,7},{1,6},{2,5},{3,4},{4,3},{5,2},{6,1},{7,0},{8,15},{9,14},{10,... | collective-permute-start | bytes 98312 | tf_op jit(solution)/shard_map/ppermute | solution.py:505
  44.0 5.1 %collective-permute-start.15 = (f32[64,128]{1,0:T(8,128)S(1)}, f32[64,128]{1,0:T(8,128)S(1)}, u32[]{:S(2)}, u32[]{:S(2)}) collective-permute-start(f32[64,128]{1,0:T(8,128)S(1)} %get-tuple-element.38.refs_0_), channel_id=1, source_target_pairs={{0,6},{1,7},{2,4},{3,5},{4,2},{5,3},{6,0},{7,1},{8,14},{9,15},{10,... | collective-permute-start | bytes 98312 | tf_op jit(solution)/shard_map/ppermute | solution.py:505
  44.0 5.1 %collective-permute-start.16 = (f32[64,128]{1,0:T(8,128)S(1)}, f32[64,128]{1,0:T(8,128)S(1)}, u32[]{:S(2)}, u32[]{:S(2)}) collective-permute-start(f32[64,128]{1,0:T(8,128)S(1)} %get-tuple-element.38.refs_0_), channel_id=1, source_target_pairs={{0,5},{1,4},{2,7},{3,6},{4,1},{5,0},{6,3},{7,2},{8,13},{9,12},{10,... | collective-permute-start | bytes 98312 | tf_op jit(solution)/shard_map/ppermute | solution.py:505
  49.1 4.5 %collective-permute-start.17 = (f32[32,128]{1,0:T(8,128)S(1)}, f32[32,128]{1,0:T(8,128)S(1)}, u32[]{:S(2)}, u32[]{:S(2)}) collective-permute-start(f32[32,128]{1,0:T(8,128)S(1)} %get-tuple-element.40.refs_0_), channel_id=1, source_target_pairs={{0,28},{4,24},{8,20},{12,16},{16,12},{20,8},{24,4},{28,0},{1,29},{... | collective-permute-start | bytes 49160 | tf_op jit(solution)/shard_map/ppermute | solution.py:495
  50.5 3.2 %collective-permute-start.18 = (f32[32,128]{1,0:T(8,128)S(1)}, f32[32,128]{1,0:T(8,128)S(1)}, u32[]{:S(2)}, u32[]{:S(2)}) collective-permute-start(f32[32,128]{1,0:T(8,128)S(1)} %get-tuple-element.40.refs_0_), channel_id=1, source_target_pairs={{0,20},{4,16},{8,28},{12,24},{16,4},{20,0},{24,12},{28,8},{1,21},{... | collective-permute-start | bytes 49160 | tf_op jit(solution)/shard_map/ppermute | solution.py:495
  51.3 3.2 %collective-permute-start.19 = (f32[32,128]{1,0:T(8,128)S(1)}, f32[32,128]{1,0:T(8,128)S(1)}, u32[]{:S(2)}, u32[]{:S(2)}) collective-permute-start(f32[32,128]{1,0:T(8,128)S(1)} %get-tuple-element.40.refs_0_), channel_id=1, source_target_pairs={{0,12},{4,8},{8,4},{12,0},{16,28},{20,24},{24,20},{28,16},{1,13},{... | collective-permute-start | bytes 49160 | tf_op jit(solution)/shard_map/ppermute | solution.py:495
  54.5 1.2 %collective-permute-start.20 = (f32[32,128]{1,0:T(8,128)S(1)}, f32[32,128]{1,0:T(8,128)S(1)}, u32[]{:S(2)}, u32[]{:S(2)}) collective-permute-start(f32[32,128]{1,0:T(8,128)S(1)} %add_parts.1.refs_0_), channel_id=1, source_target_pairs={{0,4},{4,0},{8,12},{12,8},{16,20},{20,16},{24,28},{28,24},{1,5},{5... | collective-permute-start | bytes 49160 | tf_op jit(solution)/shard_map/ppermute | solution.py:495

commit v9 on v8

--- a/solution.py
+++ b/solution.py
@@ -199,10 +199,11 @@
 
 
 def one_product(group, columns, matrix, table, out_ref):
-    block_rows, slots = columns.shape[1], columns.shape[3]
+    block_rows, slots = matrix.shape[0], matrix.shape[2] // 64
+    first = group * (block_rows * slots)
     low = iota((32, 128), 1) < 64
     for i in range(block_rows):
-        picked = [table[columns[group, i, 0, s]] for s in range(slots)]
+        picked = [table[columns[first + i * slots + s]] for s in range(slots)]
         result = jnp.dot(matrix[i], jnp.concatenate(picked, axis=0), preferred_element_type=F32)
         out_ref[i * 32 : (i + 1) * 32, :] = jnp.where(low, result[:32], result[32:]).astype(BF16)
 
@@ -541,7 +542,7 @@
     total = float(groups * ranks * block_rows * block_size)
     blocks = ranks * block_rows
     live = iota(block_columns.shape, 3) < block_counts[..., None]
-    columns = jnp.where(live, jnp.clip(block_columns, 0, blocks - 1), blocks)
+    columns = jnp.where(live, jnp.clip(block_columns, 0, blocks - 1), blocks).reshape(-1)
     panel, inv_degree, affinity = (
         pltpu.with_memory_space_constraint(value, pltpu.HBM) for value in (panel, inv_degree, affinity)
     )

time: 58.7 us -> 58.3 us (level)
  Pallas kernels: 16.3 us -> 15.3 us
    pallas_call x18, Pallas kernels: 16.3 us -> 15.3 us  [call(): pl.pallas_call(kernel, out_shape=outs, in_specs=ins, out_specs=jax.tree.m...]
  transfers between devices with their start and end apart: 21 -> 21, of which waited for: 15 -> 15; matrix products, arithmetic and copies ran while one was open for 0% -> 0% of each run, Pallas kernels for 15% -> 14%
where the time goes in v9:
time: 58.3 us; the launch traced here: 58.1 us
  starting transfers between devices  23.2 us (40%)
  waiting for transfers between devices  19.2 us (33%)
  Pallas kernels  15.3 us (26%)
    ppermute x18, starting transfers between devices, swap(): lax.ppermute(value, axis, [(index, index ^ mask) for index in range(size)])  19.5 us
    ppermute x18, waiting for transfers between devices, swap(): lax.ppermute(value, axis, [(index, index ^ mask) for index in range(size)])  16.1 us
    pallas_call x18, Pallas kernels, call(): pl.pallas_call(kernel, out_shape=outs, in_specs=ins, out_specs=jax.tree.m...  15.3 us
    ppermute x3, starting transfers between devices, swap_both(): return lax.ppermute(value, ('rows', 'cols'), pairs)  3.74 us
    ppermute x3, waiting for transfers between devices, swap_both(): return lax.ppermute(value, ('rows', 'cols'), pairs)  3.07 us
  transfers between devices with their start and end apart: 21, of which 15 were waited for; matrix products, arithmetic and copies ran while one was open for 0% of the time, Pallas kernels for 14%

profile of v9, /device:TPU:0, one launch (start us, length us, event | category | flops | bytes accessed | tf_op | source)
XLA Modules:
  0.0 58.1 jit_solution(18374754907826151538)
XLA Ops:
  1.0 3.4 %collective-permute-start = (bf16[256,128]{1,0:T(8,128)(2,1)S(1)}, bf16[256,128]{1,0:T(8,128)(2,1)S(1)}, u32[]{:S(2)}, u32[]{:S(2)}) collective-permute-start(bf16[256,128]{1,0:T(8,128)(2,1)S(1)} %get-tuple-element.27.refs_0_), channel_id=1, source_target_pairs={{0,28},{4,24},{8,20},{12,16},{16,12},{20,8},{24,4},{28,0},{1,29},{... | collective-permute-start | bytes 196616 | tf_op jit(solution)/shard_map/ppermute | solution.py:496
  5.4 2.2 %prep.2 = (bf16[3,8,64,512]{3,2,1,0:T(8,128)(2,1)S(1)}, f32[8,128]{1,0:T(8,128)S(1)}) custom-call(bf16[4,8,1,8,4096]{4,3,2,1,0:T(8,128)(2,1)} %affinity_hbm.3, f32[1,8,64]{2,1,0:T(8,128)} %inv_hbm.5), custom_call_target="tpu_custom_call" | custom-call | tf_op jit(solution)/shard_map/prep/pallas_call | solution.py:41
  8.3 1.2 %collective-permute-done.2.refs_3_ = bf16[256,128]{1,0:T(8,128)(2,1)S(1)} collective-permute-done((bf16[256,128]{1,0:T(8,128)(2,1)S(1)}, bf16[256,128]{1,0:T(8,128)(2,1)S(1)}, u32[]{:S(2)}, u32[]{:S(2)}) %collective-permute-start.2) | collective-permute-done | bytes 65568 | tf_op jit(solution)/shard_map/ppermute | solution.py:496
  10.1 1.0 %collective-permute-done.3.far_ref = bf16[4,256,128]{2,1,0:T(8,128)(2,1)S(1)} collective-permute-done((bf16[4,256,128]{2,1,0:T(8,128)(2,1)S(1)}, bf16[4,256,128]{2,1,0:T(8,128)(2,1)S(1)}, u32[]{:S(2)}, u32[]{:S(2)}) %collective-permute-start.3) | collective-permute-done | bytes 262176 | tf_op jit(solution)/shard_map/ppermute | solution.py:496
  11.2 1.3 %others.2 = (bf16[65,64,128]{2,1,0:T(8,128)(2,1)S(1)}, bf16[256,128]{1,0:T(8,128)(2,1)S(1)}, bf16[256,128]{1,0:T(8,128)(2,1)S(1)}, bf16[256,128]{1,0:T(8,128)(2,1)S(1)}) custom-call(s32[256]{0:T(256)S(1)} %reshape.14.columns_any.columns, bf16[3,8,64,512]{3,2,1,0:T(8,128)(2,1)S(1)} %get-tuple-element.26.matrix_ref, ...), custom_call_target="tpu_custom_call", output_to_operand_aliasing={{0}: (4, {})} | custom-call | tf_op jit(solution)/shard_map/others/pallas_call | solution.py:41
  12.5 3.7 %collective-permute-start.4 = (bf16[256,128]{1,0:T(8,128)(2,1)S(1)}, bf16[256,128]{1,0:T(8,128)(2,1)S(1)}, u32[]{:S(2)}, u32[]{:S(2)}) collective-permute-start(bf16[256,128]{1,0:T(8,128)(2,1)S(1)} %get-tuple-element.29), channel_id=1, source_target_pairs={{0,3},{1,2},{2,1},{3,0},{4,7},{5,6},{6,5},{7,4},{8,11},{9,10},{10,... | collective-permute-start | bytes 196616 | tf_op jit(solution)/shard_map/ppermute | solution.py:496
  16.9 1.7 %prep.3 = (bf16[1,8,64,512]{3,2,1,0:T(8,128)(2,1)S(1)}, f32[8,128]{1,0:T(8,128)}) custom-call(bf16[4,8,1,8,4096]{4,3,2,1,0:T(8,128)(2,1)} %affinity_hbm.3, f32[1,8,64]{2,1,0:T(8,128)} %inv_hbm.5), custom_call_target="tpu_custom_call" | custom-call | tf_op jit(solution)/shard_map/prep/pallas_call | solution.py:41
  19.5 2.5 %collective-permute-done.5.refs_2_ = bf16[256,128]{1,0:T(8,128)(2,1)S(1)} collective-permute-done((bf16[256,128]{1,0:T(8,128)(2,1)S(1)}, bf16[256,128]{1,0:T(8,128)(2,1)S(1)}, u32[]{:S(2)}, u32[]{:S(2)}) %collective-permute-start.5) | collective-permute-done | bytes 65568 | tf_op jit(solution)/shard_map/ppermute | solution.py:496
  23.1 1.6 %collective-permute-start.8 = (bf16[272,128]{1,0:T(8,128)(2,1)S(1)}, bf16[272,128]{1,0:T(8,128)(2,1)S(1)}, u32[]{:S(2)}, u32[]{:S(2)}) collective-permute-start(bf16[272,128]{1,0:T(8,128)(2,1)S(1)} %middle.1.refs_0_), channel_id=1, source_target_pairs={{0,20},{4,16},{8,28},{12,24},{16,4},{20,0},{24,12},{28,8},{1,21},{... | collective-permute-start | bytes 208904 | tf_op jit(solution)/shard_map/ppermute | solution.py:496
  25.1 2.6 %collective-permute-done.7.refs_1_ = bf16[272,128]{1,0:T(8,128)(2,1)S(1)} collective-permute-done((bf16[272,128]{1,0:T(8,128)(2,1)S(1)}, bf16[272,128]{1,0:T(8,128)(2,1)S(1)}, u32[]{:S(2)}, u32[]{:S(2)}) %collective-permute-start.7) | collective-permute-done | bytes 69664 | tf_op jit(solution)/shard_map/ppermute | solution.py:496
  27.7 1.3 %collective-permute-done.8.refs_2_ = bf16[272,128]{1,0:T(8,128)(2,1)S(1)} collective-permute-done((bf16[272,128]{1,0:T(8,128)(2,1)S(1)}, bf16[272,128]{1,0:T(8,128)(2,1)S(1)}, u32[]{:S(2)}, u32[]{:S(2)}) %collective-permute-start.8) | collective-permute-done | bytes 69664 | tf_op jit(solution)/shard_map/ppermute | solution.py:496
  29.5 1.3 %collective-permute-done.10.far_ref = bf16[4,272,128]{2,1,0:T(8,128)(2,1)S(1)} collective-permute-done((bf16[4,272,128]{2,1,0:T(8,128)(2,1)S(1)}, bf16[4,272,128]{2,1,0:T(8,128)(2,1)S(1)}, u32[]{:S(2)}, u32[]{:S(2)}) %collective-permute-start.10) | collective-permute-done | bytes 278560 | tf_op jit(solution)/shard_map/ppermute | solution.py:496
  30.9 1.4 %others.3 = (bf16[65,64,128]{2,1,0:T(8,128)(2,1)S(1)}, bf16[272,128]{1,0:T(8,128)(2,1)S(1)}, bf16[272,128]{1,0:T(8,128)(2,1)S(1)}, bf16[272,128]{1,0:T(8,128)(2,1)S(1)}, bf16[16,128]{1,0:T(8,128)(2,1)S(1)}) custom-call(s32[256]{0:T(256)S(1)} %reshape.14.columns_any.columns, ...), custom_call_target="tpu_custom_call", output_to_operand_aliasing={{0}: (4, {})} | custom-call | tf_op jit(solution)/shard_map/others/pallas_call | solution.py:41
  32.2 2.2 %collective-permute-start.11 = (bf16[272,128]{1,0:T(8,128)(2,1)S(1)}, bf16[272,128]{1,0:T(8,128)(2,1)S(1)}, u32[]{:S(2)}, u32[]{:S(2)}) collective-permute-start(bf16[272,128]{1,0:T(8,128)(2,1)S(1)} %get-tuple-element.34), channel_id=1, source_target_pairs={{0,3},{1,2},{2,1},{3,0},{4,7},{5,6},{6,5},{7,4},{8,11},{9,10},{10,... | collective-permute-start | bytes 208904 | tf_op jit(solution)/shard_map/ppermute | solution.py:496
  34.4 2.3 %collective-permute-start.13 = (bf16[272,128]{1,0:T(8,128)(2,1)S(1)}, bf16[272,128]{1,0:T(8,128)(2,1)S(1)}, u32[]{:S(2)}, u32[]{:S(2)}) collective-permute-start(bf16[272,128]{1,0:T(8,128)(2,1)S(1)} %get-tuple-element.36), channel_id=1, source_target_pairs={{0,1},{1,0},{2,3},{3,2},{4,5},{5,4},{6,7},{7,6},{8,9},{9,8},{10,11... | collective-permute-start | bytes 208904 | tf_op jit(solution)/shard_map/ppermute | solution.py:496
  39.2 2.1 %collective-permute-done.12.refs_2_ = bf16[272,128]{1,0:T(8,128)(2,1)S(1)} collective-permute-done((bf16[272,128]{1,0:T(8,128)(2,1)S(1)}, bf16[272,128]{1,0:T(8,128)(2,1)S(1)}, u32[]{:S(2)}, u32[]{:S(2)}) %collective-permute-start.12) | collective-permute-done | bytes 69664 | tf_op jit(solution)/shard_map/ppermute | solution.py:496
  41.8 1.7 %collective-permute-start.14 = (f32[64,128]{1,0:T(8,128)S(1)}, f32[64,128]{1,0:T(8,128)S(1)}, u32[]{:S(2)}, u32[]{:S(2)}) collective-permute-start(f32[64,128]{1,0:T(8,128)S(1)} %get-tuple-element.38.refs_0_), channel_id=1, source_target_pairs={{0,7},{1,6},{2,5},{3,4},{4,3},{5,2},{6,1},{7,0},{8,15},{9,14},{10,... | collective-permute-start | bytes 98312 | tf_op jit(solution)/shard_map/ppermute | solution.py:506
  43.5 2.0 %collective-permute-start.16 = (f32[64,128]{1,0:T(8,128)S(1)}, f32[64,128]{1,0:T(8,128)S(1)}, u32[]{:S(2)}, u32[]{:S(2)}) collective-permute-start(f32[64,128]{1,0:T(8,128)S(1)} %get-tuple-element.38.refs_0_), channel_id=1, source_target_pairs={{0,5},{1,4},{2,7},{3,6},{4,1},{5,0},{6,3},{7,2},{8,13},{9,12},{10,... | collective-permute-start | bytes 98312 | tf_op jit(solution)/shard_map/ppermute | solution.py:506
  45.5 1.6 %collective-permute-done.14.refs_1_ = f32[64,128]{1,0:T(8,128)S(1)} collective-permute-done((f32[64,128]{1,0:T(8,128)S(1)}, f32[64,128]{1,0:T(8,128)S(1)}, u32[]{:S(2)}, u32[]{:S(2)}) %collective-permute-start.14) | collective-permute-done | bytes 32800 | tf_op jit(solution)/shard_map/ppermute | solution.py:506
  47.1 1.5 %collective-permute-done.15.refs_2_ = f32[64,128]{1,0:T(8,128)S(1)} collective-permute-done((f32[64,128]{1,0:T(8,128)S(1)}, f32[64,128]{1,0:T(8,128)S(1)}, u32[]{:S(2)}, u32[]{:S(2)}) %collective-permute-start.15) | collective-permute-done | bytes 32800 | tf_op jit(solution)/shard_map/ppermute | solution.py:506
  48.6 1.5 %collective-permute-start.17 = (f32[32,128]{1,0:T(8,128)S(1)}, f32[32,128]{1,0:T(8,128)S(1)}, u32[]{:S(2)}, u32[]{:S(2)}) collective-permute-start(f32[32,128]{1,0:T(8,128)S(1)} %get-tuple-element.40.refs_0_), channel_id=1, source_target_pairs={{0,28},{4,24},{8,20},{12,16},{16,12},{20,8},{24,4},{28,0},{1,29},{... | collective-permute-start | bytes 49160 | tf_op jit(solution)/shard_map/ppermute | solution.py:496
  51.6 1.5 %first_factor.1.refs_4_.inverse_ref = f32[64,64]{1,0:T(8,128)S(1)} custom-call(f32[32,128]{1,0:T(8,128)S(1)} %get-tuple-element.39.gram_ref), custom_call_target="tpu_custom_call" | custom-call | tf_op jit(solution)/shard_map/first_factor/pallas_call | solution.py:41
  54.1 1.1 %collective-permute-done.20.refs_1_ = f32[32,128]{1,0:T(8,128)S(1)} collective-permute-done((f32[32,128]{1,0:T(8,128)S(1)}, f32[32,128]{1,0:T(8,128)S(1)}, u32[]{:S(2)}, u32[]{:S(2)}) %collective-permute-start.20) | collective-permute-done | bytes 16416 | tf_op jit(solution)/shard_map/ppermute | solution.py:496
  55.2 2.9 %finish.1 = f32[1,8,4096]{2,1,0:T(8,128)} custom-call(f32[256,128]{1,0:T(8,128)S(1)} %get-tuple-element.37.rows_ref, f32[64,64]{1,0:T(8,128)S(1)} %first_factor.1.refs_4_.inverse_ref, f32[32,128]{1,0:T(8,128)S(1)} %add_parts.1.refs_0_, f32[32,128]{1,0:T(8,128)S(1)} %collective-permute-done.20.refs_1_), custom_call_target="tpu_custom_call" | custom-call | tf_op jit(solution)/shard_map/finish/pallas_call | solution.py:41
  (42 shorter events, 12.3 us)
Async XLA Ops:
  1.0 8.7 %copy-start = (s32[4,8,1,8]{3,2,1,0:T(1,128)S(1)}, s32[4,8,1,8]{3,2,1,0:T(1,128)}, u32[]{:S(2)}) copy-start(s32[4,8,1,8]{3,2,1,0:T(1,128)} %param.6) | copy-start | bytes 3076
  1.0 8.7 %copy-start.1 = (s32[4,8,1]{1,2,0:T(1,128)S(1)}, s32[4,8,1]{1,2,0:T(1,128)}, u32[]{:S(2)}) copy-start(s32[4,8,1]{1,2,0:T(1,128)} %param.7) | copy-start | bytes 388
  1.0 6.5 %collective-permute-start = (bf16[256,128]{1,0:T(8,128)(2,1)S(1)}, bf16[256,128]{1,0:T(8,128)(2,1)S(1)}, u32[]{:S(2)}, u32[]{:S(2)}) collective-permute-start(bf16[256,128]{1,0:T(8,128)(2,1)S(1)} %get-tuple-element.27.refs_0_), channel_id=1, source_target_pairs={{0,28},{4,24},{8,20},{12,16},{16,12},{20,8},{24,4},{28,0},{1,29},{... | collective-permute-start | bytes 196616 | tf_op jit(solution)/shard_map/ppermute | solution.py:496
  4.4 3.9 %collective-permute-start.1 = (bf16[256,128]{1,0:T(8,128)(2,1)S(1)}, bf16[256,128]{1,0:T(8,128)(2,1)S(1)}, u32[]{:S(2)}, u32[]{:S(2)}) collective-permute-start(bf16[256,128]{1,0:T(8,128)(2,1)S(1)} %get-tuple-element.27.refs_0_), channel_id=1, source_target_pairs={{0,20},{4,16},{8,28},{12,24},{16,4},{20,0},{24,12},{28,8},{1,21},{... | collective-permute-start | bytes 196616 | tf_op jit(solution)/shard_map/ppermute | solution.py:496
  5.2 4.3 %collective-permute-start.2 = (bf16[256,128]{1,0:T(8,128)(2,1)S(1)}, bf16[256,128]{1,0:T(8,128)(2,1)S(1)}, u32[]{:S(2)}, u32[]{:S(2)}) collective-permute-start(bf16[256,128]{1,0:T(8,128)(2,1)S(1)} %get-tuple-element.27.refs_0_), channel_id=1, source_target_pairs={{0,12},{4,8},{8,4},{12,0},{16,28},{20,24},{24,20},{28,16},{1,13},{... | collective-permute-start | bytes 196616 | tf_op jit(solution)/shard_map/ppermute | solution.py:496
  9.6 1.6 %collective-permute-start.3 = (bf16[4,256,128]{2,1,0:T(8,128)(2,1)S(1)}, bf16[4,256,128]{2,1,0:T(8,128)(2,1)S(1)}, u32[]{:S(2)}, u32[]{:S(2)}) collective-permute-start(bf16[4,256,128]{2,1,0:T(8,128)(2,1)S(1)} %stack.2.near_ref), channel_id=1, source_target_pairs={{0,4},{4,0},{8,12},{12,8},{16,20},{20,16},{24,28},{28,24},{1,5},{5... | collective-permute-start | bytes 786440 | tf_op jit(solution)/shard_map/ppermute | solution.py:496
  12.5 7.0 %collective-permute-start.4 = (bf16[256,128]{1,0:T(8,128)(2,1)S(1)}, bf16[256,128]{1,0:T(8,128)(2,1)S(1)}, u32[]{:S(2)}, u32[]{:S(2)}) collective-permute-start(bf16[256,128]{1,0:T(8,128)(2,1)S(1)} %get-tuple-element.29), channel_id=1, source_target_pairs={{0,3},{1,2},{2,1},{3,0},{4,7},{5,6},{6,5},{7,4},{8,11},{9,10},{10,... | collective-permute-start | bytes 196616 | tf_op jit(solution)/shard_map/ppermute | solution.py:496
  16.2 5.9 %collective-permute-start.5 = (bf16[256,128]{1,0:T(8,128)(2,1)S(1)}, bf16[256,128]{1,0:T(8,128)(2,1)S(1)}, u32[]{:S(2)}, u32[]{:S(2)}) collective-permute-start(bf16[256,128]{1,0:T(8,128)(2,1)S(1)} %get-tuple-element.30), channel_id=1, source_target_pairs={{0,2},{1,3},{2,0},{3,1},{4,6},{5,7},{6,4},{7,5},{8,10},{9,11},{10,... | collective-permute-start | bytes 196616 | tf_op jit(solution)/shard_map/ppermute | solution.py:496
  16.2 5.9 %collective-permute-start.6 = (bf16[256,128]{1,0:T(8,128)(2,1)S(1)}, bf16[256,128]{1,0:T(8,128)(2,1)S(1)}, u32[]{:S(2)}, u32[]{:S(2)}) collective-permute-start(bf16[256,128]{1,0:T(8,128)(2,1)S(1)} %get-tuple-element.31), channel_id=1, source_target_pairs={{0,1},{1,0},{2,3},{3,2},{4,5},{5,4},{6,7},{7,6},{8,9},{9,8},{10,11... | collective-permute-start | bytes 196616 | tf_op jit(solution)/shard_map/ppermute | solution.py:496
  22.3 5.4 %collective-permute-start.7 = (bf16[272,128]{1,0:T(8,128)(2,1)S(1)}, bf16[272,128]{1,0:T(8,128)(2,1)S(1)}, u32[]{:S(2)}, u32[]{:S(2)}) collective-permute-start(bf16[272,128]{1,0:T(8,128)(2,1)S(1)} %middle.1.refs_0_), channel_id=1, source_target_pairs={{0,28},{4,24},{8,20},{12,16},{16,12},{20,8},{24,4},{28,0},{1,29},{... | collective-permute-start | bytes 208904 | tf_op jit(solution)/shard_map/ppermute | solution.py:496
  23.1 5.8 %collective-permute-start.8 = (bf16[272,128]{1,0:T(8,128)(2,1)S(1)}, bf16[272,128]{1,0:T(8,128)(2,1)S(1)}, u32[]{:S(2)}, u32[]{:S(2)}) collective-permute-start(bf16[272,128]{1,0:T(8,128)(2,1)S(1)} %middle.1.refs_0_), channel_id=1, source_target_pairs={{0,20},{4,16},{8,28},{12,24},{16,4},{20,0},{24,12},{28,8},{1,21},{... | collective-permute-start | bytes 208904 | tf_op jit(solution)/shard_map/ppermute | solution.py:496
  24.8 4.4 %collective-permute-start.9 = (bf16[272,128]{1,0:T(8,128)(2,1)S(1)}, bf16[272,128]{1,0:T(8,128)(2,1)S(1)}, u32[]{:S(2)}, u32[]{:S(2)}) collective-permute-start(bf16[272,128]{1,0:T(8,128)(2,1)S(1)} %middle.1.refs_0_), channel_id=1, source_target_pairs={{0,12},{4,8},{8,4},{12,0},{16,28},{20,24},{24,20},{28,16},{1,13},{... | collective-permute-start | bytes 208904 | tf_op jit(solution)/shard_map/ppermute | solution.py:496
  29.2 1.6 %collective-permute-start.10 = (bf16[4,272,128]{2,1,0:T(8,128)(2,1)S(1)}, bf16[4,272,128]{2,1,0:T(8,128)(2,1)S(1)}, u32[]{:S(2)}, u32[]{:S(2)}) collective-permute-start(bf16[4,272,128]{2,1,0:T(8,128)(2,1)S(1)} %stack.3.near_ref), channel_id=1, source_target_pairs={{0,4},{4,0},{8,12},{12,8},{16,20},{20,16},{24,28},{28,24},{1,5},{5... | collective-permute-start | bytes 835592 | tf_op jit(solution)/shard_map/ppermute | solution.py:496
  32.2 6.9 %collective-permute-start.11 = (bf16[272,128]{1,0:T(8,128)(2,1)S(1)}, bf16[272,128]{1,0:T(8,128)(2,1)S(1)}, u32[]{:S(2)}, u32[]{:S(2)}) collective-permute-start(bf16[272,128]{1,0:T(8,128)(2,1)S(1)} %get-tuple-element.34), channel_id=1, source_target_pairs={{0,3},{1,2},{2,1},{3,0},{4,7},{5,6},{6,5},{7,4},{8,11},{9,10},{10,... | collective-permute-start | bytes 208904 | tf_op jit(solution)/shard_map/ppermute | solution.py:496
  34.4 6.9 %collective-permute-start.12 = (bf16[272,128]{1,0:T(8,128)(2,1)S(1)}, bf16[272,128]{1,0:T(8,128)(2,1)S(1)}, u32[]{:S(2)}, u32[]{:S(2)}) collective-permute-start(bf16[272,128]{1,0:T(8,128)(2,1)S(1)} %get-tuple-element.35), channel_id=1, source_target_pairs={{0,2},{1,3},{2,0},{3,1},{4,6},{5,7},{6,4},{7,5},{8,10},{9,11},{10,... | collective-permute-start | bytes 208904 | tf_op jit(solution)/shard_map/ppermute | solution.py:496
  34.4 6.9 %collective-permute-start.13 = (bf16[272,128]{1,0:T(8,128)(2,1)S(1)}, bf16[272,128]{1,0:T(8,128)(2,1)S(1)}, u32[]{:S(2)}, u32[]{:S(2)}) collective-permute-start(bf16[272,128]{1,0:T(8,128)(2,1)S(1)} %get-tuple-element.36), channel_id=1, source_target_pairs={{0,1},{1,0},{2,3},{3,2},{4,5},{5,4},{6,7},{7,6},{8,9},{9,8},{10,11... | collective-permute-start | bytes 208904 | tf_op jit(solution)/shard_map/ppermute | solution.py:496
  41.8 5.3 %collective-permute-start.14 = (f32[64,128]{1,0:T(8,128)S(1)}, f32[64,128]{1,0:T(8,128)S(1)}, u32[]{:S(2)}, u32[]{:S(2)}) collective-permute-start(f32[64,128]{1,0:T(8,128)S(1)} %get-tuple-element.38.refs_0_), channel_id=1, source_target_pairs={{0,7},{1,6},{2,5},{3,4},{4,3},{5,2},{6,1},{7,0},{8,15},{9,14},{10,... | collective-permute-start | bytes 98312 | tf_op jit(solution)/shard_map/ppermute | solution.py:506
  43.5 5.1 %collective-permute-start.15 = (f32[64,128]{1,0:T(8,128)S(1)}, f32[64,128]{1,0:T(8,128)S(1)}, u32[]{:S(2)}, u32[]{:S(2)}) collective-permute-start(f32[64,128]{1,0:T(8,128)S(1)} %get-tuple-element.38.refs_0_), channel_id=1, source_target_pairs={{0,6},{1,7},{2,4},{3,5},{4,2},{5,3},{6,0},{7,1},{8,14},{9,15},{10,... | collective-permute-start | bytes 98312 | tf_op jit(solution)/shard_map/ppermute | solution.py:506
  43.5 5.1 %collective-permute-start.16 = (f32[64,128]{1,0:T(8,128)S(1)}, f32[64,128]{1,0:T(8,128)S(1)}, u32[]{:S(2)}, u32[]{:S(2)}) collective-permute-start(f32[64,128]{1,0:T(8,128)S(1)} %get-tuple-element.38.refs_0_), channel_id=1, source_target_pairs={{0,5},{1,4},{2,7},{3,6},{4,1},{5,0},{6,3},{7,2},{8,13},{9,12},{10,... | collective-permute-start | bytes 98312 | tf_op jit(solution)/shard_map/ppermute | solution.py:506
  48.6 4.5 %collective-permute-start.17 = (f32[32,128]{1,0:T(8,128)S(1)}, f32[32,128]{1,0:T(8,128)S(1)}, u32[]{:S(2)}, u32[]{:S(2)}) collective-permute-start(f32[32,128]{1,0:T(8,128)S(1)} %get-tuple-element.40.refs_0_), channel_id=1, source_target_pairs={{0,28},{4,24},{8,20},{12,16},{16,12},{20,8},{24,4},{28,0},{1,29},{... | collective-permute-start | bytes 49160 | tf_op jit(solution)/shard_map/ppermute | solution.py:496
  50.1 3.2 %collective-permute-start.18 = (f32[32,128]{1,0:T(8,128)S(1)}, f32[32,128]{1,0:T(8,128)S(1)}, u32[]{:S(2)}, u32[]{:S(2)}) collective-permute-start(f32[32,128]{1,0:T(8,128)S(1)} %get-tuple-element.40.refs_0_), channel_id=1, source_target_pairs={{0,20},{4,16},{8,28},{12,24},{16,4},{20,0},{24,12},{28,8},{1,21},{... | collective-permute-start | bytes 49160 | tf_op jit(solution)/shard_map/ppermute | solution.py:496
  50.9 3.2 %collective-permute-start.19 = (f32[32,128]{1,0:T(8,128)S(1)}, f32[32,128]{1,0:T(8,128)S(1)}, u32[]{:S(2)}, u32[]{:S(2)}) collective-permute-start(f32[32,128]{1,0:T(8,128)S(1)} %get-tuple-element.40.refs_0_), channel_id=1, source_target_pairs={{0,12},{4,8},{8,4},{12,0},{16,28},{20,24},{24,20},{28,16},{1,13},{... | collective-permute-start | bytes 49160 | tf_op jit(solution)/shard_map/ppermute | solution.py:496
  54.0 1.2 %collective-permute-start.20 = (f32[32,128]{1,0:T(8,128)S(1)}, f32[32,128]{1,0:T(8,128)S(1)}, u32[]{:S(2)}, u32[]{:S(2)}) collective-permute-start(f32[32,128]{1,0:T(8,128)S(1)} %add_parts.1.refs_0_), channel_id=1, source_target_pairs={{0,4},{4,0},{8,12},{12,8},{16,20},{20,16},{24,28},{28,24},{1,5},{5... | collective-permute-start | bytes 49160 | tf_op jit(solution)/shard_map/ppermute | solution.py:496

commit v10 on v9

--- a/solution.py
+++ b/solution.py
@@ -170,31 +170,33 @@
     )
 
 
-def fill_table(pieces_ref, offsets, table):
+def fill_table(stacks, offsets, table):
     block_rows = (table.shape[0] - 1) // (2 * len(offsets))
     low = iota((32, 128), 1) < 64
-    for index, offset in enumerate(offsets):
+    pieces = [(ref, index) for ref in stacks for index in range(ref.shape[0])]
+    for (ref, index), offset in zip(pieces, offsets):
         base = (lax.axis_index("rows") ^ offset) * block_rows
         for i in range(block_rows):
-            block = pieces_ref[index, i * 32 : (i + 1) * 32, :]
+            block = ref[index, i * 32 : (i + 1) * 32, :]
             turned = jnp.concatenate([block[:, 64:], block[:, :64]], axis=1)
             table[base + i, :32] = jnp.where(low, block, turned)
             table[base + i, 32:] = jnp.where(low, turned, block)
 
 
-def near_kernel(offsets, near_ref, table):
+def near_kernel(offsets, *refs):
+    *near_refs, table = refs
     table[table.shape[0] - 1] = jnp.zeros(table.shape[1:], BF16)
-    fill_table(near_ref, offsets, table)
+    fill_table(near_refs, offsets, table)
 
 
 def near_table(offsets, near, block_rows):
-    count = near.shape[0]
+    count = len(offsets) // 2
     return call(
         functools.partial(near_kernel, offsets[:count]),
         "near",
-        [vmem()],
+        [vmem()] * len(near),
         shaped((2 * count * block_rows + 1, 64, 128), BF16),
-        (near,),
+        near,
     )
 
 
@@ -215,16 +217,17 @@
     return largest
 
 
-def others_kernel(offsets, ranges, columns_any, matrix_ref, far_ref, near_ref, old_table, table, *refs):
+def others_kernel(offsets, ranges, stacks, old_table, columns_any, matrix_ref, *refs):
     del old_table
-    *outs, columns, sem = refs
+    far_refs, near_refs = refs[:stacks], refs[stacks : 2 * stacks]
+    table, *outs, columns, sem = refs[2 * stacks :]
     copy = pltpu.make_async_copy(columns_any, columns, sem)
     copy.start()
-    fill_table(far_ref, offsets, table)
+    fill_table(far_refs, offsets, table)
     terms, first = outs[: len(ranges)], matrix_ref.shape[1] * 32
     if len(outs) > len(ranges):
         notes = largest_notes(
-            [ref[index, first:] for ref in (near_ref, far_ref) for index in range(len(offsets))]
+            [ref[index, first:] for ref in near_refs + far_refs for index in range(ref.shape[0])]
         ).astype(BF16)
         for ref in outs[len(ranges) :]:
             ref[...] = notes
@@ -241,20 +244,20 @@
 
 
 def products(offsets, ranges, columns, matrix, own_matrix, near, far, table):
-    block_rows, count = matrix.shape[1], near.shape[0]
-    extra = near.shape[1] > block_rows * 32
+    block_rows, count = matrix.shape[1], len(offsets) // 2
+    extra = near[0].shape[1] > block_rows * 32
     rows = block_rows * 32
     outs = [shaped(table.shape, BF16)] + [shaped((rows + 16 * extra, 128), BF16)] * len(ranges)
     if extra:
         outs.append(shaped((16, 128), BF16))
     table, *outs = call(
-        functools.partial(others_kernel, offsets[count:], ranges),
+        functools.partial(others_kernel, offsets[count:], ranges, len(near)),
         "others",
-        [pl.BlockSpec(memory_space=pl.ANY)] + [vmem()] * 4,
+        [vmem(), pl.BlockSpec(memory_space=pl.ANY)] + [vmem()] * (1 + 2 * len(near)),
         outs,
-        (columns, matrix, far, near, table),
+        (table, columns, matrix, *far, *near),
         [pltpu.SMEM(columns.shape, jnp.int32), pltpu.SemaphoreType.DMA],
-        input_output_aliases={4: 0},
+        input_output_aliases={0: 0},
     )
     terms = [swap(term, "cols", m) for m, term in zip(ranges, outs)]
     own = call(
@@ -308,36 +311,36 @@
     )
 
 
-def row_gram_kernel(near_ref, far_ref, gram_ref, rows):
+def row_gram_kernel(*refs):
+    *stacks, gram_ref, rows = refs
     lane = iota((32, 128), 1)
     pair = lane % 64 // 2 == iota((32, 128), 0)
     spread = (iota((128, 128), 0) % 2 == iota((128, 128), 1) // 64).astype(BF16)
-    count = near_ref.shape[1] - 16
-    size = near_ref.shape[0]
-    for index in range(2 * size):
-        ref = (near_ref, far_ref)[index // size]
-        notes = ref[index % size, count:].astype(F32)
+    count = stacks[0].shape[1] - 16
+    pieces = [(ref, index) for ref in stacks for index in range(ref.shape[0])]
+    for place, (ref, index) in enumerate(pieces):
+        notes = ref[index, count:].astype(F32)
         masked = [
             jnp.where(pair, jnp.broadcast_to(notes[i : i + 1], (32, 128)), 0.0).astype(BF16)
             for i in range(count // 32)
         ]
         inverse = jnp.dot(jnp.concatenate(masked, axis=0), spread, preferred_element_type=F32)
-        block = ref[index % size, :count].astype(F32) * inverse
-        rows[index * count : (index + 1) * count, :] = block.astype(BF16)
+        block = ref[index, :count].astype(F32) * inverse
+        rows[place * count : (place + 1) * count, :] = block.astype(BF16)
     both = lax.dot_general(
         rows[...], rows[...], (((0,), (0,)), ((), ())), preferred_element_type=F32
     )
     gram_ref[...] = folded(both)
 
 
-def row_gram(near, far):
-    count = 2 * near.shape[0] * (near.shape[1] - 16)
+def row_gram(stacks):
+    count = sum(stack.shape[0] for stack in stacks) * (stacks[0].shape[1] - 16)
     return call(
         row_gram_kernel,
         "row_gram",
-        [vmem(), vmem()],
+        [vmem()] * len(stacks),
         shaped((32, 128), F32),
-        (near, far),
+        stacks,
         [pltpu.VMEM((count, 128), BF16)],
     )
 
@@ -522,10 +525,12 @@
     for masks in plan[:-1]:
         held = held + [swap(piece, "rows", mask) for mask in masks for piece in held]
         offsets = offsets + [mask ^ offset for mask in masks for offset in offsets]
-    near = stack(held, after)
+    split = len(held) // 2
+    held, offsets = held[split:] + held[:split], offsets[split:] + offsets[:split]
+    near = [stack(held[:split], []), stack(held[split:], after)]
     (last,) = plan[-1]
     offsets = offsets + [last ^ offset for offset in offsets]
-    return near, swap(near, "rows", last), offsets
+    return near, [swap(pieces, "rows", last) for pieces in near], offsets
 
 
 def add_rows(gram, after):
@@ -558,7 +563,7 @@
     table = near_table(offsets, near, block_rows)
     terms, (notes,) = products(offsets, ranges, columns, matrix, own_matrix, near, far, table)
     devices = float(groups * ranks)
-    rows, grams = collect(devices, total, degree, row_gram(near, far), notes, terms)
+    rows, grams = collect(devices, total, degree, row_gram(near + far), notes, terms)
     flip = 1 if ranks == 8 else 0
     gram, first = add_columns(total, [grams] + [swap_both(grams, flip, m) for m in ranges])
     inverse = first_factor(first)

time: 58.3 us -> 57.9 us (level)
  waiting for transfers between devices: 19.2 us -> 18.6 us
    ppermute x18 -> x20, waiting for transfers between devices: 16.1 us -> 15.5 us  [swap(): lax.ppermute(value, axis, [(index, index ^ mask) for index in range(size)])]
    ppermute x18 -> x20, starting transfers between devices: 19.5 us -> 19.6 us  [swap(): lax.ppermute(value, axis, [(index, index ^ mask) for index in range(size)])]
    pallas_call x18 -> x20, Pallas kernels: 15.3 us -> 15.3 us  [call(): pl.pallas_call(kernel, out_shape=outs, in_specs=ins, out_specs=jax.tree.m...]
  transfers between devices with their start and end apart: 21 -> 23, of which waited for: 15 -> 15; matrix products, arithmetic and copies ran while one was open for 0% -> 0% of each run, Pallas kernels for 14% -> 14%
where the time goes in v10:
time: 57.9 us; the launch traced here: 57.7 us
  starting transfers between devices  23.4 us (40%)
  waiting for transfers between devices  18.6 us (32%)
  Pallas kernels  15.3 us (26%)
    ppermute x20, starting transfers between devices, swap(): lax.ppermute(value, axis, [(index, index ^ mask) for index in range(size)])  19.6 us
    ppermute x20, waiting for transfers between devices, swap(): lax.ppermute(value, axis, [(index, index ^ mask) for index in range(size)])  15.5 us
    pallas_call x20, Pallas kernels, call(): pl.pallas_call(kernel, out_shape=outs, in_specs=ins, out_specs=jax.tree.m...  15.3 us
    ppermute x3, starting transfers between devices, swap_both(): return lax.ppermute(value, ('rows', 'cols'), pairs)  3.75 us
    ppermute x3, waiting for transfers between devices, swap_both(): return lax.ppermute(value, ('rows', 'cols'), pairs)  3.1 us
  transfers between devices with their start and end apart: 23, of which 15 were waited for; matrix products, arithmetic and copies ran while one was open for 0% of the time, Pallas kernels for 14%

profile of v10, /device:TPU:0, one launch (start us, length us, event | category | flops | bytes accessed | tf_op | source)
XLA Modules:
  0.0 57.7 jit_solution(7955718662890217907)
XLA Ops:
  0.0 1.0 %start.1 = (bf16[256,128]{1,0:T(8,128)(2,1)S(1)}, f32[256,128]{1,0:T(8,128)S(1)}) custom-call(f32[1,8,4096]{2,1,0:T(8,128)} %panel_hbm.1, f32[1,8,64]{2,1,0:T(8,128)} %inv_hbm.5), custom_call_target="tpu_custom_call" | custom-call | tf_op jit(solution)/shard_map/start/pallas_call | solution.py:41
  1.0 3.4 %collective-permute-start.2 = (bf16[256,128]{1,0:T(8,128)(2,1)S(1)}, bf16[256,128]{1,0:T(8,128)(2,1)S(1)}, u32[]{:S(2)}, u32[]{:S(2)}) collective-permute-start(bf16[256,128]{1,0:T(8,128)(2,1)S(1)} %get-tuple-element.26.refs_0_), channel_id=1, source_target_pairs={{0,28},{4,24},{8,20},{12,16},{16,12},{20,8},{24,4},{28,0},{1,29},{... | collective-permute-start | bytes 196616 | tf_op jit(solution)/shard_map/ppermute | solution.py:499
  5.4 2.2 %prep.2 = (bf16[3,8,64,512]{3,2,1,0:T(8,128)(2,1)S(1)}, f32[8,128]{1,0:T(8,128)S(1)}) custom-call(bf16[4,8,1,8,4096]{4,3,2,1,0:T(8,128)(2,1)} %affinity_hbm.3, f32[1,8,64]{2,1,0:T(8,128)} %inv_hbm.5), custom_call_target="tpu_custom_call" | custom-call | tf_op jit(solution)/shard_map/prep/pallas_call | solution.py:41
  8.3 1.2 %collective-permute-done.1.refs_1_ = bf16[256,128]{1,0:T(8,128)(2,1)S(1)} collective-permute-done((bf16[256,128]{1,0:T(8,128)(2,1)S(1)}, bf16[256,128]{1,0:T(8,128)(2,1)S(1)}, u32[]{:S(2)}, u32[]{:S(2)}) %collective-permute-start.1) | collective-permute-done | bytes 65568 | tf_op jit(solution)/shard_map/ppermute | solution.py:499
  11.0 1.3 %others.2 = (bf16[65,64,128]{2,1,0:T(8,128)(2,1)S(1)}, bf16[256,128]{1,0:T(8,128)(2,1)S(1)}, bf16[256,128]{1,0:T(8,128)(2,1)S(1)}, bf16[256,128]{1,0:T(8,128)(2,1)S(1)}) custom-call(bf16[65,64,128]{2,1,0:T(8,128)(2,1)S(1)} %near.2.old_table, s32[256]{0:T(256)S(1)} %reshape.14.columns_any.columns, ...), custom_call_target="tpu_custom_call", output_to_operand_aliasing={{0}: (0, {})} | custom-call | tf_op jit(solution)/shard_map/others/pallas_call | solution.py:41
  12.3 3.7 %collective-permute-start.5 = (bf16[256,128]{1,0:T(8,128)(2,1)S(1)}, bf16[256,128]{1,0:T(8,128)(2,1)S(1)}, u32[]{:S(2)}, u32[]{:S(2)}) collective-permute-start(bf16[256,128]{1,0:T(8,128)(2,1)S(1)} %get-tuple-element.29), channel_id=1, source_target_pairs={{0,3},{1,2},{2,1},{3,0},{4,7},{5,6},{6,5},{7,4},{8,11},{9,10},{10,... | collective-permute-start | bytes 196616 | tf_op jit(solution)/shard_map/ppermute | solution.py:499
  16.8 1.7 %prep.3 = (bf16[1,8,64,512]{3,2,1,0:T(8,128)(2,1)S(1)}, f32[8,128]{1,0:T(8,128)}) custom-call(bf16[4,8,1,8,4096]{4,3,2,1,0:T(8,128)(2,1)} %affinity_hbm.3, f32[1,8,64]{2,1,0:T(8,128)} %inv_hbm.5), custom_call_target="tpu_custom_call" | custom-call | tf_op jit(solution)/shard_map/prep/pallas_call | solution.py:41
  19.3 2.5 %collective-permute-done.6.refs_2_ = bf16[256,128]{1,0:T(8,128)(2,1)S(1)} collective-permute-done((bf16[256,128]{1,0:T(8,128)(2,1)S(1)}, bf16[256,128]{1,0:T(8,128)(2,1)S(1)}, u32[]{:S(2)}, u32[]{:S(2)}) %collective-permute-start.6) | collective-permute-done | bytes 65568 | tf_op jit(solution)/shard_map/ppermute | solution.py:499
  23.0 1.6 %collective-permute-start.8 = (bf16[272,128]{1,0:T(8,128)(2,1)S(1)}, bf16[272,128]{1,0:T(8,128)(2,1)S(1)}, u32[]{:S(2)}, u32[]{:S(2)}) collective-permute-start(bf16[272,128]{1,0:T(8,128)(2,1)S(1)} %middle.1.refs_0_), channel_id=1, source_target_pairs={{0,20},{4,16},{8,28},{12,24},{16,4},{20,0},{24,12},{28,8},{1,21},{... | collective-permute-start | bytes 208904 | tf_op jit(solution)/shard_map/ppermute | solution.py:499
  24.9 2.6 %collective-permute-done.10.refs_1_ = bf16[272,128]{1,0:T(8,128)(2,1)S(1)} collective-permute-done((bf16[272,128]{1,0:T(8,128)(2,1)S(1)}, bf16[272,128]{1,0:T(8,128)(2,1)S(1)}, u32[]{:S(2)}, u32[]{:S(2)}) %collective-permute-start.10) | collective-permute-done | bytes 69664 | tf_op jit(solution)/shard_map/ppermute | solution.py:499
  27.6 1.2 %collective-permute-done.8.refs_0_ = bf16[272,128]{1,0:T(8,128)(2,1)S(1)} collective-permute-done((bf16[272,128]{1,0:T(8,128)(2,1)S(1)}, bf16[272,128]{1,0:T(8,128)(2,1)S(1)}, u32[]{:S(2)}, u32[]{:S(2)}) %collective-permute-start.8) | collective-permute-done | bytes 69664 | tf_op jit(solution)/shard_map/ppermute | solution.py:499
  29.3 1.1 %collective-permute-done.11.refs_2_.refs_0_ = bf16[2,272,128]{2,1,0:T(8,128)(2,1)S(1)} collective-permute-done((bf16[2,272,128]{2,1,0:T(8,128)(2,1)S(1)}, bf16[2,272,128]{2,1,0:T(8,128)(2,1)S(1)}, u32[]{:S(2)}, u32[]{:S(2)}) %collective-permute-start.11) | collective-permute-done | bytes 139296 | tf_op jit(solution)/shard_map/ppermute | solution.py:499
  30.5 1.4 %others.3 = (bf16[65,64,128]{2,1,0:T(8,128)(2,1)S(1)}, bf16[272,128]{1,0:T(8,128)(2,1)S(1)}, bf16[272,128]{1,0:T(8,128)(2,1)S(1)}, bf16[272,128]{1,0:T(8,128)(2,1)S(1)}, bf16[16,128]{1,0:T(8,128)(2,1)S(1)}) custom-call(bf16[65,64,128]{2,1,0:T(8,128)(2,1)S(1)} %near.3.old_table, s32[256]{0:T(256)S(1)} %reshape.14.columns_any.columns, ...), custom_call_target="tpu_custom_call", output_to_operand_aliasing={{0}: (0, {})} | custom-call | tf_op jit(solution)/shard_map/others/pallas_call | solution.py:41
  31.8 2.1 %collective-permute-start.13 = (bf16[272,128]{1,0:T(8,128)(2,1)S(1)}, bf16[272,128]{1,0:T(8,128)(2,1)S(1)}, u32[]{:S(2)}, u32[]{:S(2)}) collective-permute-start(bf16[272,128]{1,0:T(8,128)(2,1)S(1)} %get-tuple-element.34), channel_id=1, source_target_pairs={{0,3},{1,2},{2,1},{3,0},{4,7},{5,6},{6,5},{7,4},{8,11},{9,10},{10,... | collective-permute-start | bytes 208904 | tf_op jit(solution)/shard_map/ppermute | solution.py:499
  34.0 2.3 %collective-permute-start.15 = (bf16[272,128]{1,0:T(8,128)(2,1)S(1)}, bf16[272,128]{1,0:T(8,128)(2,1)S(1)}, u32[]{:S(2)}, u32[]{:S(2)}) collective-permute-start(bf16[272,128]{1,0:T(8,128)(2,1)S(1)} %get-tuple-element.36), channel_id=1, source_target_pairs={{0,1},{1,0},{2,3},{3,2},{4,5},{5,4},{6,7},{7,6},{8,9},{9,8},{10,11... | collective-permute-start | bytes 208904 | tf_op jit(solution)/shard_map/ppermute | solution.py:499
  38.8 2.1 %collective-permute-done.14.refs_2_ = bf16[272,128]{1,0:T(8,128)(2,1)S(1)} collective-permute-done((bf16[272,128]{1,0:T(8,128)(2,1)S(1)}, bf16[272,128]{1,0:T(8,128)(2,1)S(1)}, u32[]{:S(2)}, u32[]{:S(2)}) %collective-permute-start.14) | collective-permute-done | bytes 69664 | tf_op jit(solution)/shard_map/ppermute | solution.py:499
  41.4 1.7 %collective-permute-start.16 = (f32[64,128]{1,0:T(8,128)S(1)}, f32[64,128]{1,0:T(8,128)S(1)}, u32[]{:S(2)}, u32[]{:S(2)}) collective-permute-start(f32[64,128]{1,0:T(8,128)S(1)} %get-tuple-element.38.refs_0_), channel_id=1, source_target_pairs={{0,7},{1,6},{2,5},{3,4},{4,3},{5,2},{6,1},{7,0},{8,15},{9,14},{10,... | collective-permute-start | bytes 98312 | tf_op jit(solution)/shard_map/ppermute | solution.py:509
  43.1 2.0 %collective-permute-start.18 = (f32[64,128]{1,0:T(8,128)S(1)}, f32[64,128]{1,0:T(8,128)S(1)}, u32[]{:S(2)}, u32[]{:S(2)}) collective-permute-start(f32[64,128]{1,0:T(8,128)S(1)} %get-tuple-element.38.refs_0_), channel_id=1, source_target_pairs={{0,5},{1,4},{2,7},{3,6},{4,1},{5,0},{6,3},{7,2},{8,13},{9,12},{10,... | collective-permute-start | bytes 98312 | tf_op jit(solution)/shard_map/ppermute | solution.py:509
  45.1 1.6 %collective-permute-done.16.refs_1_ = f32[64,128]{1,0:T(8,128)S(1)} collective-permute-done((f32[64,128]{1,0:T(8,128)S(1)}, f32[64,128]{1,0:T(8,128)S(1)}, u32[]{:S(2)}, u32[]{:S(2)}) %collective-permute-start.16) | collective-permute-done | bytes 32800 | tf_op jit(solution)/shard_map/ppermute | solution.py:509
  46.7 1.5 %collective-permute-done.17.refs_2_ = f32[64,128]{1,0:T(8,128)S(1)} collective-permute-done((f32[64,128]{1,0:T(8,128)S(1)}, f32[64,128]{1,0:T(8,128)S(1)}, u32[]{:S(2)}, u32[]{:S(2)}) %collective-permute-start.17) | collective-permute-done | bytes 32800 | tf_op jit(solution)/shard_map/ppermute | solution.py:509
  48.3 1.4 %collective-permute-start.19 = (f32[32,128]{1,0:T(8,128)S(1)}, f32[32,128]{1,0:T(8,128)S(1)}, u32[]{:S(2)}, u32[]{:S(2)}) collective-permute-start(f32[32,128]{1,0:T(8,128)S(1)} %get-tuple-element.40.refs_0_), channel_id=1, source_target_pairs={{0,28},{4,24},{8,20},{12,16},{16,12},{20,8},{24,4},{28,0},{1,29},{... | collective-permute-start | bytes 49160 | tf_op jit(solution)/shard_map/ppermute | solution.py:499
  51.3 1.5 %first_factor.1.refs_4_.inverse_ref = f32[64,64]{1,0:T(8,128)S(1)} custom-call(f32[32,128]{1,0:T(8,128)S(1)} %get-tuple-element.39.gram_ref), custom_call_target="tpu_custom_call" | custom-call | tf_op jit(solution)/shard_map/first_factor/pallas_call | solution.py:41
  53.8 1.1 %collective-permute-done.22.refs_1_ = f32[32,128]{1,0:T(8,128)S(1)} collective-permute-done((f32[32,128]{1,0:T(8,128)S(1)}, f32[32,128]{1,0:T(8,128)S(1)}, u32[]{:S(2)}, u32[]{:S(2)}) %collective-permute-start.22) | collective-permute-done | bytes 16416 | tf_op jit(solution)/shard_map/ppermute | solution.py:499
  54.9 2.9 %finish.1 = f32[1,8,4096]{2,1,0:T(8,128)} custom-call(f32[256,128]{1,0:T(8,128)S(1)} %get-tuple-element.37.rows_ref, f32[64,64]{1,0:T(8,128)S(1)} %first_factor.1.refs_4_.inverse_ref, f32[32,128]{1,0:T(8,128)S(1)} %add_parts.1.refs_0_, f32[32,128]{1,0:T(8,128)S(1)} %collective-permute-done.22.refs_1_), custom_call_target="tpu_custom_call" | custom-call | tf_op jit(solution)/shard_map/finish/pallas_call | solution.py:41
  (48 shorter events, 12.4 us)
Async XLA Ops:
  1.0 8.7 %copy-start = (s32[4,8,1,8]{3,2,1,0:T(1,128)S(1)}, s32[4,8,1,8]{3,2,1,0:T(1,128)}, u32[]{:S(2)}) copy-start(s32[4,8,1,8]{3,2,1,0:T(1,128)} %param.6) | copy-start | bytes 3076
  1.0 6.5 %collective-permute-start.2 = (bf16[256,128]{1,0:T(8,128)(2,1)S(1)}, bf16[256,128]{1,0:T(8,128)(2,1)S(1)}, u32[]{:S(2)}, u32[]{:S(2)}) collective-permute-start(bf16[256,128]{1,0:T(8,128)(2,1)S(1)} %get-tuple-element.26.refs_0_), channel_id=1, source_target_pairs={{0,28},{4,24},{8,20},{12,16},{16,12},{20,8},{24,4},{28,0},{1,29},{... | collective-permute-start | bytes 196616 | tf_op jit(solution)/shard_map/ppermute | solution.py:499
  4.4 3.9 %collective-permute-start = (bf16[256,128]{1,0:T(8,128)(2,1)S(1)}, bf16[256,128]{1,0:T(8,128)(2,1)S(1)}, u32[]{:S(2)}, u32[]{:S(2)}) collective-permute-start(bf16[256,128]{1,0:T(8,128)(2,1)S(1)} %get-tuple-element.26.refs_0_), channel_id=1, source_target_pairs={{0,20},{4,16},{8,28},{12,24},{16,4},{20,0},{24,12},{28,8},{1,21},{... | collective-permute-start | bytes 196616 | tf_op jit(solution)/shard_map/ppermute | solution.py:499
  5.2 4.3 %collective-permute-start.1 = (bf16[256,128]{1,0:T(8,128)(2,1)S(1)}, bf16[256,128]{1,0:T(8,128)(2,1)S(1)}, u32[]{:S(2)}, u32[]{:S(2)}) collective-permute-start(bf16[256,128]{1,0:T(8,128)(2,1)S(1)} %get-tuple-element.26.refs_0_), channel_id=1, source_target_pairs={{0,12},{4,8},{8,4},{12,0},{16,28},{20,24},{24,20},{28,16},{1,13},{... | collective-permute-start | bytes 196616 | tf_op jit(solution)/shard_map/ppermute | solution.py:499
  7.6 2.5 %collective-permute-start.4 = (bf16[2,256,128]{2,1,0:T(8,128)(2,1)S(1)}, bf16[2,256,128]{2,1,0:T(8,128)(2,1)S(1)}, u32[]{:S(2)}, u32[]{:S(2)}) collective-permute-start(bf16[2,256,128]{2,1,0:T(8,128)(2,1)S(1)} %stack.5.refs_1_.refs_3_), channel_id=1, source_target_pairs={{0,4},{4,0},{8,12},{12,8},{16,20},{20,16},{24,28},{28,24},{1,5},{5... | collective-permute-start | bytes 393224 | tf_op jit(solution)/shard_map/ppermute | solution.py:499
  9.5 1.4 %collective-permute-start.3 = (bf16[2,256,128]{2,1,0:T(8,128)(2,1)S(1)}, bf16[2,256,128]{2,1,0:T(8,128)(2,1)S(1)}, u32[]{:S(2)}, u32[]{:S(2)}) collective-permute-start(bf16[2,256,128]{2,1,0:T(8,128)(2,1)S(1)} %stack.4.refs_0_.refs_2_), channel_id=1, source_target_pairs={{0,4},{4,0},{8,12},{12,8},{16,20},{20,16},{24,28},{28,24},{1,5},{5... | collective-permute-start | bytes 393224 | tf_op jit(solution)/shard_map/ppermute | solution.py:499
  12.3 7.0 %collective-permute-start.5 = (bf16[256,128]{1,0:T(8,128)(2,1)S(1)}, bf16[256,128]{1,0:T(8,128)(2,1)S(1)}, u32[]{:S(2)}, u32[]{:S(2)}) collective-permute-start(bf16[256,128]{1,0:T(8,128)(2,1)S(1)} %get-tuple-element.29), channel_id=1, source_target_pairs={{0,3},{1,2},{2,1},{3,0},{4,7},{5,6},{6,5},{7,4},{8,11},{9,10},{10,... | collective-permute-start | bytes 196616 | tf_op jit(solution)/shard_map/ppermute | solution.py:499
  16.0 5.9 %collective-permute-start.6 = (bf16[256,128]{1,0:T(8,128)(2,1)S(1)}, bf16[256,128]{1,0:T(8,128)(2,1)S(1)}, u32[]{:S(2)}, u32[]{:S(2)}) collective-permute-start(bf16[256,128]{1,0:T(8,128)(2,1)S(1)} %get-tuple-element.30), channel_id=1, source_target_pairs={{0,2},{1,3},{2,0},{3,1},{4,6},{5,7},{6,4},{7,5},{8,10},{9,11},{10,... | collective-permute-start | bytes 196616 | tf_op jit(solution)/shard_map/ppermute | solution.py:499
  16.0 5.9 %collective-permute-start.7 = (bf16[256,128]{1,0:T(8,128)(2,1)S(1)}, bf16[256,128]{1,0:T(8,128)(2,1)S(1)}, u32[]{:S(2)}, u32[]{:S(2)}) collective-permute-start(bf16[256,128]{1,0:T(8,128)(2,1)S(1)} %get-tuple-element.31), channel_id=1, source_target_pairs={{0,1},{1,0},{2,3},{3,2},{4,5},{5,4},{6,7},{7,6},{8,9},{9,8},{10,11... | collective-permute-start | bytes 196616 | tf_op jit(solution)/shard_map/ppermute | solution.py:499
  22.1 5.4 %collective-permute-start.10 = (bf16[272,128]{1,0:T(8,128)(2,1)S(1)}, bf16[272,128]{1,0:T(8,128)(2,1)S(1)}, u32[]{:S(2)}, u32[]{:S(2)}) collective-permute-start(bf16[272,128]{1,0:T(8,128)(2,1)S(1)} %middle.1.refs_0_), channel_id=1, source_target_pairs={{0,28},{4,24},{8,20},{12,16},{16,12},{20,8},{24,4},{28,0},{1,29},{... | collective-permute-start | bytes 208904 | tf_op jit(solution)/shard_map/ppermute | solution.py:499
  23.0 5.8 %collective-permute-start.8 = (bf16[272,128]{1,0:T(8,128)(2,1)S(1)}, bf16[272,128]{1,0:T(8,128)(2,1)S(1)}, u32[]{:S(2)}, u32[]{:S(2)}) collective-permute-start(bf16[272,128]{1,0:T(8,128)(2,1)S(1)} %middle.1.refs_0_), channel_id=1, source_target_pairs={{0,20},{4,16},{8,28},{12,24},{16,4},{20,0},{24,12},{28,8},{1,21},{... | collective-permute-start | bytes 208904 | tf_op jit(solution)/shard_map/ppermute | solution.py:499
  24.6 4.4 %collective-permute-start.9 = (bf16[272,128]{1,0:T(8,128)(2,1)S(1)}, bf16[272,128]{1,0:T(8,128)(2,1)S(1)}, u32[]{:S(2)}, u32[]{:S(2)}) collective-permute-start(bf16[272,128]{1,0:T(8,128)(2,1)S(1)} %middle.1.refs_0_), channel_id=1, source_target_pairs={{0,12},{4,8},{8,4},{12,0},{16,28},{20,24},{24,20},{28,16},{1,13},{... | collective-permute-start | bytes 208904 | tf_op jit(solution)/shard_map/ppermute | solution.py:499
  27.5 1.8 %collective-permute-start.12 = (bf16[2,272,128]{2,1,0:T(8,128)(2,1)S(1)}, bf16[2,272,128]{2,1,0:T(8,128)(2,1)S(1)}, u32[]{:S(2)}, u32[]{:S(2)}) collective-permute-start(bf16[2,272,128]{2,1,0:T(8,128)(2,1)S(1)} %stack.7.refs_1_.refs_3_), channel_id=1, source_target_pairs={{0,4},{4,0},{8,12},{12,8},{16,20},{20,16},{24,28},{28,24},{1,5},{5... | collective-permute-start | bytes 417800 | tf_op jit(solution)/shard_map/ppermute | solution.py:499
  29.0 1.4 %collective-permute-start.11 = (bf16[2,272,128]{2,1,0:T(8,128)(2,1)S(1)}, bf16[2,272,128]{2,1,0:T(8,128)(2,1)S(1)}, u32[]{:S(2)}, u32[]{:S(2)}) collective-permute-start(bf16[2,272,128]{2,1,0:T(8,128)(2,1)S(1)} %stack.6.refs_0_.refs_2_), channel_id=1, source_target_pairs={{0,4},{4,0},{8,12},{12,8},{16,20},{20,16},{24,28},{28,24},{1,5},{5... | collective-permute-start | bytes 417800 | tf_op jit(solution)/shard_map/ppermute | solution.py:499
  31.8 6.9 %collective-permute-start.13 = (bf16[272,128]{1,0:T(8,128)(2,1)S(1)}, bf16[272,128]{1,0:T(8,128)(2,1)S(1)}, u32[]{:S(2)}, u32[]{:S(2)}) collective-permute-start(bf16[272,128]{1,0:T(8,128)(2,1)S(1)} %get-tuple-element.34), channel_id=1, source_target_pairs={{0,3},{1,2},{2,1},{3,0},{4,7},{5,6},{6,5},{7,4},{8,11},{9,10},{10,... | collective-permute-start | bytes 208904 | tf_op jit(solution)/shard_map/ppermute | solution.py:499
  34.0 7.0 %collective-permute-start.14 = (bf16[272,128]{1,0:T(8,128)(2,1)S(1)}, bf16[272,128]{1,0:T(8,128)(2,1)S(1)}, u32[]{:S(2)}, u32[]{:S(2)}) collective-permute-start(bf16[272,128]{1,0:T(8,128)(2,1)S(1)} %get-tuple-element.35), channel_id=1, source_target_pairs={{0,2},{1,3},{2,0},{3,1},{4,6},{5,7},{6,4},{7,5},{8,10},{9,11},{10,... | collective-permute-start | bytes 208904 | tf_op jit(solution)/shard_map/ppermute | solution.py:499
  34.0 6.9 %collective-permute-start.15 = (bf16[272,128]{1,0:T(8,128)(2,1)S(1)}, bf16[272,128]{1,0:T(8,128)(2,1)S(1)}, u32[]{:S(2)}, u32[]{:S(2)}) collective-permute-start(bf16[272,128]{1,0:T(8,128)(2,1)S(1)} %get-tuple-element.36), channel_id=1, source_target_pairs={{0,1},{1,0},{2,3},{3,2},{4,5},{5,4},{6,7},{7,6},{8,9},{9,8},{10,11... | collective-permute-start | bytes 208904 | tf_op jit(solution)/shard_map/ppermute | solution.py:499
  41.4 5.3 %collective-permute-start.16 = (f32[64,128]{1,0:T(8,128)S(1)}, f32[64,128]{1,0:T(8,128)S(1)}, u32[]{:S(2)}, u32[]{:S(2)}) collective-permute-start(f32[64,128]{1,0:T(8,128)S(1)} %get-tuple-element.38.refs_0_), channel_id=1, source_target_pairs={{0,7},{1,6},{2,5},{3,4},{4,3},{5,2},{6,1},{7,0},{8,15},{9,14},{10,... | collective-permute-start | bytes 98312 | tf_op jit(solution)/shard_map/ppermute | solution.py:509
  43.1 5.1 %collective-permute-start.17 = (f32[64,128]{1,0:T(8,128)S(1)}, f32[64,128]{1,0:T(8,128)S(1)}, u32[]{:S(2)}, u32[]{:S(2)}) collective-permute-start(f32[64,128]{1,0:T(8,128)S(1)} %get-tuple-element.38.refs_0_), channel_id=1, source_target_pairs={{0,6},{1,7},{2,4},{3,5},{4,2},{5,3},{6,0},{7,1},{8,14},{9,15},{10,... | collective-permute-start | bytes 98312 | tf_op jit(solution)/shard_map/ppermute | solution.py:509
  43.1 5.1 %collective-permute-start.18 = (f32[64,128]{1,0:T(8,128)S(1)}, f32[64,128]{1,0:T(8,128)S(1)}, u32[]{:S(2)}, u32[]{:S(2)}) collective-permute-start(f32[64,128]{1,0:T(8,128)S(1)} %get-tuple-element.38.refs_0_), channel_id=1, source_target_pairs={{0,5},{1,4},{2,7},{3,6},{4,1},{5,0},{6,3},{7,2},{8,13},{9,12},{10,... | collective-permute-start | bytes 98312 | tf_op jit(solution)/shard_map/ppermute | solution.py:509
  48.3 4.5 %collective-permute-start.19 = (f32[32,128]{1,0:T(8,128)S(1)}, f32[32,128]{1,0:T(8,128)S(1)}, u32[]{:S(2)}, u32[]{:S(2)}) collective-permute-start(f32[32,128]{1,0:T(8,128)S(1)} %get-tuple-element.40.refs_0_), channel_id=1, source_target_pairs={{0,28},{4,24},{8,20},{12,16},{16,12},{20,8},{24,4},{28,0},{1,29},{... | collective-permute-start | bytes 49160 | tf_op jit(solution)/shard_map/ppermute | solution.py:499
  49.7 3.2 %collective-permute-start.20 = (f32[32,128]{1,0:T(8,128)S(1)}, f32[32,128]{1,0:T(8,128)S(1)}, u32[]{:S(2)}, u32[]{:S(2)}) collective-permute-start(f32[32,128]{1,0:T(8,128)S(1)} %get-tuple-element.40.refs_0_), channel_id=1, source_target_pairs={{0,20},{4,16},{8,28},{12,24},{16,4},{20,0},{24,12},{28,8},{1,21},{... | collective-permute-start | bytes 49160 | tf_op jit(solution)/shard_map/ppermute | solution.py:499
  50.5 3.2 %collective-permute-start.21 = (f32[32,128]{1,0:T(8,128)S(1)}, f32[32,128]{1,0:T(8,128)S(1)}, u32[]{:S(2)}, u32[]{:S(2)}) collective-permute-start(f32[32,128]{1,0:T(8,128)S(1)} %get-tuple-element.40.refs_0_), channel_id=1, source_target_pairs={{0,12},{4,8},{8,4},{12,0},{16,28},{20,24},{24,20},{28,16},{1,13},{... | collective-permute-start | bytes 49160 | tf_op jit(solution)/shard_map/ppermute | solution.py:499
  53.7 1.2 %collective-permute-start.22 = (f32[32,128]{1,0:T(8,128)S(1)}, f32[32,128]{1,0:T(8,128)S(1)}, u32[]{:S(2)}, u32[]{:S(2)}) collective-permute-start(f32[32,128]{1,0:T(8,128)S(1)} %add_parts.1.refs_0_), channel_id=1, source_target_pairs={{0,4},{4,0},{8,12},{12,8},{16,20},{20,16},{24,28},{28,24},{1,5},{5... | collective-permute-start | bytes 49160 | tf_op jit(solution)/shard_map/ppermute | solution.py:499
  (1 other events, 8.7 us)

commit v11 on v10

--- a/solution.py
+++ b/solution.py
@@ -23,10 +23,6 @@
 
 def hbm():
     return pl.BlockSpec(memory_space=pltpu.HBM)
-
-
-def smem():
-    return pl.BlockSpec(memory_space=pltpu.SMEM)
 
 
 def shaped(shape, dtype):
@@ -202,10 +198,10 @@
 
 def one_product(group, columns, matrix, table, out_ref):
     block_rows, slots = matrix.shape[0], matrix.shape[2] // 64
-    first = group * (block_rows * slots)
+    chosen = columns[group]
     low = iota((32, 128), 1) < 64
     for i in range(block_rows):
-        picked = [table[columns[first + i * slots + s]] for s in range(slots)]
+        picked = [table[chosen[i, s]] for s in range(slots)]
         result = jnp.dot(matrix[i], jnp.concatenate(picked, axis=0), preferred_element_type=F32)
         out_ref[i * 32 : (i + 1) * 32, :] = jnp.where(low, result[:32], result[32:]).astype(BF16)
 
@@ -217,12 +213,10 @@
     return largest
 
 
-def others_kernel(offsets, ranges, stacks, old_table, columns_any, matrix_ref, *refs):
+def others_kernel(offsets, ranges, stacks, old_table, columns, matrix_ref, *refs):
     del old_table
     far_refs, near_refs = refs[:stacks], refs[stacks : 2 * stacks]
-    table, *outs, columns, sem = refs[2 * stacks :]
-    copy = pltpu.make_async_copy(columns_any, columns, sem)
-    copy.start()
+    table, *outs = refs[2 * stacks :]
     fill_table(far_refs, offsets, table)
     terms, first = outs[: len(ranges)], matrix_ref.shape[1] * 32
     if len(outs) > len(ranges):
@@ -233,7 +227,6 @@
             ref[...] = notes
         for term in terms:
             term[first:, :] = notes
-    copy.wait()
     for place, m in enumerate(ranges):
         group = m ^ lax.axis_index("cols")
         one_product(group, columns, matrix_ref.at[place], table, terms[place])
@@ -253,17 +246,16 @@
     table, *outs = call(
         functools.partial(others_kernel, offsets[count:], ranges, len(near)),
         "others",
-        [vmem(), pl.BlockSpec(memory_space=pl.ANY)] + [vmem()] * (1 + 2 * len(near)),
+        [vmem()] * (3 + 2 * len(near)),
         outs,
         (table, columns, matrix, *far, *near),
-        [pltpu.SMEM(columns.shape, jnp.int32), pltpu.SemaphoreType.DMA],
         input_output_aliases={0: 0},
     )
     terms = [swap(term, "cols", m) for m, term in zip(ranges, outs)]
     own = call(
         own_kernel,
         "own",
-        [smem(), vmem(), vmem()],
+        [vmem()] * 3,
         shaped((rows, 128), BF16),
         (columns, own_matrix, table),
     )
@@ -547,7 +539,7 @@
     total = float(groups * ranks * block_rows * block_size)
     blocks = ranks * block_rows
     live = iota(block_columns.shape, 3) < block_counts[..., None]
-    columns = jnp.where(live, jnp.clip(block_columns, 0, blocks - 1), blocks).reshape(-1)
+    columns = jnp.where(live, jnp.clip(block_columns, 0, blocks - 1), blocks)[:, :, 0]
     panel, inv_degree, affinity = (
         pltpu.with_memory_space_constraint(value, pltpu.HBM) for value in (panel, inv_degree, affinity)
     )

time: 57.9 us -> 56.9 us (0.983)
  Pallas kernels: 15.3 us -> 13.3 us
  waiting for transfers between devices: 18.6 us -> 19.7 us
    pallas_call x20, Pallas kernels: 15.3 us -> 13.3 us  [call(): pl.pallas_call(kernel, out_shape=outs, in_specs=ins, out_specs=jax.tree.m...]
    ppermute x20, waiting for transfers between devices: 15.5 us -> 16.6 us  [swap(): lax.ppermute(value, axis, [(index, index ^ mask) for index in range(size)])]
  transfers between devices with their start and end apart: 23 -> 23, of which waited for: 15 -> 15; matrix products, arithmetic and copies ran while one was open for 0% -> 0% of each run, Pallas kernels for 14% -> 13%
where the time goes in v11:
time: 56.9 us; the launch traced here: 56.7 us
  starting transfers between devices  23.4 us (41%)
  waiting for transfers between devices  19.7 us (35%)
  Pallas kernels  13.3 us (23%)
    ppermute x20, starting transfers between devices, swap(): lax.ppermute(value, axis, [(index, index ^ mask) for index in range(size)])  19.6 us
    ppermute x20, waiting for transfers between devices, swap(): lax.ppermute(value, axis, [(index, index ^ mask) for index in range(size)])  16.6 us
    pallas_call x20, Pallas kernels, call(): pl.pallas_call(kernel, out_shape=outs, in_specs=ins, out_specs=jax.tree.m...  13.3 us
    ppermute x3, starting transfers between devices, swap_both(): return lax.ppermute(value, ('rows', 'cols'), pairs)  3.75 us
    ppermute x3, waiting for transfers between devices, swap_both(): return lax.ppermute(value, ('rows', 'cols'), pairs)  3.1 us
  transfers between devices with their start and end apart: 23, of which 15 were waited for; matrix products, arithmetic and copies ran while one was open for 0% of the time, Pallas kernels for 13%

profile of v11, /device:TPU:0, one launch (start us, length us, event | category | flops | bytes accessed | tf_op | source)
XLA Modules:
  0.0 56.7 jit_solution(12031152856349380204)
XLA Ops:
  0.0 1.0 %start.1 = (bf16[256,128]{1,0:T(8,128)(2,1)S(1)}, f32[256,128]{1,0:T(8,128)S(1)}) custom-call(f32[1,8,4096]{2,1,0:T(8,128)} %panel_hbm.1, f32[1,8,64]{2,1,0:T(8,128)} %inv_hbm.5), custom_call_target="tpu_custom_call" | custom-call | tf_op jit(solution)/shard_map/start/pallas_call | solution.py:37
  1.0 3.4 %collective-permute-start.2 = (bf16[256,128]{1,0:T(8,128)(2,1)S(1)}, bf16[256,128]{1,0:T(8,128)(2,1)S(1)}, u32[]{:S(2)}, u32[]{:S(2)}) collective-permute-start(bf16[256,128]{1,0:T(8,128)(2,1)S(1)} %get-tuple-element.26.refs_0_), channel_id=1, source_target_pairs={{0,28},{4,24},{8,20},{12,16},{16,12},{20,8},{24,4},{28,0},{1,29},{... | collective-permute-start | bytes 196616 | tf_op jit(solution)/shard_map/ppermute | solution.py:491
  5.4 2.2 %prep.2 = (bf16[3,8,64,512]{3,2,1,0:T(8,128)(2,1)S(1)}, f32[8,128]{1,0:T(8,128)S(1)}) custom-call(bf16[4,8,1,8,4096]{4,3,2,1,0:T(8,128)(2,1)} %affinity_hbm.3, f32[1,8,64]{2,1,0:T(8,128)} %inv_hbm.5), custom_call_target="tpu_custom_call" | custom-call | tf_op jit(solution)/shard_map/prep/pallas_call | solution.py:37
  8.3 1.2 %collective-permute-done.1.refs_1_ = bf16[256,128]{1,0:T(8,128)(2,1)S(1)} collective-permute-done((bf16[256,128]{1,0:T(8,128)(2,1)S(1)}, bf16[256,128]{1,0:T(8,128)(2,1)S(1)}, u32[]{:S(2)}, u32[]{:S(2)}) %collective-permute-start.1) | collective-permute-done | bytes 65568 | tf_op jit(solution)/shard_map/ppermute | solution.py:491
  10.0 1.0 %collective-permute-done.3.refs_0_ = bf16[2,256,128]{2,1,0:T(8,128)(2,1)S(1)} collective-permute-done((bf16[2,256,128]{2,1,0:T(8,128)(2,1)S(1)}, bf16[2,256,128]{2,1,0:T(8,128)(2,1)S(1)}, u32[]{:S(2)}, u32[]{:S(2)}) %collective-permute-start.3) | collective-permute-done | bytes 131104 | tf_op jit(solution)/shard_map/ppermute | solution.py:491
  11.8 3.7 %collective-permute-start.5 = (bf16[256,128]{1,0:T(8,128)(2,1)S(1)}, bf16[256,128]{1,0:T(8,128)(2,1)S(1)}, u32[]{:S(2)}, u32[]{:S(2)}) collective-permute-start(bf16[256,128]{1,0:T(8,128)(2,1)S(1)} %get-tuple-element.29), channel_id=1, source_target_pairs={{0,3},{1,2},{2,1},{3,0},{4,7},{5,6},{6,5},{7,4},{8,11},{9,10},{10,... | collective-permute-start | bytes 196616 | tf_op jit(solution)/shard_map/ppermute | solution.py:491
  16.2 1.7 %prep.3 = (bf16[1,8,64,512]{3,2,1,0:T(8,128)(2,1)S(1)}, f32[8,128]{1,0:T(8,128)}) custom-call(bf16[4,8,1,8,4096]{4,3,2,1,0:T(8,128)(2,1)} %affinity_hbm.3, f32[1,8,64]{2,1,0:T(8,128)} %inv_hbm.5), custom_call_target="tpu_custom_call" | custom-call | tf_op jit(solution)/shard_map/prep/pallas_call | solution.py:37
  18.3 3.0 %collective-permute-done.6.refs_2_ = bf16[256,128]{1,0:T(8,128)(2,1)S(1)} collective-permute-done((bf16[256,128]{1,0:T(8,128)(2,1)S(1)}, bf16[256,128]{1,0:T(8,128)(2,1)S(1)}, u32[]{:S(2)}, u32[]{:S(2)}) %collective-permute-start.6) | collective-permute-done | bytes 65568 | tf_op jit(solution)/shard_map/ppermute | solution.py:491
  22.4 1.6 %collective-permute-start.8 = (bf16[272,128]{1,0:T(8,128)(2,1)S(1)}, bf16[272,128]{1,0:T(8,128)(2,1)S(1)}, u32[]{:S(2)}, u32[]{:S(2)}) collective-permute-start(bf16[272,128]{1,0:T(8,128)(2,1)S(1)} %middle.1.refs_0_), channel_id=1, source_target_pairs={{0,20},{4,16},{8,28},{12,24},{16,4},{20,0},{24,12},{28,8},{1,21},{... | collective-permute-start | bytes 208904 | tf_op jit(solution)/shard_map/ppermute | solution.py:491
  24.4 2.6 %collective-permute-done.10.refs_1_ = bf16[272,128]{1,0:T(8,128)(2,1)S(1)} collective-permute-done((bf16[272,128]{1,0:T(8,128)(2,1)S(1)}, bf16[272,128]{1,0:T(8,128)(2,1)S(1)}, u32[]{:S(2)}, u32[]{:S(2)}) %collective-permute-start.10) | collective-permute-done | bytes 69664 | tf_op jit(solution)/shard_map/ppermute | solution.py:491
  27.1 1.2 %collective-permute-done.8.refs_0_ = bf16[272,128]{1,0:T(8,128)(2,1)S(1)} collective-permute-done((bf16[272,128]{1,0:T(8,128)(2,1)S(1)}, bf16[272,128]{1,0:T(8,128)(2,1)S(1)}, u32[]{:S(2)}, u32[]{:S(2)}) %collective-permute-start.8) | collective-permute-done | bytes 69664 | tf_op jit(solution)/shard_map/ppermute | solution.py:491
  28.8 1.1 %collective-permute-done.11.refs_2_.refs_0_ = bf16[2,272,128]{2,1,0:T(8,128)(2,1)S(1)} collective-permute-done((bf16[2,272,128]{2,1,0:T(8,128)(2,1)S(1)}, bf16[2,272,128]{2,1,0:T(8,128)(2,1)S(1)}, u32[]{:S(2)}, u32[]{:S(2)}) %collective-permute-start.11) | collective-permute-done | bytes 139296 | tf_op jit(solution)/shard_map/ppermute | solution.py:491
  30.8 2.1 %collective-permute-start.13 = (bf16[272,128]{1,0:T(8,128)(2,1)S(1)}, bf16[272,128]{1,0:T(8,128)(2,1)S(1)}, u32[]{:S(2)}, u32[]{:S(2)}) collective-permute-start(bf16[272,128]{1,0:T(8,128)(2,1)S(1)} %get-tuple-element.34), channel_id=1, source_target_pairs={{0,3},{1,2},{2,1},{3,0},{4,7},{5,6},{6,5},{7,4},{8,11},{9,10},{10,... | collective-permute-start | bytes 208904 | tf_op jit(solution)/shard_map/ppermute | solution.py:491
  33.0 2.3 %collective-permute-start.15 = (bf16[272,128]{1,0:T(8,128)(2,1)S(1)}, bf16[272,128]{1,0:T(8,128)(2,1)S(1)}, u32[]{:S(2)}, u32[]{:S(2)}) collective-permute-start(bf16[272,128]{1,0:T(8,128)(2,1)S(1)} %get-tuple-element.36), channel_id=1, source_target_pairs={{0,1},{1,0},{2,3},{3,2},{4,5},{5,4},{6,7},{7,6},{8,9},{9,8},{10,11... | collective-permute-start | bytes 208904 | tf_op jit(solution)/shard_map/ppermute | solution.py:491
  36.3 1.4 %collective-permute-done.13.refs_1_ = bf16[272,128]{1,0:T(8,128)(2,1)S(1)} collective-permute-done((bf16[272,128]{1,0:T(8,128)(2,1)S(1)}, bf16[272,128]{1,0:T(8,128)(2,1)S(1)}, u32[]{:S(2)}, u32[]{:S(2)}) %collective-permute-start.13) | collective-permute-done | bytes 69664 | tf_op jit(solution)/shard_map/ppermute | solution.py:491
  37.7 2.1 %collective-permute-done.14.refs_2_ = bf16[272,128]{1,0:T(8,128)(2,1)S(1)} collective-permute-done((bf16[272,128]{1,0:T(8,128)(2,1)S(1)}, bf16[272,128]{1,0:T(8,128)(2,1)S(1)}, u32[]{:S(2)}, u32[]{:S(2)}) %collective-permute-start.14) | collective-permute-done | bytes 69664 | tf_op jit(solution)/shard_map/ppermute | solution.py:491
  40.3 1.7 %collective-permute-start.16 = (f32[64,128]{1,0:T(8,128)S(1)}, f32[64,128]{1,0:T(8,128)S(1)}, u32[]{:S(2)}, u32[]{:S(2)}) collective-permute-start(f32[64,128]{1,0:T(8,128)S(1)} %get-tuple-element.38.refs_0_), channel_id=1, source_target_pairs={{0,7},{1,6},{2,5},{3,4},{4,3},{5,2},{6,1},{7,0},{8,15},{9,14},{10,... | collective-permute-start | bytes 98312 | tf_op jit(solution)/shard_map/ppermute | solution.py:501
  42.1 2.0 %collective-permute-start.18 = (f32[64,128]{1,0:T(8,128)S(1)}, f32[64,128]{1,0:T(8,128)S(1)}, u32[]{:S(2)}, u32[]{:S(2)}) collective-permute-start(f32[64,128]{1,0:T(8,128)S(1)} %get-tuple-element.38.refs_0_), channel_id=1, source_target_pairs={{0,5},{1,4},{2,7},{3,6},{4,1},{5,0},{6,3},{7,2},{8,13},{9,12},{10,... | collective-permute-start | bytes 98312 | tf_op jit(solution)/shard_map/ppermute | solution.py:501
  44.1 1.6 %collective-permute-done.16.refs_1_ = f32[64,128]{1,0:T(8,128)S(1)} collective-permute-done((f32[64,128]{1,0:T(8,128)S(1)}, f32[64,128]{1,0:T(8,128)S(1)}, u32[]{:S(2)}, u32[]{:S(2)}) %collective-permute-start.16) | collective-permute-done | bytes 32800 | tf_op jit(solution)/shard_map/ppermute | solution.py:501
  45.7 1.5 %collective-permute-done.17.refs_2_ = f32[64,128]{1,0:T(8,128)S(1)} collective-permute-done((f32[64,128]{1,0:T(8,128)S(1)}, f32[64,128]{1,0:T(8,128)S(1)}, u32[]{:S(2)}, u32[]{:S(2)}) %collective-permute-start.17) | collective-permute-done | bytes 32800 | tf_op jit(solution)/shard_map/ppermute | solution.py:501
  47.2 1.5 %collective-permute-start.19 = (f32[32,128]{1,0:T(8,128)S(1)}, f32[32,128]{1,0:T(8,128)S(1)}, u32[]{:S(2)}, u32[]{:S(2)}) collective-permute-start(f32[32,128]{1,0:T(8,128)S(1)} %get-tuple-element.40.refs_0_), channel_id=1, source_target_pairs={{0,28},{4,24},{8,20},{12,16},{16,12},{20,8},{24,4},{28,0},{1,29},{... | collective-permute-start | bytes 49160 | tf_op jit(solution)/shard_map/ppermute | solution.py:491
  50.2 1.5 %first_factor.1.refs_4_.inverse_ref = f32[64,64]{1,0:T(8,128)S(1)} custom-call(f32[32,128]{1,0:T(8,128)S(1)} %get-tuple-element.39.gram_ref), custom_call_target="tpu_custom_call" | custom-call | tf_op jit(solution)/shard_map/first_factor/pallas_call | solution.py:37
  52.8 1.1 %collective-permute-done.22.refs_1_ = f32[32,128]{1,0:T(8,128)S(1)} collective-permute-done((f32[32,128]{1,0:T(8,128)S(1)}, f32[32,128]{1,0:T(8,128)S(1)}, u32[]{:S(2)}, u32[]{:S(2)}) %collective-permute-start.22) | collective-permute-done | bytes 16416 | tf_op jit(solution)/shard_map/ppermute | solution.py:491
  53.8 2.8 %finish.1 = f32[1,8,4096]{2,1,0:T(8,128)} custom-call(f32[256,128]{1,0:T(8,128)S(1)} %get-tuple-element.37.rows_ref, f32[64,64]{1,0:T(8,128)S(1)} %first_factor.1.refs_4_.inverse_ref, f32[32,128]{1,0:T(8,128)S(1)} %add_parts.1.refs_0_, f32[32,128]{1,0:T(8,128)S(1)} %collective-permute-done.22.refs_1_), custom_call_target="tpu_custom_call" | custom-call | tf_op jit(solution)/shard_map/finish/pallas_call | solution.py:37
  (47 shorter events, 11.1 us)
Async XLA Ops:
  1.0 8.7 %copy-start = (s32[4,8,1,8]{3,2,1,0:T(1,128)S(1)}, s32[4,8,1,8]{3,2,1,0:T(1,128)}, u32[]{:S(2)}) copy-start(s32[4,8,1,8]{3,2,1,0:T(1,128)} %param.6) | copy-start | bytes 3076
  1.0 6.5 %collective-permute-start.2 = (bf16[256,128]{1,0:T(8,128)(2,1)S(1)}, bf16[256,128]{1,0:T(8,128)(2,1)S(1)}, u32[]{:S(2)}, u32[]{:S(2)}) collective-permute-start(bf16[256,128]{1,0:T(8,128)(2,1)S(1)} %get-tuple-element.26.refs_0_), channel_id=1, source_target_pairs={{0,28},{4,24},{8,20},{12,16},{16,12},{20,8},{24,4},{28,0},{1,29},{... | collective-permute-start | bytes 196616 | tf_op jit(solution)/shard_map/ppermute | solution.py:491
  4.4 3.9 %collective-permute-start = (bf16[256,128]{1,0:T(8,128)(2,1)S(1)}, bf16[256,128]{1,0:T(8,128)(2,1)S(1)}, u32[]{:S(2)}, u32[]{:S(2)}) collective-permute-start(bf16[256,128]{1,0:T(8,128)(2,1)S(1)} %get-tuple-element.26.refs_0_), channel_id=1, source_target_pairs={{0,20},{4,16},{8,28},{12,24},{16,4},{20,0},{24,12},{28,8},{1,21},{... | collective-permute-start | bytes 196616 | tf_op jit(solution)/shard_map/ppermute | solution.py:491
  5.2 4.3 %collective-permute-start.1 = (bf16[256,128]{1,0:T(8,128)(2,1)S(1)}, bf16[256,128]{1,0:T(8,128)(2,1)S(1)}, u32[]{:S(2)}, u32[]{:S(2)}) collective-permute-start(bf16[256,128]{1,0:T(8,128)(2,1)S(1)} %get-tuple-element.26.refs_0_), channel_id=1, source_target_pairs={{0,12},{4,8},{8,4},{12,0},{16,28},{20,24},{24,20},{28,16},{1,13},{... | collective-permute-start | bytes 196616 | tf_op jit(solution)/shard_map/ppermute | solution.py:491
  7.6 2.4 %collective-permute-start.4 = (bf16[2,256,128]{2,1,0:T(8,128)(2,1)S(1)}, bf16[2,256,128]{2,1,0:T(8,128)(2,1)S(1)}, u32[]{:S(2)}, u32[]{:S(2)}) collective-permute-start(bf16[2,256,128]{2,1,0:T(8,128)(2,1)S(1)} %stack.5.refs_1_.refs_3_), channel_id=1, source_target_pairs={{0,4},{4,0},{8,12},{12,8},{16,20},{20,16},{24,28},{28,24},{1,5},{5... | collective-permute-start | bytes 393224 | tf_op jit(solution)/shard_map/ppermute | solution.py:491
  9.5 1.4 %collective-permute-start.3 = (bf16[2,256,128]{2,1,0:T(8,128)(2,1)S(1)}, bf16[2,256,128]{2,1,0:T(8,128)(2,1)S(1)}, u32[]{:S(2)}, u32[]{:S(2)}) collective-permute-start(bf16[2,256,128]{2,1,0:T(8,128)(2,1)S(1)} %stack.4.refs_0_.refs_2_), channel_id=1, source_target_pairs={{0,4},{4,0},{8,12},{12,8},{16,20},{20,16},{24,28},{28,24},{1,5},{5... | collective-permute-start | bytes 393224 | tf_op jit(solution)/shard_map/ppermute | solution.py:491
  11.8 6.5 %collective-permute-start.5 = (bf16[256,128]{1,0:T(8,128)(2,1)S(1)}, bf16[256,128]{1,0:T(8,128)(2,1)S(1)}, u32[]{:S(2)}, u32[]{:S(2)}) collective-permute-start(bf16[256,128]{1,0:T(8,128)(2,1)S(1)} %get-tuple-element.29), channel_id=1, source_target_pairs={{0,3},{1,2},{2,1},{3,0},{4,7},{5,6},{6,5},{7,4},{8,11},{9,10},{10,... | collective-permute-start | bytes 196616 | tf_op jit(solution)/shard_map/ppermute | solution.py:491
  15.5 5.9 %collective-permute-start.6 = (bf16[256,128]{1,0:T(8,128)(2,1)S(1)}, bf16[256,128]{1,0:T(8,128)(2,1)S(1)}, u32[]{:S(2)}, u32[]{:S(2)}) collective-permute-start(bf16[256,128]{1,0:T(8,128)(2,1)S(1)} %get-tuple-element.30), channel_id=1, source_target_pairs={{0,2},{1,3},{2,0},{3,1},{4,6},{5,7},{6,4},{7,5},{8,10},{9,11},{10,... | collective-permute-start | bytes 196616 | tf_op jit(solution)/shard_map/ppermute | solution.py:491
  15.5 5.9 %collective-permute-start.7 = (bf16[256,128]{1,0:T(8,128)(2,1)S(1)}, bf16[256,128]{1,0:T(8,128)(2,1)S(1)}, u32[]{:S(2)}, u32[]{:S(2)}) collective-permute-start(bf16[256,128]{1,0:T(8,128)(2,1)S(1)} %get-tuple-element.31), channel_id=1, source_target_pairs={{0,1},{1,0},{2,3},{3,2},{4,5},{5,4},{6,7},{7,6},{8,9},{9,8},{10,11... | collective-permute-start | bytes 196616 | tf_op jit(solution)/shard_map/ppermute | solution.py:491
  21.5 5.4 %collective-permute-start.10 = (bf16[272,128]{1,0:T(8,128)(2,1)S(1)}, bf16[272,128]{1,0:T(8,128)(2,1)S(1)}, u32[]{:S(2)}, u32[]{:S(2)}) collective-permute-start(bf16[272,128]{1,0:T(8,128)(2,1)S(1)} %middle.1.refs_0_), channel_id=1, source_target_pairs={{0,28},{4,24},{8,20},{12,16},{16,12},{20,8},{24,4},{28,0},{1,29},{... | collective-permute-start | bytes 208904 | tf_op jit(solution)/shard_map/ppermute | solution.py:491
  22.4 5.8 %collective-permute-start.8 = (bf16[272,128]{1,0:T(8,128)(2,1)S(1)}, bf16[272,128]{1,0:T(8,128)(2,1)S(1)}, u32[]{:S(2)}, u32[]{:S(2)}) collective-permute-start(bf16[272,128]{1,0:T(8,128)(2,1)S(1)} %middle.1.refs_0_), channel_id=1, source_target_pairs={{0,20},{4,16},{8,28},{12,24},{16,4},{20,0},{24,12},{28,8},{1,21},{... | collective-permute-start | bytes 208904 | tf_op jit(solution)/shard_map/ppermute | solution.py:491
  24.1 4.4 %collective-permute-start.9 = (bf16[272,128]{1,0:T(8,128)(2,1)S(1)}, bf16[272,128]{1,0:T(8,128)(2,1)S(1)}, u32[]{:S(2)}, u32[]{:S(2)}) collective-permute-start(bf16[272,128]{1,0:T(8,128)(2,1)S(1)} %middle.1.refs_0_), channel_id=1, source_target_pairs={{0,12},{4,8},{8,4},{12,0},{16,28},{20,24},{24,20},{28,16},{1,13},{... | collective-permute-start | bytes 208904 | tf_op jit(solution)/shard_map/ppermute | solution.py:491
  27.0 1.8 %collective-permute-start.12 = (bf16[2,272,128]{2,1,0:T(8,128)(2,1)S(1)}, bf16[2,272,128]{2,1,0:T(8,128)(2,1)S(1)}, u32[]{:S(2)}, u32[]{:S(2)}) collective-permute-start(bf16[2,272,128]{2,1,0:T(8,128)(2,1)S(1)} %stack.7.refs_1_.refs_3_), channel_id=1, source_target_pairs={{0,4},{4,0},{8,12},{12,8},{16,20},{20,16},{24,28},{28,24},{1,5},{5... | collective-permute-start | bytes 417800 | tf_op jit(solution)/shard_map/ppermute | solution.py:491
  28.5 1.4 %collective-permute-start.11 = (bf16[2,272,128]{2,1,0:T(8,128)(2,1)S(1)}, bf16[2,272,128]{2,1,0:T(8,128)(2,1)S(1)}, u32[]{:S(2)}, u32[]{:S(2)}) collective-permute-start(bf16[2,272,128]{2,1,0:T(8,128)(2,1)S(1)} %stack.6.refs_0_.refs_2_), channel_id=1, source_target_pairs={{0,4},{4,0},{8,12},{12,8},{16,20},{20,16},{24,28},{28,24},{1,5},{5... | collective-permute-start | bytes 417800 | tf_op jit(solution)/shard_map/ppermute | solution.py:491
  30.8 6.9 %collective-permute-start.13 = (bf16[272,128]{1,0:T(8,128)(2,1)S(1)}, bf16[272,128]{1,0:T(8,128)(2,1)S(1)}, u32[]{:S(2)}, u32[]{:S(2)}) collective-permute-start(bf16[272,128]{1,0:T(8,128)(2,1)S(1)} %get-tuple-element.34), channel_id=1, source_target_pairs={{0,3},{1,2},{2,1},{3,0},{4,7},{5,6},{6,5},{7,4},{8,11},{9,10},{10,... | collective-permute-start | bytes 208904 | tf_op jit(solution)/shard_map/ppermute | solution.py:491
  32.9 6.9 %collective-permute-start.14 = (bf16[272,128]{1,0:T(8,128)(2,1)S(1)}, bf16[272,128]{1,0:T(8,128)(2,1)S(1)}, u32[]{:S(2)}, u32[]{:S(2)}) collective-permute-start(bf16[272,128]{1,0:T(8,128)(2,1)S(1)} %get-tuple-element.35), channel_id=1, source_target_pairs={{0,2},{1,3},{2,0},{3,1},{4,6},{5,7},{6,4},{7,5},{8,10},{9,11},{10,... | collective-permute-start | bytes 208904 | tf_op jit(solution)/shard_map/ppermute | solution.py:491
  33.0 6.9 %collective-permute-start.15 = (bf16[272,128]{1,0:T(8,128)(2,1)S(1)}, bf16[272,128]{1,0:T(8,128)(2,1)S(1)}, u32[]{:S(2)}, u32[]{:S(2)}) collective-permute-start(bf16[272,128]{1,0:T(8,128)(2,1)S(1)} %get-tuple-element.36), channel_id=1, source_target_pairs={{0,1},{1,0},{2,3},{3,2},{4,5},{5,4},{6,7},{7,6},{8,9},{9,8},{10,11... | collective-permute-start | bytes 208904 | tf_op jit(solution)/shard_map/ppermute | solution.py:491
  40.3 5.3 %collective-permute-start.16 = (f32[64,128]{1,0:T(8,128)S(1)}, f32[64,128]{1,0:T(8,128)S(1)}, u32[]{:S(2)}, u32[]{:S(2)}) collective-permute-start(f32[64,128]{1,0:T(8,128)S(1)} %get-tuple-element.38.refs_0_), channel_id=1, source_target_pairs={{0,7},{1,6},{2,5},{3,4},{4,3},{5,2},{6,1},{7,0},{8,15},{9,14},{10,... | collective-permute-start | bytes 98312 | tf_op jit(solution)/shard_map/ppermute | solution.py:501
  42.0 5.1 %collective-permute-start.17 = (f32[64,128]{1,0:T(8,128)S(1)}, f32[64,128]{1,0:T(8,128)S(1)}, u32[]{:S(2)}, u32[]{:S(2)}) collective-permute-start(f32[64,128]{1,0:T(8,128)S(1)} %get-tuple-element.38.refs_0_), channel_id=1, source_target_pairs={{0,6},{1,7},{2,4},{3,5},{4,2},{5,3},{6,0},{7,1},{8,14},{9,15},{10,... | collective-permute-start | bytes 98312 | tf_op jit(solution)/shard_map/ppermute | solution.py:501
  42.1 5.1 %collective-permute-start.18 = (f32[64,128]{1,0:T(8,128)S(1)}, f32[64,128]{1,0:T(8,128)S(1)}, u32[]{:S(2)}, u32[]{:S(2)}) collective-permute-start(f32[64,128]{1,0:T(8,128)S(1)} %get-tuple-element.38.refs_0_), channel_id=1, source_target_pairs={{0,5},{1,4},{2,7},{3,6},{4,1},{5,0},{6,3},{7,2},{8,13},{9,12},{10,... | collective-permute-start | bytes 98312 | tf_op jit(solution)/shard_map/ppermute | solution.py:501
  47.2 4.5 %collective-permute-start.19 = (f32[32,128]{1,0:T(8,128)S(1)}, f32[32,128]{1,0:T(8,128)S(1)}, u32[]{:S(2)}, u32[]{:S(2)}) collective-permute-start(f32[32,128]{1,0:T(8,128)S(1)} %get-tuple-element.40.refs_0_), channel_id=1, source_target_pairs={{0,28},{4,24},{8,20},{12,16},{16,12},{20,8},{24,4},{28,0},{1,29},{... | collective-permute-start | bytes 49160 | tf_op jit(solution)/shard_map/ppermute | solution.py:491
  48.7 3.2 %collective-permute-start.20 = (f32[32,128]{1,0:T(8,128)S(1)}, f32[32,128]{1,0:T(8,128)S(1)}, u32[]{:S(2)}, u32[]{:S(2)}) collective-permute-start(f32[32,128]{1,0:T(8,128)S(1)} %get-tuple-element.40.refs_0_), channel_id=1, source_target_pairs={{0,20},{4,16},{8,28},{12,24},{16,4},{20,0},{24,12},{28,8},{1,21},{... | collective-permute-start | bytes 49160 | tf_op jit(solution)/shard_map/ppermute | solution.py:491
  49.5 3.2 %collective-permute-start.21 = (f32[32,128]{1,0:T(8,128)S(1)}, f32[32,128]{1,0:T(8,128)S(1)}, u32[]{:S(2)}, u32[]{:S(2)}) collective-permute-start(f32[32,128]{1,0:T(8,128)S(1)} %get-tuple-element.40.refs_0_), channel_id=1, source_target_pairs={{0,12},{4,8},{8,4},{12,0},{16,28},{20,24},{24,20},{28,16},{1,13},{... | collective-permute-start | bytes 49160 | tf_op jit(solution)/shard_map/ppermute | solution.py:491
  52.6 1.2 %collective-permute-start.22 = (f32[32,128]{1,0:T(8,128)S(1)}, f32[32,128]{1,0:T(8,128)S(1)}, u32[]{:S(2)}, u32[]{:S(2)}) collective-permute-start(f32[32,128]{1,0:T(8,128)S(1)} %add_parts.1.refs_0_), channel_id=1, source_target_pairs={{0,4},{4,0},{8,12},{12,8},{16,20},{20,16},{24,28},{28,24},{1,5},{5... | collective-permute-start | bytes 49160 | tf_op jit(solution)/shard_map/ppermute | solution.py:491
  (1 other events, 8.7 us)

commit v12 on v11

--- a/solution.py
+++ b/solution.py
@@ -557,7 +557,8 @@
     devices = float(groups * ranks)
     rows, grams = collect(devices, total, degree, row_gram(near + far), notes, terms)
     flip = 1 if ranks == 8 else 0
-    gram, first = add_columns(total, [grams] + [swap_both(grams, flip, m) for m in ranges])
+    order = [2, 3, 1] if groups == 4 else ranges
+    gram, first = add_columns(total, [grams] + [swap_both(grams, flip, m) for m in order])
     inverse = first_factor(first)
     return finish(total, block_rows, rows, inverse, add_rows(gram, [inverse]))
 

time: 56.9 us -> 56.5 us (level)
  starting transfers between devices: 23.4 us -> 22.5 us
  waiting for transfers between devices: 19.7 us -> 20.3 us
    ppermute x3, starting transfers between devices: 3.75 us -> 2.84 us  [swap_both(): return lax.ppermute(value, ('rows', 'cols'), pairs)]
where the time goes in v12:
time: 56.5 us; the launch traced here: 56.3 us
  starting transfers between devices  22.5 us (40%)
  waiting for transfers between devices  20.3 us (36%)
  Pallas kernels  13.3 us (24%)
    ppermute x20, starting transfers between devices, swap(): lax.ppermute(value, axis, [(index, index ^ mask) for index in range(size)])  19.6 us
    ppermute x20, waiting for transfers between devices, swap(): lax.ppermute(value, axis, [(index, index ^ mask) for index in range(size)])  16.8 us
    pallas_call x20, Pallas kernels, call(): pl.pallas_call(kernel, out_shape=outs, in_specs=ins, out_specs=jax.tree.m...  13.3 us
    ppermute x3, waiting for transfers between devices, swap_both(): return lax.ppermute(value, ('rows', 'cols'), pairs)  3.51 us
    ppermute x3, starting transfers between devices, swap_both(): return lax.ppermute(value, ('rows', 'cols'), pairs)  2.84 us
  transfers between devices with their start and end apart: 23, of which 15 were waited for; matrix products, arithmetic and copies ran while one was open for 0% of the time, Pallas kernels for 13%

profile of v12, /device:TPU:0, one launch (start us, length us, event | category | flops | bytes accessed | tf_op | source)
XLA Modules:
  0.0 56.3 jit_solution(8328686164247216869)
XLA Ops:
  0.0 1.0 %start.1 = (bf16[256,128]{1,0:T(8,128)(2,1)S(1)}, f32[256,128]{1,0:T(8,128)S(1)}) custom-call(f32[1,8,4096]{2,1,0:T(8,128)} %panel_hbm.1, f32[1,8,64]{2,1,0:T(8,128)} %inv_hbm.5), custom_call_target="tpu_custom_call" | custom-call | tf_op jit(solution)/shard_map/start/pallas_call | solution.py:37
  1.0 3.4 %collective-permute-start.2 = (bf16[256,128]{1,0:T(8,128)(2,1)S(1)}, bf16[256,128]{1,0:T(8,128)(2,1)S(1)}, u32[]{:S(2)}, u32[]{:S(2)}) collective-permute-start(bf16[256,128]{1,0:T(8,128)(2,1)S(1)} %get-tuple-element.26.refs_0_), channel_id=1, source_target_pairs={{0,28},{4,24},{8,20},{12,16},{16,12},{20,8},{24,4},{28,0},{1,29},{... | collective-permute-start | bytes 196616 | tf_op jit(solution)/shard_map/ppermute | solution.py:491
  5.4 2.2 %prep.2 = (bf16[3,8,64,512]{3,2,1,0:T(8,128)(2,1)S(1)}, f32[8,128]{1,0:T(8,128)S(1)}) custom-call(bf16[4,8,1,8,4096]{4,3,2,1,0:T(8,128)(2,1)} %affinity_hbm.3, f32[1,8,64]{2,1,0:T(8,128)} %inv_hbm.5), custom_call_target="tpu_custom_call" | custom-call | tf_op jit(solution)/shard_map/prep/pallas_call | solution.py:37
  8.3 1.2 %collective-permute-done.1.refs_1_ = bf16[256,128]{1,0:T(8,128)(2,1)S(1)} collective-permute-done((bf16[256,128]{1,0:T(8,128)(2,1)S(1)}, bf16[256,128]{1,0:T(8,128)(2,1)S(1)}, u32[]{:S(2)}, u32[]{:S(2)}) %collective-permute-start.1) | collective-permute-done | bytes 65568 | tf_op jit(solution)/shard_map/ppermute | solution.py:491
  10.0 1.0 %collective-permute-done.3.refs_0_ = bf16[2,256,128]{2,1,0:T(8,128)(2,1)S(1)} collective-permute-done((bf16[2,256,128]{2,1,0:T(8,128)(2,1)S(1)}, bf16[2,256,128]{2,1,0:T(8,128)(2,1)S(1)}, u32[]{:S(2)}, u32[]{:S(2)}) %collective-permute-start.3) | collective-permute-done | bytes 131104 | tf_op jit(solution)/shard_map/ppermute | solution.py:491
  11.8 3.7 %collective-permute-start.5 = (bf16[256,128]{1,0:T(8,128)(2,1)S(1)}, bf16[256,128]{1,0:T(8,128)(2,1)S(1)}, u32[]{:S(2)}, u32[]{:S(2)}) collective-permute-start(bf16[256,128]{1,0:T(8,128)(2,1)S(1)} %get-tuple-element.29), channel_id=1, source_target_pairs={{0,3},{1,2},{2,1},{3,0},{4,7},{5,6},{6,5},{7,4},{8,11},{9,10},{10,... | collective-permute-start | bytes 196616 | tf_op jit(solution)/shard_map/ppermute | solution.py:491
  16.2 1.7 %prep.3 = (bf16[1,8,64,512]{3,2,1,0:T(8,128)(2,1)S(1)}, f32[8,128]{1,0:T(8,128)}) custom-call(bf16[4,8,1,8,4096]{4,3,2,1,0:T(8,128)(2,1)} %affinity_hbm.3, f32[1,8,64]{2,1,0:T(8,128)} %inv_hbm.5), custom_call_target="tpu_custom_call" | custom-call | tf_op jit(solution)/shard_map/prep/pallas_call | solution.py:37
  18.3 3.0 %collective-permute-done.6.refs_2_ = bf16[256,128]{1,0:T(8,128)(2,1)S(1)} collective-permute-done((bf16[256,128]{1,0:T(8,128)(2,1)S(1)}, bf16[256,128]{1,0:T(8,128)(2,1)S(1)}, u32[]{:S(2)}, u32[]{:S(2)}) %collective-permute-start.6) | collective-permute-done | bytes 65568 | tf_op jit(solution)/shard_map/ppermute | solution.py:491
  22.4 1.6 %collective-permute-start.8 = (bf16[272,128]{1,0:T(8,128)(2,1)S(1)}, bf16[272,128]{1,0:T(8,128)(2,1)S(1)}, u32[]{:S(2)}, u32[]{:S(2)}) collective-permute-start(bf16[272,128]{1,0:T(8,128)(2,1)S(1)} %middle.1.refs_0_), channel_id=1, source_target_pairs={{0,20},{4,16},{8,28},{12,24},{16,4},{20,0},{24,12},{28,8},{1,21},{... | collective-permute-start | bytes 208904 | tf_op jit(solution)/shard_map/ppermute | solution.py:491
  24.4 2.6 %collective-permute-done.10.refs_1_ = bf16[272,128]{1,0:T(8,128)(2,1)S(1)} collective-permute-done((bf16[272,128]{1,0:T(8,128)(2,1)S(1)}, bf16[272,128]{1,0:T(8,128)(2,1)S(1)}, u32[]{:S(2)}, u32[]{:S(2)}) %collective-permute-start.10) | collective-permute-done | bytes 69664 | tf_op jit(solution)/shard_map/ppermute | solution.py:491
  27.1 1.2 %collective-permute-done.8.refs_0_ = bf16[272,128]{1,0:T(8,128)(2,1)S(1)} collective-permute-done((bf16[272,128]{1,0:T(8,128)(2,1)S(1)}, bf16[272,128]{1,0:T(8,128)(2,1)S(1)}, u32[]{:S(2)}, u32[]{:S(2)}) %collective-permute-start.8) | collective-permute-done | bytes 69664 | tf_op jit(solution)/shard_map/ppermute | solution.py:491
  28.8 1.1 %collective-permute-done.11.refs_2_.refs_0_ = bf16[2,272,128]{2,1,0:T(8,128)(2,1)S(1)} collective-permute-done((bf16[2,272,128]{2,1,0:T(8,128)(2,1)S(1)}, bf16[2,272,128]{2,1,0:T(8,128)(2,1)S(1)}, u32[]{:S(2)}, u32[]{:S(2)}) %collective-permute-start.11) | collective-permute-done | bytes 139296 | tf_op jit(solution)/shard_map/ppermute | solution.py:491
  30.8 2.1 %collective-permute-start.13 = (bf16[272,128]{1,0:T(8,128)(2,1)S(1)}, bf16[272,128]{1,0:T(8,128)(2,1)S(1)}, u32[]{:S(2)}, u32[]{:S(2)}) collective-permute-start(bf16[272,128]{1,0:T(8,128)(2,1)S(1)} %get-tuple-element.34), channel_id=1, source_target_pairs={{0,3},{1,2},{2,1},{3,0},{4,7},{5,6},{6,5},{7,4},{8,11},{9,10},{10,... | collective-permute-start | bytes 208904 | tf_op jit(solution)/shard_map/ppermute | solution.py:491
  33.0 2.3 %collective-permute-start.15 = (bf16[272,128]{1,0:T(8,128)(2,1)S(1)}, bf16[272,128]{1,0:T(8,128)(2,1)S(1)}, u32[]{:S(2)}, u32[]{:S(2)}) collective-permute-start(bf16[272,128]{1,0:T(8,128)(2,1)S(1)} %get-tuple-element.36), channel_id=1, source_target_pairs={{0,1},{1,0},{2,3},{3,2},{4,5},{5,4},{6,7},{7,6},{8,9},{9,8},{10,11... | collective-permute-start | bytes 208904 | tf_op jit(solution)/shard_map/ppermute | solution.py:491
  36.3 1.4 %collective-permute-done.13.refs_1_ = bf16[272,128]{1,0:T(8,128)(2,1)S(1)} collective-permute-done((bf16[272,128]{1,0:T(8,128)(2,1)S(1)}, bf16[272,128]{1,0:T(8,128)(2,1)S(1)}, u32[]{:S(2)}, u32[]{:S(2)}) %collective-permute-start.13) | collective-permute-done | bytes 69664 | tf_op jit(solution)/shard_map/ppermute | solution.py:491
  37.7 2.1 %collective-permute-done.14.refs_2_ = bf16[272,128]{1,0:T(8,128)(2,1)S(1)} collective-permute-done((bf16[272,128]{1,0:T(8,128)(2,1)S(1)}, bf16[272,128]{1,0:T(8,128)(2,1)S(1)}, u32[]{:S(2)}, u32[]{:S(2)}) %collective-permute-start.14) | collective-permute-done | bytes 69664 | tf_op jit(solution)/shard_map/ppermute | solution.py:491
  40.4 2.3 %collective-permute-start.17 = (f32[64,128]{1,0:T(8,128)S(1)}, f32[64,128]{1,0:T(8,128)S(1)}, u32[]{:S(2)}, u32[]{:S(2)}) collective-permute-start(f32[64,128]{1,0:T(8,128)S(1)} %get-tuple-element.38.refs_0_), channel_id=1, source_target_pairs={{0,7},{1,6},{2,5},{3,4},{4,3},{5,2},{6,1},{7,0},{8,15},{9,14},{10,... | collective-permute-start | bytes 98312 | tf_op jit(solution)/shard_map/ppermute | solution.py:501
  43.2 2.5 %collective-permute-done.16.refs_1_ = f32[64,128]{1,0:T(8,128)S(1)} collective-permute-done((f32[64,128]{1,0:T(8,128)S(1)}, f32[64,128]{1,0:T(8,128)S(1)}, u32[]{:S(2)}, u32[]{:S(2)}) %collective-permute-start.16) | collective-permute-done | bytes 32800 | tf_op jit(solution)/shard_map/ppermute | solution.py:501
  45.7 1.0 %collective-permute-done.18.refs_3_ = f32[64,128]{1,0:T(8,128)S(1)} collective-permute-done((f32[64,128]{1,0:T(8,128)S(1)}, f32[64,128]{1,0:T(8,128)S(1)}, u32[]{:S(2)}, u32[]{:S(2)}) %collective-permute-start.18) | collective-permute-done | bytes 32800 | tf_op jit(solution)/shard_map/ppermute | solution.py:501
  46.7 1.5 %collective-permute-start.19 = (f32[32,128]{1,0:T(8,128)S(1)}, f32[32,128]{1,0:T(8,128)S(1)}, u32[]{:S(2)}, u32[]{:S(2)}) collective-permute-start(f32[32,128]{1,0:T(8,128)S(1)} %get-tuple-element.40.refs_0_), channel_id=1, source_target_pairs={{0,28},{4,24},{8,20},{12,16},{16,12},{20,8},{24,4},{28,0},{1,29},{... | collective-permute-start | bytes 49160 | tf_op jit(solution)/shard_map/ppermute | solution.py:491
  48.2 0.9 %collective-permute-start.20 = (f32[32,128]{1,0:T(8,128)S(1)}, f32[32,128]{1,0:T(8,128)S(1)}, u32[]{:S(2)}, u32[]{:S(2)}) collective-permute-start(f32[32,128]{1,0:T(8,128)S(1)} %get-tuple-element.40.refs_0_), channel_id=1, source_target_pairs={{0,20},{4,16},{8,28},{12,24},{16,4},{20,0},{24,12},{28,8},{1,21},{... | collective-permute-start | bytes 49160 | tf_op jit(solution)/shard_map/ppermute | solution.py:491
  49.7 1.5 %first_factor.1.refs_4_.inverse_ref = f32[64,64]{1,0:T(8,128)S(1)} custom-call(f32[32,128]{1,0:T(8,128)S(1)} %get-tuple-element.39.gram_ref), custom_call_target="tpu_custom_call" | custom-call | tf_op jit(solution)/shard_map/first_factor/pallas_call | solution.py:37
  52.4 1.1 %collective-permute-done.22.refs_1_ = f32[32,128]{1,0:T(8,128)S(1)} collective-permute-done((f32[32,128]{1,0:T(8,128)S(1)}, f32[32,128]{1,0:T(8,128)S(1)}, u32[]{:S(2)}, u32[]{:S(2)}) %collective-permute-start.22) | collective-permute-done | bytes 16416 | tf_op jit(solution)/shard_map/ppermute | solution.py:491
  53.4 2.9 %finish.1 = f32[1,8,4096]{2,1,0:T(8,128)} custom-call(f32[256,128]{1,0:T(8,128)S(1)} %get-tuple-element.37.rows_ref, f32[64,64]{1,0:T(8,128)S(1)} %first_factor.1.refs_4_.inverse_ref, f32[32,128]{1,0:T(8,128)S(1)} %add_parts.1.refs_0_, f32[32,128]{1,0:T(8,128)S(1)} %collective-permute-done.22.refs_1_), custom_call_target="tpu_custom_call" | custom-call | tf_op jit(solution)/shard_map/finish/pallas_call | solution.py:37
  (47 shorter events, 10.8 us)
Async XLA Ops:
  1.0 8.7 %copy-start = (s32[4,8,1,8]{3,2,1,0:T(1,128)S(1)}, s32[4,8,1,8]{3,2,1,0:T(1,128)}, u32[]{:S(2)}) copy-start(s32[4,8,1,8]{3,2,1,0:T(1,128)} %param.6) | copy-start | bytes 3076
  1.0 6.5 %collective-permute-start.2 = (bf16[256,128]{1,0:T(8,128)(2,1)S(1)}, bf16[256,128]{1,0:T(8,128)(2,1)S(1)}, u32[]{:S(2)}, u32[]{:S(2)}) collective-permute-start(bf16[256,128]{1,0:T(8,128)(2,1)S(1)} %get-tuple-element.26.refs_0_), channel_id=1, source_target_pairs={{0,28},{4,24},{8,20},{12,16},{16,12},{20,8},{24,4},{28,0},{1,29},{... | collective-permute-start | bytes 196616 | tf_op jit(solution)/shard_map/ppermute | solution.py:491
  4.4 3.9 %collective-permute-start = (bf16[256,128]{1,0:T(8,128)(2,1)S(1)}, bf16[256,128]{1,0:T(8,128)(2,1)S(1)}, u32[]{:S(2)}, u32[]{:S(2)}) collective-permute-start(bf16[256,128]{1,0:T(8,128)(2,1)S(1)} %get-tuple-element.26.refs_0_), channel_id=1, source_target_pairs={{0,20},{4,16},{8,28},{12,24},{16,4},{20,0},{24,12},{28,8},{1,21},{... | collective-permute-start | bytes 196616 | tf_op jit(solution)/shard_map/ppermute | solution.py:491
  5.2 4.3 %collective-permute-start.1 = (bf16[256,128]{1,0:T(8,128)(2,1)S(1)}, bf16[256,128]{1,0:T(8,128)(2,1)S(1)}, u32[]{:S(2)}, u32[]{:S(2)}) collective-permute-start(bf16[256,128]{1,0:T(8,128)(2,1)S(1)} %get-tuple-element.26.refs_0_), channel_id=1, source_target_pairs={{0,12},{4,8},{8,4},{12,0},{16,28},{20,24},{24,20},{28,16},{1,13},{... | collective-permute-start | bytes 196616 | tf_op jit(solution)/shard_map/ppermute | solution.py:491
  7.6 2.4 %collective-permute-start.4 = (bf16[2,256,128]{2,1,0:T(8,128)(2,1)S(1)}, bf16[2,256,128]{2,1,0:T(8,128)(2,1)S(1)}, u32[]{:S(2)}, u32[]{:S(2)}) collective-permute-start(bf16[2,256,128]{2,1,0:T(8,128)(2,1)S(1)} %stack.5.refs_1_.refs_3_), channel_id=1, source_target_pairs={{0,4},{4,0},{8,12},{12,8},{16,20},{20,16},{24,28},{28,24},{1,5},{5... | collective-permute-start | bytes 393224 | tf_op jit(solution)/shard_map/ppermute | solution.py:491
  9.5 1.4 %collective-permute-start.3 = (bf16[2,256,128]{2,1,0:T(8,128)(2,1)S(1)}, bf16[2,256,128]{2,1,0:T(8,128)(2,1)S(1)}, u32[]{:S(2)}, u32[]{:S(2)}) collective-permute-start(bf16[2,256,128]{2,1,0:T(8,128)(2,1)S(1)} %stack.4.refs_0_.refs_2_), channel_id=1, source_target_pairs={{0,4},{4,0},{8,12},{12,8},{16,20},{20,16},{24,28},{28,24},{1,5},{5... | collective-permute-start | bytes 393224 | tf_op jit(solution)/shard_map/ppermute | solution.py:491
  11.8 6.5 %collective-permute-start.5 = (bf16[256,128]{1,0:T(8,128)(2,1)S(1)}, bf16[256,128]{1,0:T(8,128)(2,1)S(1)}, u32[]{:S(2)}, u32[]{:S(2)}) collective-permute-start(bf16[256,128]{1,0:T(8,128)(2,1)S(1)} %get-tuple-element.29), channel_id=1, source_target_pairs={{0,3},{1,2},{2,1},{3,0},{4,7},{5,6},{6,5},{7,4},{8,11},{9,10},{10,... | collective-permute-start | bytes 196616 | tf_op jit(solution)/shard_map/ppermute | solution.py:491
  15.5 5.9 %collective-permute-start.6 = (bf16[256,128]{1,0:T(8,128)(2,1)S(1)}, bf16[256,128]{1,0:T(8,128)(2,1)S(1)}, u32[]{:S(2)}, u32[]{:S(2)}) collective-permute-start(bf16[256,128]{1,0:T(8,128)(2,1)S(1)} %get-tuple-element.30), channel_id=1, source_target_pairs={{0,2},{1,3},{2,0},{3,1},{4,6},{5,7},{6,4},{7,5},{8,10},{9,11},{10,... | collective-permute-start | bytes 196616 | tf_op jit(solution)/shard_map/ppermute | solution.py:491
  15.5 5.9 %collective-permute-start.7 = (bf16[256,128]{1,0:T(8,128)(2,1)S(1)}, bf16[256,128]{1,0:T(8,128)(2,1)S(1)}, u32[]{:S(2)}, u32[]{:S(2)}) collective-permute-start(bf16[256,128]{1,0:T(8,128)(2,1)S(1)} %get-tuple-element.31), channel_id=1, source_target_pairs={{0,1},{1,0},{2,3},{3,2},{4,5},{5,4},{6,7},{7,6},{8,9},{9,8},{10,11... | collective-permute-start | bytes 196616 | tf_op jit(solution)/shard_map/ppermute | solution.py:491
  21.5 5.4 %collective-permute-start.10 = (bf16[272,128]{1,0:T(8,128)(2,1)S(1)}, bf16[272,128]{1,0:T(8,128)(2,1)S(1)}, u32[]{:S(2)}, u32[]{:S(2)}) collective-permute-start(bf16[272,128]{1,0:T(8,128)(2,1)S(1)} %middle.1.refs_0_), channel_id=1, source_target_pairs={{0,28},{4,24},{8,20},{12,16},{16,12},{20,8},{24,4},{28,0},{1,29},{... | collective-permute-start | bytes 208904 | tf_op jit(solution)/shard_map/ppermute | solution.py:491
  22.4 5.8 %collective-permute-start.8 = (bf16[272,128]{1,0:T(8,128)(2,1)S(1)}, bf16[272,128]{1,0:T(8,128)(2,1)S(1)}, u32[]{:S(2)}, u32[]{:S(2)}) collective-permute-start(bf16[272,128]{1,0:T(8,128)(2,1)S(1)} %middle.1.refs_0_), channel_id=1, source_target_pairs={{0,20},{4,16},{8,28},{12,24},{16,4},{20,0},{24,12},{28,8},{1,21},{... | collective-permute-start | bytes 208904 | tf_op jit(solution)/shard_map/ppermute | solution.py:491
  24.1 4.4 %collective-permute-start.9 = (bf16[272,128]{1,0:T(8,128)(2,1)S(1)}, bf16[272,128]{1,0:T(8,128)(2,1)S(1)}, u32[]{:S(2)}, u32[]{:S(2)}) collective-permute-start(bf16[272,128]{1,0:T(8,128)(2,1)S(1)} %middle.1.refs_0_), channel_id=1, source_target_pairs={{0,12},{4,8},{8,4},{12,0},{16,28},{20,24},{24,20},{28,16},{1,13},{... | collective-permute-start | bytes 208904 | tf_op jit(solution)/shard_map/ppermute | solution.py:491
  27.0 1.8 %collective-permute-start.12 = (bf16[2,272,128]{2,1,0:T(8,128)(2,1)S(1)}, bf16[2,272,128]{2,1,0:T(8,128)(2,1)S(1)}, u32[]{:S(2)}, u32[]{:S(2)}) collective-permute-start(bf16[2,272,128]{2,1,0:T(8,128)(2,1)S(1)} %stack.7.refs_1_.refs_3_), channel_id=1, source_target_pairs={{0,4},{4,0},{8,12},{12,8},{16,20},{20,16},{24,28},{28,24},{1,5},{5... | collective-permute-start | bytes 417800 | tf_op jit(solution)/shard_map/ppermute | solution.py:491
  28.5 1.4 %collective-permute-start.11 = (bf16[2,272,128]{2,1,0:T(8,128)(2,1)S(1)}, bf16[2,272,128]{2,1,0:T(8,128)(2,1)S(1)}, u32[]{:S(2)}, u32[]{:S(2)}) collective-permute-start(bf16[2,272,128]{2,1,0:T(8,128)(2,1)S(1)} %stack.6.refs_0_.refs_2_), channel_id=1, source_target_pairs={{0,4},{4,0},{8,12},{12,8},{16,20},{20,16},{24,28},{28,24},{1,5},{5... | collective-permute-start | bytes 417800 | tf_op jit(solution)/shard_map/ppermute | solution.py:491
  30.8 6.9 %collective-permute-start.13 = (bf16[272,128]{1,0:T(8,128)(2,1)S(1)}, bf16[272,128]{1,0:T(8,128)(2,1)S(1)}, u32[]{:S(2)}, u32[]{:S(2)}) collective-permute-start(bf16[272,128]{1,0:T(8,128)(2,1)S(1)} %get-tuple-element.34), channel_id=1, source_target_pairs={{0,3},{1,2},{2,1},{3,0},{4,7},{5,6},{6,5},{7,4},{8,11},{9,10},{10,... | collective-permute-start | bytes 208904 | tf_op jit(solution)/shard_map/ppermute | solution.py:491
  32.9 6.9 %collective-permute-start.14 = (bf16[272,128]{1,0:T(8,128)(2,1)S(1)}, bf16[272,128]{1,0:T(8,128)(2,1)S(1)}, u32[]{:S(2)}, u32[]{:S(2)}) collective-permute-start(bf16[272,128]{1,0:T(8,128)(2,1)S(1)} %get-tuple-element.35), channel_id=1, source_target_pairs={{0,2},{1,3},{2,0},{3,1},{4,6},{5,7},{6,4},{7,5},{8,10},{9,11},{10,... | collective-permute-start | bytes 208904 | tf_op jit(solution)/shard_map/ppermute | solution.py:491
  33.0 6.9 %collective-permute-start.15 = (bf16[272,128]{1,0:T(8,128)(2,1)S(1)}, bf16[272,128]{1,0:T(8,128)(2,1)S(1)}, u32[]{:S(2)}, u32[]{:S(2)}) collective-permute-start(bf16[272,128]{1,0:T(8,128)(2,1)S(1)} %get-tuple-element.36), channel_id=1, source_target_pairs={{0,1},{1,0},{2,3},{3,2},{4,5},{5,4},{6,7},{7,6},{8,9},{9,8},{10,11... | collective-permute-start | bytes 208904 | tf_op jit(solution)/shard_map/ppermute | solution.py:491
  40.3 5.4 %collective-permute-start.16 = (f32[64,128]{1,0:T(8,128)S(1)}, f32[64,128]{1,0:T(8,128)S(1)}, u32[]{:S(2)}, u32[]{:S(2)}) collective-permute-start(f32[64,128]{1,0:T(8,128)S(1)} %get-tuple-element.38.refs_0_), channel_id=1, source_target_pairs={{0,6},{1,7},{2,4},{3,5},{4,2},{5,3},{6,0},{7,1},{8,14},{9,15},{10,... | collective-permute-start | bytes 98312 | tf_op jit(solution)/shard_map/ppermute | solution.py:501
  40.4 5.3 %collective-permute-start.17 = (f32[64,128]{1,0:T(8,128)S(1)}, f32[64,128]{1,0:T(8,128)S(1)}, u32[]{:S(2)}, u32[]{:S(2)}) collective-permute-start(f32[64,128]{1,0:T(8,128)S(1)} %get-tuple-element.38.refs_0_), channel_id=1, source_target_pairs={{0,7},{1,6},{2,5},{3,4},{4,3},{5,2},{6,1},{7,0},{8,15},{9,14},{10,... | collective-permute-start | bytes 98312 | tf_op jit(solution)/shard_map/ppermute | solution.py:501
  42.7 4.0 %collective-permute-start.18 = (f32[64,128]{1,0:T(8,128)S(1)}, f32[64,128]{1,0:T(8,128)S(1)}, u32[]{:S(2)}, u32[]{:S(2)}) collective-permute-start(f32[64,128]{1,0:T(8,128)S(1)} %get-tuple-element.38.refs_0_), channel_id=1, source_target_pairs={{0,5},{1,4},{2,7},{3,6},{4,1},{5,0},{6,3},{7,2},{8,13},{9,12},{10,... | collective-permute-start | bytes 98312 | tf_op jit(solution)/shard_map/ppermute | solution.py:501
  46.7 4.5 %collective-permute-start.19 = (f32[32,128]{1,0:T(8,128)S(1)}, f32[32,128]{1,0:T(8,128)S(1)}, u32[]{:S(2)}, u32[]{:S(2)}) collective-permute-start(f32[32,128]{1,0:T(8,128)S(1)} %get-tuple-element.40.refs_0_), channel_id=1, source_target_pairs={{0,28},{4,24},{8,20},{12,16},{16,12},{20,8},{24,4},{28,0},{1,29},{... | collective-permute-start | bytes 49160 | tf_op jit(solution)/shard_map/ppermute | solution.py:491
  48.2 3.2 %collective-permute-start.20 = (f32[32,128]{1,0:T(8,128)S(1)}, f32[32,128]{1,0:T(8,128)S(1)}, u32[]{:S(2)}, u32[]{:S(2)}) collective-permute-start(f32[32,128]{1,0:T(8,128)S(1)} %get-tuple-element.40.refs_0_), channel_id=1, source_target_pairs={{0,20},{4,16},{8,28},{12,24},{16,4},{20,0},{24,12},{28,8},{1,21},{... | collective-permute-start | bytes 49160 | tf_op jit(solution)/shard_map/ppermute | solution.py:491
  49.1 3.2 %collective-permute-start.21 = (f32[32,128]{1,0:T(8,128)S(1)}, f32[32,128]{1,0:T(8,128)S(1)}, u32[]{:S(2)}, u32[]{:S(2)}) collective-permute-start(f32[32,128]{1,0:T(8,128)S(1)} %get-tuple-element.40.refs_0_), channel_id=1, source_target_pairs={{0,12},{4,8},{8,4},{12,0},{16,28},{20,24},{24,20},{28,16},{1,13},{... | collective-permute-start | bytes 49160 | tf_op jit(solution)/shard_map/ppermute | solution.py:491
  52.3 1.2 %collective-permute-start.22 = (f32[32,128]{1,0:T(8,128)S(1)}, f32[32,128]{1,0:T(8,128)S(1)}, u32[]{:S(2)}, u32[]{:S(2)}) collective-permute-start(f32[32,128]{1,0:T(8,128)S(1)} %add_parts.1.refs_0_), channel_id=1, source_target_pairs={{0,4},{4,0},{8,12},{12,8},{16,20},{20,16},{24,28},{28,24},{1,5},{5... | collective-permute-start | bytes 49160 | tf_op jit(solution)/shard_map/ppermute | solution.py:491
  (1 other events, 8.7 us)

commit v13 on v12

--- a/solution.py
+++ b/solution.py
@@ -46,9 +46,8 @@
     )(*operands)
 
 
-def start_kernel(panel_hbm, inv_hbm, scaled_ref, degree_ref, panel_ref, inv_ref, scratch, sems):
-    block_rows, block_size = inv_ref.shape[1], inv_ref.shape[2]
-    half = block_size // 2
+def start_kernel(panel_hbm, inv_hbm, scaled_ref, panel_ref, inv_ref, scratch, sems):
+    block_rows, half = inv_ref.shape[1], inv_ref.shape[2] // 2
     copies = [
         pltpu.make_async_copy(inv_hbm, inv_ref, sems.at[0]),
         pltpu.make_async_copy(panel_hbm, panel_ref, sems.at[1]),
@@ -56,22 +55,22 @@
     for copy in copies:
         copy.start()
     copies[0].wait()
-    pair = iota((half, block_size), 1) // 2 == iota((half, block_size), 0)
-    spread = (iota((block_size, 128), 0) % 2 == iota((block_size, 128), 1) // 64).astype(F32)
-    rows = [
-        jnp.where(pair, jnp.broadcast_to(inv_ref[0, i : i + 1, :], (half, block_size)), 0.0)
-        for i in range(block_rows)
-    ]
-    degree_ref[...] = jnp.dot(
-        jnp.concatenate(rows, axis=0), spread, precision=HIGHEST, preferred_element_type=F32
-    )
+    inv = inv_ref[0]
+    low = iota((block_rows, 128), 1) < 64
+    scales = []
+    for t in range(half):
+        even, odd = (
+            jnp.broadcast_to(inv[:, a : a + 1], (block_rows, 128)) for a in (2 * t, 2 * t + 1)
+        )
+        scales.append(jnp.where(low, even, odd))
     copies[1].wait()
     for t in range(half):
-        scratch[t * block_rows : (t + 1) * block_rows, :] = panel_ref[0, :, t * 128 : (t + 1) * 128]
+        scratch[t * block_rows : (t + 1) * block_rows, :] = (
+            panel_ref[0, :, t * 128 : (t + 1) * 128] * scales[t]
+        )
     for i in range(block_rows):
-        where = slice(i * half, (i + 1) * half)
-        part = scratch[pl.ds(i, half, stride=block_rows), :] * degree_ref[where, :]
-        scaled_ref[where, :] = part.astype(BF16)
+        part = scratch[pl.ds(i, half, stride=block_rows), :]
+        scaled_ref[i * half : (i + 1) * half, :] = part.astype(BF16)
 
 
 def start(panel, inv_degree):
@@ -81,7 +80,7 @@
         start_kernel,
         "start",
         [hbm(), hbm()],
-        (shaped(shape, BF16), shaped(shape, F32)),
+        shaped(shape, BF16),
         (panel, inv_degree),
         [
             pltpu.VMEM(panel.shape, F32),
@@ -92,9 +91,25 @@
     )
 
 
-def prep_kernel(
-    ranges, affinity_hbm, inv_hbm, out_ref, inverse_ref, affinity_ref, inv_ref, scratch, sems, inv_sem
-):
+def prepare_scales(inv, degree_ref, inverse_ref):
+    block_rows, block_size = inv.shape
+    half = block_size // 2
+    pair = iota((half, block_size), 1) // 2 == iota((half, block_size), 0)
+    spread = (iota((block_size, 128), 0) % 2 == iota((block_size, 128), 1) // 64).astype(F32)
+    rows = [
+        jnp.where(pair, jnp.broadcast_to(inv[i : i + 1, :], (half, block_size)), 0.0)
+        for i in range(block_rows)
+    ]
+    degree_ref[...] = jnp.dot(
+        jnp.concatenate(rows, axis=0), spread, precision=HIGHEST, preferred_element_type=F32
+    )
+    inverse = 1.0 / inv
+    high = inverse.astype(BF16).astype(F32)
+    inverse_ref[...] = jnp.concatenate([high, inverse - high], axis=1)
+
+
+def prep_kernel(ranges, affinity_hbm, *refs):
+    *scale_refs, out_ref, affinity_ref, inv_ref, scratch, sems = refs
     count, block_rows, _, slots, flat = affinity_ref.shape
     half = flat // 128
     own = lax.axis_index("cols")
@@ -102,17 +117,17 @@
         pltpu.make_async_copy(affinity_hbm.at[m ^ own], affinity_ref.at[place], sems.at[place])
         for place, m in enumerate(ranges)
     ]
-    inv_copy = pltpu.make_async_copy(inv_hbm, inv_ref, inv_sem)
-    inv_copy.start()
+    if scale_refs:
+        inv_copy = pltpu.make_async_copy(scale_refs[0], inv_ref, sems.at[count])
+        inv_copy.start()
     for copy in copies:
         copy.start()
     source, target = iota((256, 256), 0), iota((256, 256), 1)
     moved = (source // 64 % 2) * 128 + (source // 128) * 64 + (source % 2) * 32 + source % 64 // 2
     permute = (moved == target).astype(BF16)
-    inv_copy.wait()
-    inverse = 1.0 / inv_ref[0]
-    high = inverse.astype(BF16).astype(F32)
-    inverse_ref[...] = jnp.concatenate([high, inverse - high], axis=1)
+    if scale_refs:
+        inv_copy.wait()
+        prepare_scales(inv_ref[0], *scale_refs[1:])
     for m in range(count):
         copies[m].wait()
         for i in range(block_rows):
@@ -132,21 +147,23 @@
                 out_ref[m, i, half:, s * 128 : (s + 1) * 128] = piece[:, 128:]
 
 
-def prep(ranges, affinity, inv_degree):
+def prep(ranges, affinity, *scale_from):
     _, block_rows, _, slots, flat = affinity.shape
     count = len(ranges)
+    outs = [shaped((count, block_rows, 64, slots * 64), BF16)]
+    if scale_from:
+        outs = [shaped((block_rows * 32, 128), F32), shaped((block_rows, 128), F32)] + outs
     return call(
         functools.partial(prep_kernel, ranges),
         "prep",
-        [hbm(), hbm()],
-        (shaped((count, block_rows, 64, slots * 64), BF16), shaped((block_rows, 128), F32)),
-        (affinity, inv_degree),
+        [hbm()] * (1 + len(scale_from)),
+        outs,
+        (affinity, *scale_from),
         [
             pltpu.VMEM((count,) + affinity.shape[1:], BF16),
-            pltpu.VMEM(inv_degree.shape, F32),
+            pltpu.VMEM((1, block_rows, 64), F32),
             pltpu.VMEM((2, flat // 128 * slots, 128), F32),
-            pltpu.SemaphoreType.DMA((count,)),
-            pltpu.SemaphoreType.DMA,
+            pltpu.SemaphoreType.DMA((count + 1,)),
         ],
     )
 
@@ -373,28 +390,27 @@
     def spread(block, row):
         return jnp.broadcast_to(block[row : row + 1], (8, 128))
 
-    current = [columns(0, q) for q in range(8)]
+    ahead = []
     for b in range(blocks):
         count = blocks - b
-        later = []
+        current = ahead + [columns(b, 8 * b + q) for q in range(len(ahead), 8)]
+        ahead = []
         if count > 1:
-            later = [columns(b + 1, 8 * (b + 1) + q) for q in range(8)]
+            ahead = [columns(b + 1, 8 * (b + 1) + q) for q in range(4)]
         for q in range(8):
             root = lax.rsqrt(spread(current[q][0], q))
-            inverse = root * root
-            raw = spread(rows[b], q)
-            scaled = raw * inverse
+            row = spread(rows[b], q) * root
+            column = [x * root for x in current[q]]
             for p in range(q + 1, 8):
-                weight = spread(current[q][0], p) * inverse
-                current[p] = [x - y * weight for x, y in zip(current[p], current[q])]
-            below = rows[b] - current[q][0] * scaled
-            rows[b] = jnp.where(at == q, raw * root, jnp.where(at > q, below, rows[b]))
+                weight = spread(current[q][0], p) * root
+                current[p] = [x - y * weight for x, y in zip(current[p], column)]
+            below = rows[b] - column[0] * row
+            rows[b] = jnp.where(at == q, row, jnp.where(at > q, below, rows[b]))
             for i in range(1, count):
-                rows[b + i] = rows[b + i] - current[q][i] * scaled
-            for p in range(len(later)):
-                weight = spread(current[q][1], p) * inverse
-                later[p] = [x - y * weight for x, y in zip(later[p], current[q][1:])]
-        current = later
+                rows[b + i] = rows[b + i] - column[i] * row
+            for p in range(len(ahead)):
+                weight = spread(current[q][1], p) * root
+                ahead[p] = [x - y * weight for x, y in zip(ahead[p], column[1:])]
     return jnp.concatenate(rows, axis=0)[:, 64:]
 
 
@@ -545,9 +561,9 @@
     )
     ranges = list(range(groups - 1, 0, -1))
 
-    scaled, degree = start(panel, inv_degree)
-    matrix, inverse = prep(ranges, affinity, inv_degree)
-    own_matrix, _ = prep([0], affinity, inv_degree)
+    scaled = start(panel, inv_degree)
+    degree, inverse, matrix = prep(ranges, affinity, inv_degree)
+    (own_matrix,) = prep([0], affinity)
     near, far, offsets = gather_rows(scaled, [inverse])
     table = near_table(offsets, near, block_rows)
     terms, _ = products(offsets, ranges, columns, matrix, own_matrix, near, far, table)

time: 56.5 us -> 56.3 us (level)
  transfers between devices with their start and end apart: 23 -> 23, of which waited for: 15 -> 16; matrix products, arithmetic and copies ran while one was open for 0% -> 0% of each run, Pallas kernels for 13% -> 12%
where the time goes in v13:
time: 56.3 us; the launch traced here: 56.1 us
  starting transfers between devices  22.4 us (40%)
  waiting for transfers between devices  20.6 us (37%)
  Pallas kernels  12.8 us (23%)
    ppermute x20, starting transfers between devices, swap(): lax.ppermute(value, axis, [(index, index ^ mask) for index in range(size)])  19.6 us
    ppermute x20, waiting for transfers between devices, swap(): lax.ppermute(value, axis, [(index, index ^ mask) for index in range(size)])  17 us
    pallas_call x20, Pallas kernels, call(): pl.pallas_call(kernel, out_shape=outs, in_specs=ins, out_specs=jax.tree.m...  12.8 us
    ppermute x3, waiting for transfers between devices, swap_both(): return lax.ppermute(value, ('rows', 'cols'), pairs)  3.57 us
    ppermute x3, starting transfers between devices, swap_both(): return lax.ppermute(value, ('rows', 'cols'), pairs)  2.84 us
  transfers between devices with their start and end apart: 23, of which 16 were waited for; matrix products, arithmetic and copies ran while one was open for 0% of the time, Pallas kernels for 12%

profile of v13, /device:TPU:0, one launch (start us, length us, event | category | flops | bytes accessed | tf_op | source)
XLA Modules:
  0.0 56.1 jit_solution(9613629105345350757)
XLA Ops:
  0.0 1.0 %start.1.refs_0_ = bf16[256,128]{1,0:T(8,128)(2,1)S(1)} custom-call(f32[1,8,4096]{2,1,0:T(8,128)} %panel_hbm.1, f32[1,8,64]{2,1,0:T(8,128)} %inv_hbm.1), custom_call_target="tpu_custom_call" | custom-call | tf_op jit(solution)/shard_map/start/pallas_call | solution.py:37
  1.0 3.4 %collective-permute-start.2 = (bf16[256,128]{1,0:T(8,128)(2,1)S(1)}, bf16[256,128]{1,0:T(8,128)(2,1)S(1)}, u32[]{:S(2)}, u32[]{:S(2)}) collective-permute-start(bf16[256,128]{1,0:T(8,128)(2,1)S(1)} %start.1.refs_0_), channel_id=1, source_target_pairs={{0,28},{4,24},{8,20},{12,16},{16,12},{20,8},{24,4},{28,0},{1,29},{... | collective-permute-start | bytes 196616 | tf_op jit(solution)/shard_map/ppermute | solution.py:507
  5.3 2.3 %prep.2 = (f32[256,128]{1,0:T(8,128)S(1)}, f32[8,128]{1,0:T(8,128)S(1)}, bf16[3,8,64,512]{3,2,1,0:T(8,128)(2,1)S(1)}) custom-call(bf16[4,8,1,8,4096]{4,3,2,1,0:T(8,128)(2,1)} %affinity_hbm.3, f32[1,8,64]{2,1,0:T(8,128)} %inv_hbm.1), custom_call_target="tpu_custom_call" | custom-call | tf_op jit(solution)/shard_map/prep/pallas_call | solution.py:37
  8.3 1.2 %collective-permute-done.1.refs_1_ = bf16[256,128]{1,0:T(8,128)(2,1)S(1)} collective-permute-done((bf16[256,128]{1,0:T(8,128)(2,1)S(1)}, bf16[256,128]{1,0:T(8,128)(2,1)S(1)}, u32[]{:S(2)}, u32[]{:S(2)}) %collective-permute-start.1) | collective-permute-done | bytes 65568 | tf_op jit(solution)/shard_map/ppermute | solution.py:507
  9.9 1.0 %collective-permute-done.3.refs_0_ = bf16[2,256,128]{2,1,0:T(8,128)(2,1)S(1)} collective-permute-done((bf16[2,256,128]{2,1,0:T(8,128)(2,1)S(1)}, bf16[2,256,128]{2,1,0:T(8,128)(2,1)S(1)}, u32[]{:S(2)}, u32[]{:S(2)}) %collective-permute-start.3) | collective-permute-done | bytes 131104 | tf_op jit(solution)/shard_map/ppermute | solution.py:507
  11.8 3.7 %collective-permute-start.5 = (bf16[256,128]{1,0:T(8,128)(2,1)S(1)}, bf16[256,128]{1,0:T(8,128)(2,1)S(1)}, u32[]{:S(2)}, u32[]{:S(2)}) collective-permute-start(bf16[256,128]{1,0:T(8,128)(2,1)S(1)} %get-tuple-element.25), channel_id=1, source_target_pairs={{0,3},{1,2},{2,1},{3,0},{4,7},{5,6},{6,5},{7,4},{8,11},{9,10},{10,... | collective-permute-start | bytes 196616 | tf_op jit(solution)/shard_map/ppermute | solution.py:507
  16.2 1.4 %prep.3.matrix_ref = bf16[1,8,64,512]{3,2,1,0:T(8,128)(2,1)S(1)} custom-call(bf16[4,8,1,8,4096]{4,3,2,1,0:T(8,128)(2,1)} %affinity_hbm.3), custom_call_target="tpu_custom_call" | custom-call | tf_op jit(solution)/shard_map/prep/pallas_call | solution.py:37
  18.1 3.2 %collective-permute-done.6.refs_2_ = bf16[256,128]{1,0:T(8,128)(2,1)S(1)} collective-permute-done((bf16[256,128]{1,0:T(8,128)(2,1)S(1)}, bf16[256,128]{1,0:T(8,128)(2,1)S(1)}, u32[]{:S(2)}, u32[]{:S(2)}) %collective-permute-start.6) | collective-permute-done | bytes 65568 | tf_op jit(solution)/shard_map/ppermute | solution.py:507
  21.5 0.9 %collective-permute-start.10 = (bf16[272,128]{1,0:T(8,128)(2,1)S(1)}, bf16[272,128]{1,0:T(8,128)(2,1)S(1)}, u32[]{:S(2)}, u32[]{:S(2)}) collective-permute-start(bf16[272,128]{1,0:T(8,128)(2,1)S(1)} %middle.1.refs_0_), channel_id=1, source_target_pairs={{0,28},{4,24},{8,20},{12,16},{16,12},{20,8},{24,4},{28,0},{1,29},{... | collective-permute-start | bytes 208904 | tf_op jit(solution)/shard_map/ppermute | solution.py:507
  22.4 1.6 %collective-permute-start.8 = (bf16[272,128]{1,0:T(8,128)(2,1)S(1)}, bf16[272,128]{1,0:T(8,128)(2,1)S(1)}, u32[]{:S(2)}, u32[]{:S(2)}) collective-permute-start(bf16[272,128]{1,0:T(8,128)(2,1)S(1)} %middle.1.refs_0_), channel_id=1, source_target_pairs={{0,20},{4,16},{8,28},{12,24},{16,4},{20,0},{24,12},{28,8},{1,21},{... | collective-permute-start | bytes 208904 | tf_op jit(solution)/shard_map/ppermute | solution.py:507
  24.4 2.6 %collective-permute-done.10.refs_1_ = bf16[272,128]{1,0:T(8,128)(2,1)S(1)} collective-permute-done((bf16[272,128]{1,0:T(8,128)(2,1)S(1)}, bf16[272,128]{1,0:T(8,128)(2,1)S(1)}, u32[]{:S(2)}, u32[]{:S(2)}) %collective-permute-start.10) | collective-permute-done | bytes 69664 | tf_op jit(solution)/shard_map/ppermute | solution.py:507
  27.0 1.2 %collective-permute-done.8.refs_0_ = bf16[272,128]{1,0:T(8,128)(2,1)S(1)} collective-permute-done((bf16[272,128]{1,0:T(8,128)(2,1)S(1)}, bf16[272,128]{1,0:T(8,128)(2,1)S(1)}, u32[]{:S(2)}, u32[]{:S(2)}) %collective-permute-start.8) | collective-permute-done | bytes 69664 | tf_op jit(solution)/shard_map/ppermute | solution.py:507
  28.8 1.1 %collective-permute-done.11.refs_2_.refs_0_ = bf16[2,272,128]{2,1,0:T(8,128)(2,1)S(1)} collective-permute-done((bf16[2,272,128]{2,1,0:T(8,128)(2,1)S(1)}, bf16[2,272,128]{2,1,0:T(8,128)(2,1)S(1)}, u32[]{:S(2)}, u32[]{:S(2)}) %collective-permute-start.11) | collective-permute-done | bytes 139296 | tf_op jit(solution)/shard_map/ppermute | solution.py:507
  30.8 2.2 %collective-permute-start.13 = (bf16[272,128]{1,0:T(8,128)(2,1)S(1)}, bf16[272,128]{1,0:T(8,128)(2,1)S(1)}, u32[]{:S(2)}, u32[]{:S(2)}) collective-permute-start(bf16[272,128]{1,0:T(8,128)(2,1)S(1)} %get-tuple-element.30), channel_id=1, source_target_pairs={{0,3},{1,2},{2,1},{3,0},{4,7},{5,6},{6,5},{7,4},{8,11},{9,10},{10,... | collective-permute-start | bytes 208904 | tf_op jit(solution)/shard_map/ppermute | solution.py:507
  32.9 2.3 %collective-permute-start.15 = (bf16[272,128]{1,0:T(8,128)(2,1)S(1)}, bf16[272,128]{1,0:T(8,128)(2,1)S(1)}, u32[]{:S(2)}, u32[]{:S(2)}) collective-permute-start(bf16[272,128]{1,0:T(8,128)(2,1)S(1)} %get-tuple-element.32), channel_id=1, source_target_pairs={{0,1},{1,0},{2,3},{3,2},{4,5},{5,4},{6,7},{7,6},{8,9},{9,8},{10,11... | collective-permute-start | bytes 208904 | tf_op jit(solution)/shard_map/ppermute | solution.py:507
  36.3 1.4 %collective-permute-done.13.refs_1_ = bf16[272,128]{1,0:T(8,128)(2,1)S(1)} collective-permute-done((bf16[272,128]{1,0:T(8,128)(2,1)S(1)}, bf16[272,128]{1,0:T(8,128)(2,1)S(1)}, u32[]{:S(2)}, u32[]{:S(2)}) %collective-permute-start.13) | collective-permute-done | bytes 69664 | tf_op jit(solution)/shard_map/ppermute | solution.py:507
  37.7 2.1 %collective-permute-done.14.refs_2_ = bf16[272,128]{1,0:T(8,128)(2,1)S(1)} collective-permute-done((bf16[272,128]{1,0:T(8,128)(2,1)S(1)}, bf16[272,128]{1,0:T(8,128)(2,1)S(1)}, u32[]{:S(2)}, u32[]{:S(2)}) %collective-permute-start.14) | collective-permute-done | bytes 69664 | tf_op jit(solution)/shard_map/ppermute | solution.py:507
  40.3 2.4 %collective-permute-start.17 = (f32[64,128]{1,0:T(8,128)S(1)}, f32[64,128]{1,0:T(8,128)S(1)}, u32[]{:S(2)}, u32[]{:S(2)}) collective-permute-start(f32[64,128]{1,0:T(8,128)S(1)} %get-tuple-element.34.refs_0_), channel_id=1, source_target_pairs={{0,7},{1,6},{2,5},{3,4},{4,3},{5,2},{6,1},{7,0},{8,15},{9,14},{10,... | collective-permute-start | bytes 98312 | tf_op jit(solution)/shard_map/ppermute | solution.py:517
  43.2 2.6 %collective-permute-done.16.refs_1_ = f32[64,128]{1,0:T(8,128)S(1)} collective-permute-done((f32[64,128]{1,0:T(8,128)S(1)}, f32[64,128]{1,0:T(8,128)S(1)}, u32[]{:S(2)}, u32[]{:S(2)}) %collective-permute-start.16) | collective-permute-done | bytes 32800 | tf_op jit(solution)/shard_map/ppermute | solution.py:517
  45.7 1.0 %collective-permute-done.18.refs_3_ = f32[64,128]{1,0:T(8,128)S(1)} collective-permute-done((f32[64,128]{1,0:T(8,128)S(1)}, f32[64,128]{1,0:T(8,128)S(1)}, u32[]{:S(2)}, u32[]{:S(2)}) %collective-permute-start.18) | collective-permute-done | bytes 32800 | tf_op jit(solution)/shard_map/ppermute | solution.py:517
  46.7 1.4 %collective-permute-start.19 = (f32[32,128]{1,0:T(8,128)S(1)}, f32[32,128]{1,0:T(8,128)S(1)}, u32[]{:S(2)}, u32[]{:S(2)}) collective-permute-start(f32[32,128]{1,0:T(8,128)S(1)} %get-tuple-element.36.refs_0_), channel_id=1, source_target_pairs={{0,28},{4,24},{8,20},{12,16},{16,12},{20,8},{24,4},{28,0},{1,29},{... | collective-permute-start | bytes 49160 | tf_op jit(solution)/shard_map/ppermute | solution.py:507
  49.7 1.3 %first_factor.1.refs_4_.inverse_ref = f32[64,64]{1,0:T(8,128)S(1)} custom-call(f32[32,128]{1,0:T(8,128)S(1)} %get-tuple-element.35.gram_ref), custom_call_target="tpu_custom_call" | custom-call | tf_op jit(solution)/shard_map/first_factor/pallas_call | solution.py:37
  52.3 1.1 %collective-permute-done.22.refs_1_ = f32[32,128]{1,0:T(8,128)S(1)} collective-permute-done((f32[32,128]{1,0:T(8,128)S(1)}, f32[32,128]{1,0:T(8,128)S(1)}, u32[]{:S(2)}, u32[]{:S(2)}) %collective-permute-start.22) | collective-permute-done | bytes 16416 | tf_op jit(solution)/shard_map/ppermute | solution.py:507
  53.4 2.7 %finish.1 = f32[1,8,4096]{2,1,0:T(8,128)} custom-call(f32[256,128]{1,0:T(8,128)S(1)} %get-tuple-element.33.rows_ref, f32[64,64]{1,0:T(8,128)S(1)} %first_factor.1.refs_4_.inverse_ref, f32[32,128]{1,0:T(8,128)S(1)} %add_parts.1.refs_0_, f32[32,128]{1,0:T(8,128)S(1)} %collective-permute-done.22.refs_1_), custom_call_target="tpu_custom_call" | custom-call | tf_op jit(solution)/shard_map/finish/pallas_call | solution.py:37
  (47 shorter events, 10.9 us)
Async XLA Ops:
  1.0 8.7 %copy-start = (s32[4,8,1,8]{3,2,1,0:T(1,128)S(1)}, s32[4,8,1,8]{3,2,1,0:T(1,128)}, u32[]{:S(2)}) copy-start(s32[4,8,1,8]{3,2,1,0:T(1,128)} %param.6) | copy-start | bytes 3076
  1.0 6.6 %collective-permute-start.2 = (bf16[256,128]{1,0:T(8,128)(2,1)S(1)}, bf16[256,128]{1,0:T(8,128)(2,1)S(1)}, u32[]{:S(2)}, u32[]{:S(2)}) collective-permute-start(bf16[256,128]{1,0:T(8,128)(2,1)S(1)} %start.1.refs_0_), channel_id=1, source_target_pairs={{0,28},{4,24},{8,20},{12,16},{16,12},{20,8},{24,4},{28,0},{1,29},{... | collective-permute-start | bytes 196616 | tf_op jit(solution)/shard_map/ppermute | solution.py:507
  4.4 3.9 %collective-permute-start = (bf16[256,128]{1,0:T(8,128)(2,1)S(1)}, bf16[256,128]{1,0:T(8,128)(2,1)S(1)}, u32[]{:S(2)}, u32[]{:S(2)}) collective-permute-start(bf16[256,128]{1,0:T(8,128)(2,1)S(1)} %start.1.refs_0_), channel_id=1, source_target_pairs={{0,20},{4,16},{8,28},{12,24},{16,4},{20,0},{24,12},{28,8},{1,21},{... | collective-permute-start | bytes 196616 | tf_op jit(solution)/shard_map/ppermute | solution.py:507
  5.2 4.3 %collective-permute-start.1 = (bf16[256,128]{1,0:T(8,128)(2,1)S(1)}, bf16[256,128]{1,0:T(8,128)(2,1)S(1)}, u32[]{:S(2)}, u32[]{:S(2)}) collective-permute-start(bf16[256,128]{1,0:T(8,128)(2,1)S(1)} %start.1.refs_0_), channel_id=1, source_target_pairs={{0,12},{4,8},{8,4},{12,0},{16,28},{20,24},{24,20},{28,16},{1,13},{... | collective-permute-start | bytes 196616 | tf_op jit(solution)/shard_map/ppermute | solution.py:507
  7.7 2.3 %collective-permute-start.4 = (bf16[2,256,128]{2,1,0:T(8,128)(2,1)S(1)}, bf16[2,256,128]{2,1,0:T(8,128)(2,1)S(1)}, u32[]{:S(2)}, u32[]{:S(2)}) collective-permute-start(bf16[2,256,128]{2,1,0:T(8,128)(2,1)S(1)} %stack.5.refs_1_.refs_3_), channel_id=1, source_target_pairs={{0,4},{4,0},{8,12},{12,8},{16,20},{20,16},{24,28},{28,24},{1,5},{5... | collective-permute-start | bytes 393224 | tf_op jit(solution)/shard_map/ppermute | solution.py:507
  9.5 1.4 %collective-permute-start.3 = (bf16[2,256,128]{2,1,0:T(8,128)(2,1)S(1)}, bf16[2,256,128]{2,1,0:T(8,128)(2,1)S(1)}, u32[]{:S(2)}, u32[]{:S(2)}) collective-permute-start(bf16[2,256,128]{2,1,0:T(8,128)(2,1)S(1)} %stack.4.refs_0_.refs_2_), channel_id=1, source_target_pairs={{0,4},{4,0},{8,12},{12,8},{16,20},{20,16},{24,28},{28,24},{1,5},{5... | collective-permute-start | bytes 393224 | tf_op jit(solution)/shard_map/ppermute | solution.py:507
  11.8 6.4 %collective-permute-start.5 = (bf16[256,128]{1,0:T(8,128)(2,1)S(1)}, bf16[256,128]{1,0:T(8,128)(2,1)S(1)}, u32[]{:S(2)}, u32[]{:S(2)}) collective-permute-start(bf16[256,128]{1,0:T(8,128)(2,1)S(1)} %get-tuple-element.25), channel_id=1, source_target_pairs={{0,3},{1,2},{2,1},{3,0},{4,7},{5,6},{6,5},{7,4},{8,11},{9,10},{10,... | collective-permute-start | bytes 196616 | tf_op jit(solution)/shard_map/ppermute | solution.py:507
  15.4 5.9 %collective-permute-start.6 = (bf16[256,128]{1,0:T(8,128)(2,1)S(1)}, bf16[256,128]{1,0:T(8,128)(2,1)S(1)}, u32[]{:S(2)}, u32[]{:S(2)}) collective-permute-start(bf16[256,128]{1,0:T(8,128)(2,1)S(1)} %get-tuple-element.26), channel_id=1, source_target_pairs={{0,2},{1,3},{2,0},{3,1},{4,6},{5,7},{6,4},{7,5},{8,10},{9,11},{10,... | collective-permute-start | bytes 196616 | tf_op jit(solution)/shard_map/ppermute | solution.py:507
  15.4 5.9 %collective-permute-start.7 = (bf16[256,128]{1,0:T(8,128)(2,1)S(1)}, bf16[256,128]{1,0:T(8,128)(2,1)S(1)}, u32[]{:S(2)}, u32[]{:S(2)}) collective-permute-start(bf16[256,128]{1,0:T(8,128)(2,1)S(1)} %get-tuple-element.27), channel_id=1, source_target_pairs={{0,1},{1,0},{2,3},{3,2},{4,5},{5,4},{6,7},{7,6},{8,9},{9,8},{10,11... | collective-permute-start | bytes 196616 | tf_op jit(solution)/shard_map/ppermute | solution.py:507
  21.5 5.4 %collective-permute-start.10 = (bf16[272,128]{1,0:T(8,128)(2,1)S(1)}, bf16[272,128]{1,0:T(8,128)(2,1)S(1)}, u32[]{:S(2)}, u32[]{:S(2)}) collective-permute-start(bf16[272,128]{1,0:T(8,128)(2,1)S(1)} %middle.1.refs_0_), channel_id=1, source_target_pairs={{0,28},{4,24},{8,20},{12,16},{16,12},{20,8},{24,4},{28,0},{1,29},{... | collective-permute-start | bytes 208904 | tf_op jit(solution)/shard_map/ppermute | solution.py:507
  22.4 5.8 %collective-permute-start.8 = (bf16[272,128]{1,0:T(8,128)(2,1)S(1)}, bf16[272,128]{1,0:T(8,128)(2,1)S(1)}, u32[]{:S(2)}, u32[]{:S(2)}) collective-permute-start(bf16[272,128]{1,0:T(8,128)(2,1)S(1)} %middle.1.refs_0_), channel_id=1, source_target_pairs={{0,20},{4,16},{8,28},{12,24},{16,4},{20,0},{24,12},{28,8},{1,21},{... | collective-permute-start | bytes 208904 | tf_op jit(solution)/shard_map/ppermute | solution.py:507
  24.1 4.4 %collective-permute-start.9 = (bf16[272,128]{1,0:T(8,128)(2,1)S(1)}, bf16[272,128]{1,0:T(8,128)(2,1)S(1)}, u32[]{:S(2)}, u32[]{:S(2)}) collective-permute-start(bf16[272,128]{1,0:T(8,128)(2,1)S(1)} %middle.1.refs_0_), channel_id=1, source_target_pairs={{0,12},{4,8},{8,4},{12,0},{16,28},{20,24},{24,20},{28,16},{1,13},{... | collective-permute-start | bytes 208904 | tf_op jit(solution)/shard_map/ppermute | solution.py:507
  27.0 1.8 %collective-permute-start.12 = (bf16[2,272,128]{2,1,0:T(8,128)(2,1)S(1)}, bf16[2,272,128]{2,1,0:T(8,128)(2,1)S(1)}, u32[]{:S(2)}, u32[]{:S(2)}) collective-permute-start(bf16[2,272,128]{2,1,0:T(8,128)(2,1)S(1)} %stack.7.refs_1_.refs_3_), channel_id=1, source_target_pairs={{0,4},{4,0},{8,12},{12,8},{16,20},{20,16},{24,28},{28,24},{1,5},{5... | collective-permute-start | bytes 417800 | tf_op jit(solution)/shard_map/ppermute | solution.py:507
  28.5 1.4 %collective-permute-start.11 = (bf16[2,272,128]{2,1,0:T(8,128)(2,1)S(1)}, bf16[2,272,128]{2,1,0:T(8,128)(2,1)S(1)}, u32[]{:S(2)}, u32[]{:S(2)}) collective-permute-start(bf16[2,272,128]{2,1,0:T(8,128)(2,1)S(1)} %stack.6.refs_0_.refs_2_), channel_id=1, source_target_pairs={{0,4},{4,0},{8,12},{12,8},{16,20},{20,16},{24,28},{28,24},{1,5},{5... | collective-permute-start | bytes 417800 | tf_op jit(solution)/shard_map/ppermute | solution.py:507
  30.8 6.9 %collective-permute-start.13 = (bf16[272,128]{1,0:T(8,128)(2,1)S(1)}, bf16[272,128]{1,0:T(8,128)(2,1)S(1)}, u32[]{:S(2)}, u32[]{:S(2)}) collective-permute-start(bf16[272,128]{1,0:T(8,128)(2,1)S(1)} %get-tuple-element.30), channel_id=1, source_target_pairs={{0,3},{1,2},{2,1},{3,0},{4,7},{5,6},{6,5},{7,4},{8,11},{9,10},{10,... | collective-permute-start | bytes 208904 | tf_op jit(solution)/shard_map/ppermute | solution.py:507
  32.9 6.9 %collective-permute-start.14 = (bf16[272,128]{1,0:T(8,128)(2,1)S(1)}, bf16[272,128]{1,0:T(8,128)(2,1)S(1)}, u32[]{:S(2)}, u32[]{:S(2)}) collective-permute-start(bf16[272,128]{1,0:T(8,128)(2,1)S(1)} %get-tuple-element.31), channel_id=1, source_target_pairs={{0,2},{1,3},{2,0},{3,1},{4,6},{5,7},{6,4},{7,5},{8,10},{9,11},{10,... | collective-permute-start | bytes 208904 | tf_op jit(solution)/shard_map/ppermute | solution.py:507
  32.9 6.9 %collective-permute-start.15 = (bf16[272,128]{1,0:T(8,128)(2,1)S(1)}, bf16[272,128]{1,0:T(8,128)(2,1)S(1)}, u32[]{:S(2)}, u32[]{:S(2)}) collective-permute-start(bf16[272,128]{1,0:T(8,128)(2,1)S(1)} %get-tuple-element.32), channel_id=1, source_target_pairs={{0,1},{1,0},{2,3},{3,2},{4,5},{5,4},{6,7},{7,6},{8,9},{9,8},{10,11... | collective-permute-start | bytes 208904 | tf_op jit(solution)/shard_map/ppermute | solution.py:507
  40.3 5.4 %collective-permute-start.16 = (f32[64,128]{1,0:T(8,128)S(1)}, f32[64,128]{1,0:T(8,128)S(1)}, u32[]{:S(2)}, u32[]{:S(2)}) collective-permute-start(f32[64,128]{1,0:T(8,128)S(1)} %get-tuple-element.34.refs_0_), channel_id=1, source_target_pairs={{0,6},{1,7},{2,4},{3,5},{4,2},{5,3},{6,0},{7,1},{8,14},{9,15},{10,... | collective-permute-start | bytes 98312 | tf_op jit(solution)/shard_map/ppermute | solution.py:517
  40.3 5.4 %collective-permute-start.17 = (f32[64,128]{1,0:T(8,128)S(1)}, f32[64,128]{1,0:T(8,128)S(1)}, u32[]{:S(2)}, u32[]{:S(2)}) collective-permute-start(f32[64,128]{1,0:T(8,128)S(1)} %get-tuple-element.34.refs_0_), channel_id=1, source_target_pairs={{0,7},{1,6},{2,5},{3,4},{4,3},{5,2},{6,1},{7,0},{8,15},{9,14},{10,... | collective-permute-start | bytes 98312 | tf_op jit(solution)/shard_map/ppermute | solution.py:517
  42.7 4.0 %collective-permute-start.18 = (f32[64,128]{1,0:T(8,128)S(1)}, f32[64,128]{1,0:T(8,128)S(1)}, u32[]{:S(2)}, u32[]{:S(2)}) collective-permute-start(f32[64,128]{1,0:T(8,128)S(1)} %get-tuple-element.34.refs_0_), channel_id=1, source_target_pairs={{0,5},{1,4},{2,7},{3,6},{4,1},{5,0},{6,3},{7,2},{8,13},{9,12},{10,... | collective-permute-start | bytes 98312 | tf_op jit(solution)/shard_map/ppermute | solution.py:517
  46.7 4.3 %collective-permute-start.19 = (f32[32,128]{1,0:T(8,128)S(1)}, f32[32,128]{1,0:T(8,128)S(1)}, u32[]{:S(2)}, u32[]{:S(2)}) collective-permute-start(f32[32,128]{1,0:T(8,128)S(1)} %get-tuple-element.36.refs_0_), channel_id=1, source_target_pairs={{0,28},{4,24},{8,20},{12,16},{16,12},{20,8},{24,4},{28,0},{1,29},{... | collective-permute-start | bytes 49160 | tf_op jit(solution)/shard_map/ppermute | solution.py:507
  48.2 3.2 %collective-permute-start.20 = (f32[32,128]{1,0:T(8,128)S(1)}, f32[32,128]{1,0:T(8,128)S(1)}, u32[]{:S(2)}, u32[]{:S(2)}) collective-permute-start(f32[32,128]{1,0:T(8,128)S(1)} %get-tuple-element.36.refs_0_), channel_id=1, source_target_pairs={{0,20},{4,16},{8,28},{12,24},{16,4},{20,0},{24,12},{28,8},{1,21},{... | collective-permute-start | bytes 49160 | tf_op jit(solution)/shard_map/ppermute | solution.py:507
  49.1 3.2 %collective-permute-start.21 = (f32[32,128]{1,0:T(8,128)S(1)}, f32[32,128]{1,0:T(8,128)S(1)}, u32[]{:S(2)}, u32[]{:S(2)}) collective-permute-start(f32[32,128]{1,0:T(8,128)S(1)} %get-tuple-element.36.refs_0_), channel_id=1, source_target_pairs={{0,12},{4,8},{8,4},{12,0},{16,28},{20,24},{24,20},{28,16},{1,13},{... | collective-permute-start | bytes 49160 | tf_op jit(solution)/shard_map/ppermute | solution.py:507
  52.2 1.2 %collective-permute-start.22 = (f32[32,128]{1,0:T(8,128)S(1)}, f32[32,128]{1,0:T(8,128)S(1)}, u32[]{:S(2)}, u32[]{:S(2)}) collective-permute-start(f32[32,128]{1,0:T(8,128)S(1)} %add_parts.1.refs_0_), channel_id=1, source_target_pairs={{0,4},{4,0},{8,12},{12,8},{16,20},{20,16},{24,28},{28,24},{1,5},{5... | collective-permute-start | bytes 49160 | tf_op jit(solution)/shard_map/ppermute | solution.py:507
  (1 other events, 8.7 us)

commit v14 on v13

--- a/solution.py
+++ b/solution.py
@@ -223,66 +223,38 @@
         out_ref[i * 32 : (i + 1) * 32, :] = jnp.where(low, result[:32], result[32:]).astype(BF16)
 
 
-def largest_notes(notes):
-    largest = notes[0].astype(F32)
-    for note in notes[1:]:
-        largest = jnp.maximum(largest, note.astype(F32))
-    return largest
-
-
 def others_kernel(offsets, ranges, stacks, old_table, columns, matrix_ref, *refs):
     del old_table
-    far_refs, near_refs = refs[:stacks], refs[stacks : 2 * stacks]
-    table, *outs = refs[2 * stacks :]
+    far_refs, (table, *outs) = refs[:stacks], refs[stacks:]
     fill_table(far_refs, offsets, table)
-    terms, first = outs[: len(ranges)], matrix_ref.shape[1] * 32
-    if len(outs) > len(ranges):
-        notes = largest_notes(
-            [ref[index, first:] for ref in near_refs + far_refs for index in range(ref.shape[0])]
-        ).astype(BF16)
-        for ref in outs[len(ranges) :]:
-            ref[...] = notes
-        for term in terms:
-            term[first:, :] = notes
     for place, m in enumerate(ranges):
         group = m ^ lax.axis_index("cols")
-        one_product(group, columns, matrix_ref.at[place], table, terms[place])
+        one_product(group, columns, matrix_ref.at[place], table, outs[place])
 
 
 def own_kernel(columns, matrix_ref, table, out_ref):
     one_product(lax.axis_index("cols"), columns, matrix_ref.at[0], table, out_ref)
 
 
-def products(offsets, ranges, columns, matrix, own_matrix, near, far, table):
-    block_rows, count = matrix.shape[1], len(offsets) // 2
-    extra = near[0].shape[1] > block_rows * 32
-    rows = block_rows * 32
-    outs = [shaped(table.shape, BF16)] + [shaped((rows + 16 * extra, 128), BF16)] * len(ranges)
-    if extra:
-        outs.append(shaped((16, 128), BF16))
+def products(offsets, ranges, columns, matrix, own_matrix, far, table):
+    rows = shaped((matrix.shape[1] * 32, 128), BF16)
     table, *outs = call(
-        functools.partial(others_kernel, offsets[count:], ranges, len(near)),
+        functools.partial(others_kernel, offsets[len(offsets) // 2 :], ranges, len(far)),
         "others",
-        [vmem()] * (3 + 2 * len(near)),
-        outs,
-        (table, columns, matrix, *far, *near),
+        [vmem()] * (3 + len(far)),
+        [shaped(table.shape, BF16)] + [rows] * len(ranges),
+        (table, columns, matrix, *far),
         input_output_aliases={0: 0},
     )
     terms = [swap(term, "cols", m) for m, term in zip(ranges, outs)]
-    own = call(
-        own_kernel,
-        "own",
-        [vmem()] * 3,
-        shaped((rows, 128), BF16),
-        (columns, own_matrix, table),
-    )
-    return [own] + terms, outs[len(ranges) :]
-
-
-def add_terms(terms, rows):
-    summed = terms[0][:rows].astype(F32)
+    own = call(own_kernel, "own", [vmem()] * 3, rows, (columns, own_matrix, table))
+    return [own] + terms
+
+
+def add_terms(terms):
+    summed = terms[0][...].astype(F32)
     for term in terms[1:]:
-        summed = summed + term[:rows].astype(F32)
+        summed = summed + term[...].astype(F32)
     return summed
 
 
@@ -302,12 +274,9 @@
     terms, out_ref = refs[:-1], refs[-1]
     count = degree_ref.shape[0]
     degree = degree_ref[...]
-    rows = add_terms(terms, count) * degree
-    out_ref[:count] = (rows * degree).astype(BF16)
-    squares = jnp.sum(rows * rows, axis=(0, 1), keepdims=True)
-    out_ref[count:] = jnp.concatenate(
-        [inverse_ref[...], jnp.broadcast_to(squares, (8, 128))], axis=0
-    ).astype(BF16)
+    out_ref[:count] = (add_terms(terms) * degree * degree).astype(BF16)
+    inverse = inverse_ref[...]
+    out_ref[count:] = jnp.concatenate([inverse, inverse], axis=0).astype(BF16)
 
 
 def middle(degree, inverse, terms):
@@ -354,25 +323,36 @@
     )
 
 
-def collect_kernel(devices, total, degree_ref, first_ref, notes_ref, *refs):
+def collect_kernel(degree_ref, first_ref, *refs):
     terms, (rows_ref, grams_ref) = refs[:-2], refs[-2:]
-    count = degree_ref.shape[0]
-    largest = largest_notes([notes_ref[...]] + [term[count:] for term in terms[1:]])
-    scale = lax.rsqrt(largest[8:9] * (devices / total))
-    rows = add_terms(terms, count) * degree_ref[...] * scale
+    rows = add_terms(terms) * degree_ref[...]
+    largest = jnp.max(jnp.abs(rows), axis=(0, 1), keepdims=True)
+    scale = 1.0 / jnp.maximum(largest, 1e-30)
+    rows = rows * scale
     rows_ref[...] = rows
-    grams_ref[32:] = first_ref[...] * (scale * scale)
     grams_ref[:32] = local_gram(rows)
-
-
-def collect(devices, total, degree, first, notes, terms):
-    return call(
-        functools.partial(collect_kernel, devices, total),
+    grams_ref[32:40] = jnp.broadcast_to(scale, (8, 128))
+    grams_ref[40:] = first_ref[...]
+
+
+def collect(degree, first, terms):
+    return call(
+        collect_kernel,
         "collect",
-        [vmem()] * (3 + len(terms)),
-        (shaped(degree.shape, F32), shaped((64, 128), F32)),
-        (degree, first, notes, *terms),
-    )
+        [vmem()] * (2 + len(terms)),
+        (shaped(degree.shape, F32), shaped((72, 128), F32)),
+        (degree, first, *terms),
+    )
+
+
+def add_scaled(refs):
+    scales = [ref[32:33] for ref in refs]
+    smallest = functools.reduce(jnp.minimum, scales)
+    summed = 0.0
+    for ref, scale in zip(refs, scales):
+        ratio = smallest / scale
+        summed = summed + ref[:32] * (ratio * ratio)
+    return summed, smallest
 
 
 def lower_solve(gram, right):
@@ -418,30 +398,31 @@
     return jnp.concatenate([packed[:, :64], packed[:, 64:]], axis=0)
 
 
-def add_columns_kernel(total, *refs):
+def add_columns_kernel(*refs):
     parts, (gram_ref, first_ref) = refs[:-2], refs[-2:]
-    summed = parts[0][...]
+    summed, smallest = add_scaled(parts)
+    gram_ref[:32] = summed
+    gram_ref[32:] = jnp.broadcast_to(smallest, (8, 128))
+    first = parts[0][40:]
     for part in parts[1:]:
-        summed = summed + part[...]
-    gram_ref[...] = summed[:32]
-    first_ref[...] = summed[32:] / total
-
-
-def add_columns(total, parts):
-    return call(
-        functools.partial(add_columns_kernel, total),
+        first = first + part[40:]
+    first_ref[...] = first
+
+
+def add_columns(parts):
+    return call(
+        add_columns_kernel,
         "add_columns",
         [vmem()] * len(parts),
-        (shaped((32, 128), F32), shaped((32, 128), F32)),
+        (shaped((40, 128), F32), shaped((32, 128), F32)),
         parts,
     )
 
 
 def add_parts_kernel(count, *refs):
-    summed = refs[0][...]
-    for part in refs[1:count]:
-        summed = summed + part[...]
-    refs[-1][...] = summed
+    summed, smallest = add_scaled(refs[:count])
+    refs[-1][:32] = summed
+    refs[-1][32:] = jnp.broadcast_to(smallest, (8, 128))
 
 
 def add_parts(parts, after):
@@ -449,14 +430,16 @@
         functools.partial(add_parts_kernel, len(parts)),
         "add_parts",
         [vmem()] * (len(parts) + len(after)),
-        shaped(parts[0].shape, F32),
+        shaped((40, 128), F32),
         (*parts, *after),
     )
 
 
 def first_factor_kernel(gram_ref, out_ref):
+    gram = unpacked(gram_ref[...])
     unit = (iota((64, 64), 0) == iota((64, 64), 1)).astype(F32)
-    out_ref[...] = lower_solve(unpacked(gram_ref[...]), unit)
+    gram = gram / (jnp.sum(gram * unit, axis=(0, 1), keepdims=True) / 64.0)
+    out_ref[...] = lower_solve(gram, unit)
 
 
 def first_factor(gram):
@@ -469,17 +452,15 @@
     )
 
 
-def finish_kernel(total, rows_ref, inverse_ref, *refs):
+def finish_kernel(total, rows_ref, sent_ref, inverse_ref, *refs):
     out_ref, scratch = refs[-2:]
     block_rows = out_ref.shape[1]
-    packed = refs[0][...]
-    for part in refs[1:-2]:
-        packed = packed + part[...]
+    packed, smallest = add_scaled(refs[:-2])
     first = inverse_ref[...]
     gram = dot_turned(
         jnp.dot(first, unpacked(packed), precision=HIGHEST, preferred_element_type=F32), first
     )
-    inverse = lower_solve(gram / total, first)
+    inverse = lower_solve(gram / total, first) * (smallest / sent_ref[32:33])[:, :64]
     zero = jnp.zeros_like(inverse)
     both = jnp.concatenate(
         [jnp.concatenate([inverse, zero], axis=1), jnp.concatenate([zero, inverse], axis=1)], axis=0
@@ -491,13 +472,13 @@
         out_ref[0, :, t * 128 : (t + 1) * 128] = scratch[t * block_rows : (t + 1) * block_rows, :]
 
 
-def finish(total, block_rows, rows, inverse, grams):
+def finish(total, block_rows, rows, sent, inverse, grams):
     return call(
         functools.partial(finish_kernel, total),
         "finish",
-        [vmem()] * (2 + len(grams)),
+        [vmem()] * (3 + len(grams)),
         shaped((1, block_rows, 32 * 128), F32),
-        (rows, inverse, *grams),
+        (rows, sent, inverse, *grams),
         [pltpu.VMEM(rows.shape, F32)],
     )
 
@@ -519,7 +500,7 @@
 
 def stages(size):
     if size == 8:
-        return [[7, 5, 3], [1]]
+        return [[7, 3, 5], [1]]
     bits, bit = [], 1
     while bit < size:
         bits.append([bit])
@@ -534,7 +515,6 @@
         held = held + [swap(piece, "rows", mask) for mask in masks for piece in held]
         offsets = offsets + [mask ^ offset for mask in masks for offset in offsets]
     split = len(held) // 2
-    held, offsets = held[split:] + held[:split], offsets[split:] + offsets[:split]
     near = [stack(held[:split], []), stack(held[split:], after)]
     (last,) = plan[-1]
     offsets = offsets + [last ^ offset for offset in offsets]
@@ -544,7 +524,7 @@
 def add_rows(gram, after):
     *plan, (last,) = stages(lax.axis_size("rows"))
     for masks in plan:
-        gram = add_parts([gram] + [swap(gram, "rows", mask) for mask in masks], after)
+        gram = add_parts([gram] + [swap(gram, "rows", mask) for mask in reversed(masks)], after)
     return [gram, swap(gram, "rows", last)]
 
 
@@ -566,17 +546,16 @@
     (own_matrix,) = prep([0], affinity)
     near, far, offsets = gather_rows(scaled, [inverse])
     table = near_table(offsets, near, block_rows)
-    terms, _ = products(offsets, ranges, columns, matrix, own_matrix, near, far, table)
+    terms = products(offsets, ranges, columns, matrix, own_matrix, far, table)
     near, far, offsets = gather_rows(middle(degree, inverse, terms), [])
     table = near_table(offsets, near, block_rows)
-    terms, (notes,) = products(offsets, ranges, columns, matrix, own_matrix, near, far, table)
-    devices = float(groups * ranks)
-    rows, grams = collect(devices, total, degree, row_gram(near + far), notes, terms)
+    terms = products(offsets, ranges, columns, matrix, own_matrix, far, table)
+    rows, grams = collect(degree, row_gram(near + far), terms)
     flip = 1 if ranks == 8 else 0
-    order = [2, 3, 1] if groups == 4 else ranges
-    gram, first = add_columns(total, [grams] + [swap_both(grams, flip, m) for m in order])
+    order = [1, 3, 2] if groups == 4 else ranges
+    gram, first = add_columns([grams] + [swap_both(grams, flip, m) for m in order])
     inverse = first_factor(first)
-    return finish(total, block_rows, rows, inverse, add_rows(gram, [inverse]))
+    return finish(total, block_rows, rows, grams, inverse, add_rows(gram, [inverse]))
 
 
 def solution(mesh):

time: 56.3 us -> 56.7 us (level)
  no operation moved by 1% of the time
where the time goes in v14:
time: 56.7 us; the launch traced here: 56.5 us
  starting transfers between devices  22.5 us (40%)
  waiting for transfers between devices  20.8 us (37%)
  Pallas kernels  12.9 us (23%)
    ppermute x20, starting transfers between devices, swap(): lax.ppermute(value, axis, [(index, index ^ mask) for index in range(size)])  19.7 us
    ppermute x20, waiting for transfers between devices, swap(): lax.ppermute(value, axis, [(index, index ^ mask) for index in range(size)])  16.8 us
    pallas_call x20, Pallas kernels, call(): pl.pallas_call(kernel, out_shape=outs, in_specs=ins, out_specs=jax.tree.m...  12.9 us
    ppermute x3, waiting for transfers between devices, swap_both(): return lax.ppermute(value, ('rows', 'cols'), pairs)  3.95 us
    ppermute x3, starting transfers between devices, swap_both(): return lax.ppermute(value, ('rows', 'cols'), pairs)  2.85 us
  transfers between devices with their start and end apart: 23, of which 16 were waited for; matrix products, arithmetic and copies ran while one was open for 0% of the time, Pallas kernels for 12%

profile of v14, /device:TPU:0, one launch (start us, length us, event | category | flops | bytes accessed | tf_op | source)
XLA Modules:
  0.0 56.5 jit_solution(11821794463951158700)
XLA Ops:
  1.0 3.4 %collective-permute-start = (bf16[256,128]{1,0:T(8,128)(2,1)S(1)}, bf16[256,128]{1,0:T(8,128)(2,1)S(1)}, u32[]{:S(2)}, u32[]{:S(2)}) collective-permute-start(bf16[256,128]{1,0:T(8,128)(2,1)S(1)} %start.1.refs_0_), channel_id=1, source_target_pairs={{0,28},{4,24},{8,20},{12,16},{16,12},{20,8},{24,4},{28,0},{1,29},{... | collective-permute-start | bytes 196616 | tf_op jit(solution)/shard_map/ppermute | solution.py:488
  5.3 2.3 %prep.2 = (f32[256,128]{1,0:T(8,128)S(1)}, f32[8,128]{1,0:T(8,128)S(1)}, bf16[3,8,64,512]{3,2,1,0:T(8,128)(2,1)S(1)}) custom-call(bf16[4,8,1,8,4096]{4,3,2,1,0:T(8,128)(2,1)} %affinity_hbm.3, f32[1,8,64]{2,1,0:T(8,128)} %inv_hbm.1), custom_call_target="tpu_custom_call" | custom-call | tf_op jit(solution)/shard_map/prep/pallas_call | solution.py:37
  8.3 1.2 %collective-permute-done.1.refs_0_ = bf16[256,128]{1,0:T(8,128)(2,1)S(1)} collective-permute-done((bf16[256,128]{1,0:T(8,128)(2,1)S(1)}, bf16[256,128]{1,0:T(8,128)(2,1)S(1)}, u32[]{:S(2)}, u32[]{:S(2)}) %collective-permute-start.1) | collective-permute-done | bytes 65568 | tf_op jit(solution)/shard_map/ppermute | solution.py:488
  9.9 1.0 %collective-permute-done.4.refs_1_ = bf16[2,256,128]{2,1,0:T(8,128)(2,1)S(1)} collective-permute-done((bf16[2,256,128]{2,1,0:T(8,128)(2,1)S(1)}, bf16[2,256,128]{2,1,0:T(8,128)(2,1)S(1)}, u32[]{:S(2)}, u32[]{:S(2)}) %collective-permute-start.4) | collective-permute-done | bytes 131104 | tf_op jit(solution)/shard_map/ppermute | solution.py:488
  11.8 3.7 %collective-permute-start.5 = (bf16[256,128]{1,0:T(8,128)(2,1)S(1)}, bf16[256,128]{1,0:T(8,128)(2,1)S(1)}, u32[]{:S(2)}, u32[]{:S(2)}) collective-permute-start(bf16[256,128]{1,0:T(8,128)(2,1)S(1)} %get-tuple-element.24), channel_id=1, source_target_pairs={{0,3},{1,2},{2,1},{3,0},{4,7},{5,6},{6,5},{7,4},{8,11},{9,10},{10,... | collective-permute-start | bytes 196616 | tf_op jit(solution)/shard_map/ppermute | solution.py:488
  16.2 1.4 %prep.3.matrix_ref = bf16[1,8,64,512]{3,2,1,0:T(8,128)(2,1)S(1)} custom-call(bf16[4,8,1,8,4096]{4,3,2,1,0:T(8,128)(2,1)} %affinity_hbm.3), custom_call_target="tpu_custom_call" | custom-call | tf_op jit(solution)/shard_map/prep/pallas_call | solution.py:37
  18.1 3.2 %collective-permute-done.6.refs_2_ = bf16[256,128]{1,0:T(8,128)(2,1)S(1)} collective-permute-done((bf16[256,128]{1,0:T(8,128)(2,1)S(1)}, bf16[256,128]{1,0:T(8,128)(2,1)S(1)}, u32[]{:S(2)}, u32[]{:S(2)}) %collective-permute-start.6) | collective-permute-done | bytes 65568 | tf_op jit(solution)/shard_map/ppermute | solution.py:488
  22.3 1.6 %collective-permute-start.10 = (bf16[272,128]{1,0:T(8,128)(2,1)S(1)}, bf16[272,128]{1,0:T(8,128)(2,1)S(1)}, u32[]{:S(2)}, u32[]{:S(2)}) collective-permute-start(bf16[272,128]{1,0:T(8,128)(2,1)S(1)} %middle.1.refs_0_), channel_id=1, source_target_pairs={{0,20},{4,16},{8,28},{12,24},{16,4},{20,0},{24,12},{28,8},{1,21},{... | collective-permute-start | bytes 208904 | tf_op jit(solution)/shard_map/ppermute | solution.py:488
  24.2 2.6 %collective-permute-done.8.refs_1_ = bf16[272,128]{1,0:T(8,128)(2,1)S(1)} collective-permute-done((bf16[272,128]{1,0:T(8,128)(2,1)S(1)}, bf16[272,128]{1,0:T(8,128)(2,1)S(1)}, u32[]{:S(2)}, u32[]{:S(2)}) %collective-permute-start.8) | collective-permute-done | bytes 69664 | tf_op jit(solution)/shard_map/ppermute | solution.py:488
  26.9 1.2 %collective-permute-done.10.refs_1_ = bf16[272,128]{1,0:T(8,128)(2,1)S(1)} collective-permute-done((bf16[272,128]{1,0:T(8,128)(2,1)S(1)}, bf16[272,128]{1,0:T(8,128)(2,1)S(1)}, u32[]{:S(2)}, u32[]{:S(2)}) %collective-permute-start.10) | collective-permute-done | bytes 69664 | tf_op jit(solution)/shard_map/ppermute | solution.py:488
  28.6 1.1 %collective-permute-done.12.refs_3_.refs_1_ = bf16[2,272,128]{2,1,0:T(8,128)(2,1)S(1)} collective-permute-done((bf16[2,272,128]{2,1,0:T(8,128)(2,1)S(1)}, bf16[2,272,128]{2,1,0:T(8,128)(2,1)S(1)}, u32[]{:S(2)}, u32[]{:S(2)}) %collective-permute-start.12) | collective-permute-done | bytes 139296 | tf_op jit(solution)/shard_map/ppermute | solution.py:488
  30.6 2.2 %collective-permute-start.13 = (bf16[256,128]{1,0:T(8,128)(2,1)S(1)}, bf16[256,128]{1,0:T(8,128)(2,1)S(1)}, u32[]{:S(2)}, u32[]{:S(2)}) collective-permute-start(bf16[256,128]{1,0:T(8,128)(2,1)S(1)} %get-tuple-element.28), channel_id=1, source_target_pairs={{0,3},{1,2},{2,1},{3,0},{4,7},{5,6},{6,5},{7,4},{8,11},{9,10},{10,... | collective-permute-start | bytes 196616 | tf_op jit(solution)/shard_map/ppermute | solution.py:488
  32.8 2.3 %collective-permute-start.15 = (bf16[256,128]{1,0:T(8,128)(2,1)S(1)}, bf16[256,128]{1,0:T(8,128)(2,1)S(1)}, u32[]{:S(2)}, u32[]{:S(2)}) collective-permute-start(bf16[256,128]{1,0:T(8,128)(2,1)S(1)} %get-tuple-element.30), channel_id=1, source_target_pairs={{0,1},{1,0},{2,3},{3,2},{4,5},{5,4},{6,7},{7,6},{8,9},{9,8},{10,11... | collective-permute-start | bytes 196616 | tf_op jit(solution)/shard_map/ppermute | solution.py:488
  36.1 1.3 %collective-permute-done.13.refs_1_ = bf16[256,128]{1,0:T(8,128)(2,1)S(1)} collective-permute-done((bf16[256,128]{1,0:T(8,128)(2,1)S(1)}, bf16[256,128]{1,0:T(8,128)(2,1)S(1)}, u32[]{:S(2)}, u32[]{:S(2)}) %collective-permute-start.13) | collective-permute-done | bytes 65568 | tf_op jit(solution)/shard_map/ppermute | solution.py:488
  37.4 2.0 %collective-permute-done.14.refs_2_ = bf16[256,128]{1,0:T(8,128)(2,1)S(1)} collective-permute-done((bf16[256,128]{1,0:T(8,128)(2,1)S(1)}, bf16[256,128]{1,0:T(8,128)(2,1)S(1)}, u32[]{:S(2)}, u32[]{:S(2)}) %collective-permute-start.14) | collective-permute-done | bytes 65568 | tf_op jit(solution)/shard_map/ppermute | solution.py:488
  40.1 2.4 %collective-permute-start.17 = (f32[72,128]{1,0:T(8,128)S(1)}, f32[72,128]{1,0:T(8,128)S(1)}, u32[]{:S(2)}, u32[]{:S(2)}) collective-permute-start(f32[72,128]{1,0:T(8,128)S(1)} %get-tuple-element.32.refs_0_.sent_ref), channel_id=1, source_target_pairs={{0,7},{1,6},{2,5},{3,4},{4,3},{5,2},{6,1},{7,0},{8,15},{9,14},{10,... | collective-permute-start | bytes 110600 | tf_op jit(solution)/shard_map/ppermute | solution.py:498
  42.9 2.8 %collective-permute-done.18.refs_3_ = f32[72,128]{1,0:T(8,128)S(1)} collective-permute-done((f32[72,128]{1,0:T(8,128)S(1)}, f32[72,128]{1,0:T(8,128)S(1)}, u32[]{:S(2)}, u32[]{:S(2)}) %collective-permute-start.18) | collective-permute-done | bytes 36896 | tf_op jit(solution)/shard_map/ppermute | solution.py:498
  45.7 1.2 %collective-permute-done.16.refs_1_ = f32[72,128]{1,0:T(8,128)S(1)} collective-permute-done((f32[72,128]{1,0:T(8,128)S(1)}, f32[72,128]{1,0:T(8,128)S(1)}, u32[]{:S(2)}, u32[]{:S(2)}) %collective-permute-start.16) | collective-permute-done | bytes 36896 | tf_op jit(solution)/shard_map/ppermute | solution.py:498
  46.9 1.5 %collective-permute-start.21 = (f32[40,128]{1,0:T(8,128)S(1)}, f32[40,128]{1,0:T(8,128)S(1)}, u32[]{:S(2)}, u32[]{:S(2)}) collective-permute-start(f32[40,128]{1,0:T(8,128)S(1)} %get-tuple-element.34.refs_0_), channel_id=1, source_target_pairs={{0,28},{4,24},{8,20},{12,16},{16,12},{20,8},{24,4},{28,0},{1,29},{... | collective-permute-start | bytes 61448 | tf_op jit(solution)/shard_map/ppermute | solution.py:488
  48.3 1.0 %collective-permute-start.20 = (f32[40,128]{1,0:T(8,128)S(1)}, f32[40,128]{1,0:T(8,128)S(1)}, u32[]{:S(2)}, u32[]{:S(2)}) collective-permute-start(f32[40,128]{1,0:T(8,128)S(1)} %get-tuple-element.34.refs_0_), channel_id=1, source_target_pairs={{0,12},{4,8},{8,4},{12,0},{16,28},{20,24},{24,20},{28,16},{1,13},{... | collective-permute-start | bytes 61448 | tf_op jit(solution)/shard_map/ppermute | solution.py:488
  49.9 1.4 %first_factor.1.refs_4_.inverse_ref = f32[64,64]{1,0:T(8,128)S(1)} custom-call(f32[32,128]{1,0:T(8,128)S(1)} %get-tuple-element.33.gram_ref), custom_call_target="tpu_custom_call" | custom-call | tf_op jit(solution)/shard_map/first_factor/pallas_call | solution.py:37
  51.5 1.0 %collective-permute-done.19.refs_1_ = f32[40,128]{1,0:T(8,128)S(1)} collective-permute-done((f32[40,128]{1,0:T(8,128)S(1)}, f32[40,128]{1,0:T(8,128)S(1)}, u32[]{:S(2)}, u32[]{:S(2)}) %collective-permute-start.19) | collective-permute-done | bytes 20512 | tf_op jit(solution)/shard_map/ppermute | solution.py:488
  52.7 1.1 %collective-permute-done.22.refs_1_ = f32[40,128]{1,0:T(8,128)S(1)} collective-permute-done((f32[40,128]{1,0:T(8,128)S(1)}, f32[40,128]{1,0:T(8,128)S(1)}, u32[]{:S(2)}, u32[]{:S(2)}) %collective-permute-start.22) | collective-permute-done | bytes 20512 | tf_op jit(solution)/shard_map/ppermute | solution.py:488
  53.8 2.7 %finish.1 = f32[1,8,4096]{2,1,0:T(8,128)} custom-call(f32[256,128]{1,0:T(8,128)S(1)} %get-tuple-element.31.rows_ref, f32[72,128]{1,0:T(8,128)S(1)} %get-tuple-element.32.refs_0_.sent_ref, f32[64,64]{1,0:T(8,128)S(1)} %first_factor.1.refs_4_.inverse_ref, f32[40,128]{1,0:T(8,128)S(1)} %add_parts.1.refs_0_, f32[40,128]{1,0:T(8,128)S(1)} %collective-permute-done.22.refs_1_), custom_call_target="tpu_custom_call" | custom-call | tf_op jit(solution)/shard_map/finish/pallas_call | solution.py:37
  (47 shorter events, 10.8 us)
Async XLA Ops:
  1.0 8.7 %copy-start = (s32[4,8,1,8]{3,2,1,0:T(1,128)S(1)}, s32[4,8,1,8]{3,2,1,0:T(1,128)}, u32[]{:S(2)}) copy-start(s32[4,8,1,8]{3,2,1,0:T(1,128)} %param.6) | copy-start | bytes 3076
  1.0 6.6 %collective-permute-start = (bf16[256,128]{1,0:T(8,128)(2,1)S(1)}, bf16[256,128]{1,0:T(8,128)(2,1)S(1)}, u32[]{:S(2)}, u32[]{:S(2)}) collective-permute-start(bf16[256,128]{1,0:T(8,128)(2,1)S(1)} %start.1.refs_0_), channel_id=1, source_target_pairs={{0,28},{4,24},{8,20},{12,16},{16,12},{20,8},{24,4},{28,0},{1,29},{... | collective-permute-start | bytes 196616 | tf_op jit(solution)/shard_map/ppermute | solution.py:488
  4.4 3.9 %collective-permute-start.2 = (bf16[256,128]{1,0:T(8,128)(2,1)S(1)}, bf16[256,128]{1,0:T(8,128)(2,1)S(1)}, u32[]{:S(2)}, u32[]{:S(2)}) collective-permute-start(bf16[256,128]{1,0:T(8,128)(2,1)S(1)} %start.1.refs_0_), channel_id=1, source_target_pairs={{0,20},{4,16},{8,28},{12,24},{16,4},{20,0},{24,12},{28,8},{1,21},{... | collective-permute-start | bytes 196616 | tf_op jit(solution)/shard_map/ppermute | solution.py:488
  5.2 4.3 %collective-permute-start.1 = (bf16[256,128]{1,0:T(8,128)(2,1)S(1)}, bf16[256,128]{1,0:T(8,128)(2,1)S(1)}, u32[]{:S(2)}, u32[]{:S(2)}) collective-permute-start(bf16[256,128]{1,0:T(8,128)(2,1)S(1)} %start.1.refs_0_), channel_id=1, source_target_pairs={{0,12},{4,8},{8,4},{12,0},{16,28},{20,24},{24,20},{28,16},{1,13},{... | collective-permute-start | bytes 196616 | tf_op jit(solution)/shard_map/ppermute | solution.py:488
  7.7 2.3 %collective-permute-start.3 = (bf16[2,256,128]{2,1,0:T(8,128)(2,1)S(1)}, bf16[2,256,128]{2,1,0:T(8,128)(2,1)S(1)}, u32[]{:S(2)}, u32[]{:S(2)}) collective-permute-start(bf16[2,256,128]{2,1,0:T(8,128)(2,1)S(1)} %stack.4.refs_0_), channel_id=1, source_target_pairs={{0,4},{4,0},{8,12},{12,8},{16,20},{20,16},{24,28},{28,24},{1,5},{5... | collective-permute-start | bytes 393224 | tf_op jit(solution)/shard_map/ppermute | solution.py:488
  9.5 1.4 %collective-permute-start.4 = (bf16[2,256,128]{2,1,0:T(8,128)(2,1)S(1)}, bf16[2,256,128]{2,1,0:T(8,128)(2,1)S(1)}, u32[]{:S(2)}, u32[]{:S(2)}) collective-permute-start(bf16[2,256,128]{2,1,0:T(8,128)(2,1)S(1)} %stack.5.refs_1_), channel_id=1, source_target_pairs={{0,4},{4,0},{8,12},{12,8},{16,20},{20,16},{24,28},{28,24},{1,5},{5... | collective-permute-start | bytes 393224 | tf_op jit(solution)/shard_map/ppermute | solution.py:488
  11.8 6.4 %collective-permute-start.5 = (bf16[256,128]{1,0:T(8,128)(2,1)S(1)}, bf16[256,128]{1,0:T(8,128)(2,1)S(1)}, u32[]{:S(2)}, u32[]{:S(2)}) collective-permute-start(bf16[256,128]{1,0:T(8,128)(2,1)S(1)} %get-tuple-element.24), channel_id=1, source_target_pairs={{0,3},{1,2},{2,1},{3,0},{4,7},{5,6},{6,5},{7,4},{8,11},{9,10},{10,... | collective-permute-start | bytes 196616 | tf_op jit(solution)/shard_map/ppermute | solution.py:488
  15.4 5.9 %collective-permute-start.6 = (bf16[256,128]{1,0:T(8,128)(2,1)S(1)}, bf16[256,128]{1,0:T(8,128)(2,1)S(1)}, u32[]{:S(2)}, u32[]{:S(2)}) collective-permute-start(bf16[256,128]{1,0:T(8,128)(2,1)S(1)} %get-tuple-element.25), channel_id=1, source_target_pairs={{0,2},{1,3},{2,0},{3,1},{4,6},{5,7},{6,4},{7,5},{8,10},{9,11},{10,... | collective-permute-start | bytes 196616 | tf_op jit(solution)/shard_map/ppermute | solution.py:488
  15.4 5.9 %collective-permute-start.7 = (bf16[256,128]{1,0:T(8,128)(2,1)S(1)}, bf16[256,128]{1,0:T(8,128)(2,1)S(1)}, u32[]{:S(2)}, u32[]{:S(2)}) collective-permute-start(bf16[256,128]{1,0:T(8,128)(2,1)S(1)} %get-tuple-element.26), channel_id=1, source_target_pairs={{0,1},{1,0},{2,3},{3,2},{4,5},{5,4},{6,7},{7,6},{8,9},{9,8},{10,11... | collective-permute-start | bytes 196616 | tf_op jit(solution)/shard_map/ppermute | solution.py:488
  21.4 5.4 %collective-permute-start.8 = (bf16[272,128]{1,0:T(8,128)(2,1)S(1)}, bf16[272,128]{1,0:T(8,128)(2,1)S(1)}, u32[]{:S(2)}, u32[]{:S(2)}) collective-permute-start(bf16[272,128]{1,0:T(8,128)(2,1)S(1)} %middle.1.refs_0_), channel_id=1, source_target_pairs={{0,28},{4,24},{8,20},{12,16},{16,12},{20,8},{24,4},{28,0},{1,29},{... | collective-permute-start | bytes 208904 | tf_op jit(solution)/shard_map/ppermute | solution.py:488
  22.3 5.8 %collective-permute-start.10 = (bf16[272,128]{1,0:T(8,128)(2,1)S(1)}, bf16[272,128]{1,0:T(8,128)(2,1)S(1)}, u32[]{:S(2)}, u32[]{:S(2)}) collective-permute-start(bf16[272,128]{1,0:T(8,128)(2,1)S(1)} %middle.1.refs_0_), channel_id=1, source_target_pairs={{0,20},{4,16},{8,28},{12,24},{16,4},{20,0},{24,12},{28,8},{1,21},{... | collective-permute-start | bytes 208904 | tf_op jit(solution)/shard_map/ppermute | solution.py:488
  23.9 4.4 %collective-permute-start.9 = (bf16[272,128]{1,0:T(8,128)(2,1)S(1)}, bf16[272,128]{1,0:T(8,128)(2,1)S(1)}, u32[]{:S(2)}, u32[]{:S(2)}) collective-permute-start(bf16[272,128]{1,0:T(8,128)(2,1)S(1)} %middle.1.refs_0_), channel_id=1, source_target_pairs={{0,12},{4,8},{8,4},{12,0},{16,28},{20,24},{24,20},{28,16},{1,13},{... | collective-permute-start | bytes 208904 | tf_op jit(solution)/shard_map/ppermute | solution.py:488
  26.8 1.8 %collective-permute-start.11 = (bf16[2,272,128]{2,1,0:T(8,128)(2,1)S(1)}, bf16[2,272,128]{2,1,0:T(8,128)(2,1)S(1)}, u32[]{:S(2)}, u32[]{:S(2)}) collective-permute-start(bf16[2,272,128]{2,1,0:T(8,128)(2,1)S(1)} %stack.6.refs_0_), channel_id=1, source_target_pairs={{0,4},{4,0},{8,12},{12,8},{16,20},{20,16},{24,28},{28,24},{1,5},{5... | collective-permute-start | bytes 417800 | tf_op jit(solution)/shard_map/ppermute | solution.py:488
  28.4 1.4 %collective-permute-start.12 = (bf16[2,272,128]{2,1,0:T(8,128)(2,1)S(1)}, bf16[2,272,128]{2,1,0:T(8,128)(2,1)S(1)}, u32[]{:S(2)}, u32[]{:S(2)}) collective-permute-start(bf16[2,272,128]{2,1,0:T(8,128)(2,1)S(1)} %stack.7.refs_1_), channel_id=1, source_target_pairs={{0,4},{4,0},{8,12},{12,8},{16,20},{20,16},{24,28},{28,24},{1,5},{5... | collective-permute-start | bytes 417800 | tf_op jit(solution)/shard_map/ppermute | solution.py:488
  30.6 6.8 %collective-permute-start.13 = (bf16[256,128]{1,0:T(8,128)(2,1)S(1)}, bf16[256,128]{1,0:T(8,128)(2,1)S(1)}, u32[]{:S(2)}, u32[]{:S(2)}) collective-permute-start(bf16[256,128]{1,0:T(8,128)(2,1)S(1)} %get-tuple-element.28), channel_id=1, source_target_pairs={{0,3},{1,2},{2,1},{3,0},{4,7},{5,6},{6,5},{7,4},{8,11},{9,10},{10,... | collective-permute-start | bytes 196616 | tf_op jit(solution)/shard_map/ppermute | solution.py:488
  32.8 6.6 %collective-permute-start.14 = (bf16[256,128]{1,0:T(8,128)(2,1)S(1)}, bf16[256,128]{1,0:T(8,128)(2,1)S(1)}, u32[]{:S(2)}, u32[]{:S(2)}) collective-permute-start(bf16[256,128]{1,0:T(8,128)(2,1)S(1)} %get-tuple-element.29), channel_id=1, source_target_pairs={{0,2},{1,3},{2,0},{3,1},{4,6},{5,7},{6,4},{7,5},{8,10},{9,11},{10,... | collective-permute-start | bytes 196616 | tf_op jit(solution)/shard_map/ppermute | solution.py:488
  32.8 6.6 %collective-permute-start.15 = (bf16[256,128]{1,0:T(8,128)(2,1)S(1)}, bf16[256,128]{1,0:T(8,128)(2,1)S(1)}, u32[]{:S(2)}, u32[]{:S(2)}) collective-permute-start(bf16[256,128]{1,0:T(8,128)(2,1)S(1)} %get-tuple-element.30), channel_id=1, source_target_pairs={{0,1},{1,0},{2,3},{3,2},{4,5},{5,4},{6,7},{7,6},{8,9},{9,8},{10,11... | collective-permute-start | bytes 196616 | tf_op jit(solution)/shard_map/ppermute | solution.py:488
  40.0 5.6 %collective-permute-start.18 = (f32[72,128]{1,0:T(8,128)S(1)}, f32[72,128]{1,0:T(8,128)S(1)}, u32[]{:S(2)}, u32[]{:S(2)}) collective-permute-start(f32[72,128]{1,0:T(8,128)S(1)} %get-tuple-element.32.refs_0_.sent_ref), channel_id=1, source_target_pairs={{0,6},{1,7},{2,4},{3,5},{4,2},{5,3},{6,0},{7,1},{8,14},{9,15},{10,... | collective-permute-start | bytes 110600 | tf_op jit(solution)/shard_map/ppermute | solution.py:498
  40.1 5.6 %collective-permute-start.17 = (f32[72,128]{1,0:T(8,128)S(1)}, f32[72,128]{1,0:T(8,128)S(1)}, u32[]{:S(2)}, u32[]{:S(2)}) collective-permute-start(f32[72,128]{1,0:T(8,128)S(1)} %get-tuple-element.32.refs_0_.sent_ref), channel_id=1, source_target_pairs={{0,7},{1,6},{2,5},{3,4},{4,3},{5,2},{6,1},{7,0},{8,15},{9,14},{10,... | collective-permute-start | bytes 110600 | tf_op jit(solution)/shard_map/ppermute | solution.py:498
  42.4 4.4 %collective-permute-start.16 = (f32[72,128]{1,0:T(8,128)S(1)}, f32[72,128]{1,0:T(8,128)S(1)}, u32[]{:S(2)}, u32[]{:S(2)}) collective-permute-start(f32[72,128]{1,0:T(8,128)S(1)} %get-tuple-element.32.refs_0_.sent_ref), channel_id=1, source_target_pairs={{0,5},{1,4},{2,7},{3,6},{4,1},{5,0},{6,3},{7,2},{8,13},{9,12},{10,... | collective-permute-start | bytes 110600 | tf_op jit(solution)/shard_map/ppermute | solution.py:498
  46.9 4.4 %collective-permute-start.21 = (f32[40,128]{1,0:T(8,128)S(1)}, f32[40,128]{1,0:T(8,128)S(1)}, u32[]{:S(2)}, u32[]{:S(2)}) collective-permute-start(f32[40,128]{1,0:T(8,128)S(1)} %get-tuple-element.34.refs_0_), channel_id=1, source_target_pairs={{0,28},{4,24},{8,20},{12,16},{16,12},{20,8},{24,4},{28,0},{1,29},{... | collective-permute-start | bytes 61448 | tf_op jit(solution)/shard_map/ppermute | solution.py:488
  48.3 3.2 %collective-permute-start.20 = (f32[40,128]{1,0:T(8,128)S(1)}, f32[40,128]{1,0:T(8,128)S(1)}, u32[]{:S(2)}, u32[]{:S(2)}) collective-permute-start(f32[40,128]{1,0:T(8,128)S(1)} %get-tuple-element.34.refs_0_), channel_id=1, source_target_pairs={{0,12},{4,8},{8,4},{12,0},{16,28},{20,24},{24,20},{28,16},{1,13},{... | collective-permute-start | bytes 61448 | tf_op jit(solution)/shard_map/ppermute | solution.py:488
  49.3 3.2 %collective-permute-start.19 = (f32[40,128]{1,0:T(8,128)S(1)}, f32[40,128]{1,0:T(8,128)S(1)}, u32[]{:S(2)}, u32[]{:S(2)}) collective-permute-start(f32[40,128]{1,0:T(8,128)S(1)} %get-tuple-element.34.refs_0_), channel_id=1, source_target_pairs={{0,20},{4,16},{8,28},{12,24},{16,4},{20,0},{24,12},{28,8},{1,21},{... | collective-permute-start | bytes 61448 | tf_op jit(solution)/shard_map/ppermute | solution.py:488
  52.5 1.3 %collective-permute-start.22 = (f32[40,128]{1,0:T(8,128)S(1)}, f32[40,128]{1,0:T(8,128)S(1)}, u32[]{:S(2)}, u32[]{:S(2)}) collective-permute-start(f32[40,128]{1,0:T(8,128)S(1)} %add_parts.1.refs_0_), channel_id=1, source_target_pairs={{0,4},{4,0},{8,12},{12,8},{16,20},{20,16},{24,28},{28,24},{1,5},{5... | collective-permute-start | bytes 61448 | tf_op jit(solution)/shard_map/ppermute | solution.py:488
  (1 other events, 8.7 us)

commit v15 on v13

--- a/solution.py
+++ b/solution.py
@@ -239,7 +239,9 @@
     if len(outs) > len(ranges):
         notes = largest_notes(
             [ref[index, first:] for ref in near_refs + far_refs for index in range(ref.shape[0])]
-        ).astype(BF16)
+        )
+        notes = jnp.sum(notes[8:], axis=(0, 1), keepdims=True)
+        notes = jnp.broadcast_to(notes, (16, 128)).astype(BF16)
         for ref in outs[len(ranges) :]:
             ref[...] = notes
         for term in terms:
@@ -304,10 +306,8 @@
     degree = degree_ref[...]
     rows = add_terms(terms, count) * degree
     out_ref[:count] = (rows * degree).astype(BF16)
-    squares = jnp.sum(rows * rows, axis=(0, 1), keepdims=True)
-    out_ref[count:] = jnp.concatenate(
-        [inverse_ref[...], jnp.broadcast_to(squares, (8, 128))], axis=0
-    ).astype(BF16)
+    squares = jnp.sum((rows * rows).reshape(-1, 8, 128), axis=0)
+    out_ref[count:] = jnp.concatenate([inverse_ref[...], squares], axis=0).astype(BF16)
 
 
 def middle(degree, inverse, terms):
@@ -358,7 +358,7 @@
     terms, (rows_ref, grams_ref) = refs[:-2], refs[-2:]
     count = degree_ref.shape[0]
     largest = largest_notes([notes_ref[...]] + [term[count:] for term in terms[1:]])
-    scale = lax.rsqrt(largest[8:9] * (devices / total))
+    scale = lax.rsqrt(largest[:1] * (devices / total))
     rows = add_terms(terms, count) * degree_ref[...] * scale
     rows_ref[...] = rows
     grams_ref[32:] = first_ref[...] * (scale * scale)

time: 56.3 us -> 56.1 us (level)
  no operation moved by 1% of the time
where the time goes in v15:
time: 56.1 us; the launch traced here: 55.9 us
  starting transfers between devices  22.5 us (40%)
  waiting for transfers between devices  20.6 us (37%)
  Pallas kernels  12.6 us (22%)
    ppermute x20, starting transfers between devices, swap(): lax.ppermute(value, axis, [(index, index ^ mask) for index in range(size)])  19.6 us
    ppermute x20, waiting for transfers between devices, swap(): lax.ppermute(value, axis, [(index, index ^ mask) for index in range(size)])  17 us
    pallas_call x20, Pallas kernels, call(): pl.pallas_call(kernel, out_shape=outs, in_specs=ins, out_specs=jax.tree.m...  12.6 us
    ppermute x3, waiting for transfers between devices, swap_both(): return lax.ppermute(value, ('rows', 'cols'), pairs)  3.55 us
    ppermute x3, starting transfers between devices, swap_both(): return lax.ppermute(value, ('rows', 'cols'), pairs)  2.84 us
  transfers between devices with their start and end apart: 23, of which 16 were waited for; matrix products, arithmetic and copies ran while one was open for 0% of the time, Pallas kernels for 12%

profile of v15, /device:TPU:0, one launch (start us, length us, event | category | flops | bytes accessed | tf_op | source)
XLA Modules:
  0.0 55.9 jit_solution(1014721700085642555)
XLA Ops:
  0.0 1.0 %start.1.refs_0_ = bf16[256,128]{1,0:T(8,128)(2,1)S(1)} custom-call(f32[1,8,4096]{2,1,0:T(8,128)} %panel_hbm.1, f32[1,8,64]{2,1,0:T(8,128)} %inv_hbm.1), custom_call_target="tpu_custom_call" | custom-call | tf_op jit(solution)/shard_map/start/pallas_call | solution.py:37
  1.0 3.4 %collective-permute-start.2 = (bf16[256,128]{1,0:T(8,128)(2,1)S(1)}, bf16[256,128]{1,0:T(8,128)(2,1)S(1)}, u32[]{:S(2)}, u32[]{:S(2)}) collective-permute-start(bf16[256,128]{1,0:T(8,128)(2,1)S(1)} %start.1.refs_0_), channel_id=1, source_target_pairs={{0,28},{4,24},{8,20},{12,16},{16,12},{20,8},{24,4},{28,0},{1,29},{... | collective-permute-start | bytes 196616 | tf_op jit(solution)/shard_map/ppermute | solution.py:507
  5.3 2.3 %prep.2 = (f32[256,128]{1,0:T(8,128)S(1)}, f32[8,128]{1,0:T(8,128)S(1)}, bf16[3,8,64,512]{3,2,1,0:T(8,128)(2,1)S(1)}) custom-call(bf16[4,8,1,8,4096]{4,3,2,1,0:T(8,128)(2,1)} %affinity_hbm.3, f32[1,8,64]{2,1,0:T(8,128)} %inv_hbm.1), custom_call_target="tpu_custom_call" | custom-call | tf_op jit(solution)/shard_map/prep/pallas_call | solution.py:37
  8.3 1.2 %collective-permute-done.1.refs_1_ = bf16[256,128]{1,0:T(8,128)(2,1)S(1)} collective-permute-done((bf16[256,128]{1,0:T(8,128)(2,1)S(1)}, bf16[256,128]{1,0:T(8,128)(2,1)S(1)}, u32[]{:S(2)}, u32[]{:S(2)}) %collective-permute-start.1) | collective-permute-done | bytes 65568 | tf_op jit(solution)/shard_map/ppermute | solution.py:507
  9.9 1.0 %collective-permute-done.3.refs_0_ = bf16[2,256,128]{2,1,0:T(8,128)(2,1)S(1)} collective-permute-done((bf16[2,256,128]{2,1,0:T(8,128)(2,1)S(1)}, bf16[2,256,128]{2,1,0:T(8,128)(2,1)S(1)}, u32[]{:S(2)}, u32[]{:S(2)}) %collective-permute-start.3) | collective-permute-done | bytes 131104 | tf_op jit(solution)/shard_map/ppermute | solution.py:507
  11.8 3.7 %collective-permute-start.5 = (bf16[256,128]{1,0:T(8,128)(2,1)S(1)}, bf16[256,128]{1,0:T(8,128)(2,1)S(1)}, u32[]{:S(2)}, u32[]{:S(2)}) collective-permute-start(bf16[256,128]{1,0:T(8,128)(2,1)S(1)} %get-tuple-element.25), channel_id=1, source_target_pairs={{0,3},{1,2},{2,1},{3,0},{4,7},{5,6},{6,5},{7,4},{8,11},{9,10},{10,... | collective-permute-start | bytes 196616 | tf_op jit(solution)/shard_map/ppermute | solution.py:507
  16.2 1.4 %prep.3.matrix_ref = bf16[1,8,64,512]{3,2,1,0:T(8,128)(2,1)S(1)} custom-call(bf16[4,8,1,8,4096]{4,3,2,1,0:T(8,128)(2,1)} %affinity_hbm.3), custom_call_target="tpu_custom_call" | custom-call | tf_op jit(solution)/shard_map/prep/pallas_call | solution.py:37
  18.1 3.2 %collective-permute-done.6.refs_2_ = bf16[256,128]{1,0:T(8,128)(2,1)S(1)} collective-permute-done((bf16[256,128]{1,0:T(8,128)(2,1)S(1)}, bf16[256,128]{1,0:T(8,128)(2,1)S(1)}, u32[]{:S(2)}, u32[]{:S(2)}) %collective-permute-start.6) | collective-permute-done | bytes 65568 | tf_op jit(solution)/shard_map/ppermute | solution.py:507
  21.4 0.9 %collective-permute-start.10 = (bf16[272,128]{1,0:T(8,128)(2,1)S(1)}, bf16[272,128]{1,0:T(8,128)(2,1)S(1)}, u32[]{:S(2)}, u32[]{:S(2)}) collective-permute-start(bf16[272,128]{1,0:T(8,128)(2,1)S(1)} %middle.1.refs_0_), channel_id=1, source_target_pairs={{0,28},{4,24},{8,20},{12,16},{16,12},{20,8},{24,4},{28,0},{1,29},{... | collective-permute-start | bytes 208904 | tf_op jit(solution)/shard_map/ppermute | solution.py:507
  22.3 1.6 %collective-permute-start.8 = (bf16[272,128]{1,0:T(8,128)(2,1)S(1)}, bf16[272,128]{1,0:T(8,128)(2,1)S(1)}, u32[]{:S(2)}, u32[]{:S(2)}) collective-permute-start(bf16[272,128]{1,0:T(8,128)(2,1)S(1)} %middle.1.refs_0_), channel_id=1, source_target_pairs={{0,20},{4,16},{8,28},{12,24},{16,4},{20,0},{24,12},{28,8},{1,21},{... | collective-permute-start | bytes 208904 | tf_op jit(solution)/shard_map/ppermute | solution.py:507
  24.2 2.6 %collective-permute-done.10.refs_1_ = bf16[272,128]{1,0:T(8,128)(2,1)S(1)} collective-permute-done((bf16[272,128]{1,0:T(8,128)(2,1)S(1)}, bf16[272,128]{1,0:T(8,128)(2,1)S(1)}, u32[]{:S(2)}, u32[]{:S(2)}) %collective-permute-start.10) | collective-permute-done | bytes 69664 | tf_op jit(solution)/shard_map/ppermute | solution.py:507
  26.9 1.2 %collective-permute-done.8.refs_0_ = bf16[272,128]{1,0:T(8,128)(2,1)S(1)} collective-permute-done((bf16[272,128]{1,0:T(8,128)(2,1)S(1)}, bf16[272,128]{1,0:T(8,128)(2,1)S(1)}, u32[]{:S(2)}, u32[]{:S(2)}) %collective-permute-start.8) | collective-permute-done | bytes 69664 | tf_op jit(solution)/shard_map/ppermute | solution.py:507
  28.6 1.1 %collective-permute-done.11.refs_2_.refs_0_ = bf16[2,272,128]{2,1,0:T(8,128)(2,1)S(1)} collective-permute-done((bf16[2,272,128]{2,1,0:T(8,128)(2,1)S(1)}, bf16[2,272,128]{2,1,0:T(8,128)(2,1)S(1)}, u32[]{:S(2)}, u32[]{:S(2)}) %collective-permute-start.11) | collective-permute-done | bytes 139296 | tf_op jit(solution)/shard_map/ppermute | solution.py:507
  30.6 2.2 %collective-permute-start.13 = (bf16[272,128]{1,0:T(8,128)(2,1)S(1)}, bf16[272,128]{1,0:T(8,128)(2,1)S(1)}, u32[]{:S(2)}, u32[]{:S(2)}) collective-permute-start(bf16[272,128]{1,0:T(8,128)(2,1)S(1)} %get-tuple-element.30), channel_id=1, source_target_pairs={{0,3},{1,2},{2,1},{3,0},{4,7},{5,6},{6,5},{7,4},{8,11},{9,10},{10,... | collective-permute-start | bytes 208904 | tf_op jit(solution)/shard_map/ppermute | solution.py:507
  32.8 2.3 %collective-permute-start.15 = (bf16[272,128]{1,0:T(8,128)(2,1)S(1)}, bf16[272,128]{1,0:T(8,128)(2,1)S(1)}, u32[]{:S(2)}, u32[]{:S(2)}) collective-permute-start(bf16[272,128]{1,0:T(8,128)(2,1)S(1)} %get-tuple-element.32), channel_id=1, source_target_pairs={{0,1},{1,0},{2,3},{3,2},{4,5},{5,4},{6,7},{7,6},{8,9},{9,8},{10,11... | collective-permute-start | bytes 208904 | tf_op jit(solution)/shard_map/ppermute | solution.py:507
  36.1 1.4 %collective-permute-done.13.refs_1_ = bf16[272,128]{1,0:T(8,128)(2,1)S(1)} collective-permute-done((bf16[272,128]{1,0:T(8,128)(2,1)S(1)}, bf16[272,128]{1,0:T(8,128)(2,1)S(1)}, u32[]{:S(2)}, u32[]{:S(2)}) %collective-permute-start.13) | collective-permute-done | bytes 69664 | tf_op jit(solution)/shard_map/ppermute | solution.py:507
  37.6 2.1 %collective-permute-done.14.refs_2_ = bf16[272,128]{1,0:T(8,128)(2,1)S(1)} collective-permute-done((bf16[272,128]{1,0:T(8,128)(2,1)S(1)}, bf16[272,128]{1,0:T(8,128)(2,1)S(1)}, u32[]{:S(2)}, u32[]{:S(2)}) %collective-permute-start.14) | collective-permute-done | bytes 69664 | tf_op jit(solution)/shard_map/ppermute | solution.py:507
  40.2 2.4 %collective-permute-start.17 = (f32[64,128]{1,0:T(8,128)S(1)}, f32[64,128]{1,0:T(8,128)S(1)}, u32[]{:S(2)}, u32[]{:S(2)}) collective-permute-start(f32[64,128]{1,0:T(8,128)S(1)} %get-tuple-element.34.refs_0_), channel_id=1, source_target_pairs={{0,7},{1,6},{2,5},{3,4},{4,3},{5,2},{6,1},{7,0},{8,15},{9,14},{10,... | collective-permute-start | bytes 98312 | tf_op jit(solution)/shard_map/ppermute | solution.py:517
  43.0 2.6 %collective-permute-done.16.refs_1_ = f32[64,128]{1,0:T(8,128)S(1)} collective-permute-done((f32[64,128]{1,0:T(8,128)S(1)}, f32[64,128]{1,0:T(8,128)S(1)}, u32[]{:S(2)}, u32[]{:S(2)}) %collective-permute-start.16) | collective-permute-done | bytes 32800 | tf_op jit(solution)/shard_map/ppermute | solution.py:517
  45.6 1.0 %collective-permute-done.18.refs_3_ = f32[64,128]{1,0:T(8,128)S(1)} collective-permute-done((f32[64,128]{1,0:T(8,128)S(1)}, f32[64,128]{1,0:T(8,128)S(1)}, u32[]{:S(2)}, u32[]{:S(2)}) %collective-permute-start.18) | collective-permute-done | bytes 32800 | tf_op jit(solution)/shard_map/ppermute | solution.py:517
  46.6 1.5 %collective-permute-start.19 = (f32[32,128]{1,0:T(8,128)S(1)}, f32[32,128]{1,0:T(8,128)S(1)}, u32[]{:S(2)}, u32[]{:S(2)}) collective-permute-start(f32[32,128]{1,0:T(8,128)S(1)} %get-tuple-element.36.refs_0_), channel_id=1, source_target_pairs={{0,28},{4,24},{8,20},{12,16},{16,12},{20,8},{24,4},{28,0},{1,29},{... | collective-permute-start | bytes 49160 | tf_op jit(solution)/shard_map/ppermute | solution.py:507
  49.6 1.3 %first_factor.1.refs_4_.inverse_ref = f32[64,64]{1,0:T(8,128)S(1)} custom-call(f32[32,128]{1,0:T(8,128)S(1)} %get-tuple-element.35.gram_ref), custom_call_target="tpu_custom_call" | custom-call | tf_op jit(solution)/shard_map/first_factor/pallas_call | solution.py:37
  52.2 1.1 %collective-permute-done.22.refs_1_ = f32[32,128]{1,0:T(8,128)S(1)} collective-permute-done((f32[32,128]{1,0:T(8,128)S(1)}, f32[32,128]{1,0:T(8,128)S(1)}, u32[]{:S(2)}, u32[]{:S(2)}) %collective-permute-start.22) | collective-permute-done | bytes 16416 | tf_op jit(solution)/shard_map/ppermute | solution.py:507
  53.3 2.7 %finish.1 = f32[1,8,4096]{2,1,0:T(8,128)} custom-call(f32[256,128]{1,0:T(8,128)S(1)} %get-tuple-element.33.rows_ref, f32[64,64]{1,0:T(8,128)S(1)} %first_factor.1.refs_4_.inverse_ref, f32[32,128]{1,0:T(8,128)S(1)} %add_parts.1.refs_0_, f32[32,128]{1,0:T(8,128)S(1)} %collective-permute-done.22.refs_1_), custom_call_target="tpu_custom_call" | custom-call | tf_op jit(solution)/shard_map/finish/pallas_call | solution.py:37
  (47 shorter events, 10.7 us)
Async XLA Ops:
  1.0 8.7 %copy-start = (s32[4,8,1,8]{3,2,1,0:T(1,128)S(1)}, s32[4,8,1,8]{3,2,1,0:T(1,128)}, u32[]{:S(2)}) copy-start(s32[4,8,1,8]{3,2,1,0:T(1,128)} %param.6) | copy-start | bytes 3076
  1.0 6.6 %collective-permute-start.2 = (bf16[256,128]{1,0:T(8,128)(2,1)S(1)}, bf16[256,128]{1,0:T(8,128)(2,1)S(1)}, u32[]{:S(2)}, u32[]{:S(2)}) collective-permute-start(bf16[256,128]{1,0:T(8,128)(2,1)S(1)} %start.1.refs_0_), channel_id=1, source_target_pairs={{0,28},{4,24},{8,20},{12,16},{16,12},{20,8},{24,4},{28,0},{1,29},{... | collective-permute-start | bytes 196616 | tf_op jit(solution)/shard_map/ppermute | solution.py:507
  4.4 3.9 %collective-permute-start = (bf16[256,128]{1,0:T(8,128)(2,1)S(1)}, bf16[256,128]{1,0:T(8,128)(2,1)S(1)}, u32[]{:S(2)}, u32[]{:S(2)}) collective-permute-start(bf16[256,128]{1,0:T(8,128)(2,1)S(1)} %start.1.refs_0_), channel_id=1, source_target_pairs={{0,20},{4,16},{8,28},{12,24},{16,4},{20,0},{24,12},{28,8},{1,21},{... | collective-permute-start | bytes 196616 | tf_op jit(solution)/shard_map/ppermute | solution.py:507
  5.2 4.3 %collective-permute-start.1 = (bf16[256,128]{1,0:T(8,128)(2,1)S(1)}, bf16[256,128]{1,0:T(8,128)(2,1)S(1)}, u32[]{:S(2)}, u32[]{:S(2)}) collective-permute-start(bf16[256,128]{1,0:T(8,128)(2,1)S(1)} %start.1.refs_0_), channel_id=1, source_target_pairs={{0,12},{4,8},{8,4},{12,0},{16,28},{20,24},{24,20},{28,16},{1,13},{... | collective-permute-start | bytes 196616 | tf_op jit(solution)/shard_map/ppermute | solution.py:507
  7.7 2.3 %collective-permute-start.4 = (bf16[2,256,128]{2,1,0:T(8,128)(2,1)S(1)}, bf16[2,256,128]{2,1,0:T(8,128)(2,1)S(1)}, u32[]{:S(2)}, u32[]{:S(2)}) collective-permute-start(bf16[2,256,128]{2,1,0:T(8,128)(2,1)S(1)} %stack.5.refs_1_.refs_3_), channel_id=1, source_target_pairs={{0,4},{4,0},{8,12},{12,8},{16,20},{20,16},{24,28},{28,24},{1,5},{5... | collective-permute-start | bytes 393224 | tf_op jit(solution)/shard_map/ppermute | solution.py:507
  9.5 1.4 %collective-permute-start.3 = (bf16[2,256,128]{2,1,0:T(8,128)(2,1)S(1)}, bf16[2,256,128]{2,1,0:T(8,128)(2,1)S(1)}, u32[]{:S(2)}, u32[]{:S(2)}) collective-permute-start(bf16[2,256,128]{2,1,0:T(8,128)(2,1)S(1)} %stack.4.refs_0_.refs_2_), channel_id=1, source_target_pairs={{0,4},{4,0},{8,12},{12,8},{16,20},{20,16},{24,28},{28,24},{1,5},{5... | collective-permute-start | bytes 393224 | tf_op jit(solution)/shard_map/ppermute | solution.py:507
  11.8 6.4 %collective-permute-start.5 = (bf16[256,128]{1,0:T(8,128)(2,1)S(1)}, bf16[256,128]{1,0:T(8,128)(2,1)S(1)}, u32[]{:S(2)}, u32[]{:S(2)}) collective-permute-start(bf16[256,128]{1,0:T(8,128)(2,1)S(1)} %get-tuple-element.25), channel_id=1, source_target_pairs={{0,3},{1,2},{2,1},{3,0},{4,7},{5,6},{6,5},{7,4},{8,11},{9,10},{10,... | collective-permute-start | bytes 196616 | tf_op jit(solution)/shard_map/ppermute | solution.py:507
  15.4 5.9 %collective-permute-start.6 = (bf16[256,128]{1,0:T(8,128)(2,1)S(1)}, bf16[256,128]{1,0:T(8,128)(2,1)S(1)}, u32[]{:S(2)}, u32[]{:S(2)}) collective-permute-start(bf16[256,128]{1,0:T(8,128)(2,1)S(1)} %get-tuple-element.26), channel_id=1, source_target_pairs={{0,2},{1,3},{2,0},{3,1},{4,6},{5,7},{6,4},{7,5},{8,10},{9,11},{10,... | collective-permute-start | bytes 196616 | tf_op jit(solution)/shard_map/ppermute | solution.py:507
  15.4 5.9 %collective-permute-start.7 = (bf16[256,128]{1,0:T(8,128)(2,1)S(1)}, bf16[256,128]{1,0:T(8,128)(2,1)S(1)}, u32[]{:S(2)}, u32[]{:S(2)}) collective-permute-start(bf16[256,128]{1,0:T(8,128)(2,1)S(1)} %get-tuple-element.27), channel_id=1, source_target_pairs={{0,1},{1,0},{2,3},{3,2},{4,5},{5,4},{6,7},{7,6},{8,9},{9,8},{10,11... | collective-permute-start | bytes 196616 | tf_op jit(solution)/shard_map/ppermute | solution.py:507
  21.4 5.4 %collective-permute-start.10 = (bf16[272,128]{1,0:T(8,128)(2,1)S(1)}, bf16[272,128]{1,0:T(8,128)(2,1)S(1)}, u32[]{:S(2)}, u32[]{:S(2)}) collective-permute-start(bf16[272,128]{1,0:T(8,128)(2,1)S(1)} %middle.1.refs_0_), channel_id=1, source_target_pairs={{0,28},{4,24},{8,20},{12,16},{16,12},{20,8},{24,4},{28,0},{1,29},{... | collective-permute-start | bytes 208904 | tf_op jit(solution)/shard_map/ppermute | solution.py:507
  22.3 5.8 %collective-permute-start.8 = (bf16[272,128]{1,0:T(8,128)(2,1)S(1)}, bf16[272,128]{1,0:T(8,128)(2,1)S(1)}, u32[]{:S(2)}, u32[]{:S(2)}) collective-permute-start(bf16[272,128]{1,0:T(8,128)(2,1)S(1)} %middle.1.refs_0_), channel_id=1, source_target_pairs={{0,20},{4,16},{8,28},{12,24},{16,4},{20,0},{24,12},{28,8},{1,21},{... | collective-permute-start | bytes 208904 | tf_op jit(solution)/shard_map/ppermute | solution.py:507
  23.9 4.4 %collective-permute-start.9 = (bf16[272,128]{1,0:T(8,128)(2,1)S(1)}, bf16[272,128]{1,0:T(8,128)(2,1)S(1)}, u32[]{:S(2)}, u32[]{:S(2)}) collective-permute-start(bf16[272,128]{1,0:T(8,128)(2,1)S(1)} %middle.1.refs_0_), channel_id=1, source_target_pairs={{0,12},{4,8},{8,4},{12,0},{16,28},{20,24},{24,20},{28,16},{1,13},{... | collective-permute-start | bytes 208904 | tf_op jit(solution)/shard_map/ppermute | solution.py:507
  26.8 1.8 %collective-permute-start.12 = (bf16[2,272,128]{2,1,0:T(8,128)(2,1)S(1)}, bf16[2,272,128]{2,1,0:T(8,128)(2,1)S(1)}, u32[]{:S(2)}, u32[]{:S(2)}) collective-permute-start(bf16[2,272,128]{2,1,0:T(8,128)(2,1)S(1)} %stack.7.refs_1_.refs_3_), channel_id=1, source_target_pairs={{0,4},{4,0},{8,12},{12,8},{16,20},{20,16},{24,28},{28,24},{1,5},{5... | collective-permute-start | bytes 417800 | tf_op jit(solution)/shard_map/ppermute | solution.py:507
  28.4 1.4 %collective-permute-start.11 = (bf16[2,272,128]{2,1,0:T(8,128)(2,1)S(1)}, bf16[2,272,128]{2,1,0:T(8,128)(2,1)S(1)}, u32[]{:S(2)}, u32[]{:S(2)}) collective-permute-start(bf16[2,272,128]{2,1,0:T(8,128)(2,1)S(1)} %stack.6.refs_0_.refs_2_), channel_id=1, source_target_pairs={{0,4},{4,0},{8,12},{12,8},{16,20},{20,16},{24,28},{28,24},{1,5},{5... | collective-permute-start | bytes 417800 | tf_op jit(solution)/shard_map/ppermute | solution.py:507
  30.6 6.9 %collective-permute-start.13 = (bf16[272,128]{1,0:T(8,128)(2,1)S(1)}, bf16[272,128]{1,0:T(8,128)(2,1)S(1)}, u32[]{:S(2)}, u32[]{:S(2)}) collective-permute-start(bf16[272,128]{1,0:T(8,128)(2,1)S(1)} %get-tuple-element.30), channel_id=1, source_target_pairs={{0,3},{1,2},{2,1},{3,0},{4,7},{5,6},{6,5},{7,4},{8,11},{9,10},{10,... | collective-permute-start | bytes 208904 | tf_op jit(solution)/shard_map/ppermute | solution.py:507
  32.8 6.9 %collective-permute-start.14 = (bf16[272,128]{1,0:T(8,128)(2,1)S(1)}, bf16[272,128]{1,0:T(8,128)(2,1)S(1)}, u32[]{:S(2)}, u32[]{:S(2)}) collective-permute-start(bf16[272,128]{1,0:T(8,128)(2,1)S(1)} %get-tuple-element.31), channel_id=1, source_target_pairs={{0,2},{1,3},{2,0},{3,1},{4,6},{5,7},{6,4},{7,5},{8,10},{9,11},{10,... | collective-permute-start | bytes 208904 | tf_op jit(solution)/shard_map/ppermute | solution.py:507
  32.8 6.9 %collective-permute-start.15 = (bf16[272,128]{1,0:T(8,128)(2,1)S(1)}, bf16[272,128]{1,0:T(8,128)(2,1)S(1)}, u32[]{:S(2)}, u32[]{:S(2)}) collective-permute-start(bf16[272,128]{1,0:T(8,128)(2,1)S(1)} %get-tuple-element.32), channel_id=1, source_target_pairs={{0,1},{1,0},{2,3},{3,2},{4,5},{5,4},{6,7},{7,6},{8,9},{9,8},{10,11... | collective-permute-start | bytes 208904 | tf_op jit(solution)/shard_map/ppermute | solution.py:507
  40.2 5.4 %collective-permute-start.16 = (f32[64,128]{1,0:T(8,128)S(1)}, f32[64,128]{1,0:T(8,128)S(1)}, u32[]{:S(2)}, u32[]{:S(2)}) collective-permute-start(f32[64,128]{1,0:T(8,128)S(1)} %get-tuple-element.34.refs_0_), channel_id=1, source_target_pairs={{0,6},{1,7},{2,4},{3,5},{4,2},{5,3},{6,0},{7,1},{8,14},{9,15},{10,... | collective-permute-start | bytes 98312 | tf_op jit(solution)/shard_map/ppermute | solution.py:517
  40.2 5.4 %collective-permute-start.17 = (f32[64,128]{1,0:T(8,128)S(1)}, f32[64,128]{1,0:T(8,128)S(1)}, u32[]{:S(2)}, u32[]{:S(2)}) collective-permute-start(f32[64,128]{1,0:T(8,128)S(1)} %get-tuple-element.34.refs_0_), channel_id=1, source_target_pairs={{0,7},{1,6},{2,5},{3,4},{4,3},{5,2},{6,1},{7,0},{8,15},{9,14},{10,... | collective-permute-start | bytes 98312 | tf_op jit(solution)/shard_map/ppermute | solution.py:517
  42.6 4.0 %collective-permute-start.18 = (f32[64,128]{1,0:T(8,128)S(1)}, f32[64,128]{1,0:T(8,128)S(1)}, u32[]{:S(2)}, u32[]{:S(2)}) collective-permute-start(f32[64,128]{1,0:T(8,128)S(1)} %get-tuple-element.34.refs_0_), channel_id=1, source_target_pairs={{0,5},{1,4},{2,7},{3,6},{4,1},{5,0},{6,3},{7,2},{8,13},{9,12},{10,... | collective-permute-start | bytes 98312 | tf_op jit(solution)/shard_map/ppermute | solution.py:517
  46.6 4.3 %collective-permute-start.19 = (f32[32,128]{1,0:T(8,128)S(1)}, f32[32,128]{1,0:T(8,128)S(1)}, u32[]{:S(2)}, u32[]{:S(2)}) collective-permute-start(f32[32,128]{1,0:T(8,128)S(1)} %get-tuple-element.36.refs_0_), channel_id=1, source_target_pairs={{0,28},{4,24},{8,20},{12,16},{16,12},{20,8},{24,4},{28,0},{1,29},{... | collective-permute-start | bytes 49160 | tf_op jit(solution)/shard_map/ppermute | solution.py:507
  48.0 3.2 %collective-permute-start.20 = (f32[32,128]{1,0:T(8,128)S(1)}, f32[32,128]{1,0:T(8,128)S(1)}, u32[]{:S(2)}, u32[]{:S(2)}) collective-permute-start(f32[32,128]{1,0:T(8,128)S(1)} %get-tuple-element.36.refs_0_), channel_id=1, source_target_pairs={{0,20},{4,16},{8,28},{12,24},{16,4},{20,0},{24,12},{28,8},{1,21},{... | collective-permute-start | bytes 49160 | tf_op jit(solution)/shard_map/ppermute | solution.py:507
  48.9 3.2 %collective-permute-start.21 = (f32[32,128]{1,0:T(8,128)S(1)}, f32[32,128]{1,0:T(8,128)S(1)}, u32[]{:S(2)}, u32[]{:S(2)}) collective-permute-start(f32[32,128]{1,0:T(8,128)S(1)} %get-tuple-element.36.refs_0_), channel_id=1, source_target_pairs={{0,12},{4,8},{8,4},{12,0},{16,28},{20,24},{24,20},{28,16},{1,13},{... | collective-permute-start | bytes 49160 | tf_op jit(solution)/shard_map/ppermute | solution.py:507
  52.1 1.2 %collective-permute-start.22 = (f32[32,128]{1,0:T(8,128)S(1)}, f32[32,128]{1,0:T(8,128)S(1)}, u32[]{:S(2)}, u32[]{:S(2)}) collective-permute-start(f32[32,128]{1,0:T(8,128)S(1)} %add_parts.1.refs_0_), channel_id=1, source_target_pairs={{0,4},{4,0},{8,12},{12,8},{16,20},{20,16},{24,28},{28,24},{1,5},{5... | collective-permute-start | bytes 49160 | tf_op jit(solution)/shard_map/ppermute | solution.py:507
  (1 other events, 8.7 us)

commit v16 on v15

--- a/solution.py
+++ b/solution.py
@@ -534,8 +534,11 @@
         held = held + [swap(piece, "rows", mask) for mask in masks for piece in held]
         offsets = offsets + [mask ^ offset for mask in masks for offset in offsets]
     split = len(held) // 2
-    held, offsets = held[split:] + held[:split], offsets[split:] + offsets[:split]
-    near = [stack(held[:split], []), stack(held[split:], after)]
+    if after:
+        held, offsets = held[split:] + held[:split], offsets[split:] + offsets[:split]
+        near = [stack(held[:split], []), stack(held[split:], after)]
+    else:
+        near = [piece[None] for piece in held]
     (last,) = plan[-1]
     offsets = offsets + [last ^ offset for offset in offsets]
     return near, [swap(pieces, "rows", last) for pieces in near], offsets

time: 56.1 us -> 56.3 us (level)
  starting transfers between devices: 22.5 us -> 23.3 us
  waiting for transfers between devices: 20.6 us -> 19.9 us
    ppermute x20 -> x22, starting transfers between devices: 19.6 us -> 20.4 us  [swap(): lax.ppermute(value, axis, [(index, index ^ mask) for index in range(size)])]
    ppermute x20 -> x22, waiting for transfers between devices: 17 us -> 16.3 us  [swap(): lax.ppermute(value, axis, [(index, index ^ mask) for index in range(size)])]
    pallas_call x20 -> x18, Pallas kernels: 12.6 us -> 12.6 us  [call(): pl.pallas_call(kernel, out_shape=outs, in_specs=ins, out_specs=jax.tree.m...]
  transfers between devices with their start and end apart: 23 -> 25, of which waited for: 16 -> 16; matrix products, arithmetic and copies ran while one was open for 0% -> 0% of each run, Pallas kernels for 12% -> 12%
where the time goes in v16:
time: 56.3 us; the launch traced here: 56.1 us
  starting transfers between devices  23.3 us (41%)
  waiting for transfers between devices  19.9 us (35%)
  Pallas kernels  12.6 us (22%)
    ppermute x22, starting transfers between devices, swap(): lax.ppermute(value, axis, [(index, index ^ mask) for index in range(size)])  20.4 us
    ppermute x22, waiting for transfers between devices, swap(): lax.ppermute(value, axis, [(index, index ^ mask) for index in range(size)])  16.3 us
    pallas_call x18, Pallas kernels, call(): pl.pallas_call(kernel, out_shape=outs, in_specs=ins, out_specs=jax.tree.m...  12.6 us
    ppermute x3, waiting for transfers between devices, swap_both(): return lax.ppermute(value, ('rows', 'cols'), pairs)  3.58 us
    ppermute x3, starting transfers between devices, swap_both(): return lax.ppermute(value, ('rows', 'cols'), pairs)  2.84 us
  transfers between devices with their start and end apart: 25, of which 16 were waited for; matrix products, arithmetic and copies ran while one was open for 0% of the time, Pallas kernels for 12%

profile of v16, /device:TPU:0, one launch (start us, length us, event | category | flops | bytes accessed | tf_op | source)
XLA Modules:
  0.0 56.1 jit_solution(3164057709518612780)
XLA Ops:
  0.0 1.0 %start.1.refs_0_ = bf16[256,128]{1,0:T(8,128)(2,1)S(1)} custom-call(f32[1,8,4096]{2,1,0:T(8,128)} %panel_hbm.1, f32[1,8,64]{2,1,0:T(8,128)} %inv_hbm.1), custom_call_target="tpu_custom_call" | custom-call | tf_op jit(solution)/shard_map/start/pallas_call | solution.py:37
  1.0 3.4 %collective-permute-start.2 = (bf16[256,128]{1,0:T(8,128)(2,1)S(1)}, bf16[256,128]{1,0:T(8,128)(2,1)S(1)}, u32[]{:S(2)}, u32[]{:S(2)}) collective-permute-start(bf16[256,128]{1,0:T(8,128)(2,1)S(1)} %start.1.refs_0_), channel_id=1, source_target_pairs={{0,28},{4,24},{8,20},{12,16},{16,12},{20,8},{24,4},{28,0},{1,29},{... | collective-permute-start | bytes 196616 | tf_op jit(solution)/shard_map/ppermute | solution.py:507
  5.3 2.3 %prep.2 = (f32[256,128]{1,0:T(8,128)S(1)}, f32[8,128]{1,0:T(8,128)S(1)}, bf16[3,8,64,512]{3,2,1,0:T(8,128)(2,1)S(1)}) custom-call(bf16[4,8,1,8,4096]{4,3,2,1,0:T(8,128)(2,1)} %affinity_hbm.3, f32[1,8,64]{2,1,0:T(8,128)} %inv_hbm.1), custom_call_target="tpu_custom_call" | custom-call | tf_op jit(solution)/shard_map/prep/pallas_call | solution.py:37
  8.3 1.2 %collective-permute-done.1.refs_1_ = bf16[256,128]{1,0:T(8,128)(2,1)S(1)} collective-permute-done((bf16[256,128]{1,0:T(8,128)(2,1)S(1)}, bf16[256,128]{1,0:T(8,128)(2,1)S(1)}, u32[]{:S(2)}, u32[]{:S(2)}) %collective-permute-start.1) | collective-permute-done | bytes 65568 | tf_op jit(solution)/shard_map/ppermute | solution.py:507
  9.9 1.0 %collective-permute-done.3.refs_0_ = bf16[2,256,128]{2,1,0:T(8,128)(2,1)S(1)} collective-permute-done((bf16[2,256,128]{2,1,0:T(8,128)(2,1)S(1)}, bf16[2,256,128]{2,1,0:T(8,128)(2,1)S(1)}, u32[]{:S(2)}, u32[]{:S(2)}) %collective-permute-start.3) | collective-permute-done | bytes 131104 | tf_op jit(solution)/shard_map/ppermute | solution.py:507
  11.8 3.7 %collective-permute-start.5 = (bf16[256,128]{1,0:T(8,128)(2,1)S(1)}, bf16[256,128]{1,0:T(8,128)(2,1)S(1)}, u32[]{:S(2)}, u32[]{:S(2)}) collective-permute-start(bf16[256,128]{1,0:T(8,128)(2,1)S(1)} %get-tuple-element.25), channel_id=1, source_target_pairs={{0,3},{1,2},{2,1},{3,0},{4,7},{5,6},{6,5},{7,4},{8,11},{9,10},{10,... | collective-permute-start | bytes 196616 | tf_op jit(solution)/shard_map/ppermute | solution.py:507
  16.2 1.4 %prep.3.matrix_ref = bf16[1,8,64,512]{3,2,1,0:T(8,128)(2,1)S(1)} custom-call(bf16[4,8,1,8,4096]{4,3,2,1,0:T(8,128)(2,1)} %affinity_hbm.3), custom_call_target="tpu_custom_call" | custom-call | tf_op jit(solution)/shard_map/prep/pallas_call | solution.py:37
  18.1 3.2 %collective-permute-done.6.refs_2_ = bf16[256,128]{1,0:T(8,128)(2,1)S(1)} collective-permute-done((bf16[256,128]{1,0:T(8,128)(2,1)S(1)}, bf16[256,128]{1,0:T(8,128)(2,1)S(1)}, u32[]{:S(2)}, u32[]{:S(2)}) %collective-permute-start.6) | collective-permute-done | bytes 65568 | tf_op jit(solution)/shard_map/ppermute | solution.py:507
  22.3 1.6 %collective-permute-start.9 = (bf16[272,128]{1,0:T(8,128)(2,1)S(1)}, bf16[272,128]{1,0:T(8,128)(2,1)S(1)}, u32[]{:S(2)}, u32[]{:S(2)}) collective-permute-start(bf16[272,128]{1,0:T(8,128)(2,1)S(1)} %middle.1), channel_id=1, source_target_pairs={{0,20},{4,16},{8,28},{12,24},{16,4},{20,0},{24,12},{28,8},{1,21},{... | collective-permute-start | bytes 208904 | tf_op jit(solution)/shard_map/ppermute | solution.py:507
  24.8 2.0 %collective-permute-done.8 = bf16[272,128]{1,0:T(8,128)(2,1)S(1)} collective-permute-done((bf16[272,128]{1,0:T(8,128)(2,1)S(1)}, bf16[272,128]{1,0:T(8,128)(2,1)S(1)}, u32[]{:S(2)}, u32[]{:S(2)}) %collective-permute-start.8) | collective-permute-done | bytes 69664 | tf_op jit(solution)/shard_map/ppermute | solution.py:507
  26.8 1.3 %collective-permute-done.9 = bf16[272,128]{1,0:T(8,128)(2,1)S(1)} collective-permute-done((bf16[272,128]{1,0:T(8,128)(2,1)S(1)}, bf16[272,128]{1,0:T(8,128)(2,1)S(1)}, u32[]{:S(2)}, u32[]{:S(2)}) %collective-permute-start.9) | collective-permute-done | bytes 69664 | tf_op jit(solution)/shard_map/ppermute | solution.py:507
  30.4 2.2 %collective-permute-start.15 = (bf16[272,128]{1,0:T(8,128)(2,1)S(1)}, bf16[272,128]{1,0:T(8,128)(2,1)S(1)}, u32[]{:S(2)}, u32[]{:S(2)}) collective-permute-start(bf16[272,128]{1,0:T(8,128)(2,1)S(1)} %get-tuple-element.30), channel_id=1, source_target_pairs={{0,3},{1,2},{2,1},{3,0},{4,7},{5,6},{6,5},{7,4},{8,11},{9,10},{10,... | collective-permute-start | bytes 208904 | tf_op jit(solution)/shard_map/ppermute | solution.py:507
  32.6 2.3 %collective-permute-start.17 = (bf16[272,128]{1,0:T(8,128)(2,1)S(1)}, bf16[272,128]{1,0:T(8,128)(2,1)S(1)}, u32[]{:S(2)}, u32[]{:S(2)}) collective-permute-start(bf16[272,128]{1,0:T(8,128)(2,1)S(1)} %get-tuple-element.32), channel_id=1, source_target_pairs={{0,1},{1,0},{2,3},{3,2},{4,5},{5,4},{6,7},{7,6},{8,9},{9,8},{10,11... | collective-permute-start | bytes 208904 | tf_op jit(solution)/shard_map/ppermute | solution.py:507
  36.0 1.4 %collective-permute-done.15.refs_1_ = bf16[272,128]{1,0:T(8,128)(2,1)S(1)} collective-permute-done((bf16[272,128]{1,0:T(8,128)(2,1)S(1)}, bf16[272,128]{1,0:T(8,128)(2,1)S(1)}, u32[]{:S(2)}, u32[]{:S(2)}) %collective-permute-start.15) | collective-permute-done | bytes 69664 | tf_op jit(solution)/shard_map/ppermute | solution.py:507
  37.4 2.2 %collective-permute-done.16.refs_2_ = bf16[272,128]{1,0:T(8,128)(2,1)S(1)} collective-permute-done((bf16[272,128]{1,0:T(8,128)(2,1)S(1)}, bf16[272,128]{1,0:T(8,128)(2,1)S(1)}, u32[]{:S(2)}, u32[]{:S(2)}) %collective-permute-start.16) | collective-permute-done | bytes 69664 | tf_op jit(solution)/shard_map/ppermute | solution.py:507
  40.1 2.4 %collective-permute-start.19 = (f32[64,128]{1,0:T(8,128)S(1)}, f32[64,128]{1,0:T(8,128)S(1)}, u32[]{:S(2)}, u32[]{:S(2)}) collective-permute-start(f32[64,128]{1,0:T(8,128)S(1)} %get-tuple-element.34.refs_0_), channel_id=1, source_target_pairs={{0,7},{1,6},{2,5},{3,4},{4,3},{5,2},{6,1},{7,0},{8,15},{9,14},{10,... | collective-permute-start | bytes 98312 | tf_op jit(solution)/shard_map/ppermute | solution.py:517
  42.9 2.6 %collective-permute-done.18.refs_1_ = f32[64,128]{1,0:T(8,128)S(1)} collective-permute-done((f32[64,128]{1,0:T(8,128)S(1)}, f32[64,128]{1,0:T(8,128)S(1)}, u32[]{:S(2)}, u32[]{:S(2)}) %collective-permute-start.18) | collective-permute-done | bytes 32800 | tf_op jit(solution)/shard_map/ppermute | solution.py:517
  45.5 1.0 %collective-permute-done.20.refs_3_ = f32[64,128]{1,0:T(8,128)S(1)} collective-permute-done((f32[64,128]{1,0:T(8,128)S(1)}, f32[64,128]{1,0:T(8,128)S(1)}, u32[]{:S(2)}, u32[]{:S(2)}) %collective-permute-start.20) | collective-permute-done | bytes 32800 | tf_op jit(solution)/shard_map/ppermute | solution.py:517
  46.5 1.3 %collective-permute-start.21 = (f32[32,128]{1,0:T(8,128)S(1)}, f32[32,128]{1,0:T(8,128)S(1)}, u32[]{:S(2)}, u32[]{:S(2)}) collective-permute-start(f32[32,128]{1,0:T(8,128)S(1)} %get-tuple-element.36.refs_0_), channel_id=1, source_target_pairs={{0,28},{4,24},{8,20},{12,16},{16,12},{20,8},{24,4},{28,0},{1,29},{... | collective-permute-start | bytes 49160 | tf_op jit(solution)/shard_map/ppermute | solution.py:507
  47.9 1.1 %collective-permute-start.22 = (f32[32,128]{1,0:T(8,128)S(1)}, f32[32,128]{1,0:T(8,128)S(1)}, u32[]{:S(2)}, u32[]{:S(2)}) collective-permute-start(f32[32,128]{1,0:T(8,128)S(1)} %get-tuple-element.36.refs_0_), channel_id=1, source_target_pairs={{0,20},{4,16},{8,28},{12,24},{16,4},{20,0},{24,12},{28,8},{1,21},{... | collective-permute-start | bytes 49160 | tf_op jit(solution)/shard_map/ppermute | solution.py:507
  49.5 1.3 %first_factor.1.refs_4_.inverse_ref = f32[64,64]{1,0:T(8,128)S(1)} custom-call(f32[32,128]{1,0:T(8,128)S(1)} %get-tuple-element.35.gram_ref), custom_call_target="tpu_custom_call" | custom-call | tf_op jit(solution)/shard_map/first_factor/pallas_call | solution.py:37
  51.1 1.1 %collective-permute-done.23.refs_3_ = f32[32,128]{1,0:T(8,128)S(1)} collective-permute-done((f32[32,128]{1,0:T(8,128)S(1)}, f32[32,128]{1,0:T(8,128)S(1)}, u32[]{:S(2)}, u32[]{:S(2)}) %collective-permute-start.23) | collective-permute-done | bytes 16416 | tf_op jit(solution)/shard_map/ppermute | solution.py:507
  52.3 1.1 %collective-permute-done.24.refs_1_ = f32[32,128]{1,0:T(8,128)S(1)} collective-permute-done((f32[32,128]{1,0:T(8,128)S(1)}, f32[32,128]{1,0:T(8,128)S(1)}, u32[]{:S(2)}, u32[]{:S(2)}) %collective-permute-start.24) | collective-permute-done | bytes 16416 | tf_op jit(solution)/shard_map/ppermute | solution.py:507
  53.4 2.7 %finish.1 = f32[1,8,4096]{2,1,0:T(8,128)} custom-call(f32[256,128]{1,0:T(8,128)S(1)} %get-tuple-element.33.rows_ref, f32[64,64]{1,0:T(8,128)S(1)} %first_factor.1.refs_4_.inverse_ref, f32[32,128]{1,0:T(8,128)S(1)} %add_parts.1.refs_0_, f32[32,128]{1,0:T(8,128)S(1)} %collective-permute-done.24.refs_1_), custom_call_target="tpu_custom_call" | custom-call | tf_op jit(solution)/shard_map/finish/pallas_call | solution.py:37
  (49 shorter events, 11.1 us)
Async XLA Ops:
  1.0 6.6 %collective-permute-start.2 = (bf16[256,128]{1,0:T(8,128)(2,1)S(1)}, bf16[256,128]{1,0:T(8,128)(2,1)S(1)}, u32[]{:S(2)}, u32[]{:S(2)}) collective-permute-start(bf16[256,128]{1,0:T(8,128)(2,1)S(1)} %start.1.refs_0_), channel_id=1, source_target_pairs={{0,28},{4,24},{8,20},{12,16},{16,12},{20,8},{24,4},{28,0},{1,29},{... | collective-permute-start | bytes 196616 | tf_op jit(solution)/shard_map/ppermute | solution.py:507
  4.4 3.9 %collective-permute-start = (bf16[256,128]{1,0:T(8,128)(2,1)S(1)}, bf16[256,128]{1,0:T(8,128)(2,1)S(1)}, u32[]{:S(2)}, u32[]{:S(2)}) collective-permute-start(bf16[256,128]{1,0:T(8,128)(2,1)S(1)} %start.1.refs_0_), channel_id=1, source_target_pairs={{0,20},{4,16},{8,28},{12,24},{16,4},{20,0},{24,12},{28,8},{1,21},{... | collective-permute-start | bytes 196616 | tf_op jit(solution)/shard_map/ppermute | solution.py:507
  5.2 4.3 %collective-permute-start.1 = (bf16[256,128]{1,0:T(8,128)(2,1)S(1)}, bf16[256,128]{1,0:T(8,128)(2,1)S(1)}, u32[]{:S(2)}, u32[]{:S(2)}) collective-permute-start(bf16[256,128]{1,0:T(8,128)(2,1)S(1)} %start.1.refs_0_), channel_id=1, source_target_pairs={{0,12},{4,8},{8,4},{12,0},{16,28},{20,24},{24,20},{28,16},{1,13},{... | collective-permute-start | bytes 196616 | tf_op jit(solution)/shard_map/ppermute | solution.py:507
  7.7 2.3 %collective-permute-start.4 = (bf16[2,256,128]{2,1,0:T(8,128)(2,1)S(1)}, bf16[2,256,128]{2,1,0:T(8,128)(2,1)S(1)}, u32[]{:S(2)}, u32[]{:S(2)}) collective-permute-start(bf16[2,256,128]{2,1,0:T(8,128)(2,1)S(1)} %stack.3.refs_1_.refs_3_), channel_id=1, source_target_pairs={{0,4},{4,0},{8,12},{12,8},{16,20},{20,16},{24,28},{28,24},{1,5},{5... | collective-permute-start | bytes 393224 | tf_op jit(solution)/shard_map/ppermute | solution.py:507
  9.5 1.4 %collective-permute-start.3 = (bf16[2,256,128]{2,1,0:T(8,128)(2,1)S(1)}, bf16[2,256,128]{2,1,0:T(8,128)(2,1)S(1)}, u32[]{:S(2)}, u32[]{:S(2)}) collective-permute-start(bf16[2,256,128]{2,1,0:T(8,128)(2,1)S(1)} %stack.2.refs_0_.refs_2_), channel_id=1, source_target_pairs={{0,4},{4,0},{8,12},{12,8},{16,20},{20,16},{24,28},{28,24},{1,5},{5... | collective-permute-start | bytes 393224 | tf_op jit(solution)/shard_map/ppermute | solution.py:507
  11.8 6.4 %collective-permute-start.5 = (bf16[256,128]{1,0:T(8,128)(2,1)S(1)}, bf16[256,128]{1,0:T(8,128)(2,1)S(1)}, u32[]{:S(2)}, u32[]{:S(2)}) collective-permute-start(bf16[256,128]{1,0:T(8,128)(2,1)S(1)} %get-tuple-element.25), channel_id=1, source_target_pairs={{0,3},{1,2},{2,1},{3,0},{4,7},{5,6},{6,5},{7,4},{8,11},{9,10},{10,... | collective-permute-start | bytes 196616 | tf_op jit(solution)/shard_map/ppermute | solution.py:507
  15.4 5.9 %collective-permute-start.6 = (bf16[256,128]{1,0:T(8,128)(2,1)S(1)}, bf16[256,128]{1,0:T(8,128)(2,1)S(1)}, u32[]{:S(2)}, u32[]{:S(2)}) collective-permute-start(bf16[256,128]{1,0:T(8,128)(2,1)S(1)} %get-tuple-element.26), channel_id=1, source_target_pairs={{0,2},{1,3},{2,0},{3,1},{4,6},{5,7},{6,4},{7,5},{8,10},{9,11},{10,... | collective-permute-start | bytes 196616 | tf_op jit(solution)/shard_map/ppermute | solution.py:507
  15.4 5.9 %collective-permute-start.7 = (bf16[256,128]{1,0:T(8,128)(2,1)S(1)}, bf16[256,128]{1,0:T(8,128)(2,1)S(1)}, u32[]{:S(2)}, u32[]{:S(2)}) collective-permute-start(bf16[256,128]{1,0:T(8,128)(2,1)S(1)} %get-tuple-element.27), channel_id=1, source_target_pairs={{0,1},{1,0},{2,3},{3,2},{4,5},{5,4},{6,7},{7,6},{8,9},{9,8},{10,11... | collective-permute-start | bytes 196616 | tf_op jit(solution)/shard_map/ppermute | solution.py:507
  21.4 5.4 %collective-permute-start.8 = (bf16[272,128]{1,0:T(8,128)(2,1)S(1)}, bf16[272,128]{1,0:T(8,128)(2,1)S(1)}, u32[]{:S(2)}, u32[]{:S(2)}) collective-permute-start(bf16[272,128]{1,0:T(8,128)(2,1)S(1)} %middle.1), channel_id=1, source_target_pairs={{0,28},{4,24},{8,20},{12,16},{16,12},{20,8},{24,4},{28,0},{1,29},{... | collective-permute-start | bytes 208904 | tf_op jit(solution)/shard_map/ppermute | solution.py:507
  22.3 5.8 %collective-permute-start.9 = (bf16[272,128]{1,0:T(8,128)(2,1)S(1)}, bf16[272,128]{1,0:T(8,128)(2,1)S(1)}, u32[]{:S(2)}, u32[]{:S(2)}) collective-permute-start(bf16[272,128]{1,0:T(8,128)(2,1)S(1)} %middle.1), channel_id=1, source_target_pairs={{0,20},{4,16},{8,28},{12,24},{16,4},{20,0},{24,12},{28,8},{1,21},{... | collective-permute-start | bytes 208904 | tf_op jit(solution)/shard_map/ppermute | solution.py:507
  23.9 4.4 %collective-permute-start.10 = (bf16[272,128]{1,0:T(8,128)(2,1)S(1)}, bf16[272,128]{1,0:T(8,128)(2,1)S(1)}, u32[]{:S(2)}, u32[]{:S(2)}) collective-permute-start(bf16[272,128]{1,0:T(8,128)(2,1)S(1)} %middle.1), channel_id=1, source_target_pairs={{0,12},{4,8},{8,4},{12,0},{16,28},{20,24},{24,20},{28,16},{1,13},{... | collective-permute-start | bytes 208904 | tf_op jit(solution)/shard_map/ppermute | solution.py:507
  24.2 4.5 %collective-permute-start.11 = (bf16[1,272,128]{2,1,0:T(8,128)(2,1)S(1)}, bf16[1,272,128]{2,1,0:T(8,128)(2,1)S(1)}, u32[]{:S(2)}, u32[]{:S(2)}) collective-permute-start(bf16[1,272,128]{2,1,0:T(8,128)(2,1)S(1)} %bitcast.8), channel_id=1, source_target_pairs={{0,4},{4,0},{8,12},{12,8},{16,20},{20,16},{24,28},{28,24},{1,5},{5... | collective-permute-start | bytes 208904 | tf_op jit(solution)/shard_map/ppermute | solution.py:507
  26.8 2.0 %collective-permute-start.12 = (bf16[1,272,128]{2,1,0:T(8,128)(2,1)S(1)}, bf16[1,272,128]{2,1,0:T(8,128)(2,1)S(1)}, u32[]{:S(2)}, u32[]{:S(2)}) collective-permute-start(bf16[1,272,128]{2,1,0:T(8,128)(2,1)S(1)} %bitcast.12), channel_id=1, source_target_pairs={{0,4},{4,0},{8,12},{12,8},{16,20},{20,16},{24,28},{28,24},{1,5},{5... | collective-permute-start | bytes 208904 | tf_op jit(solution)/shard_map/ppermute | solution.py:507
  28.1 1.3 %collective-permute-start.13 = (bf16[1,272,128]{2,1,0:T(8,128)(2,1)S(1)}, bf16[1,272,128]{2,1,0:T(8,128)(2,1)S(1)}, u32[]{:S(2)}, u32[]{:S(2)}) collective-permute-start(bf16[1,272,128]{2,1,0:T(8,128)(2,1)S(1)} %bitcast.16), channel_id=1, source_target_pairs={{0,4},{4,0},{8,12},{12,8},{16,20},{20,16},{24,28},{28,24},{1,5},{5... | collective-permute-start | bytes 208904 | tf_op jit(solution)/shard_map/ppermute | solution.py:507
  28.3 1.3 %collective-permute-start.14 = (bf16[1,272,128]{2,1,0:T(8,128)(2,1)S(1)}, bf16[1,272,128]{2,1,0:T(8,128)(2,1)S(1)}, u32[]{:S(2)}, u32[]{:S(2)}) collective-permute-start(bf16[1,272,128]{2,1,0:T(8,128)(2,1)S(1)} %bitcast.20), channel_id=1, source_target_pairs={{0,4},{4,0},{8,12},{12,8},{16,20},{20,16},{24,28},{28,24},{1,5},{5... | collective-permute-start | bytes 208904 | tf_op jit(solution)/shard_map/ppermute | solution.py:507
  30.4 7.0 %collective-permute-start.15 = (bf16[272,128]{1,0:T(8,128)(2,1)S(1)}, bf16[272,128]{1,0:T(8,128)(2,1)S(1)}, u32[]{:S(2)}, u32[]{:S(2)}) collective-permute-start(bf16[272,128]{1,0:T(8,128)(2,1)S(1)} %get-tuple-element.30), channel_id=1, source_target_pairs={{0,3},{1,2},{2,1},{3,0},{4,7},{5,6},{6,5},{7,4},{8,11},{9,10},{10,... | collective-permute-start | bytes 208904 | tf_op jit(solution)/shard_map/ppermute | solution.py:507
  32.6 7.0 %collective-permute-start.16 = (bf16[272,128]{1,0:T(8,128)(2,1)S(1)}, bf16[272,128]{1,0:T(8,128)(2,1)S(1)}, u32[]{:S(2)}, u32[]{:S(2)}) collective-permute-start(bf16[272,128]{1,0:T(8,128)(2,1)S(1)} %get-tuple-element.31), channel_id=1, source_target_pairs={{0,2},{1,3},{2,0},{3,1},{4,6},{5,7},{6,4},{7,5},{8,10},{9,11},{10,... | collective-permute-start | bytes 208904 | tf_op jit(solution)/shard_map/ppermute | solution.py:507
  32.6 7.0 %collective-permute-start.17 = (bf16[272,128]{1,0:T(8,128)(2,1)S(1)}, bf16[272,128]{1,0:T(8,128)(2,1)S(1)}, u32[]{:S(2)}, u32[]{:S(2)}) collective-permute-start(bf16[272,128]{1,0:T(8,128)(2,1)S(1)} %get-tuple-element.32), channel_id=1, source_target_pairs={{0,1},{1,0},{2,3},{3,2},{4,5},{5,4},{6,7},{7,6},{8,9},{9,8},{10,11... | collective-permute-start | bytes 208904 | tf_op jit(solution)/shard_map/ppermute | solution.py:507
  40.1 5.4 %collective-permute-start.18 = (f32[64,128]{1,0:T(8,128)S(1)}, f32[64,128]{1,0:T(8,128)S(1)}, u32[]{:S(2)}, u32[]{:S(2)}) collective-permute-start(f32[64,128]{1,0:T(8,128)S(1)} %get-tuple-element.34.refs_0_), channel_id=1, source_target_pairs={{0,6},{1,7},{2,4},{3,5},{4,2},{5,3},{6,0},{7,1},{8,14},{9,15},{10,... | collective-permute-start | bytes 98312 | tf_op jit(solution)/shard_map/ppermute | solution.py:517
  40.1 5.4 %collective-permute-start.19 = (f32[64,128]{1,0:T(8,128)S(1)}, f32[64,128]{1,0:T(8,128)S(1)}, u32[]{:S(2)}, u32[]{:S(2)}) collective-permute-start(f32[64,128]{1,0:T(8,128)S(1)} %get-tuple-element.34.refs_0_), channel_id=1, source_target_pairs={{0,7},{1,6},{2,5},{3,4},{4,3},{5,2},{6,1},{7,0},{8,15},{9,14},{10,... | collective-permute-start | bytes 98312 | tf_op jit(solution)/shard_map/ppermute | solution.py:517
  42.5 4.0 %collective-permute-start.20 = (f32[64,128]{1,0:T(8,128)S(1)}, f32[64,128]{1,0:T(8,128)S(1)}, u32[]{:S(2)}, u32[]{:S(2)}) collective-permute-start(f32[64,128]{1,0:T(8,128)S(1)} %get-tuple-element.34.refs_0_), channel_id=1, source_target_pairs={{0,5},{1,4},{2,7},{3,6},{4,1},{5,0},{6,3},{7,2},{8,13},{9,12},{10,... | collective-permute-start | bytes 98312 | tf_op jit(solution)/shard_map/ppermute | solution.py:517
  46.5 4.3 %collective-permute-start.21 = (f32[32,128]{1,0:T(8,128)S(1)}, f32[32,128]{1,0:T(8,128)S(1)}, u32[]{:S(2)}, u32[]{:S(2)}) collective-permute-start(f32[32,128]{1,0:T(8,128)S(1)} %get-tuple-element.36.refs_0_), channel_id=1, source_target_pairs={{0,28},{4,24},{8,20},{12,16},{16,12},{20,8},{24,4},{28,0},{1,29},{... | collective-permute-start | bytes 49160 | tf_op jit(solution)/shard_map/ppermute | solution.py:507
  47.9 3.2 %collective-permute-start.22 = (f32[32,128]{1,0:T(8,128)S(1)}, f32[32,128]{1,0:T(8,128)S(1)}, u32[]{:S(2)}, u32[]{:S(2)}) collective-permute-start(f32[32,128]{1,0:T(8,128)S(1)} %get-tuple-element.36.refs_0_), channel_id=1, source_target_pairs={{0,20},{4,16},{8,28},{12,24},{16,4},{20,0},{24,12},{28,8},{1,21},{... | collective-permute-start | bytes 49160 | tf_op jit(solution)/shard_map/ppermute | solution.py:507
  49.0 3.2 %collective-permute-start.23 = (f32[32,128]{1,0:T(8,128)S(1)}, f32[32,128]{1,0:T(8,128)S(1)}, u32[]{:S(2)}, u32[]{:S(2)}) collective-permute-start(f32[32,128]{1,0:T(8,128)S(1)} %get-tuple-element.36.refs_0_), channel_id=1, source_target_pairs={{0,12},{4,8},{8,4},{12,0},{16,28},{20,24},{24,20},{28,16},{1,13},{... | collective-permute-start | bytes 49160 | tf_op jit(solution)/shard_map/ppermute | solution.py:507
  (3 other events, 18.6 us)

commit v17 on v15

--- a/solution.py
+++ b/solution.py
@@ -533,9 +533,9 @@
     for masks in plan[:-1]:
         held = held + [swap(piece, "rows", mask) for mask in masks for piece in held]
         offsets = offsets + [mask ^ offset for mask in masks for offset in offsets]
-    split = len(held) // 2
-    held, offsets = held[split:] + held[:split], offsets[split:] + offsets[:split]
-    near = [stack(held[:split], []), stack(held[split:], after)]
+    near = [piece[None] for piece in held]
+    if after:
+        near[1] = stack([held[1]], after)
     (last,) = plan[-1]
     offsets = offsets + [last ^ offset for offset in offsets]
     return near, [swap(pieces, "rows", last) for pieces in near], offsets

time: 56.1 us -> 56.4 us (level)
  starting transfers between devices: 22.5 us -> 24.6 us
  waiting for transfers between devices: 20.6 us -> 18.8 us
    ppermute x20 -> x24, starting transfers between devices: 19.6 us -> 21.6 us  [swap(): lax.ppermute(value, axis, [(index, index ^ mask) for index in range(size)])]
    ppermute x20 -> x24, waiting for transfers between devices: 17 us -> 15.3 us  [swap(): lax.ppermute(value, axis, [(index, index ^ mask) for index in range(size)])]
    pallas_call x20 -> x17, Pallas kernels: 12.6 us -> 12.6 us  [call(): pl.pallas_call(kernel, out_shape=outs, in_specs=ins, out_specs=jax.tree.m...]
  transfers between devices with their start and end apart: 23 -> 27, of which waited for: 16 -> 16; matrix products, arithmetic and copies ran while one was open for 0% -> 0% of each run, Pallas kernels for 12% -> 12%
where the time goes in v17:
time: 56.4 us; the launch traced here: 56.2 us
  starting transfers between devices  24.6 us (44%)
  waiting for transfers between devices  18.8 us (33%)
  Pallas kernels  12.6 us (22%)
    ppermute x24, starting transfers between devices, swap(): lax.ppermute(value, axis, [(index, index ^ mask) for index in range(size)])  21.6 us
    ppermute x24, waiting for transfers between devices, swap(): lax.ppermute(value, axis, [(index, index ^ mask) for index in range(size)])  15.3 us
    pallas_call x17, Pallas kernels, call(): pl.pallas_call(kernel, out_shape=outs, in_specs=ins, out_specs=jax.tree.m...  12.6 us
    ppermute x3, waiting for transfers between devices, swap_both(): return lax.ppermute(value, ('rows', 'cols'), pairs)  3.52 us
    ppermute x3, starting transfers between devices, swap_both(): return lax.ppermute(value, ('rows', 'cols'), pairs)  2.94 us
  transfers between devices with their start and end apart: 27, of which 16 were waited for; matrix products, arithmetic and copies ran while one was open for 0% of the time, Pallas kernels for 12%

profile of v17, /device:TPU:0, one launch (start us, length us, event | category | flops | bytes accessed | tf_op | source)
XLA Modules:
  0.0 56.2 jit_solution(3035302120814500940)
XLA Ops:
  0.0 1.0 %start.1 = bf16[256,128]{1,0:T(8,128)(2,1)S(1)} custom-call(f32[1,8,4096]{2,1,0:T(8,128)} %panel_hbm.1, f32[1,8,64]{2,1,0:T(8,128)} %inv_hbm.1), custom_call_target="tpu_custom_call" | custom-call | tf_op jit(solution)/shard_map/start/pallas_call | solution.py:37
  1.0 3.4 %collective-permute-start = (bf16[256,128]{1,0:T(8,128)(2,1)S(1)}, bf16[256,128]{1,0:T(8,128)(2,1)S(1)}, u32[]{:S(2)}, u32[]{:S(2)}) collective-permute-start(bf16[256,128]{1,0:T(8,128)(2,1)S(1)} %start.1), channel_id=1, source_target_pairs={{0,28},{4,24},{8,20},{12,16},{16,12},{20,8},{24,4},{28,0},{1,29},{... | collective-permute-start | bytes 196616 | tf_op jit(solution)/shard_map/ppermute | solution.py:507
  5.3 2.3 %prep.2 = (f32[256,128]{1,0:T(8,128)S(1)}, f32[8,128]{1,0:T(8,128)S(1)}, bf16[3,8,64,512]{3,2,1,0:T(8,128)(2,1)S(1)}) custom-call(bf16[4,8,1,8,4096]{4,3,2,1,0:T(8,128)(2,1)} %affinity_hbm.3, f32[1,8,64]{2,1,0:T(8,128)} %inv_hbm.1), custom_call_target="tpu_custom_call" | custom-call | tf_op jit(solution)/shard_map/prep/pallas_call | solution.py:37
  11.6 3.7 %collective-permute-start.7 = (bf16[256,128]{1,0:T(8,128)(2,1)S(1)}, bf16[256,128]{1,0:T(8,128)(2,1)S(1)}, u32[]{:S(2)}, u32[]{:S(2)}) collective-permute-start(bf16[256,128]{1,0:T(8,128)(2,1)S(1)} %get-tuple-element.25), channel_id=1, source_target_pairs={{0,3},{1,2},{2,1},{3,0},{4,7},{5,6},{6,5},{7,4},{8,11},{9,10},{10,... | collective-permute-start | bytes 196616 | tf_op jit(solution)/shard_map/ppermute | solution.py:507
  16.0 1.4 %prep.3.matrix_ref = bf16[1,8,64,512]{3,2,1,0:T(8,128)(2,1)S(1)} custom-call(bf16[4,8,1,8,4096]{4,3,2,1,0:T(8,128)(2,1)} %affinity_hbm.3), custom_call_target="tpu_custom_call" | custom-call | tf_op jit(solution)/shard_map/prep/pallas_call | solution.py:37
  17.9 3.2 %collective-permute-done.8.refs_2_ = bf16[256,128]{1,0:T(8,128)(2,1)S(1)} collective-permute-done((bf16[256,128]{1,0:T(8,128)(2,1)S(1)}, bf16[256,128]{1,0:T(8,128)(2,1)S(1)}, u32[]{:S(2)}, u32[]{:S(2)}) %collective-permute-start.8) | collective-permute-done | bytes 65568 | tf_op jit(solution)/shard_map/ppermute | solution.py:507
  21.2 1.1 %collective-permute-start.10 = (bf16[272,128]{1,0:T(8,128)(2,1)S(1)}, bf16[272,128]{1,0:T(8,128)(2,1)S(1)}, u32[]{:S(2)}, u32[]{:S(2)}) collective-permute-start(bf16[272,128]{1,0:T(8,128)(2,1)S(1)} %middle.1), channel_id=1, source_target_pairs={{0,28},{4,24},{8,20},{12,16},{16,12},{20,8},{24,4},{28,0},{1,29},{... | collective-permute-start | bytes 208904 | tf_op jit(solution)/shard_map/ppermute | solution.py:507
  22.2 1.5 %collective-permute-start.11 = (bf16[272,128]{1,0:T(8,128)(2,1)S(1)}, bf16[272,128]{1,0:T(8,128)(2,1)S(1)}, u32[]{:S(2)}, u32[]{:S(2)}) collective-permute-start(bf16[272,128]{1,0:T(8,128)(2,1)S(1)} %middle.1), channel_id=1, source_target_pairs={{0,20},{4,16},{8,28},{12,24},{16,4},{20,0},{24,12},{28,8},{1,21},{... | collective-permute-start | bytes 208904 | tf_op jit(solution)/shard_map/ppermute | solution.py:507
  24.6 2.0 %collective-permute-done.10 = bf16[272,128]{1,0:T(8,128)(2,1)S(1)} collective-permute-done((bf16[272,128]{1,0:T(8,128)(2,1)S(1)}, bf16[272,128]{1,0:T(8,128)(2,1)S(1)}, u32[]{:S(2)}, u32[]{:S(2)}) %collective-permute-start.10) | collective-permute-done | bytes 69664 | tf_op jit(solution)/shard_map/ppermute | solution.py:507
  26.6 1.3 %collective-permute-done.11 = bf16[272,128]{1,0:T(8,128)(2,1)S(1)} collective-permute-done((bf16[272,128]{1,0:T(8,128)(2,1)S(1)}, bf16[272,128]{1,0:T(8,128)(2,1)S(1)}, u32[]{:S(2)}, u32[]{:S(2)}) %collective-permute-start.11) | collective-permute-done | bytes 69664 | tf_op jit(solution)/shard_map/ppermute | solution.py:507
  29.4 0.8 %others.3 = (bf16[65,64,128]{2,1,0:T(8,128)(2,1)S(1)}, bf16[272,128]{1,0:T(8,128)(2,1)S(1)}, bf16[272,128]{1,0:T(8,128)(2,1)S(1)}, bf16[272,128]{1,0:T(8,128)(2,1)S(1)}, bf16[16,128]{1,0:T(8,128)(2,1)S(1)}) custom-call(bf16[65,64,128]{2,1,0:T(8,128)(2,1)S(1)} %near.3.old_table, ...), custom_call_target="tpu_custom_call", output_to_operand_aliasing={{0}: (0, {})} | custom-call | tf_op jit(solution)/shard_map/others/pallas_call | solution.py:37
  30.3 2.3 %collective-permute-start.17 = (bf16[272,128]{1,0:T(8,128)(2,1)S(1)}, bf16[272,128]{1,0:T(8,128)(2,1)S(1)}, u32[]{:S(2)}, u32[]{:S(2)}) collective-permute-start(bf16[272,128]{1,0:T(8,128)(2,1)S(1)} %get-tuple-element.30), channel_id=1, source_target_pairs={{0,3},{1,2},{2,1},{3,0},{4,7},{5,6},{6,5},{7,4},{8,11},{9,10},{10,... | collective-permute-start | bytes 208904 | tf_op jit(solution)/shard_map/ppermute | solution.py:507
  32.8 1.9 %collective-permute-start.19 = (bf16[272,128]{1,0:T(8,128)(2,1)S(1)}, bf16[272,128]{1,0:T(8,128)(2,1)S(1)}, u32[]{:S(2)}, u32[]{:S(2)}) collective-permute-start(bf16[272,128]{1,0:T(8,128)(2,1)S(1)} %get-tuple-element.32), channel_id=1, source_target_pairs={{0,1},{1,0},{2,3},{3,2},{4,5},{5,4},{6,7},{7,6},{8,9},{9,8},{10,11... | collective-permute-start | bytes 208904 | tf_op jit(solution)/shard_map/ppermute | solution.py:507
  35.8 1.4 %collective-permute-done.17.refs_1_ = bf16[272,128]{1,0:T(8,128)(2,1)S(1)} collective-permute-done((bf16[272,128]{1,0:T(8,128)(2,1)S(1)}, bf16[272,128]{1,0:T(8,128)(2,1)S(1)}, u32[]{:S(2)}, u32[]{:S(2)}) %collective-permute-start.17) | collective-permute-done | bytes 69664 | tf_op jit(solution)/shard_map/ppermute | solution.py:507
  37.3 2.2 %collective-permute-done.18.refs_2_ = bf16[272,128]{1,0:T(8,128)(2,1)S(1)} collective-permute-done((bf16[272,128]{1,0:T(8,128)(2,1)S(1)}, bf16[272,128]{1,0:T(8,128)(2,1)S(1)}, u32[]{:S(2)}, u32[]{:S(2)}) %collective-permute-start.18) | collective-permute-done | bytes 69664 | tf_op jit(solution)/shard_map/ppermute | solution.py:507
  40.0 2.4 %collective-permute-start.21 = (f32[64,128]{1,0:T(8,128)S(1)}, f32[64,128]{1,0:T(8,128)S(1)}, u32[]{:S(2)}, u32[]{:S(2)}) collective-permute-start(f32[64,128]{1,0:T(8,128)S(1)} %get-tuple-element.34.refs_0_), channel_id=1, source_target_pairs={{0,7},{1,6},{2,5},{3,4},{4,3},{5,2},{6,1},{7,0},{8,15},{9,14},{10,... | collective-permute-start | bytes 98312 | tf_op jit(solution)/shard_map/ppermute | solution.py:517
  42.9 2.5 %collective-permute-done.20.refs_1_ = f32[64,128]{1,0:T(8,128)S(1)} collective-permute-done((f32[64,128]{1,0:T(8,128)S(1)}, f32[64,128]{1,0:T(8,128)S(1)}, u32[]{:S(2)}, u32[]{:S(2)}) %collective-permute-start.20) | collective-permute-done | bytes 32800 | tf_op jit(solution)/shard_map/ppermute | solution.py:517
  45.4 1.0 %collective-permute-done.22.refs_3_ = f32[64,128]{1,0:T(8,128)S(1)} collective-permute-done((f32[64,128]{1,0:T(8,128)S(1)}, f32[64,128]{1,0:T(8,128)S(1)}, u32[]{:S(2)}, u32[]{:S(2)}) %collective-permute-start.22) | collective-permute-done | bytes 32800 | tf_op jit(solution)/shard_map/ppermute | solution.py:517
  46.4 1.4 %collective-permute-start.23 = (f32[32,128]{1,0:T(8,128)S(1)}, f32[32,128]{1,0:T(8,128)S(1)}, u32[]{:S(2)}, u32[]{:S(2)}) collective-permute-start(f32[32,128]{1,0:T(8,128)S(1)} %get-tuple-element.36.refs_0_), channel_id=1, source_target_pairs={{0,28},{4,24},{8,20},{12,16},{16,12},{20,8},{24,4},{28,0},{1,29},{... | collective-permute-start | bytes 49160 | tf_op jit(solution)/shard_map/ppermute | solution.py:507
  47.8 1.3 %collective-permute-start.24 = (f32[32,128]{1,0:T(8,128)S(1)}, f32[32,128]{1,0:T(8,128)S(1)}, u32[]{:S(2)}, u32[]{:S(2)}) collective-permute-start(f32[32,128]{1,0:T(8,128)S(1)} %get-tuple-element.36.refs_0_), channel_id=1, source_target_pairs={{0,20},{4,16},{8,28},{12,24},{16,4},{20,0},{24,12},{28,8},{1,21},{... | collective-permute-start | bytes 49160 | tf_op jit(solution)/shard_map/ppermute | solution.py:507
  49.4 1.3 %first_factor.1.refs_4_.inverse_ref = f32[64,64]{1,0:T(8,128)S(1)} custom-call(f32[32,128]{1,0:T(8,128)S(1)} %get-tuple-element.35.gram_ref), custom_call_target="tpu_custom_call" | custom-call | tf_op jit(solution)/shard_map/first_factor/pallas_call | solution.py:37
  51.0 1.3 %collective-permute-done.25.refs_3_ = f32[32,128]{1,0:T(8,128)S(1)} collective-permute-done((f32[32,128]{1,0:T(8,128)S(1)}, f32[32,128]{1,0:T(8,128)S(1)}, u32[]{:S(2)}, u32[]{:S(2)}) %collective-permute-start.25) | collective-permute-done | bytes 16416 | tf_op jit(solution)/shard_map/ppermute | solution.py:507
  52.5 1.1 %collective-permute-done.26.refs_1_ = f32[32,128]{1,0:T(8,128)S(1)} collective-permute-done((f32[32,128]{1,0:T(8,128)S(1)}, f32[32,128]{1,0:T(8,128)S(1)}, u32[]{:S(2)}, u32[]{:S(2)}) %collective-permute-start.26) | collective-permute-done | bytes 16416 | tf_op jit(solution)/shard_map/ppermute | solution.py:507
  53.5 2.7 %finish.1 = f32[1,8,4096]{2,1,0:T(8,128)} custom-call(f32[256,128]{1,0:T(8,128)S(1)} %get-tuple-element.33.rows_ref, f32[64,64]{1,0:T(8,128)S(1)} %first_factor.1.refs_4_.inverse_ref, f32[32,128]{1,0:T(8,128)S(1)} %add_parts.1.refs_0_, f32[32,128]{1,0:T(8,128)S(1)} %collective-permute-done.26.refs_1_), custom_call_target="tpu_custom_call" | custom-call | tf_op jit(solution)/shard_map/finish/pallas_call | solution.py:37
  (52 shorter events, 11.3 us)
Async XLA Ops:
  1.0 6.7 %collective-permute-start = (bf16[256,128]{1,0:T(8,128)(2,1)S(1)}, bf16[256,128]{1,0:T(8,128)(2,1)S(1)}, u32[]{:S(2)}, u32[]{:S(2)}) collective-permute-start(bf16[256,128]{1,0:T(8,128)(2,1)S(1)} %start.1), channel_id=1, source_target_pairs={{0,28},{4,24},{8,20},{12,16},{16,12},{20,8},{24,4},{28,0},{1,29},{... | collective-permute-start | bytes 196616 | tf_op jit(solution)/shard_map/ppermute | solution.py:507
  4.4 3.9 %collective-permute-start.1 = (bf16[256,128]{1,0:T(8,128)(2,1)S(1)}, bf16[256,128]{1,0:T(8,128)(2,1)S(1)}, u32[]{:S(2)}, u32[]{:S(2)}) collective-permute-start(bf16[256,128]{1,0:T(8,128)(2,1)S(1)} %start.1), channel_id=1, source_target_pairs={{0,20},{4,16},{8,28},{12,24},{16,4},{20,0},{24,12},{28,8},{1,21},{... | collective-permute-start | bytes 196616 | tf_op jit(solution)/shard_map/ppermute | solution.py:507
  5.2 4.3 %collective-permute-start.2 = (bf16[256,128]{1,0:T(8,128)(2,1)S(1)}, bf16[256,128]{1,0:T(8,128)(2,1)S(1)}, u32[]{:S(2)}, u32[]{:S(2)}) collective-permute-start(bf16[256,128]{1,0:T(8,128)(2,1)S(1)} %start.1), channel_id=1, source_target_pairs={{0,12},{4,8},{8,4},{12,0},{16,28},{20,24},{24,20},{28,16},{1,13},{... | collective-permute-start | bytes 196616 | tf_op jit(solution)/shard_map/ppermute | solution.py:507
  5.3 4.5 %collective-permute-start.3 = (bf16[1,256,128]{2,1,0:T(8,128)(2,1)S(1)}, bf16[1,256,128]{2,1,0:T(8,128)(2,1)S(1)}, u32[]{:S(2)}, u32[]{:S(2)}) collective-permute-start(bf16[1,256,128]{2,1,0:T(8,128)(2,1)S(1)} %bitcast.27), channel_id=1, source_target_pairs={{0,4},{4,0},{8,12},{12,8},{16,20},{20,16},{24,28},{28,24},{1,5},{5... | collective-permute-start | bytes 196616 | tf_op jit(solution)/shard_map/ppermute | solution.py:507
  7.7 2.2 %collective-permute-start.4 = (bf16[1,256,128]{2,1,0:T(8,128)(2,1)S(1)}, bf16[1,256,128]{2,1,0:T(8,128)(2,1)S(1)}, u32[]{:S(2)}, u32[]{:S(2)}) collective-permute-start(bf16[1,256,128]{2,1,0:T(8,128)(2,1)S(1)} %stack.1.refs_1_.refs_5_), channel_id=1, source_target_pairs={{0,4},{4,0},{8,12},{12,8},{16,20},{20,16},{24,28},{28,24},{1,5},{5... | collective-permute-start | bytes 196616 | tf_op jit(solution)/shard_map/ppermute | solution.py:507
  8.2 1.7 %collective-permute-start.5 = (bf16[1,256,128]{2,1,0:T(8,128)(2,1)S(1)}, bf16[1,256,128]{2,1,0:T(8,128)(2,1)S(1)}, u32[]{:S(2)}, u32[]{:S(2)}) collective-permute-start(bf16[1,256,128]{2,1,0:T(8,128)(2,1)S(1)} %bitcast.30), channel_id=1, source_target_pairs={{0,4},{4,0},{8,12},{12,8},{16,20},{20,16},{24,28},{28,24},{1,5},{5... | collective-permute-start | bytes 196616 | tf_op jit(solution)/shard_map/ppermute | solution.py:507
  11.6 6.3 %collective-permute-start.7 = (bf16[256,128]{1,0:T(8,128)(2,1)S(1)}, bf16[256,128]{1,0:T(8,128)(2,1)S(1)}, u32[]{:S(2)}, u32[]{:S(2)}) collective-permute-start(bf16[256,128]{1,0:T(8,128)(2,1)S(1)} %get-tuple-element.25), channel_id=1, source_target_pairs={{0,3},{1,2},{2,1},{3,0},{4,7},{5,6},{6,5},{7,4},{8,11},{9,10},{10,... | collective-permute-start | bytes 196616 | tf_op jit(solution)/shard_map/ppermute | solution.py:507
  15.2 5.9 %collective-permute-start.8 = (bf16[256,128]{1,0:T(8,128)(2,1)S(1)}, bf16[256,128]{1,0:T(8,128)(2,1)S(1)}, u32[]{:S(2)}, u32[]{:S(2)}) collective-permute-start(bf16[256,128]{1,0:T(8,128)(2,1)S(1)} %get-tuple-element.26), channel_id=1, source_target_pairs={{0,2},{1,3},{2,0},{3,1},{4,6},{5,7},{6,4},{7,5},{8,10},{9,11},{10,... | collective-permute-start | bytes 196616 | tf_op jit(solution)/shard_map/ppermute | solution.py:507
  15.2 5.9 %collective-permute-start.9 = (bf16[256,128]{1,0:T(8,128)(2,1)S(1)}, bf16[256,128]{1,0:T(8,128)(2,1)S(1)}, u32[]{:S(2)}, u32[]{:S(2)}) collective-permute-start(bf16[256,128]{1,0:T(8,128)(2,1)S(1)} %get-tuple-element.27), channel_id=1, source_target_pairs={{0,1},{1,0},{2,3},{3,2},{4,5},{5,4},{6,7},{7,6},{8,9},{9,8},{10,11... | collective-permute-start | bytes 196616 | tf_op jit(solution)/shard_map/ppermute | solution.py:507
  21.2 5.4 %collective-permute-start.10 = (bf16[272,128]{1,0:T(8,128)(2,1)S(1)}, bf16[272,128]{1,0:T(8,128)(2,1)S(1)}, u32[]{:S(2)}, u32[]{:S(2)}) collective-permute-start(bf16[272,128]{1,0:T(8,128)(2,1)S(1)} %middle.1), channel_id=1, source_target_pairs={{0,28},{4,24},{8,20},{12,16},{16,12},{20,8},{24,4},{28,0},{1,29},{... | collective-permute-start | bytes 208904 | tf_op jit(solution)/shard_map/ppermute | solution.py:507
  22.2 5.7 %collective-permute-start.11 = (bf16[272,128]{1,0:T(8,128)(2,1)S(1)}, bf16[272,128]{1,0:T(8,128)(2,1)S(1)}, u32[]{:S(2)}, u32[]{:S(2)}) collective-permute-start(bf16[272,128]{1,0:T(8,128)(2,1)S(1)} %middle.1), channel_id=1, source_target_pairs={{0,20},{4,16},{8,28},{12,24},{16,4},{20,0},{24,12},{28,8},{1,21},{... | collective-permute-start | bytes 208904 | tf_op jit(solution)/shard_map/ppermute | solution.py:507
  23.8 4.4 %collective-permute-start.12 = (bf16[272,128]{1,0:T(8,128)(2,1)S(1)}, bf16[272,128]{1,0:T(8,128)(2,1)S(1)}, u32[]{:S(2)}, u32[]{:S(2)}) collective-permute-start(bf16[272,128]{1,0:T(8,128)(2,1)S(1)} %middle.1), channel_id=1, source_target_pairs={{0,12},{4,8},{8,4},{12,0},{16,28},{20,24},{24,20},{28,16},{1,13},{... | collective-permute-start | bytes 208904 | tf_op jit(solution)/shard_map/ppermute | solution.py:507
  24.0 4.6 %collective-permute-start.13 = (bf16[1,272,128]{2,1,0:T(8,128)(2,1)S(1)}, bf16[1,272,128]{2,1,0:T(8,128)(2,1)S(1)}, u32[]{:S(2)}, u32[]{:S(2)}) collective-permute-start(bf16[1,272,128]{2,1,0:T(8,128)(2,1)S(1)} %bitcast.11), channel_id=1, source_target_pairs={{0,4},{4,0},{8,12},{12,8},{16,20},{20,16},{24,28},{28,24},{1,5},{5... | collective-permute-start | bytes 208904 | tf_op jit(solution)/shard_map/ppermute | solution.py:507
  26.6 2.0 %collective-permute-start.14 = (bf16[1,272,128]{2,1,0:T(8,128)(2,1)S(1)}, bf16[1,272,128]{2,1,0:T(8,128)(2,1)S(1)}, u32[]{:S(2)}, u32[]{:S(2)}) collective-permute-start(bf16[1,272,128]{2,1,0:T(8,128)(2,1)S(1)} %bitcast.15), channel_id=1, source_target_pairs={{0,4},{4,0},{8,12},{12,8},{16,20},{20,16},{24,28},{28,24},{1,5},{5... | collective-permute-start | bytes 208904 | tf_op jit(solution)/shard_map/ppermute | solution.py:507
  27.9 1.3 %collective-permute-start.15 = (bf16[1,272,128]{2,1,0:T(8,128)(2,1)S(1)}, bf16[1,272,128]{2,1,0:T(8,128)(2,1)S(1)}, u32[]{:S(2)}, u32[]{:S(2)}) collective-permute-start(bf16[1,272,128]{2,1,0:T(8,128)(2,1)S(1)} %bitcast.19), channel_id=1, source_target_pairs={{0,4},{4,0},{8,12},{12,8},{16,20},{20,16},{24,28},{28,24},{1,5},{5... | collective-permute-start | bytes 208904 | tf_op jit(solution)/shard_map/ppermute | solution.py:507
  30.3 7.0 %collective-permute-start.17 = (bf16[272,128]{1,0:T(8,128)(2,1)S(1)}, bf16[272,128]{1,0:T(8,128)(2,1)S(1)}, u32[]{:S(2)}, u32[]{:S(2)}) collective-permute-start(bf16[272,128]{1,0:T(8,128)(2,1)S(1)} %get-tuple-element.30), channel_id=1, source_target_pairs={{0,3},{1,2},{2,1},{3,0},{4,7},{5,6},{6,5},{7,4},{8,11},{9,10},{10,... | collective-permute-start | bytes 208904 | tf_op jit(solution)/shard_map/ppermute | solution.py:507
  32.6 6.9 %collective-permute-start.18 = (bf16[272,128]{1,0:T(8,128)(2,1)S(1)}, bf16[272,128]{1,0:T(8,128)(2,1)S(1)}, u32[]{:S(2)}, u32[]{:S(2)}) collective-permute-start(bf16[272,128]{1,0:T(8,128)(2,1)S(1)} %get-tuple-element.31), channel_id=1, source_target_pairs={{0,2},{1,3},{2,0},{3,1},{4,6},{5,7},{6,4},{7,5},{8,10},{9,11},{10,... | collective-permute-start | bytes 208904 | tf_op jit(solution)/shard_map/ppermute | solution.py:507
  32.8 6.7 %collective-permute-start.19 = (bf16[272,128]{1,0:T(8,128)(2,1)S(1)}, bf16[272,128]{1,0:T(8,128)(2,1)S(1)}, u32[]{:S(2)}, u32[]{:S(2)}) collective-permute-start(bf16[272,128]{1,0:T(8,128)(2,1)S(1)} %get-tuple-element.32), channel_id=1, source_target_pairs={{0,1},{1,0},{2,3},{3,2},{4,5},{5,4},{6,7},{7,6},{8,9},{9,8},{10,11... | collective-permute-start | bytes 208904 | tf_op jit(solution)/shard_map/ppermute | solution.py:507
  40.0 5.4 %collective-permute-start.20 = (f32[64,128]{1,0:T(8,128)S(1)}, f32[64,128]{1,0:T(8,128)S(1)}, u32[]{:S(2)}, u32[]{:S(2)}) collective-permute-start(f32[64,128]{1,0:T(8,128)S(1)} %get-tuple-element.34.refs_0_), channel_id=1, source_target_pairs={{0,6},{1,7},{2,4},{3,5},{4,2},{5,3},{6,0},{7,1},{8,14},{9,15},{10,... | collective-permute-start | bytes 98312 | tf_op jit(solution)/shard_map/ppermute | solution.py:517
  40.0 5.4 %collective-permute-start.21 = (f32[64,128]{1,0:T(8,128)S(1)}, f32[64,128]{1,0:T(8,128)S(1)}, u32[]{:S(2)}, u32[]{:S(2)}) collective-permute-start(f32[64,128]{1,0:T(8,128)S(1)} %get-tuple-element.34.refs_0_), channel_id=1, source_target_pairs={{0,7},{1,6},{2,5},{3,4},{4,3},{5,2},{6,1},{7,0},{8,15},{9,14},{10,... | collective-permute-start | bytes 98312 | tf_op jit(solution)/shard_map/ppermute | solution.py:517
  42.4 4.0 %collective-permute-start.22 = (f32[64,128]{1,0:T(8,128)S(1)}, f32[64,128]{1,0:T(8,128)S(1)}, u32[]{:S(2)}, u32[]{:S(2)}) collective-permute-start(f32[64,128]{1,0:T(8,128)S(1)} %get-tuple-element.34.refs_0_), channel_id=1, source_target_pairs={{0,5},{1,4},{2,7},{3,6},{4,1},{5,0},{6,3},{7,2},{8,13},{9,12},{10,... | collective-permute-start | bytes 98312 | tf_op jit(solution)/shard_map/ppermute | solution.py:517
  46.4 4.3 %collective-permute-start.23 = (f32[32,128]{1,0:T(8,128)S(1)}, f32[32,128]{1,0:T(8,128)S(1)}, u32[]{:S(2)}, u32[]{:S(2)}) collective-permute-start(f32[32,128]{1,0:T(8,128)S(1)} %get-tuple-element.36.refs_0_), channel_id=1, source_target_pairs={{0,28},{4,24},{8,20},{12,16},{16,12},{20,8},{24,4},{28,0},{1,29},{... | collective-permute-start | bytes 49160 | tf_op jit(solution)/shard_map/ppermute | solution.py:507
  47.8 3.2 %collective-permute-start.24 = (f32[32,128]{1,0:T(8,128)S(1)}, f32[32,128]{1,0:T(8,128)S(1)}, u32[]{:S(2)}, u32[]{:S(2)}) collective-permute-start(f32[32,128]{1,0:T(8,128)S(1)} %get-tuple-element.36.refs_0_), channel_id=1, source_target_pairs={{0,20},{4,16},{8,28},{12,24},{16,4},{20,0},{24,12},{28,8},{1,21},{... | collective-permute-start | bytes 49160 | tf_op jit(solution)/shard_map/ppermute | solution.py:507
  49.2 3.2 %collective-permute-start.25 = (f32[32,128]{1,0:T(8,128)S(1)}, f32[32,128]{1,0:T(8,128)S(1)}, u32[]{:S(2)}, u32[]{:S(2)}) collective-permute-start(f32[32,128]{1,0:T(8,128)S(1)} %get-tuple-element.36.refs_0_), channel_id=1, source_target_pairs={{0,12},{4,8},{8,4},{12,0},{16,28},{20,24},{24,20},{28,16},{1,13},{... | collective-permute-start | bytes 49160 | tf_op jit(solution)/shard_map/ppermute | solution.py:507
  (5 other events, 12.3 us)

commit v18 on v17

--- a/solution.py
+++ b/solution.py
@@ -85,7 +85,7 @@
         [
             pltpu.VMEM(panel.shape, F32),
             pltpu.VMEM(inv_degree.shape, F32),
-            pltpu.VMEM(shape, F32),
+            pltpu.VMEM((shape[0] + block_rows, 128), F32),
             pltpu.SemaphoreType.DMA((2,)),
         ],
     )
@@ -162,7 +162,7 @@
         [
             pltpu.VMEM((count,) + affinity.shape[1:], BF16),
             pltpu.VMEM((1, block_rows, 64), F32),
-            pltpu.VMEM((2, flat // 128 * slots, 128), F32),
+            pltpu.VMEM((2, (flat // 128 + 1) * slots, 128), F32),
             pltpu.SemaphoreType.DMA((count + 1,)),
         ],
     )
@@ -498,7 +498,7 @@
         [vmem()] * (2 + len(grams)),
         shaped((1, block_rows, 32 * 128), F32),
         (rows, inverse, *grams),
-        [pltpu.VMEM(rows.shape, F32)],
+        [pltpu.VMEM((rows.shape[0] + block_rows, 128), F32)],
     )
 
 

time: 56.4 us -> 56.4 us (level)
  no operation moved by 1% of the time
where the time goes in v18:
time: 56.4 us; the launch traced here: 56.2 us
  starting transfers between devices  24.6 us (44%)
  waiting for transfers between devices  18.8 us (33%)
  Pallas kernels  12.6 us (22%)
    ppermute x24, starting transfers between devices, swap(): lax.ppermute(value, axis, [(index, index ^ mask) for index in range(size)])  21.6 us
    ppermute x24, waiting for transfers between devices, swap(): lax.ppermute(value, axis, [(index, index ^ mask) for index in range(size)])  15.3 us
    pallas_call x17, Pallas kernels, call(): pl.pallas_call(kernel, out_shape=outs, in_specs=ins, out_specs=jax.tree.m...  12.6 us
    ppermute x3, waiting for transfers between devices, swap_both(): return lax.ppermute(value, ('rows', 'cols'), pairs)  3.51 us
    ppermute x3, starting transfers between devices, swap_both(): return lax.ppermute(value, ('rows', 'cols'), pairs)  2.94 us
  transfers between devices with their start and end apart: 27, of which 16 were waited for; matrix products, arithmetic and copies ran while one was open for 0% of the time, Pallas kernels for 12%

profile of v18, /device:TPU:0, one launch (start us, length us, event | category | flops | bytes accessed | tf_op | source)
XLA Modules:
  0.0 56.2 jit_solution(5805315903585107169)
XLA Ops:
  0.0 1.0 %start.1 = bf16[256,128]{1,0:T(8,128)(2,1)S(1)} custom-call(f32[1,8,4096]{2,1,0:T(8,128)} %panel_hbm.1, f32[1,8,64]{2,1,0:T(8,128)} %inv_hbm.1), custom_call_target="tpu_custom_call" | custom-call | tf_op jit(solution)/shard_map/start/pallas_call | solution.py:37
  1.0 3.4 %collective-permute-start = (bf16[256,128]{1,0:T(8,128)(2,1)S(1)}, bf16[256,128]{1,0:T(8,128)(2,1)S(1)}, u32[]{:S(2)}, u32[]{:S(2)}) collective-permute-start(bf16[256,128]{1,0:T(8,128)(2,1)S(1)} %start.1), channel_id=1, source_target_pairs={{0,28},{4,24},{8,20},{12,16},{16,12},{20,8},{24,4},{28,0},{1,29},{... | collective-permute-start | bytes 196616 | tf_op jit(solution)/shard_map/ppermute | solution.py:507
  5.3 2.3 %prep.2 = (f32[256,128]{1,0:T(8,128)S(1)}, f32[8,128]{1,0:T(8,128)S(1)}, bf16[3,8,64,512]{3,2,1,0:T(8,128)(2,1)S(1)}) custom-call(bf16[4,8,1,8,4096]{4,3,2,1,0:T(8,128)(2,1)} %affinity_hbm.3, f32[1,8,64]{2,1,0:T(8,128)} %inv_hbm.1), custom_call_target="tpu_custom_call" | custom-call | tf_op jit(solution)/shard_map/prep/pallas_call | solution.py:37
  11.6 3.7 %collective-permute-start.7 = (bf16[256,128]{1,0:T(8,128)(2,1)S(1)}, bf16[256,128]{1,0:T(8,128)(2,1)S(1)}, u32[]{:S(2)}, u32[]{:S(2)}) collective-permute-start(bf16[256,128]{1,0:T(8,128)(2,1)S(1)} %get-tuple-element.25), channel_id=1, source_target_pairs={{0,3},{1,2},{2,1},{3,0},{4,7},{5,6},{6,5},{7,4},{8,11},{9,10},{10,... | collective-permute-start | bytes 196616 | tf_op jit(solution)/shard_map/ppermute | solution.py:507
  16.0 1.4 %prep.3.matrix_ref = bf16[1,8,64,512]{3,2,1,0:T(8,128)(2,1)S(1)} custom-call(bf16[4,8,1,8,4096]{4,3,2,1,0:T(8,128)(2,1)} %affinity_hbm.3), custom_call_target="tpu_custom_call" | custom-call | tf_op jit(solution)/shard_map/prep/pallas_call | solution.py:37
  17.9 3.2 %collective-permute-done.8.refs_2_ = bf16[256,128]{1,0:T(8,128)(2,1)S(1)} collective-permute-done((bf16[256,128]{1,0:T(8,128)(2,1)S(1)}, bf16[256,128]{1,0:T(8,128)(2,1)S(1)}, u32[]{:S(2)}, u32[]{:S(2)}) %collective-permute-start.8) | collective-permute-done | bytes 65568 | tf_op jit(solution)/shard_map/ppermute | solution.py:507
  21.2 1.1 %collective-permute-start.10 = (bf16[272,128]{1,0:T(8,128)(2,1)S(1)}, bf16[272,128]{1,0:T(8,128)(2,1)S(1)}, u32[]{:S(2)}, u32[]{:S(2)}) collective-permute-start(bf16[272,128]{1,0:T(8,128)(2,1)S(1)} %middle.1), channel_id=1, source_target_pairs={{0,28},{4,24},{8,20},{12,16},{16,12},{20,8},{24,4},{28,0},{1,29},{... | collective-permute-start | bytes 208904 | tf_op jit(solution)/shard_map/ppermute | solution.py:507
  22.2 1.5 %collective-permute-start.11 = (bf16[272,128]{1,0:T(8,128)(2,1)S(1)}, bf16[272,128]{1,0:T(8,128)(2,1)S(1)}, u32[]{:S(2)}, u32[]{:S(2)}) collective-permute-start(bf16[272,128]{1,0:T(8,128)(2,1)S(1)} %middle.1), channel_id=1, source_target_pairs={{0,20},{4,16},{8,28},{12,24},{16,4},{20,0},{24,12},{28,8},{1,21},{... | collective-permute-start | bytes 208904 | tf_op jit(solution)/shard_map/ppermute | solution.py:507
  24.6 2.0 %collective-permute-done.10 = bf16[272,128]{1,0:T(8,128)(2,1)S(1)} collective-permute-done((bf16[272,128]{1,0:T(8,128)(2,1)S(1)}, bf16[272,128]{1,0:T(8,128)(2,1)S(1)}, u32[]{:S(2)}, u32[]{:S(2)}) %collective-permute-start.10) | collective-permute-done | bytes 69664 | tf_op jit(solution)/shard_map/ppermute | solution.py:507
  26.6 1.3 %collective-permute-done.11 = bf16[272,128]{1,0:T(8,128)(2,1)S(1)} collective-permute-done((bf16[272,128]{1,0:T(8,128)(2,1)S(1)}, bf16[272,128]{1,0:T(8,128)(2,1)S(1)}, u32[]{:S(2)}, u32[]{:S(2)}) %collective-permute-start.11) | collective-permute-done | bytes 69664 | tf_op jit(solution)/shard_map/ppermute | solution.py:507
  29.4 0.8 %others.3 = (bf16[65,64,128]{2,1,0:T(8,128)(2,1)S(1)}, bf16[272,128]{1,0:T(8,128)(2,1)S(1)}, bf16[272,128]{1,0:T(8,128)(2,1)S(1)}, bf16[272,128]{1,0:T(8,128)(2,1)S(1)}, bf16[16,128]{1,0:T(8,128)(2,1)S(1)}) custom-call(bf16[65,64,128]{2,1,0:T(8,128)(2,1)S(1)} %near.3.old_table, ...), custom_call_target="tpu_custom_call", output_to_operand_aliasing={{0}: (0, {})} | custom-call | tf_op jit(solution)/shard_map/others/pallas_call | solution.py:37
  30.3 2.3 %collective-permute-start.17 = (bf16[272,128]{1,0:T(8,128)(2,1)S(1)}, bf16[272,128]{1,0:T(8,128)(2,1)S(1)}, u32[]{:S(2)}, u32[]{:S(2)}) collective-permute-start(bf16[272,128]{1,0:T(8,128)(2,1)S(1)} %get-tuple-element.30), channel_id=1, source_target_pairs={{0,3},{1,2},{2,1},{3,0},{4,7},{5,6},{6,5},{7,4},{8,11},{9,10},{10,... | collective-permute-start | bytes 208904 | tf_op jit(solution)/shard_map/ppermute | solution.py:507
  32.8 1.9 %collective-permute-start.19 = (bf16[272,128]{1,0:T(8,128)(2,1)S(1)}, bf16[272,128]{1,0:T(8,128)(2,1)S(1)}, u32[]{:S(2)}, u32[]{:S(2)}) collective-permute-start(bf16[272,128]{1,0:T(8,128)(2,1)S(1)} %get-tuple-element.32), channel_id=1, source_target_pairs={{0,1},{1,0},{2,3},{3,2},{4,5},{5,4},{6,7},{7,6},{8,9},{9,8},{10,11... | collective-permute-start | bytes 208904 | tf_op jit(solution)/shard_map/ppermute | solution.py:507
  35.8 1.4 %collective-permute-done.17.refs_1_ = bf16[272,128]{1,0:T(8,128)(2,1)S(1)} collective-permute-done((bf16[272,128]{1,0:T(8,128)(2,1)S(1)}, bf16[272,128]{1,0:T(8,128)(2,1)S(1)}, u32[]{:S(2)}, u32[]{:S(2)}) %collective-permute-start.17) | collective-permute-done | bytes 69664 | tf_op jit(solution)/shard_map/ppermute | solution.py:507
  37.3 2.2 %collective-permute-done.18.refs_2_ = bf16[272,128]{1,0:T(8,128)(2,1)S(1)} collective-permute-done((bf16[272,128]{1,0:T(8,128)(2,1)S(1)}, bf16[272,128]{1,0:T(8,128)(2,1)S(1)}, u32[]{:S(2)}, u32[]{:S(2)}) %collective-permute-start.18) | collective-permute-done | bytes 69664 | tf_op jit(solution)/shard_map/ppermute | solution.py:507
  40.0 2.4 %collective-permute-start.21 = (f32[64,128]{1,0:T(8,128)S(1)}, f32[64,128]{1,0:T(8,128)S(1)}, u32[]{:S(2)}, u32[]{:S(2)}) collective-permute-start(f32[64,128]{1,0:T(8,128)S(1)} %get-tuple-element.34.refs_0_), channel_id=1, source_target_pairs={{0,7},{1,6},{2,5},{3,4},{4,3},{5,2},{6,1},{7,0},{8,15},{9,14},{10,... | collective-permute-start | bytes 98312 | tf_op jit(solution)/shard_map/ppermute | solution.py:517
  42.9 2.5 %collective-permute-done.20.refs_1_ = f32[64,128]{1,0:T(8,128)S(1)} collective-permute-done((f32[64,128]{1,0:T(8,128)S(1)}, f32[64,128]{1,0:T(8,128)S(1)}, u32[]{:S(2)}, u32[]{:S(2)}) %collective-permute-start.20) | collective-permute-done | bytes 32800 | tf_op jit(solution)/shard_map/ppermute | solution.py:517
  45.4 1.0 %collective-permute-done.22.refs_3_ = f32[64,128]{1,0:T(8,128)S(1)} collective-permute-done((f32[64,128]{1,0:T(8,128)S(1)}, f32[64,128]{1,0:T(8,128)S(1)}, u32[]{:S(2)}, u32[]{:S(2)}) %collective-permute-start.22) | collective-permute-done | bytes 32800 | tf_op jit(solution)/shard_map/ppermute | solution.py:517
  46.4 1.4 %collective-permute-start.23 = (f32[32,128]{1,0:T(8,128)S(1)}, f32[32,128]{1,0:T(8,128)S(1)}, u32[]{:S(2)}, u32[]{:S(2)}) collective-permute-start(f32[32,128]{1,0:T(8,128)S(1)} %get-tuple-element.36.refs_0_), channel_id=1, source_target_pairs={{0,28},{4,24},{8,20},{12,16},{16,12},{20,8},{24,4},{28,0},{1,29},{... | collective-permute-start | bytes 49160 | tf_op jit(solution)/shard_map/ppermute | solution.py:507
  47.8 1.3 %collective-permute-start.24 = (f32[32,128]{1,0:T(8,128)S(1)}, f32[32,128]{1,0:T(8,128)S(1)}, u32[]{:S(2)}, u32[]{:S(2)}) collective-permute-start(f32[32,128]{1,0:T(8,128)S(1)} %get-tuple-element.36.refs_0_), channel_id=1, source_target_pairs={{0,20},{4,16},{8,28},{12,24},{16,4},{20,0},{24,12},{28,8},{1,21},{... | collective-permute-start | bytes 49160 | tf_op jit(solution)/shard_map/ppermute | solution.py:507
  49.4 1.3 %first_factor.1.refs_4_.inverse_ref = f32[64,64]{1,0:T(8,128)S(1)} custom-call(f32[32,128]{1,0:T(8,128)S(1)} %get-tuple-element.35.gram_ref), custom_call_target="tpu_custom_call" | custom-call | tf_op jit(solution)/shard_map/first_factor/pallas_call | solution.py:37
  51.0 1.3 %collective-permute-done.25.refs_3_ = f32[32,128]{1,0:T(8,128)S(1)} collective-permute-done((f32[32,128]{1,0:T(8,128)S(1)}, f32[32,128]{1,0:T(8,128)S(1)}, u32[]{:S(2)}, u32[]{:S(2)}) %collective-permute-start.25) | collective-permute-done | bytes 16416 | tf_op jit(solution)/shard_map/ppermute | solution.py:507
  52.5 1.1 %collective-permute-done.26.refs_1_ = f32[32,128]{1,0:T(8,128)S(1)} collective-permute-done((f32[32,128]{1,0:T(8,128)S(1)}, f32[32,128]{1,0:T(8,128)S(1)}, u32[]{:S(2)}, u32[]{:S(2)}) %collective-permute-start.26) | collective-permute-done | bytes 16416 | tf_op jit(solution)/shard_map/ppermute | solution.py:507
  53.5 2.7 %finish.1 = f32[1,8,4096]{2,1,0:T(8,128)} custom-call(f32[256,128]{1,0:T(8,128)S(1)} %get-tuple-element.33.rows_ref, f32[64,64]{1,0:T(8,128)S(1)} %first_factor.1.refs_4_.inverse_ref, f32[32,128]{1,0:T(8,128)S(1)} %add_parts.1.refs_0_, f32[32,128]{1,0:T(8,128)S(1)} %collective-permute-done.26.refs_1_), custom_call_target="tpu_custom_call" | custom-call | tf_op jit(solution)/shard_map/finish/pallas_call | solution.py:37
  (52 shorter events, 11.3 us)
Async XLA Ops:
  1.0 6.7 %collective-permute-start = (bf16[256,128]{1,0:T(8,128)(2,1)S(1)}, bf16[256,128]{1,0:T(8,128)(2,1)S(1)}, u32[]{:S(2)}, u32[]{:S(2)}) collective-permute-start(bf16[256,128]{1,0:T(8,128)(2,1)S(1)} %start.1), channel_id=1, source_target_pairs={{0,28},{4,24},{8,20},{12,16},{16,12},{20,8},{24,4},{28,0},{1,29},{... | collective-permute-start | bytes 196616 | tf_op jit(solution)/shard_map/ppermute | solution.py:507
  4.4 3.9 %collective-permute-start.1 = (bf16[256,128]{1,0:T(8,128)(2,1)S(1)}, bf16[256,128]{1,0:T(8,128)(2,1)S(1)}, u32[]{:S(2)}, u32[]{:S(2)}) collective-permute-start(bf16[256,128]{1,0:T(8,128)(2,1)S(1)} %start.1), channel_id=1, source_target_pairs={{0,20},{4,16},{8,28},{12,24},{16,4},{20,0},{24,12},{28,8},{1,21},{... | collective-permute-start | bytes 196616 | tf_op jit(solution)/shard_map/ppermute | solution.py:507
  5.2 4.3 %collective-permute-start.2 = (bf16[256,128]{1,0:T(8,128)(2,1)S(1)}, bf16[256,128]{1,0:T(8,128)(2,1)S(1)}, u32[]{:S(2)}, u32[]{:S(2)}) collective-permute-start(bf16[256,128]{1,0:T(8,128)(2,1)S(1)} %start.1), channel_id=1, source_target_pairs={{0,12},{4,8},{8,4},{12,0},{16,28},{20,24},{24,20},{28,16},{1,13},{... | collective-permute-start | bytes 196616 | tf_op jit(solution)/shard_map/ppermute | solution.py:507
  5.3 4.5 %collective-permute-start.3 = (bf16[1,256,128]{2,1,0:T(8,128)(2,1)S(1)}, bf16[1,256,128]{2,1,0:T(8,128)(2,1)S(1)}, u32[]{:S(2)}, u32[]{:S(2)}) collective-permute-start(bf16[1,256,128]{2,1,0:T(8,128)(2,1)S(1)} %bitcast.27), channel_id=1, source_target_pairs={{0,4},{4,0},{8,12},{12,8},{16,20},{20,16},{24,28},{28,24},{1,5},{5... | collective-permute-start | bytes 196616 | tf_op jit(solution)/shard_map/ppermute | solution.py:507
  7.7 2.2 %collective-permute-start.4 = (bf16[1,256,128]{2,1,0:T(8,128)(2,1)S(1)}, bf16[1,256,128]{2,1,0:T(8,128)(2,1)S(1)}, u32[]{:S(2)}, u32[]{:S(2)}) collective-permute-start(bf16[1,256,128]{2,1,0:T(8,128)(2,1)S(1)} %stack.1.refs_1_.refs_5_), channel_id=1, source_target_pairs={{0,4},{4,0},{8,12},{12,8},{16,20},{20,16},{24,28},{28,24},{1,5},{5... | collective-permute-start | bytes 196616 | tf_op jit(solution)/shard_map/ppermute | solution.py:507
  8.2 1.7 %collective-permute-start.5 = (bf16[1,256,128]{2,1,0:T(8,128)(2,1)S(1)}, bf16[1,256,128]{2,1,0:T(8,128)(2,1)S(1)}, u32[]{:S(2)}, u32[]{:S(2)}) collective-permute-start(bf16[1,256,128]{2,1,0:T(8,128)(2,1)S(1)} %bitcast.30), channel_id=1, source_target_pairs={{0,4},{4,0},{8,12},{12,8},{16,20},{20,16},{24,28},{28,24},{1,5},{5... | collective-permute-start | bytes 196616 | tf_op jit(solution)/shard_map/ppermute | solution.py:507
  11.6 6.3 %collective-permute-start.7 = (bf16[256,128]{1,0:T(8,128)(2,1)S(1)}, bf16[256,128]{1,0:T(8,128)(2,1)S(1)}, u32[]{:S(2)}, u32[]{:S(2)}) collective-permute-start(bf16[256,128]{1,0:T(8,128)(2,1)S(1)} %get-tuple-element.25), channel_id=1, source_target_pairs={{0,3},{1,2},{2,1},{3,0},{4,7},{5,6},{6,5},{7,4},{8,11},{9,10},{10,... | collective-permute-start | bytes 196616 | tf_op jit(solution)/shard_map/ppermute | solution.py:507
  15.2 5.9 %collective-permute-start.8 = (bf16[256,128]{1,0:T(8,128)(2,1)S(1)}, bf16[256,128]{1,0:T(8,128)(2,1)S(1)}, u32[]{:S(2)}, u32[]{:S(2)}) collective-permute-start(bf16[256,128]{1,0:T(8,128)(2,1)S(1)} %get-tuple-element.26), channel_id=1, source_target_pairs={{0,2},{1,3},{2,0},{3,1},{4,6},{5,7},{6,4},{7,5},{8,10},{9,11},{10,... | collective-permute-start | bytes 196616 | tf_op jit(solution)/shard_map/ppermute | solution.py:507
  15.2 5.9 %collective-permute-start.9 = (bf16[256,128]{1,0:T(8,128)(2,1)S(1)}, bf16[256,128]{1,0:T(8,128)(2,1)S(1)}, u32[]{:S(2)}, u32[]{:S(2)}) collective-permute-start(bf16[256,128]{1,0:T(8,128)(2,1)S(1)} %get-tuple-element.27), channel_id=1, source_target_pairs={{0,1},{1,0},{2,3},{3,2},{4,5},{5,4},{6,7},{7,6},{8,9},{9,8},{10,11... | collective-permute-start | bytes 196616 | tf_op jit(solution)/shard_map/ppermute | solution.py:507
  21.2 5.4 %collective-permute-start.10 = (bf16[272,128]{1,0:T(8,128)(2,1)S(1)}, bf16[272,128]{1,0:T(8,128)(2,1)S(1)}, u32[]{:S(2)}, u32[]{:S(2)}) collective-permute-start(bf16[272,128]{1,0:T(8,128)(2,1)S(1)} %middle.1), channel_id=1, source_target_pairs={{0,28},{4,24},{8,20},{12,16},{16,12},{20,8},{24,4},{28,0},{1,29},{... | collective-permute-start | bytes 208904 | tf_op jit(solution)/shard_map/ppermute | solution.py:507
  22.2 5.7 %collective-permute-start.11 = (bf16[272,128]{1,0:T(8,128)(2,1)S(1)}, bf16[272,128]{1,0:T(8,128)(2,1)S(1)}, u32[]{:S(2)}, u32[]{:S(2)}) collective-permute-start(bf16[272,128]{1,0:T(8,128)(2,1)S(1)} %middle.1), channel_id=1, source_target_pairs={{0,20},{4,16},{8,28},{12,24},{16,4},{20,0},{24,12},{28,8},{1,21},{... | collective-permute-start | bytes 208904 | tf_op jit(solution)/shard_map/ppermute | solution.py:507
  23.8 4.4 %collective-permute-start.12 = (bf16[272,128]{1,0:T(8,128)(2,1)S(1)}, bf16[272,128]{1,0:T(8,128)(2,1)S(1)}, u32[]{:S(2)}, u32[]{:S(2)}) collective-permute-start(bf16[272,128]{1,0:T(8,128)(2,1)S(1)} %middle.1), channel_id=1, source_target_pairs={{0,12},{4,8},{8,4},{12,0},{16,28},{20,24},{24,20},{28,16},{1,13},{... | collective-permute-start | bytes 208904 | tf_op jit(solution)/shard_map/ppermute | solution.py:507
  24.0 4.6 %collective-permute-start.13 = (bf16[1,272,128]{2,1,0:T(8,128)(2,1)S(1)}, bf16[1,272,128]{2,1,0:T(8,128)(2,1)S(1)}, u32[]{:S(2)}, u32[]{:S(2)}) collective-permute-start(bf16[1,272,128]{2,1,0:T(8,128)(2,1)S(1)} %bitcast.11), channel_id=1, source_target_pairs={{0,4},{4,0},{8,12},{12,8},{16,20},{20,16},{24,28},{28,24},{1,5},{5... | collective-permute-start | bytes 208904 | tf_op jit(solution)/shard_map/ppermute | solution.py:507
  26.6 2.0 %collective-permute-start.14 = (bf16[1,272,128]{2,1,0:T(8,128)(2,1)S(1)}, bf16[1,272,128]{2,1,0:T(8,128)(2,1)S(1)}, u32[]{:S(2)}, u32[]{:S(2)}) collective-permute-start(bf16[1,272,128]{2,1,0:T(8,128)(2,1)S(1)} %bitcast.15), channel_id=1, source_target_pairs={{0,4},{4,0},{8,12},{12,8},{16,20},{20,16},{24,28},{28,24},{1,5},{5... | collective-permute-start | bytes 208904 | tf_op jit(solution)/shard_map/ppermute | solution.py:507
  27.9 1.3 %collective-permute-start.15 = (bf16[1,272,128]{2,1,0:T(8,128)(2,1)S(1)}, bf16[1,272,128]{2,1,0:T(8,128)(2,1)S(1)}, u32[]{:S(2)}, u32[]{:S(2)}) collective-permute-start(bf16[1,272,128]{2,1,0:T(8,128)(2,1)S(1)} %bitcast.19), channel_id=1, source_target_pairs={{0,4},{4,0},{8,12},{12,8},{16,20},{20,16},{24,28},{28,24},{1,5},{5... | collective-permute-start | bytes 208904 | tf_op jit(solution)/shard_map/ppermute | solution.py:507
  30.3 7.0 %collective-permute-start.17 = (bf16[272,128]{1,0:T(8,128)(2,1)S(1)}, bf16[272,128]{1,0:T(8,128)(2,1)S(1)}, u32[]{:S(2)}, u32[]{:S(2)}) collective-permute-start(bf16[272,128]{1,0:T(8,128)(2,1)S(1)} %get-tuple-element.30), channel_id=1, source_target_pairs={{0,3},{1,2},{2,1},{3,0},{4,7},{5,6},{6,5},{7,4},{8,11},{9,10},{10,... | collective-permute-start | bytes 208904 | tf_op jit(solution)/shard_map/ppermute | solution.py:507
  32.6 6.9 %collective-permute-start.18 = (bf16[272,128]{1,0:T(8,128)(2,1)S(1)}, bf16[272,128]{1,0:T(8,128)(2,1)S(1)}, u32[]{:S(2)}, u32[]{:S(2)}) collective-permute-start(bf16[272,128]{1,0:T(8,128)(2,1)S(1)} %get-tuple-element.31), channel_id=1, source_target_pairs={{0,2},{1,3},{2,0},{3,1},{4,6},{5,7},{6,4},{7,5},{8,10},{9,11},{10,... | collective-permute-start | bytes 208904 | tf_op jit(solution)/shard_map/ppermute | solution.py:507
  32.8 6.7 %collective-permute-start.19 = (bf16[272,128]{1,0:T(8,128)(2,1)S(1)}, bf16[272,128]{1,0:T(8,128)(2,1)S(1)}, u32[]{:S(2)}, u32[]{:S(2)}) collective-permute-start(bf16[272,128]{1,0:T(8,128)(2,1)S(1)} %get-tuple-element.32), channel_id=1, source_target_pairs={{0,1},{1,0},{2,3},{3,2},{4,5},{5,4},{6,7},{7,6},{8,9},{9,8},{10,11... | collective-permute-start | bytes 208904 | tf_op jit(solution)/shard_map/ppermute | solution.py:507
  40.0 5.4 %collective-permute-start.20 = (f32[64,128]{1,0:T(8,128)S(1)}, f32[64,128]{1,0:T(8,128)S(1)}, u32[]{:S(2)}, u32[]{:S(2)}) collective-permute-start(f32[64,128]{1,0:T(8,128)S(1)} %get-tuple-element.34.refs_0_), channel_id=1, source_target_pairs={{0,6},{1,7},{2,4},{3,5},{4,2},{5,3},{6,0},{7,1},{8,14},{9,15},{10,... | collective-permute-start | bytes 98312 | tf_op jit(solution)/shard_map/ppermute | solution.py:517
  40.0 5.4 %collective-permute-start.21 = (f32[64,128]{1,0:T(8,128)S(1)}, f32[64,128]{1,0:T(8,128)S(1)}, u32[]{:S(2)}, u32[]{:S(2)}) collective-permute-start(f32[64,128]{1,0:T(8,128)S(1)} %get-tuple-element.34.refs_0_), channel_id=1, source_target_pairs={{0,7},{1,6},{2,5},{3,4},{4,3},{5,2},{6,1},{7,0},{8,15},{9,14},{10,... | collective-permute-start | bytes 98312 | tf_op jit(solution)/shard_map/ppermute | solution.py:517
  42.4 4.0 %collective-permute-start.22 = (f32[64,128]{1,0:T(8,128)S(1)}, f32[64,128]{1,0:T(8,128)S(1)}, u32[]{:S(2)}, u32[]{:S(2)}) collective-permute-start(f32[64,128]{1,0:T(8,128)S(1)} %get-tuple-element.34.refs_0_), channel_id=1, source_target_pairs={{0,5},{1,4},{2,7},{3,6},{4,1},{5,0},{6,3},{7,2},{8,13},{9,12},{10,... | collective-permute-start | bytes 98312 | tf_op jit(solution)/shard_map/ppermute | solution.py:517
  46.4 4.3 %collective-permute-start.23 = (f32[32,128]{1,0:T(8,128)S(1)}, f32[32,128]{1,0:T(8,128)S(1)}, u32[]{:S(2)}, u32[]{:S(2)}) collective-permute-start(f32[32,128]{1,0:T(8,128)S(1)} %get-tuple-element.36.refs_0_), channel_id=1, source_target_pairs={{0,28},{4,24},{8,20},{12,16},{16,12},{20,8},{24,4},{28,0},{1,29},{... | collective-permute-start | bytes 49160 | tf_op jit(solution)/shard_map/ppermute | solution.py:507
  47.8 3.2 %collective-permute-start.24 = (f32[32,128]{1,0:T(8,128)S(1)}, f32[32,128]{1,0:T(8,128)S(1)}, u32[]{:S(2)}, u32[]{:S(2)}) collective-permute-start(f32[32,128]{1,0:T(8,128)S(1)} %get-tuple-element.36.refs_0_), channel_id=1, source_target_pairs={{0,20},{4,16},{8,28},{12,24},{16,4},{20,0},{24,12},{28,8},{1,21},{... | collective-permute-start | bytes 49160 | tf_op jit(solution)/shard_map/ppermute | solution.py:507
  49.2 3.2 %collective-permute-start.25 = (f32[32,128]{1,0:T(8,128)S(1)}, f32[32,128]{1,0:T(8,128)S(1)}, u32[]{:S(2)}, u32[]{:S(2)}) collective-permute-start(f32[32,128]{1,0:T(8,128)S(1)} %get-tuple-element.36.refs_0_), channel_id=1, source_target_pairs={{0,12},{4,8},{8,4},{12,0},{16,28},{20,24},{24,20},{28,16},{1,13},{... | collective-permute-start | bytes 49160 | tf_op jit(solution)/shard_map/ppermute | solution.py:507
  (5 other events, 12.3 us)

commit v19 on v18

--- a/solution.py
+++ b/solution.py
@@ -184,7 +184,7 @@
 
 
 def fill_table(stacks, offsets, table):
-    block_rows = (table.shape[0] - 1) // (2 * len(offsets))
+    block_rows = (table.shape[0] - 1) // lax.axis_size("rows")
     low = iota((32, 128), 1) < 64
     pieces = [(ref, index) for ref in stacks for index in range(ref.shape[0])]
     for (ref, index), offset in zip(pieces, offsets):
@@ -203,12 +203,11 @@
 
 
 def near_table(offsets, near, block_rows):
-    count = len(offsets) // 2
-    return call(
-        functools.partial(near_kernel, offsets[:count]),
+    return call(
+        functools.partial(near_kernel, offsets[: len(near)]),
         "near",
         [vmem()] * len(near),
-        shaped((2 * count * block_rows + 1, 64, 128), BF16),
+        shaped((len(offsets) * block_rows + 1, 64, 128), BF16),
         near,
     )
 
@@ -230,15 +229,14 @@
     return largest
 
 
-def others_kernel(offsets, ranges, stacks, old_table, columns, matrix_ref, *refs):
+def others_kernel(offsets, ranges, filled, old_table, columns, matrix_ref, *refs):
     del old_table
-    far_refs, near_refs = refs[:stacks], refs[stacks : 2 * stacks]
-    table, *outs = refs[2 * stacks :]
-    fill_table(far_refs, offsets, table)
+    pieces, (table, *outs) = refs[: len(offsets)], refs[len(offsets) :]
+    fill_table(pieces[filled:], offsets[filled:], table)
     terms, first = outs[: len(ranges)], matrix_ref.shape[1] * 32
     if len(outs) > len(ranges):
         notes = largest_notes(
-            [ref[index, first:] for ref in near_refs + far_refs for index in range(ref.shape[0])]
+            [ref[index, first:] for ref in pieces for index in range(ref.shape[0])]
         )
         notes = jnp.sum(notes[8:], axis=(0, 1), keepdims=True)
         notes = jnp.broadcast_to(notes, (16, 128)).astype(BF16)
@@ -255,19 +253,19 @@
     one_product(lax.axis_index("cols"), columns, matrix_ref.at[0], table, out_ref)
 
 
-def products(offsets, ranges, columns, matrix, own_matrix, near, far, table):
-    block_rows, count = matrix.shape[1], len(offsets) // 2
-    extra = near[0].shape[1] > block_rows * 32
+def products(offsets, ranges, columns, matrix, own_matrix, pieces, filled, table):
+    block_rows = matrix.shape[1]
+    extra = pieces[0].shape[1] > block_rows * 32
     rows = block_rows * 32
     outs = [shaped(table.shape, BF16)] + [shaped((rows + 16 * extra, 128), BF16)] * len(ranges)
     if extra:
         outs.append(shaped((16, 128), BF16))
     table, *outs = call(
-        functools.partial(others_kernel, offsets[count:], ranges, len(near)),
+        functools.partial(others_kernel, offsets, ranges, filled),
         "others",
-        [vmem()] * (3 + 2 * len(near)),
+        [vmem()] * (3 + len(pieces)),
         outs,
-        (table, columns, matrix, *far, *near),
+        (table, columns, matrix, *pieces),
         input_output_aliases={0: 0},
     )
     terms = [swap(term, "cols", m) for m, term in zip(ranges, outs)]
@@ -565,11 +563,13 @@
     degree, inverse, matrix = prep(ranges, affinity, inv_degree)
     (own_matrix,) = prep([0], affinity)
     near, far, offsets = gather_rows(scaled, [inverse])
-    table = near_table(offsets, near, block_rows)
-    terms, _ = products(offsets, ranges, columns, matrix, own_matrix, near, far, table)
+    pieces, filled = near + far, len(near) + len(far) // 2
+    table = near_table(offsets, pieces[:filled], block_rows)
+    terms, _ = products(offsets, ranges, columns, matrix, own_matrix, pieces, filled, table)
     near, far, offsets = gather_rows(middle(degree, inverse, terms), [])
-    table = near_table(offsets, near, block_rows)
-    terms, (notes,) = products(offsets, ranges, columns, matrix, own_matrix, near, far, table)
+    pieces, filled = near + far, len(near) + len(far) // 2
+    table = near_table(offsets, pieces[:filled], block_rows)
+    terms, (notes,) = products(offsets, ranges, columns, matrix, own_matrix, pieces, filled, table)
     devices = float(groups * ranks)
     rows, grams = collect(devices, total, degree, row_gram(near + far), notes, terms)
     flip = 1 if ranks == 8 else 0

time: 56.4 us -> 56.3 us (level)
  no operation moved by 1% of the time
where the time goes in v19:
time: 56.3 us; the launch traced here: 56.1 us
  starting transfers between devices  24.6 us (44%)
  waiting for transfers between devices  18.7 us (33%)
  Pallas kernels  12.6 us (22%)
    ppermute x24, starting transfers between devices, swap(): lax.ppermute(value, axis, [(index, index ^ mask) for index in range(size)])  21.6 us
    ppermute x24, waiting for transfers between devices, swap(): lax.ppermute(value, axis, [(index, index ^ mask) for index in range(size)])  15.2 us
    pallas_call x17, Pallas kernels, call(): pl.pallas_call(kernel, out_shape=outs, in_specs=ins, out_specs=jax.tree.m...  12.6 us
    ppermute x3, waiting for transfers between devices, swap_both(): return lax.ppermute(value, ('rows', 'cols'), pairs)  3.48 us
    ppermute x3, starting transfers between devices, swap_both(): return lax.ppermute(value, ('rows', 'cols'), pairs)  2.97 us
  transfers between devices with their start and end apart: 27, of which 16 were waited for; matrix products, arithmetic and copies ran while one was open for 0% of the time, Pallas kernels for 12%

profile of v19, /device:TPU:0, one launch (start us, length us, event | category | flops | bytes accessed | tf_op | source)
XLA Modules:
  0.0 56.1 jit_solution(7800001288776554019)
XLA Ops:
  0.0 1.0 %start.1 = bf16[256,128]{1,0:T(8,128)(2,1)S(1)} custom-call(f32[1,8,4096]{2,1,0:T(8,128)} %panel_hbm.1, f32[1,8,64]{2,1,0:T(8,128)} %inv_hbm.1), custom_call_target="tpu_custom_call" | custom-call | tf_op jit(solution)/shard_map/start/pallas_call | solution.py:37
  1.0 3.4 %collective-permute-start = (bf16[256,128]{1,0:T(8,128)(2,1)S(1)}, bf16[256,128]{1,0:T(8,128)(2,1)S(1)}, u32[]{:S(2)}, u32[]{:S(2)}) collective-permute-start(bf16[256,128]{1,0:T(8,128)(2,1)S(1)} %start.1), channel_id=1, source_target_pairs={{0,28},{4,24},{8,20},{12,16},{16,12},{20,8},{24,4},{28,0},{1,29},{... | collective-permute-start | bytes 196616 | tf_op jit(solution)/shard_map/ppermute | solution.py:505
  5.3 2.3 %prep.2 = (f32[256,128]{1,0:T(8,128)S(1)}, f32[8,128]{1,0:T(8,128)S(1)}, bf16[3,8,64,512]{3,2,1,0:T(8,128)(2,1)S(1)}) custom-call(bf16[4,8,1,8,4096]{4,3,2,1,0:T(8,128)(2,1)} %affinity_hbm.3, f32[1,8,64]{2,1,0:T(8,128)} %inv_hbm.1), custom_call_target="tpu_custom_call" | custom-call | tf_op jit(solution)/shard_map/prep/pallas_call | solution.py:37
  8.2 0.8 %collective-permute-start.5 = (bf16[1,256,128]{2,1,0:T(8,128)(2,1)S(1)}, bf16[1,256,128]{2,1,0:T(8,128)(2,1)S(1)}, u32[]{:S(2)}, u32[]{:S(2)}) collective-permute-start(bf16[1,256,128]{2,1,0:T(8,128)(2,1)S(1)} %bitcast.30), channel_id=1, source_target_pairs={{0,4},{4,0},{8,12},{12,8},{16,20},{20,16},{24,28},{28,24},{1,5},{5... | collective-permute-start | bytes 196616 | tf_op jit(solution)/shard_map/ppermute | solution.py:505
  11.5 3.7 %collective-permute-start.7 = (bf16[256,128]{1,0:T(8,128)(2,1)S(1)}, bf16[256,128]{1,0:T(8,128)(2,1)S(1)}, u32[]{:S(2)}, u32[]{:S(2)}) collective-permute-start(bf16[256,128]{1,0:T(8,128)(2,1)S(1)} %get-tuple-element.25), channel_id=1, source_target_pairs={{0,3},{1,2},{2,1},{3,0},{4,7},{5,6},{6,5},{7,4},{8,11},{9,10},{10,... | collective-permute-start | bytes 196616 | tf_op jit(solution)/shard_map/ppermute | solution.py:505
  16.0 1.4 %prep.3.matrix_ref = bf16[1,8,64,512]{3,2,1,0:T(8,128)(2,1)S(1)} custom-call(bf16[4,8,1,8,4096]{4,3,2,1,0:T(8,128)(2,1)} %affinity_hbm.3), custom_call_target="tpu_custom_call" | custom-call | tf_op jit(solution)/shard_map/prep/pallas_call | solution.py:37
  17.9 3.2 %collective-permute-done.8.refs_2_ = bf16[256,128]{1,0:T(8,128)(2,1)S(1)} collective-permute-done((bf16[256,128]{1,0:T(8,128)(2,1)S(1)}, bf16[256,128]{1,0:T(8,128)(2,1)S(1)}, u32[]{:S(2)}, u32[]{:S(2)}) %collective-permute-start.8) | collective-permute-done | bytes 65568 | tf_op jit(solution)/shard_map/ppermute | solution.py:505
  21.1 1.1 %collective-permute-start.10 = (bf16[272,128]{1,0:T(8,128)(2,1)S(1)}, bf16[272,128]{1,0:T(8,128)(2,1)S(1)}, u32[]{:S(2)}, u32[]{:S(2)}) collective-permute-start(bf16[272,128]{1,0:T(8,128)(2,1)S(1)} %middle.1), channel_id=1, source_target_pairs={{0,28},{4,24},{8,20},{12,16},{16,12},{20,8},{24,4},{28,0},{1,29},{... | collective-permute-start | bytes 208904 | tf_op jit(solution)/shard_map/ppermute | solution.py:505
  22.2 1.5 %collective-permute-start.11 = (bf16[272,128]{1,0:T(8,128)(2,1)S(1)}, bf16[272,128]{1,0:T(8,128)(2,1)S(1)}, u32[]{:S(2)}, u32[]{:S(2)}) collective-permute-start(bf16[272,128]{1,0:T(8,128)(2,1)S(1)} %middle.1), channel_id=1, source_target_pairs={{0,20},{4,16},{8,28},{12,24},{16,4},{20,0},{24,12},{28,8},{1,21},{... | collective-permute-start | bytes 208904 | tf_op jit(solution)/shard_map/ppermute | solution.py:505
  24.5 2.0 %collective-permute-done.10 = bf16[272,128]{1,0:T(8,128)(2,1)S(1)} collective-permute-done((bf16[272,128]{1,0:T(8,128)(2,1)S(1)}, bf16[272,128]{1,0:T(8,128)(2,1)S(1)}, u32[]{:S(2)}, u32[]{:S(2)}) %collective-permute-start.10) | collective-permute-done | bytes 69664 | tf_op jit(solution)/shard_map/ppermute | solution.py:505
  26.6 1.3 %collective-permute-done.11 = bf16[272,128]{1,0:T(8,128)(2,1)S(1)} collective-permute-done((bf16[272,128]{1,0:T(8,128)(2,1)S(1)}, bf16[272,128]{1,0:T(8,128)(2,1)S(1)}, u32[]{:S(2)}, u32[]{:S(2)}) %collective-permute-start.11) | collective-permute-done | bytes 69664 | tf_op jit(solution)/shard_map/ppermute | solution.py:505
  30.2 2.3 %collective-permute-start.17 = (bf16[272,128]{1,0:T(8,128)(2,1)S(1)}, bf16[272,128]{1,0:T(8,128)(2,1)S(1)}, u32[]{:S(2)}, u32[]{:S(2)}) collective-permute-start(bf16[272,128]{1,0:T(8,128)(2,1)S(1)} %get-tuple-element.30), channel_id=1, source_target_pairs={{0,3},{1,2},{2,1},{3,0},{4,7},{5,6},{6,5},{7,4},{8,11},{9,10},{10,... | collective-permute-start | bytes 208904 | tf_op jit(solution)/shard_map/ppermute | solution.py:505
  32.7 1.9 %collective-permute-start.19 = (bf16[272,128]{1,0:T(8,128)(2,1)S(1)}, bf16[272,128]{1,0:T(8,128)(2,1)S(1)}, u32[]{:S(2)}, u32[]{:S(2)}) collective-permute-start(bf16[272,128]{1,0:T(8,128)(2,1)S(1)} %get-tuple-element.32), channel_id=1, source_target_pairs={{0,1},{1,0},{2,3},{3,2},{4,5},{5,4},{6,7},{7,6},{8,9},{9,8},{10,11... | collective-permute-start | bytes 208904 | tf_op jit(solution)/shard_map/ppermute | solution.py:505
  35.7 1.4 %collective-permute-done.17.refs_1_ = bf16[272,128]{1,0:T(8,128)(2,1)S(1)} collective-permute-done((bf16[272,128]{1,0:T(8,128)(2,1)S(1)}, bf16[272,128]{1,0:T(8,128)(2,1)S(1)}, u32[]{:S(2)}, u32[]{:S(2)}) %collective-permute-start.17) | collective-permute-done | bytes 69664 | tf_op jit(solution)/shard_map/ppermute | solution.py:505
  37.2 2.2 %collective-permute-done.18.refs_2_ = bf16[272,128]{1,0:T(8,128)(2,1)S(1)} collective-permute-done((bf16[272,128]{1,0:T(8,128)(2,1)S(1)}, bf16[272,128]{1,0:T(8,128)(2,1)S(1)}, u32[]{:S(2)}, u32[]{:S(2)}) %collective-permute-start.18) | collective-permute-done | bytes 69664 | tf_op jit(solution)/shard_map/ppermute | solution.py:505
  39.9 2.4 %collective-permute-start.21 = (f32[64,128]{1,0:T(8,128)S(1)}, f32[64,128]{1,0:T(8,128)S(1)}, u32[]{:S(2)}, u32[]{:S(2)}) collective-permute-start(f32[64,128]{1,0:T(8,128)S(1)} %get-tuple-element.34.refs_0_), channel_id=1, source_target_pairs={{0,7},{1,6},{2,5},{3,4},{4,3},{5,2},{6,1},{7,0},{8,15},{9,14},{10,... | collective-permute-start | bytes 98312 | tf_op jit(solution)/shard_map/ppermute | solution.py:515
  42.8 2.4 %collective-permute-done.20.refs_1_ = f32[64,128]{1,0:T(8,128)S(1)} collective-permute-done((f32[64,128]{1,0:T(8,128)S(1)}, f32[64,128]{1,0:T(8,128)S(1)}, u32[]{:S(2)}, u32[]{:S(2)}) %collective-permute-start.20) | collective-permute-done | bytes 32800 | tf_op jit(solution)/shard_map/ppermute | solution.py:515
  45.3 1.0 %collective-permute-done.22.refs_3_ = f32[64,128]{1,0:T(8,128)S(1)} collective-permute-done((f32[64,128]{1,0:T(8,128)S(1)}, f32[64,128]{1,0:T(8,128)S(1)}, u32[]{:S(2)}, u32[]{:S(2)}) %collective-permute-start.22) | collective-permute-done | bytes 32800 | tf_op jit(solution)/shard_map/ppermute | solution.py:515
  46.3 1.4 %collective-permute-start.23 = (f32[32,128]{1,0:T(8,128)S(1)}, f32[32,128]{1,0:T(8,128)S(1)}, u32[]{:S(2)}, u32[]{:S(2)}) collective-permute-start(f32[32,128]{1,0:T(8,128)S(1)} %get-tuple-element.36.refs_0_), channel_id=1, source_target_pairs={{0,28},{4,24},{8,20},{12,16},{16,12},{20,8},{24,4},{28,0},{1,29},{... | collective-permute-start | bytes 49160 | tf_op jit(solution)/shard_map/ppermute | solution.py:505
  47.7 1.3 %collective-permute-start.24 = (f32[32,128]{1,0:T(8,128)S(1)}, f32[32,128]{1,0:T(8,128)S(1)}, u32[]{:S(2)}, u32[]{:S(2)}) collective-permute-start(f32[32,128]{1,0:T(8,128)S(1)} %get-tuple-element.36.refs_0_), channel_id=1, source_target_pairs={{0,20},{4,16},{8,28},{12,24},{16,4},{20,0},{24,12},{28,8},{1,21},{... | collective-permute-start | bytes 49160 | tf_op jit(solution)/shard_map/ppermute | solution.py:505
  49.3 1.3 %first_factor.1.refs_4_.inverse_ref = f32[64,64]{1,0:T(8,128)S(1)} custom-call(f32[32,128]{1,0:T(8,128)S(1)} %get-tuple-element.35.gram_ref), custom_call_target="tpu_custom_call" | custom-call | tf_op jit(solution)/shard_map/first_factor/pallas_call | solution.py:37
  50.9 1.3 %collective-permute-done.25.refs_3_ = f32[32,128]{1,0:T(8,128)S(1)} collective-permute-done((f32[32,128]{1,0:T(8,128)S(1)}, f32[32,128]{1,0:T(8,128)S(1)}, u32[]{:S(2)}, u32[]{:S(2)}) %collective-permute-start.25) | collective-permute-done | bytes 16416 | tf_op jit(solution)/shard_map/ppermute | solution.py:505
  52.3 1.1 %collective-permute-done.26.refs_1_ = f32[32,128]{1,0:T(8,128)S(1)} collective-permute-done((f32[32,128]{1,0:T(8,128)S(1)}, f32[32,128]{1,0:T(8,128)S(1)}, u32[]{:S(2)}, u32[]{:S(2)}) %collective-permute-start.26) | collective-permute-done | bytes 16416 | tf_op jit(solution)/shard_map/ppermute | solution.py:505
  53.4 2.7 %finish.1 = f32[1,8,4096]{2,1,0:T(8,128)} custom-call(f32[256,128]{1,0:T(8,128)S(1)} %get-tuple-element.33.rows_ref, f32[64,64]{1,0:T(8,128)S(1)} %first_factor.1.refs_4_.inverse_ref, f32[32,128]{1,0:T(8,128)S(1)} %add_parts.1.refs_0_, f32[32,128]{1,0:T(8,128)S(1)} %collective-permute-done.26.refs_1_), custom_call_target="tpu_custom_call" | custom-call | tf_op jit(solution)/shard_map/finish/pallas_call | solution.py:37
  (52 shorter events, 11.4 us)
Async XLA Ops:
  1.0 6.7 %collective-permute-start = (bf16[256,128]{1,0:T(8,128)(2,1)S(1)}, bf16[256,128]{1,0:T(8,128)(2,1)S(1)}, u32[]{:S(2)}, u32[]{:S(2)}) collective-permute-start(bf16[256,128]{1,0:T(8,128)(2,1)S(1)} %start.1), channel_id=1, source_target_pairs={{0,28},{4,24},{8,20},{12,16},{16,12},{20,8},{24,4},{28,0},{1,29},{... | collective-permute-start | bytes 196616 | tf_op jit(solution)/shard_map/ppermute | solution.py:505
  4.4 3.9 %collective-permute-start.1 = (bf16[256,128]{1,0:T(8,128)(2,1)S(1)}, bf16[256,128]{1,0:T(8,128)(2,1)S(1)}, u32[]{:S(2)}, u32[]{:S(2)}) collective-permute-start(bf16[256,128]{1,0:T(8,128)(2,1)S(1)} %start.1), channel_id=1, source_target_pairs={{0,20},{4,16},{8,28},{12,24},{16,4},{20,0},{24,12},{28,8},{1,21},{... | collective-permute-start | bytes 196616 | tf_op jit(solution)/shard_map/ppermute | solution.py:505
  5.2 4.3 %collective-permute-start.2 = (bf16[256,128]{1,0:T(8,128)(2,1)S(1)}, bf16[256,128]{1,0:T(8,128)(2,1)S(1)}, u32[]{:S(2)}, u32[]{:S(2)}) collective-permute-start(bf16[256,128]{1,0:T(8,128)(2,1)S(1)} %start.1), channel_id=1, source_target_pairs={{0,12},{4,8},{8,4},{12,0},{16,28},{20,24},{24,20},{28,16},{1,13},{... | collective-permute-start | bytes 196616 | tf_op jit(solution)/shard_map/ppermute | solution.py:505
  5.3 4.4 %collective-permute-start.3 = (bf16[1,256,128]{2,1,0:T(8,128)(2,1)S(1)}, bf16[1,256,128]{2,1,0:T(8,128)(2,1)S(1)}, u32[]{:S(2)}, u32[]{:S(2)}) collective-permute-start(bf16[1,256,128]{2,1,0:T(8,128)(2,1)S(1)} %bitcast.27), channel_id=1, source_target_pairs={{0,4},{4,0},{8,12},{12,8},{16,20},{20,16},{24,28},{28,24},{1,5},{5... | collective-permute-start | bytes 196616 | tf_op jit(solution)/shard_map/ppermute | solution.py:505
  7.7 2.0 %collective-permute-start.4 = (bf16[1,256,128]{2,1,0:T(8,128)(2,1)S(1)}, bf16[1,256,128]{2,1,0:T(8,128)(2,1)S(1)}, u32[]{:S(2)}, u32[]{:S(2)}) collective-permute-start(bf16[1,256,128]{2,1,0:T(8,128)(2,1)S(1)} %stack.1.refs_1_), channel_id=1, source_target_pairs={{0,4},{4,0},{8,12},{12,8},{16,20},{20,16},{24,28},{28,24},{1,5},{5... | collective-permute-start | bytes 196616 | tf_op jit(solution)/shard_map/ppermute | solution.py:505
  8.2 1.7 %collective-permute-start.5 = (bf16[1,256,128]{2,1,0:T(8,128)(2,1)S(1)}, bf16[1,256,128]{2,1,0:T(8,128)(2,1)S(1)}, u32[]{:S(2)}, u32[]{:S(2)}) collective-permute-start(bf16[1,256,128]{2,1,0:T(8,128)(2,1)S(1)} %bitcast.30), channel_id=1, source_target_pairs={{0,4},{4,0},{8,12},{12,8},{16,20},{20,16},{24,28},{28,24},{1,5},{5... | collective-permute-start | bytes 196616 | tf_op jit(solution)/shard_map/ppermute | solution.py:505
  11.5 6.3 %collective-permute-start.7 = (bf16[256,128]{1,0:T(8,128)(2,1)S(1)}, bf16[256,128]{1,0:T(8,128)(2,1)S(1)}, u32[]{:S(2)}, u32[]{:S(2)}) collective-permute-start(bf16[256,128]{1,0:T(8,128)(2,1)S(1)} %get-tuple-element.25), channel_id=1, source_target_pairs={{0,3},{1,2},{2,1},{3,0},{4,7},{5,6},{6,5},{7,4},{8,11},{9,10},{10,... | collective-permute-start | bytes 196616 | tf_op jit(solution)/shard_map/ppermute | solution.py:505
  15.2 5.9 %collective-permute-start.8 = (bf16[256,128]{1,0:T(8,128)(2,1)S(1)}, bf16[256,128]{1,0:T(8,128)(2,1)S(1)}, u32[]{:S(2)}, u32[]{:S(2)}) collective-permute-start(bf16[256,128]{1,0:T(8,128)(2,1)S(1)} %get-tuple-element.26), channel_id=1, source_target_pairs={{0,2},{1,3},{2,0},{3,1},{4,6},{5,7},{6,4},{7,5},{8,10},{9,11},{10,... | collective-permute-start | bytes 196616 | tf_op jit(solution)/shard_map/ppermute | solution.py:505
  15.2 5.9 %collective-permute-start.9 = (bf16[256,128]{1,0:T(8,128)(2,1)S(1)}, bf16[256,128]{1,0:T(8,128)(2,1)S(1)}, u32[]{:S(2)}, u32[]{:S(2)}) collective-permute-start(bf16[256,128]{1,0:T(8,128)(2,1)S(1)} %get-tuple-element.27), channel_id=1, source_target_pairs={{0,1},{1,0},{2,3},{3,2},{4,5},{5,4},{6,7},{7,6},{8,9},{9,8},{10,11... | collective-permute-start | bytes 196616 | tf_op jit(solution)/shard_map/ppermute | solution.py:505
  21.1 5.4 %collective-permute-start.10 = (bf16[272,128]{1,0:T(8,128)(2,1)S(1)}, bf16[272,128]{1,0:T(8,128)(2,1)S(1)}, u32[]{:S(2)}, u32[]{:S(2)}) collective-permute-start(bf16[272,128]{1,0:T(8,128)(2,1)S(1)} %middle.1), channel_id=1, source_target_pairs={{0,28},{4,24},{8,20},{12,16},{16,12},{20,8},{24,4},{28,0},{1,29},{... | collective-permute-start | bytes 208904 | tf_op jit(solution)/shard_map/ppermute | solution.py:505
  22.2 5.7 %collective-permute-start.11 = (bf16[272,128]{1,0:T(8,128)(2,1)S(1)}, bf16[272,128]{1,0:T(8,128)(2,1)S(1)}, u32[]{:S(2)}, u32[]{:S(2)}) collective-permute-start(bf16[272,128]{1,0:T(8,128)(2,1)S(1)} %middle.1), channel_id=1, source_target_pairs={{0,20},{4,16},{8,28},{12,24},{16,4},{20,0},{24,12},{28,8},{1,21},{... | collective-permute-start | bytes 208904 | tf_op jit(solution)/shard_map/ppermute | solution.py:505
  23.7 4.4 %collective-permute-start.12 = (bf16[272,128]{1,0:T(8,128)(2,1)S(1)}, bf16[272,128]{1,0:T(8,128)(2,1)S(1)}, u32[]{:S(2)}, u32[]{:S(2)}) collective-permute-start(bf16[272,128]{1,0:T(8,128)(2,1)S(1)} %middle.1), channel_id=1, source_target_pairs={{0,12},{4,8},{8,4},{12,0},{16,28},{20,24},{24,20},{28,16},{1,13},{... | collective-permute-start | bytes 208904 | tf_op jit(solution)/shard_map/ppermute | solution.py:505
  24.0 4.4 %collective-permute-start.13 = (bf16[1,272,128]{2,1,0:T(8,128)(2,1)S(1)}, bf16[1,272,128]{2,1,0:T(8,128)(2,1)S(1)}, u32[]{:S(2)}, u32[]{:S(2)}) collective-permute-start(bf16[1,272,128]{2,1,0:T(8,128)(2,1)S(1)} %bitcast.11), channel_id=1, source_target_pairs={{0,4},{4,0},{8,12},{12,8},{16,20},{20,16},{24,28},{28,24},{1,5},{5... | collective-permute-start | bytes 208904 | tf_op jit(solution)/shard_map/ppermute | solution.py:505
  26.6 1.8 %collective-permute-start.14 = (bf16[1,272,128]{2,1,0:T(8,128)(2,1)S(1)}, bf16[1,272,128]{2,1,0:T(8,128)(2,1)S(1)}, u32[]{:S(2)}, u32[]{:S(2)}) collective-permute-start(bf16[1,272,128]{2,1,0:T(8,128)(2,1)S(1)} %bitcast.15), channel_id=1, source_target_pairs={{0,4},{4,0},{8,12},{12,8},{16,20},{20,16},{24,28},{28,24},{1,5},{5... | collective-permute-start | bytes 208904 | tf_op jit(solution)/shard_map/ppermute | solution.py:505
  28.1 1.3 %collective-permute-start.16 = (bf16[1,272,128]{2,1,0:T(8,128)(2,1)S(1)}, bf16[1,272,128]{2,1,0:T(8,128)(2,1)S(1)}, u32[]{:S(2)}, u32[]{:S(2)}) collective-permute-start(bf16[1,272,128]{2,1,0:T(8,128)(2,1)S(1)} %bitcast.23), channel_id=1, source_target_pairs={{0,4},{4,0},{8,12},{12,8},{16,20},{20,16},{24,28},{28,24},{1,5},{5... | collective-permute-start | bytes 208904 | tf_op jit(solution)/shard_map/ppermute | solution.py:505
  30.2 7.0 %collective-permute-start.17 = (bf16[272,128]{1,0:T(8,128)(2,1)S(1)}, bf16[272,128]{1,0:T(8,128)(2,1)S(1)}, u32[]{:S(2)}, u32[]{:S(2)}) collective-permute-start(bf16[272,128]{1,0:T(8,128)(2,1)S(1)} %get-tuple-element.30), channel_id=1, source_target_pairs={{0,3},{1,2},{2,1},{3,0},{4,7},{5,6},{6,5},{7,4},{8,11},{9,10},{10,... | collective-permute-start | bytes 208904 | tf_op jit(solution)/shard_map/ppermute | solution.py:505
  32.5 6.9 %collective-permute-start.18 = (bf16[272,128]{1,0:T(8,128)(2,1)S(1)}, bf16[272,128]{1,0:T(8,128)(2,1)S(1)}, u32[]{:S(2)}, u32[]{:S(2)}) collective-permute-start(bf16[272,128]{1,0:T(8,128)(2,1)S(1)} %get-tuple-element.31), channel_id=1, source_target_pairs={{0,2},{1,3},{2,0},{3,1},{4,6},{5,7},{6,4},{7,5},{8,10},{9,11},{10,... | collective-permute-start | bytes 208904 | tf_op jit(solution)/shard_map/ppermute | solution.py:505
  32.7 6.7 %collective-permute-start.19 = (bf16[272,128]{1,0:T(8,128)(2,1)S(1)}, bf16[272,128]{1,0:T(8,128)(2,1)S(1)}, u32[]{:S(2)}, u32[]{:S(2)}) collective-permute-start(bf16[272,128]{1,0:T(8,128)(2,1)S(1)} %get-tuple-element.32), channel_id=1, source_target_pairs={{0,1},{1,0},{2,3},{3,2},{4,5},{5,4},{6,7},{7,6},{8,9},{9,8},{10,11... | collective-permute-start | bytes 208904 | tf_op jit(solution)/shard_map/ppermute | solution.py:505
  39.9 5.4 %collective-permute-start.20 = (f32[64,128]{1,0:T(8,128)S(1)}, f32[64,128]{1,0:T(8,128)S(1)}, u32[]{:S(2)}, u32[]{:S(2)}) collective-permute-start(f32[64,128]{1,0:T(8,128)S(1)} %get-tuple-element.34.refs_0_), channel_id=1, source_target_pairs={{0,6},{1,7},{2,4},{3,5},{4,2},{5,3},{6,0},{7,1},{8,14},{9,15},{10,... | collective-permute-start | bytes 98312 | tf_op jit(solution)/shard_map/ppermute | solution.py:515
  39.9 5.4 %collective-permute-start.21 = (f32[64,128]{1,0:T(8,128)S(1)}, f32[64,128]{1,0:T(8,128)S(1)}, u32[]{:S(2)}, u32[]{:S(2)}) collective-permute-start(f32[64,128]{1,0:T(8,128)S(1)} %get-tuple-element.34.refs_0_), channel_id=1, source_target_pairs={{0,7},{1,6},{2,5},{3,4},{4,3},{5,2},{6,1},{7,0},{8,15},{9,14},{10,... | collective-permute-start | bytes 98312 | tf_op jit(solution)/shard_map/ppermute | solution.py:515
  42.3 4.0 %collective-permute-start.22 = (f32[64,128]{1,0:T(8,128)S(1)}, f32[64,128]{1,0:T(8,128)S(1)}, u32[]{:S(2)}, u32[]{:S(2)}) collective-permute-start(f32[64,128]{1,0:T(8,128)S(1)} %get-tuple-element.34.refs_0_), channel_id=1, source_target_pairs={{0,5},{1,4},{2,7},{3,6},{4,1},{5,0},{6,3},{7,2},{8,13},{9,12},{10,... | collective-permute-start | bytes 98312 | tf_op jit(solution)/shard_map/ppermute | solution.py:515
  46.3 4.3 %collective-permute-start.23 = (f32[32,128]{1,0:T(8,128)S(1)}, f32[32,128]{1,0:T(8,128)S(1)}, u32[]{:S(2)}, u32[]{:S(2)}) collective-permute-start(f32[32,128]{1,0:T(8,128)S(1)} %get-tuple-element.36.refs_0_), channel_id=1, source_target_pairs={{0,28},{4,24},{8,20},{12,16},{16,12},{20,8},{24,4},{28,0},{1,29},{... | collective-permute-start | bytes 49160 | tf_op jit(solution)/shard_map/ppermute | solution.py:505
  47.7 3.2 %collective-permute-start.24 = (f32[32,128]{1,0:T(8,128)S(1)}, f32[32,128]{1,0:T(8,128)S(1)}, u32[]{:S(2)}, u32[]{:S(2)}) collective-permute-start(f32[32,128]{1,0:T(8,128)S(1)} %get-tuple-element.36.refs_0_), channel_id=1, source_target_pairs={{0,20},{4,16},{8,28},{12,24},{16,4},{20,0},{24,12},{28,8},{1,21},{... | collective-permute-start | bytes 49160 | tf_op jit(solution)/shard_map/ppermute | solution.py:505
  49.1 3.2 %collective-permute-start.25 = (f32[32,128]{1,0:T(8,128)S(1)}, f32[32,128]{1,0:T(8,128)S(1)}, u32[]{:S(2)}, u32[]{:S(2)}) collective-permute-start(f32[32,128]{1,0:T(8,128)S(1)} %get-tuple-element.36.refs_0_), channel_id=1, source_target_pairs={{0,12},{4,8},{8,4},{12,0},{16,28},{20,24},{24,20},{28,16},{1,13},{... | collective-permute-start | bytes 49160 | tf_op jit(solution)/shard_map/ppermute | solution.py:505
  (5 other events, 12.3 us)

commit v20 on v19

--- a/solution.py
+++ b/solution.py
@@ -468,10 +468,10 @@
 
 
 def finish_kernel(total, rows_ref, inverse_ref, *refs):
-    out_ref, scratch = refs[-2:]
+    out_hbm, out_ref, scratch, sems = refs[-4:]
     block_rows = out_ref.shape[1]
     packed = refs[0][...]
-    for part in refs[1:-2]:
+    for part in refs[1:-4]:
         packed = packed + part[...]
     first = inverse_ref[...]
     gram = dot_turned(
@@ -482,22 +482,39 @@
     both = jnp.concatenate(
         [jnp.concatenate([inverse, zero], axis=1), jnp.concatenate([zero, inverse], axis=1)], axis=0
     )
-    current = dot_turned(rows_ref[...], both)
-    for i in range(block_rows):
-        scratch[pl.ds(i, 32, stride=block_rows), :] = current[i * 32 : (i + 1) * 32]
-    for t in range(32):
-        out_ref[0, :, t * 128 : (t + 1) * 128] = scratch[t * block_rows : (t + 1) * block_rows, :]
+    copies = []
+    for part in range(2):
+        rows = [rows_ref[i * 32 + part * 16 : i * 32 + (part + 1) * 16, :] for i in range(block_rows)]
+        current = dot_turned(jnp.concatenate(rows, axis=0), both)
+        first = part * 16 * block_rows
+        for i in range(block_rows):
+            scratch[pl.ds(first + i, 16, stride=block_rows), :] = current[i * 16 : (i + 1) * 16]
+        for t in range(part * 16, (part + 1) * 16):
+            out_ref[0, :, t * 128 : (t + 1) * 128] = scratch[t * block_rows : (t + 1) * block_rows, :]
+        lanes = pl.ds(part * 2048, 2048)
+        copies.append(
+            pltpu.make_async_copy(out_ref.at[:, :, lanes], out_hbm.at[:, :, lanes], sems.at[part])
+        )
+        copies[-1].start()
+    for copy in copies:
+        copy.wait()
 
 
 def finish(total, block_rows, rows, inverse, grams):
-    return call(
+    shape = (1, block_rows, 32 * 128)
+    return pl.pallas_call(
         functools.partial(finish_kernel, total),
-        "finish",
-        [vmem()] * (2 + len(grams)),
-        shaped((1, block_rows, 32 * 128), F32),
-        (rows, inverse, *grams),
-        [pltpu.VMEM((rows.shape[0] + block_rows, 128), F32)],
-    )
+        out_shape=shaped(shape, F32),
+        in_specs=[vmem()] * (2 + len(grams)),
+        out_specs=hbm(),
+        scratch_shapes=[
+            pltpu.VMEM(shape, F32),
+            pltpu.VMEM((rows.shape[0] + block_rows, 128), F32),
+            pltpu.SemaphoreType.DMA((2,)),
+        ],
+        compiler_params=params(),
+        name="finish",
+    )(rows, inverse, *grams)
 
 
 def swap(value, axis, mask):

time: 56.3 us -> 56.3 us (level)
    pallas_call x0 -> x1, Pallas kernels: none -> 2.74 us  [finish(): pl.pallas_call(functools.partial(finish_kernel, total), out_shape=shaped(...]
    pallas_call x17 -> x16, Pallas kernels: 12.6 us -> 9.93 us  [call(): pl.pallas_call(kernel, out_shape=outs, in_specs=ins, out_specs=jax.tree.m...]
where the time goes in v20:
time: 56.3 us; the launch traced here: 56.2 us
  starting transfers between devices  24.6 us (44%)
  waiting for transfers between devices  18.7 us (33%)
  Pallas kernels  12.7 us (23%)
    ppermute x24, starting transfers between devices, swap(): lax.ppermute(value, axis, [(index, index ^ mask) for index in range(size)])  21.6 us
    ppermute x24, waiting for transfers between devices, swap(): lax.ppermute(value, axis, [(index, index ^ mask) for index in range(size)])  15.2 us
    pallas_call x16, Pallas kernels, call(): pl.pallas_call(kernel, out_shape=outs, in_specs=ins, out_specs=jax.tree.m...  9.93 us
    ppermute x3, waiting for transfers between devices, swap_both(): return lax.ppermute(value, ('rows', 'cols'), pairs)  3.48 us
    ppermute x3, starting transfers between devices, swap_both(): return lax.ppermute(value, ('rows', 'cols'), pairs)  2.97 us
    pallas_call x1, Pallas kernels, finish(): pl.pallas_call(functools.partial(finish_kernel, total), out_shape=shaped(...  2.74 us
  transfers between devices with their start and end apart: 27, of which 16 were waited for; matrix products, arithmetic and copies ran while one was open for 0% of the time, Pallas kernels for 12%

profile of v20, /device:TPU:0, one launch (start us, length us, event | category | flops | bytes accessed | tf_op | source)
XLA Modules:
  0.0 56.2 jit_solution(14496958238856087441)
XLA Ops:
  0.0 1.0 %start.1 = bf16[256,128]{1,0:T(8,128)(2,1)S(1)} custom-call(f32[1,8,4096]{2,1,0:T(8,128)} %panel_hbm.1, f32[1,8,64]{2,1,0:T(8,128)} %inv_hbm.1), custom_call_target="tpu_custom_call" | custom-call | tf_op jit(solution)/shard_map/start/pallas_call | solution.py:37
  1.0 3.4 %collective-permute-start = (bf16[256,128]{1,0:T(8,128)(2,1)S(1)}, bf16[256,128]{1,0:T(8,128)(2,1)S(1)}, u32[]{:S(2)}, u32[]{:S(2)}) collective-permute-start(bf16[256,128]{1,0:T(8,128)(2,1)S(1)} %start.1), channel_id=1, source_target_pairs={{0,28},{4,24},{8,20},{12,16},{16,12},{20,8},{24,4},{28,0},{1,29},{... | collective-permute-start | bytes 196616 | tf_op jit(solution)/shard_map/ppermute | solution.py:522
  5.3 2.3 %prep.2 = (f32[256,128]{1,0:T(8,128)S(1)}, f32[8,128]{1,0:T(8,128)S(1)}, bf16[3,8,64,512]{3,2,1,0:T(8,128)(2,1)S(1)}) custom-call(bf16[4,8,1,8,4096]{4,3,2,1,0:T(8,128)(2,1)} %affinity_hbm.3, f32[1,8,64]{2,1,0:T(8,128)} %inv_hbm.1), custom_call_target="tpu_custom_call" | custom-call | tf_op jit(solution)/shard_map/prep/pallas_call | solution.py:37
  8.2 0.8 %collective-permute-start.5 = (bf16[1,256,128]{2,1,0:T(8,128)(2,1)S(1)}, bf16[1,256,128]{2,1,0:T(8,128)(2,1)S(1)}, u32[]{:S(2)}, u32[]{:S(2)}) collective-permute-start(bf16[1,256,128]{2,1,0:T(8,128)(2,1)S(1)} %bitcast.30), channel_id=1, source_target_pairs={{0,4},{4,0},{8,12},{12,8},{16,20},{20,16},{24,28},{28,24},{1,5},{5... | collective-permute-start | bytes 196616 | tf_op jit(solution)/shard_map/ppermute | solution.py:522
  11.5 3.7 %collective-permute-start.7 = (bf16[256,128]{1,0:T(8,128)(2,1)S(1)}, bf16[256,128]{1,0:T(8,128)(2,1)S(1)}, u32[]{:S(2)}, u32[]{:S(2)}) collective-permute-start(bf16[256,128]{1,0:T(8,128)(2,1)S(1)} %get-tuple-element.25), channel_id=1, source_target_pairs={{0,3},{1,2},{2,1},{3,0},{4,7},{5,6},{6,5},{7,4},{8,11},{9,10},{10,... | collective-permute-start | bytes 196616 | tf_op jit(solution)/shard_map/ppermute | solution.py:522
  16.0 1.4 %prep.3.matrix_ref = bf16[1,8,64,512]{3,2,1,0:T(8,128)(2,1)S(1)} custom-call(bf16[4,8,1,8,4096]{4,3,2,1,0:T(8,128)(2,1)} %affinity_hbm.3), custom_call_target="tpu_custom_call" | custom-call | tf_op jit(solution)/shard_map/prep/pallas_call | solution.py:37
  17.9 3.2 %collective-permute-done.8.refs_2_ = bf16[256,128]{1,0:T(8,128)(2,1)S(1)} collective-permute-done((bf16[256,128]{1,0:T(8,128)(2,1)S(1)}, bf16[256,128]{1,0:T(8,128)(2,1)S(1)}, u32[]{:S(2)}, u32[]{:S(2)}) %collective-permute-start.8) | collective-permute-done | bytes 65568 | tf_op jit(solution)/shard_map/ppermute | solution.py:522
  21.1 1.1 %collective-permute-start.10 = (bf16[272,128]{1,0:T(8,128)(2,1)S(1)}, bf16[272,128]{1,0:T(8,128)(2,1)S(1)}, u32[]{:S(2)}, u32[]{:S(2)}) collective-permute-start(bf16[272,128]{1,0:T(8,128)(2,1)S(1)} %middle.1), channel_id=1, source_target_pairs={{0,28},{4,24},{8,20},{12,16},{16,12},{20,8},{24,4},{28,0},{1,29},{... | collective-permute-start | bytes 208904 | tf_op jit(solution)/shard_map/ppermute | solution.py:522
  22.2 1.5 %collective-permute-start.11 = (bf16[272,128]{1,0:T(8,128)(2,1)S(1)}, bf16[272,128]{1,0:T(8,128)(2,1)S(1)}, u32[]{:S(2)}, u32[]{:S(2)}) collective-permute-start(bf16[272,128]{1,0:T(8,128)(2,1)S(1)} %middle.1), channel_id=1, source_target_pairs={{0,20},{4,16},{8,28},{12,24},{16,4},{20,0},{24,12},{28,8},{1,21},{... | collective-permute-start | bytes 208904 | tf_op jit(solution)/shard_map/ppermute | solution.py:522
  24.5 2.0 %collective-permute-done.10 = bf16[272,128]{1,0:T(8,128)(2,1)S(1)} collective-permute-done((bf16[272,128]{1,0:T(8,128)(2,1)S(1)}, bf16[272,128]{1,0:T(8,128)(2,1)S(1)}, u32[]{:S(2)}, u32[]{:S(2)}) %collective-permute-start.10) | collective-permute-done | bytes 69664 | tf_op jit(solution)/shard_map/ppermute | solution.py:522
  26.6 1.3 %collective-permute-done.11 = bf16[272,128]{1,0:T(8,128)(2,1)S(1)} collective-permute-done((bf16[272,128]{1,0:T(8,128)(2,1)S(1)}, bf16[272,128]{1,0:T(8,128)(2,1)S(1)}, u32[]{:S(2)}, u32[]{:S(2)}) %collective-permute-start.11) | collective-permute-done | bytes 69664 | tf_op jit(solution)/shard_map/ppermute | solution.py:522
  30.2 2.3 %collective-permute-start.17 = (bf16[272,128]{1,0:T(8,128)(2,1)S(1)}, bf16[272,128]{1,0:T(8,128)(2,1)S(1)}, u32[]{:S(2)}, u32[]{:S(2)}) collective-permute-start(bf16[272,128]{1,0:T(8,128)(2,1)S(1)} %get-tuple-element.30), channel_id=1, source_target_pairs={{0,3},{1,2},{2,1},{3,0},{4,7},{5,6},{6,5},{7,4},{8,11},{9,10},{10,... | collective-permute-start | bytes 208904 | tf_op jit(solution)/shard_map/ppermute | solution.py:522
  32.7 1.9 %collective-permute-start.19 = (bf16[272,128]{1,0:T(8,128)(2,1)S(1)}, bf16[272,128]{1,0:T(8,128)(2,1)S(1)}, u32[]{:S(2)}, u32[]{:S(2)}) collective-permute-start(bf16[272,128]{1,0:T(8,128)(2,1)S(1)} %get-tuple-element.32), channel_id=1, source_target_pairs={{0,1},{1,0},{2,3},{3,2},{4,5},{5,4},{6,7},{7,6},{8,9},{9,8},{10,11... | collective-permute-start | bytes 208904 | tf_op jit(solution)/shard_map/ppermute | solution.py:522
  35.7 1.4 %collective-permute-done.17.refs_1_ = bf16[272,128]{1,0:T(8,128)(2,1)S(1)} collective-permute-done((bf16[272,128]{1,0:T(8,128)(2,1)S(1)}, bf16[272,128]{1,0:T(8,128)(2,1)S(1)}, u32[]{:S(2)}, u32[]{:S(2)}) %collective-permute-start.17) | collective-permute-done | bytes 69664 | tf_op jit(solution)/shard_map/ppermute | solution.py:522
  37.2 2.2 %collective-permute-done.18.refs_2_ = bf16[272,128]{1,0:T(8,128)(2,1)S(1)} collective-permute-done((bf16[272,128]{1,0:T(8,128)(2,1)S(1)}, bf16[272,128]{1,0:T(8,128)(2,1)S(1)}, u32[]{:S(2)}, u32[]{:S(2)}) %collective-permute-start.18) | collective-permute-done | bytes 69664 | tf_op jit(solution)/shard_map/ppermute | solution.py:522
  39.9 2.4 %collective-permute-start.21 = (f32[64,128]{1,0:T(8,128)S(1)}, f32[64,128]{1,0:T(8,128)S(1)}, u32[]{:S(2)}, u32[]{:S(2)}) collective-permute-start(f32[64,128]{1,0:T(8,128)S(1)} %get-tuple-element.34.refs_0_), channel_id=1, source_target_pairs={{0,7},{1,6},{2,5},{3,4},{4,3},{5,2},{6,1},{7,0},{8,15},{9,14},{10,... | collective-permute-start | bytes 98312 | tf_op jit(solution)/shard_map/ppermute | solution.py:532
  42.8 2.4 %collective-permute-done.20.refs_1_ = f32[64,128]{1,0:T(8,128)S(1)} collective-permute-done((f32[64,128]{1,0:T(8,128)S(1)}, f32[64,128]{1,0:T(8,128)S(1)}, u32[]{:S(2)}, u32[]{:S(2)}) %collective-permute-start.20) | collective-permute-done | bytes 32800 | tf_op jit(solution)/shard_map/ppermute | solution.py:532
  45.3 1.0 %collective-permute-done.22.refs_3_ = f32[64,128]{1,0:T(8,128)S(1)} collective-permute-done((f32[64,128]{1,0:T(8,128)S(1)}, f32[64,128]{1,0:T(8,128)S(1)}, u32[]{:S(2)}, u32[]{:S(2)}) %collective-permute-start.22) | collective-permute-done | bytes 32800 | tf_op jit(solution)/shard_map/ppermute | solution.py:532
  46.3 1.4 %collective-permute-start.23 = (f32[32,128]{1,0:T(8,128)S(1)}, f32[32,128]{1,0:T(8,128)S(1)}, u32[]{:S(2)}, u32[]{:S(2)}) collective-permute-start(f32[32,128]{1,0:T(8,128)S(1)} %get-tuple-element.36.refs_0_), channel_id=1, source_target_pairs={{0,28},{4,24},{8,20},{12,16},{16,12},{20,8},{24,4},{28,0},{1,29},{... | collective-permute-start | bytes 49160 | tf_op jit(solution)/shard_map/ppermute | solution.py:522
  47.7 1.3 %collective-permute-start.24 = (f32[32,128]{1,0:T(8,128)S(1)}, f32[32,128]{1,0:T(8,128)S(1)}, u32[]{:S(2)}, u32[]{:S(2)}) collective-permute-start(f32[32,128]{1,0:T(8,128)S(1)} %get-tuple-element.36.refs_0_), channel_id=1, source_target_pairs={{0,20},{4,16},{8,28},{12,24},{16,4},{20,0},{24,12},{28,8},{1,21},{... | collective-permute-start | bytes 49160 | tf_op jit(solution)/shard_map/ppermute | solution.py:522
  49.3 1.3 %first_factor.1.refs_4_.inverse_ref = f32[64,64]{1,0:T(8,128)S(1)} custom-call(f32[32,128]{1,0:T(8,128)S(1)} %get-tuple-element.35.gram_ref), custom_call_target="tpu_custom_call" | custom-call | tf_op jit(solution)/shard_map/first_factor/pallas_call | solution.py:37
  50.9 1.3 %collective-permute-done.25.refs_3_ = f32[32,128]{1,0:T(8,128)S(1)} collective-permute-done((f32[32,128]{1,0:T(8,128)S(1)}, f32[32,128]{1,0:T(8,128)S(1)}, u32[]{:S(2)}, u32[]{:S(2)}) %collective-permute-start.25) | collective-permute-done | bytes 16416 | tf_op jit(solution)/shard_map/ppermute | solution.py:522
  52.3 1.1 %collective-permute-done.26.refs_1_ = f32[32,128]{1,0:T(8,128)S(1)} collective-permute-done((f32[32,128]{1,0:T(8,128)S(1)}, f32[32,128]{1,0:T(8,128)S(1)}, u32[]{:S(2)}, u32[]{:S(2)}) %collective-permute-start.26) | collective-permute-done | bytes 16416 | tf_op jit(solution)/shard_map/ppermute | solution.py:522
  53.4 2.7 %finish.1 = f32[1,8,4096]{2,1,0:T(8,128)} custom-call(f32[256,128]{1,0:T(8,128)S(1)} %get-tuple-element.33.rows_ref, f32[64,64]{1,0:T(8,128)S(1)} %first_factor.1.refs_4_.inverse_ref, f32[32,128]{1,0:T(8,128)S(1)} %add_parts.1.refs_0_, f32[32,128]{1,0:T(8,128)S(1)} %collective-permute-done.26.refs_1_), custom_call_target="tpu_custom_call" | custom-call | tf_op jit(solution)/shard_map/finish/pallas_call | solution.py:505
  (52 shorter events, 11.4 us)
Async XLA Ops:
  1.0 6.7 %collective-permute-start = (bf16[256,128]{1,0:T(8,128)(2,1)S(1)}, bf16[256,128]{1,0:T(8,128)(2,1)S(1)}, u32[]{:S(2)}, u32[]{:S(2)}) collective-permute-start(bf16[256,128]{1,0:T(8,128)(2,1)S(1)} %start.1), channel_id=1, source_target_pairs={{0,28},{4,24},{8,20},{12,16},{16,12},{20,8},{24,4},{28,0},{1,29},{... | collective-permute-start | bytes 196616 | tf_op jit(solution)/shard_map/ppermute | solution.py:522
  4.4 3.9 %collective-permute-start.1 = (bf16[256,128]{1,0:T(8,128)(2,1)S(1)}, bf16[256,128]{1,0:T(8,128)(2,1)S(1)}, u32[]{:S(2)}, u32[]{:S(2)}) collective-permute-start(bf16[256,128]{1,0:T(8,128)(2,1)S(1)} %start.1), channel_id=1, source_target_pairs={{0,20},{4,16},{8,28},{12,24},{16,4},{20,0},{24,12},{28,8},{1,21},{... | collective-permute-start | bytes 196616 | tf_op jit(solution)/shard_map/ppermute | solution.py:522
  5.2 4.3 %collective-permute-start.2 = (bf16[256,128]{1,0:T(8,128)(2,1)S(1)}, bf16[256,128]{1,0:T(8,128)(2,1)S(1)}, u32[]{:S(2)}, u32[]{:S(2)}) collective-permute-start(bf16[256,128]{1,0:T(8,128)(2,1)S(1)} %start.1), channel_id=1, source_target_pairs={{0,12},{4,8},{8,4},{12,0},{16,28},{20,24},{24,20},{28,16},{1,13},{... | collective-permute-start | bytes 196616 | tf_op jit(solution)/shard_map/ppermute | solution.py:522
  5.3 4.4 %collective-permute-start.3 = (bf16[1,256,128]{2,1,0:T(8,128)(2,1)S(1)}, bf16[1,256,128]{2,1,0:T(8,128)(2,1)S(1)}, u32[]{:S(2)}, u32[]{:S(2)}) collective-permute-start(bf16[1,256,128]{2,1,0:T(8,128)(2,1)S(1)} %bitcast.27), channel_id=1, source_target_pairs={{0,4},{4,0},{8,12},{12,8},{16,20},{20,16},{24,28},{28,24},{1,5},{5... | collective-permute-start | bytes 196616 | tf_op jit(solution)/shard_map/ppermute | solution.py:522
  7.7 2.0 %collective-permute-start.4 = (bf16[1,256,128]{2,1,0:T(8,128)(2,1)S(1)}, bf16[1,256,128]{2,1,0:T(8,128)(2,1)S(1)}, u32[]{:S(2)}, u32[]{:S(2)}) collective-permute-start(bf16[1,256,128]{2,1,0:T(8,128)(2,1)S(1)} %stack.1.refs_1_), channel_id=1, source_target_pairs={{0,4},{4,0},{8,12},{12,8},{16,20},{20,16},{24,28},{28,24},{1,5},{5... | collective-permute-start | bytes 196616 | tf_op jit(solution)/shard_map/ppermute | solution.py:522
  8.2 1.7 %collective-permute-start.5 = (bf16[1,256,128]{2,1,0:T(8,128)(2,1)S(1)}, bf16[1,256,128]{2,1,0:T(8,128)(2,1)S(1)}, u32[]{:S(2)}, u32[]{:S(2)}) collective-permute-start(bf16[1,256,128]{2,1,0:T(8,128)(2,1)S(1)} %bitcast.30), channel_id=1, source_target_pairs={{0,4},{4,0},{8,12},{12,8},{16,20},{20,16},{24,28},{28,24},{1,5},{5... | collective-permute-start | bytes 196616 | tf_op jit(solution)/shard_map/ppermute | solution.py:522
  11.5 6.3 %collective-permute-start.7 = (bf16[256,128]{1,0:T(8,128)(2,1)S(1)}, bf16[256,128]{1,0:T(8,128)(2,1)S(1)}, u32[]{:S(2)}, u32[]{:S(2)}) collective-permute-start(bf16[256,128]{1,0:T(8,128)(2,1)S(1)} %get-tuple-element.25), channel_id=1, source_target_pairs={{0,3},{1,2},{2,1},{3,0},{4,7},{5,6},{6,5},{7,4},{8,11},{9,10},{10,... | collective-permute-start | bytes 196616 | tf_op jit(solution)/shard_map/ppermute | solution.py:522
  15.2 5.9 %collective-permute-start.8 = (bf16[256,128]{1,0:T(8,128)(2,1)S(1)}, bf16[256,128]{1,0:T(8,128)(2,1)S(1)}, u32[]{:S(2)}, u32[]{:S(2)}) collective-permute-start(bf16[256,128]{1,0:T(8,128)(2,1)S(1)} %get-tuple-element.26), channel_id=1, source_target_pairs={{0,2},{1,3},{2,0},{3,1},{4,6},{5,7},{6,4},{7,5},{8,10},{9,11},{10,... | collective-permute-start | bytes 196616 | tf_op jit(solution)/shard_map/ppermute | solution.py:522
  15.2 5.9 %collective-permute-start.9 = (bf16[256,128]{1,0:T(8,128)(2,1)S(1)}, bf16[256,128]{1,0:T(8,128)(2,1)S(1)}, u32[]{:S(2)}, u32[]{:S(2)}) collective-permute-start(bf16[256,128]{1,0:T(8,128)(2,1)S(1)} %get-tuple-element.27), channel_id=1, source_target_pairs={{0,1},{1,0},{2,3},{3,2},{4,5},{5,4},{6,7},{7,6},{8,9},{9,8},{10,11... | collective-permute-start | bytes 196616 | tf_op jit(solution)/shard_map/ppermute | solution.py:522
  21.1 5.4 %collective-permute-start.10 = (bf16[272,128]{1,0:T(8,128)(2,1)S(1)}, bf16[272,128]{1,0:T(8,128)(2,1)S(1)}, u32[]{:S(2)}, u32[]{:S(2)}) collective-permute-start(bf16[272,128]{1,0:T(8,128)(2,1)S(1)} %middle.1), channel_id=1, source_target_pairs={{0,28},{4,24},{8,20},{12,16},{16,12},{20,8},{24,4},{28,0},{1,29},{... | collective-permute-start | bytes 208904 | tf_op jit(solution)/shard_map/ppermute | solution.py:522
  22.2 5.7 %collective-permute-start.11 = (bf16[272,128]{1,0:T(8,128)(2,1)S(1)}, bf16[272,128]{1,0:T(8,128)(2,1)S(1)}, u32[]{:S(2)}, u32[]{:S(2)}) collective-permute-start(bf16[272,128]{1,0:T(8,128)(2,1)S(1)} %middle.1), channel_id=1, source_target_pairs={{0,20},{4,16},{8,28},{12,24},{16,4},{20,0},{24,12},{28,8},{1,21},{... | collective-permute-start | bytes 208904 | tf_op jit(solution)/shard_map/ppermute | solution.py:522
  23.7 4.4 %collective-permute-start.12 = (bf16[272,128]{1,0:T(8,128)(2,1)S(1)}, bf16[272,128]{1,0:T(8,128)(2,1)S(1)}, u32[]{:S(2)}, u32[]{:S(2)}) collective-permute-start(bf16[272,128]{1,0:T(8,128)(2,1)S(1)} %middle.1), channel_id=1, source_target_pairs={{0,12},{4,8},{8,4},{12,0},{16,28},{20,24},{24,20},{28,16},{1,13},{... | collective-permute-start | bytes 208904 | tf_op jit(solution)/shard_map/ppermute | solution.py:522
  24.0 4.4 %collective-permute-start.13 = (bf16[1,272,128]{2,1,0:T(8,128)(2,1)S(1)}, bf16[1,272,128]{2,1,0:T(8,128)(2,1)S(1)}, u32[]{:S(2)}, u32[]{:S(2)}) collective-permute-start(bf16[1,272,128]{2,1,0:T(8,128)(2,1)S(1)} %bitcast.11), channel_id=1, source_target_pairs={{0,4},{4,0},{8,12},{12,8},{16,20},{20,16},{24,28},{28,24},{1,5},{5... | collective-permute-start | bytes 208904 | tf_op jit(solution)/shard_map/ppermute | solution.py:522
  26.6 1.8 %collective-permute-start.14 = (bf16[1,272,128]{2,1,0:T(8,128)(2,1)S(1)}, bf16[1,272,128]{2,1,0:T(8,128)(2,1)S(1)}, u32[]{:S(2)}, u32[]{:S(2)}) collective-permute-start(bf16[1,272,128]{2,1,0:T(8,128)(2,1)S(1)} %bitcast.15), channel_id=1, source_target_pairs={{0,4},{4,0},{8,12},{12,8},{16,20},{20,16},{24,28},{28,24},{1,5},{5... | collective-permute-start | bytes 208904 | tf_op jit(solution)/shard_map/ppermute | solution.py:522
  28.1 1.3 %collective-permute-start.16 = (bf16[1,272,128]{2,1,0:T(8,128)(2,1)S(1)}, bf16[1,272,128]{2,1,0:T(8,128)(2,1)S(1)}, u32[]{:S(2)}, u32[]{:S(2)}) collective-permute-start(bf16[1,272,128]{2,1,0:T(8,128)(2,1)S(1)} %bitcast.23), channel_id=1, source_target_pairs={{0,4},{4,0},{8,12},{12,8},{16,20},{20,16},{24,28},{28,24},{1,5},{5... | collective-permute-start | bytes 208904 | tf_op jit(solution)/shard_map/ppermute | solution.py:522
  30.2 7.0 %collective-permute-start.17 = (bf16[272,128]{1,0:T(8,128)(2,1)S(1)}, bf16[272,128]{1,0:T(8,128)(2,1)S(1)}, u32[]{:S(2)}, u32[]{:S(2)}) collective-permute-start(bf16[272,128]{1,0:T(8,128)(2,1)S(1)} %get-tuple-element.30), channel_id=1, source_target_pairs={{0,3},{1,2},{2,1},{3,0},{4,7},{5,6},{6,5},{7,4},{8,11},{9,10},{10,... | collective-permute-start | bytes 208904 | tf_op jit(solution)/shard_map/ppermute | solution.py:522
  32.5 6.9 %collective-permute-start.18 = (bf16[272,128]{1,0:T(8,128)(2,1)S(1)}, bf16[272,128]{1,0:T(8,128)(2,1)S(1)}, u32[]{:S(2)}, u32[]{:S(2)}) collective-permute-start(bf16[272,128]{1,0:T(8,128)(2,1)S(1)} %get-tuple-element.31), channel_id=1, source_target_pairs={{0,2},{1,3},{2,0},{3,1},{4,6},{5,7},{6,4},{7,5},{8,10},{9,11},{10,... | collective-permute-start | bytes 208904 | tf_op jit(solution)/shard_map/ppermute | solution.py:522
  32.7 6.7 %collective-permute-start.19 = (bf16[272,128]{1,0:T(8,128)(2,1)S(1)}, bf16[272,128]{1,0:T(8,128)(2,1)S(1)}, u32[]{:S(2)}, u32[]{:S(2)}) collective-permute-start(bf16[272,128]{1,0:T(8,128)(2,1)S(1)} %get-tuple-element.32), channel_id=1, source_target_pairs={{0,1},{1,0},{2,3},{3,2},{4,5},{5,4},{6,7},{7,6},{8,9},{9,8},{10,11... | collective-permute-start | bytes 208904 | tf_op jit(solution)/shard_map/ppermute | solution.py:522
  39.9 5.4 %collective-permute-start.20 = (f32[64,128]{1,0:T(8,128)S(1)}, f32[64,128]{1,0:T(8,128)S(1)}, u32[]{:S(2)}, u32[]{:S(2)}) collective-permute-start(f32[64,128]{1,0:T(8,128)S(1)} %get-tuple-element.34.refs_0_), channel_id=1, source_target_pairs={{0,6},{1,7},{2,4},{3,5},{4,2},{5,3},{6,0},{7,1},{8,14},{9,15},{10,... | collective-permute-start | bytes 98312 | tf_op jit(solution)/shard_map/ppermute | solution.py:532
  39.9 5.4 %collective-permute-start.21 = (f32[64,128]{1,0:T(8,128)S(1)}, f32[64,128]{1,0:T(8,128)S(1)}, u32[]{:S(2)}, u32[]{:S(2)}) collective-permute-start(f32[64,128]{1,0:T(8,128)S(1)} %get-tuple-element.34.refs_0_), channel_id=1, source_target_pairs={{0,7},{1,6},{2,5},{3,4},{4,3},{5,2},{6,1},{7,0},{8,15},{9,14},{10,... | collective-permute-start | bytes 98312 | tf_op jit(solution)/shard_map/ppermute | solution.py:532
  42.3 4.0 %collective-permute-start.22 = (f32[64,128]{1,0:T(8,128)S(1)}, f32[64,128]{1,0:T(8,128)S(1)}, u32[]{:S(2)}, u32[]{:S(2)}) collective-permute-start(f32[64,128]{1,0:T(8,128)S(1)} %get-tuple-element.34.refs_0_), channel_id=1, source_target_pairs={{0,5},{1,4},{2,7},{3,6},{4,1},{5,0},{6,3},{7,2},{8,13},{9,12},{10,... | collective-permute-start | bytes 98312 | tf_op jit(solution)/shard_map/ppermute | solution.py:532
  46.3 4.3 %collective-permute-start.23 = (f32[32,128]{1,0:T(8,128)S(1)}, f32[32,128]{1,0:T(8,128)S(1)}, u32[]{:S(2)}, u32[]{:S(2)}) collective-permute-start(f32[32,128]{1,0:T(8,128)S(1)} %get-tuple-element.36.refs_0_), channel_id=1, source_target_pairs={{0,28},{4,24},{8,20},{12,16},{16,12},{20,8},{24,4},{28,0},{1,29},{... | collective-permute-start | bytes 49160 | tf_op jit(solution)/shard_map/ppermute | solution.py:522
  47.7 3.2 %collective-permute-start.24 = (f32[32,128]{1,0:T(8,128)S(1)}, f32[32,128]{1,0:T(8,128)S(1)}, u32[]{:S(2)}, u32[]{:S(2)}) collective-permute-start(f32[32,128]{1,0:T(8,128)S(1)} %get-tuple-element.36.refs_0_), channel_id=1, source_target_pairs={{0,20},{4,16},{8,28},{12,24},{16,4},{20,0},{24,12},{28,8},{1,21},{... | collective-permute-start | bytes 49160 | tf_op jit(solution)/shard_map/ppermute | solution.py:522
  49.1 3.2 %collective-permute-start.25 = (f32[32,128]{1,0:T(8,128)S(1)}, f32[32,128]{1,0:T(8,128)S(1)}, u32[]{:S(2)}, u32[]{:S(2)}) collective-permute-start(f32[32,128]{1,0:T(8,128)S(1)} %get-tuple-element.36.refs_0_), channel_id=1, source_target_pairs={{0,12},{4,8},{8,4},{12,0},{16,28},{20,24},{24,20},{28,16},{1,13},{... | collective-permute-start | bytes 49160 | tf_op jit(solution)/shard_map/ppermute | solution.py:522
  (5 other events, 12.3 us)

commit v21 on v19

--- a/solution.py
+++ b/solution.py
@@ -467,6 +467,11 @@
     )
 
 
+def halves(value):
+    high = value.astype(BF16)
+    return high, (value - high.astype(F32)).astype(BF16)
+
+
 def finish_kernel(total, rows_ref, inverse_ref, *refs):
     out_ref, scratch = refs[-2:]
     block_rows = out_ref.shape[1]
@@ -482,7 +487,14 @@
     both = jnp.concatenate(
         [jnp.concatenate([inverse, zero], axis=1), jnp.concatenate([zero, inverse], axis=1)], axis=0
     )
-    current = dot_turned(rows_ref[...], both)
+    high, low = halves(rows_ref[...])
+    both_high, both_low = halves(both)
+    current = lax.dot_general(
+        jnp.concatenate([high, low, high], axis=1),
+        jnp.concatenate([both_high, both_high, both_low], axis=1),
+        (((1,), (1,)), ((), ())),
+        preferred_element_type=F32,
+    )
     for i in range(block_rows):
         scratch[pl.ds(i, 32, stride=block_rows), :] = current[i * 32 : (i + 1) * 32]
     for t in range(32):

time: 56.3 us -> 56.2 us (level)
  no operation moved by 1% of the time
where the time goes in v21:
time: 56.2 us; the launch traced here: 56 us
  starting transfers between devices  24.6 us (44%)
  waiting for transfers between devices  18.7 us (33%)
  Pallas kernels  12.5 us (22%)
    ppermute x24, starting transfers between devices, swap(): lax.ppermute(value, axis, [(index, index ^ mask) for index in range(size)])  21.6 us
    ppermute x24, waiting for transfers between devices, swap(): lax.ppermute(value, axis, [(index, index ^ mask) for index in range(size)])  15.2 us
    pallas_call x17, Pallas kernels, call(): pl.pallas_call(kernel, out_shape=outs, in_specs=ins, out_specs=jax.tree.m...  12.5 us
    ppermute x3, waiting for transfers between devices, swap_both(): return lax.ppermute(value, ('rows', 'cols'), pairs)  3.48 us
    ppermute x3, starting transfers between devices, swap_both(): return lax.ppermute(value, ('rows', 'cols'), pairs)  2.97 us
  transfers between devices with their start and end apart: 27, of which 16 were waited for; matrix products, arithmetic and copies ran while one was open for 0% of the time, Pallas kernels for 12%

profile of v21, /device:TPU:0, one launch (start us, length us, event | category | flops | bytes accessed | tf_op | source)
XLA Modules:
  0.0 56.0 jit_solution(11816248112900033171)
XLA Ops:
  0.0 1.0 %start.1 = bf16[256,128]{1,0:T(8,128)(2,1)S(1)} custom-call(f32[1,8,4096]{2,1,0:T(8,128)} %panel_hbm.1, f32[1,8,64]{2,1,0:T(8,128)} %inv_hbm.1), custom_call_target="tpu_custom_call" | custom-call | tf_op jit(solution)/shard_map/start/pallas_call | solution.py:37
  1.0 3.4 %collective-permute-start = (bf16[256,128]{1,0:T(8,128)(2,1)S(1)}, bf16[256,128]{1,0:T(8,128)(2,1)S(1)}, u32[]{:S(2)}, u32[]{:S(2)}) collective-permute-start(bf16[256,128]{1,0:T(8,128)(2,1)S(1)} %start.1), channel_id=1, source_target_pairs={{0,28},{4,24},{8,20},{12,16},{16,12},{20,8},{24,4},{28,0},{1,29},{... | collective-permute-start | bytes 196616 | tf_op jit(solution)/shard_map/ppermute | solution.py:517
  5.3 2.3 %prep.2 = (f32[256,128]{1,0:T(8,128)S(1)}, f32[8,128]{1,0:T(8,128)S(1)}, bf16[3,8,64,512]{3,2,1,0:T(8,128)(2,1)S(1)}) custom-call(bf16[4,8,1,8,4096]{4,3,2,1,0:T(8,128)(2,1)} %affinity_hbm.3, f32[1,8,64]{2,1,0:T(8,128)} %inv_hbm.1), custom_call_target="tpu_custom_call" | custom-call | tf_op jit(solution)/shard_map/prep/pallas_call | solution.py:37
  8.2 0.8 %collective-permute-start.5 = (bf16[1,256,128]{2,1,0:T(8,128)(2,1)S(1)}, bf16[1,256,128]{2,1,0:T(8,128)(2,1)S(1)}, u32[]{:S(2)}, u32[]{:S(2)}) collective-permute-start(bf16[1,256,128]{2,1,0:T(8,128)(2,1)S(1)} %bitcast.30), channel_id=1, source_target_pairs={{0,4},{4,0},{8,12},{12,8},{16,20},{20,16},{24,28},{28,24},{1,5},{5... | collective-permute-start | bytes 196616 | tf_op jit(solution)/shard_map/ppermute | solution.py:517
  11.5 3.7 %collective-permute-start.7 = (bf16[256,128]{1,0:T(8,128)(2,1)S(1)}, bf16[256,128]{1,0:T(8,128)(2,1)S(1)}, u32[]{:S(2)}, u32[]{:S(2)}) collective-permute-start(bf16[256,128]{1,0:T(8,128)(2,1)S(1)} %get-tuple-element.25), channel_id=1, source_target_pairs={{0,3},{1,2},{2,1},{3,0},{4,7},{5,6},{6,5},{7,4},{8,11},{9,10},{10,... | collective-permute-start | bytes 196616 | tf_op jit(solution)/shard_map/ppermute | solution.py:517
  16.0 1.4 %prep.3.matrix_ref = bf16[1,8,64,512]{3,2,1,0:T(8,128)(2,1)S(1)} custom-call(bf16[4,8,1,8,4096]{4,3,2,1,0:T(8,128)(2,1)} %affinity_hbm.3), custom_call_target="tpu_custom_call" | custom-call | tf_op jit(solution)/shard_map/prep/pallas_call | solution.py:37
  17.9 3.2 %collective-permute-done.8.refs_2_ = bf16[256,128]{1,0:T(8,128)(2,1)S(1)} collective-permute-done((bf16[256,128]{1,0:T(8,128)(2,1)S(1)}, bf16[256,128]{1,0:T(8,128)(2,1)S(1)}, u32[]{:S(2)}, u32[]{:S(2)}) %collective-permute-start.8) | collective-permute-done | bytes 65568 | tf_op jit(solution)/shard_map/ppermute | solution.py:517
  21.1 1.1 %collective-permute-start.10 = (bf16[272,128]{1,0:T(8,128)(2,1)S(1)}, bf16[272,128]{1,0:T(8,128)(2,1)S(1)}, u32[]{:S(2)}, u32[]{:S(2)}) collective-permute-start(bf16[272,128]{1,0:T(8,128)(2,1)S(1)} %middle.1), channel_id=1, source_target_pairs={{0,28},{4,24},{8,20},{12,16},{16,12},{20,8},{24,4},{28,0},{1,29},{... | collective-permute-start | bytes 208904 | tf_op jit(solution)/shard_map/ppermute | solution.py:517
  22.2 1.5 %collective-permute-start.11 = (bf16[272,128]{1,0:T(8,128)(2,1)S(1)}, bf16[272,128]{1,0:T(8,128)(2,1)S(1)}, u32[]{:S(2)}, u32[]{:S(2)}) collective-permute-start(bf16[272,128]{1,0:T(8,128)(2,1)S(1)} %middle.1), channel_id=1, source_target_pairs={{0,20},{4,16},{8,28},{12,24},{16,4},{20,0},{24,12},{28,8},{1,21},{... | collective-permute-start | bytes 208904 | tf_op jit(solution)/shard_map/ppermute | solution.py:517
  24.5 2.0 %collective-permute-done.10 = bf16[272,128]{1,0:T(8,128)(2,1)S(1)} collective-permute-done((bf16[272,128]{1,0:T(8,128)(2,1)S(1)}, bf16[272,128]{1,0:T(8,128)(2,1)S(1)}, u32[]{:S(2)}, u32[]{:S(2)}) %collective-permute-start.10) | collective-permute-done | bytes 69664 | tf_op jit(solution)/shard_map/ppermute | solution.py:517
  26.6 1.3 %collective-permute-done.11 = bf16[272,128]{1,0:T(8,128)(2,1)S(1)} collective-permute-done((bf16[272,128]{1,0:T(8,128)(2,1)S(1)}, bf16[272,128]{1,0:T(8,128)(2,1)S(1)}, u32[]{:S(2)}, u32[]{:S(2)}) %collective-permute-start.11) | collective-permute-done | bytes 69664 | tf_op jit(solution)/shard_map/ppermute | solution.py:517
  30.2 2.3 %collective-permute-start.17 = (bf16[272,128]{1,0:T(8,128)(2,1)S(1)}, bf16[272,128]{1,0:T(8,128)(2,1)S(1)}, u32[]{:S(2)}, u32[]{:S(2)}) collective-permute-start(bf16[272,128]{1,0:T(8,128)(2,1)S(1)} %get-tuple-element.30), channel_id=1, source_target_pairs={{0,3},{1,2},{2,1},{3,0},{4,7},{5,6},{6,5},{7,4},{8,11},{9,10},{10,... | collective-permute-start | bytes 208904 | tf_op jit(solution)/shard_map/ppermute | solution.py:517
  32.7 1.9 %collective-permute-start.19 = (bf16[272,128]{1,0:T(8,128)(2,1)S(1)}, bf16[272,128]{1,0:T(8,128)(2,1)S(1)}, u32[]{:S(2)}, u32[]{:S(2)}) collective-permute-start(bf16[272,128]{1,0:T(8,128)(2,1)S(1)} %get-tuple-element.32), channel_id=1, source_target_pairs={{0,1},{1,0},{2,3},{3,2},{4,5},{5,4},{6,7},{7,6},{8,9},{9,8},{10,11... | collective-permute-start | bytes 208904 | tf_op jit(solution)/shard_map/ppermute | solution.py:517
  35.7 1.4 %collective-permute-done.17.refs_1_ = bf16[272,128]{1,0:T(8,128)(2,1)S(1)} collective-permute-done((bf16[272,128]{1,0:T(8,128)(2,1)S(1)}, bf16[272,128]{1,0:T(8,128)(2,1)S(1)}, u32[]{:S(2)}, u32[]{:S(2)}) %collective-permute-start.17) | collective-permute-done | bytes 69664 | tf_op jit(solution)/shard_map/ppermute | solution.py:517
  37.2 2.2 %collective-permute-done.18.refs_2_ = bf16[272,128]{1,0:T(8,128)(2,1)S(1)} collective-permute-done((bf16[272,128]{1,0:T(8,128)(2,1)S(1)}, bf16[272,128]{1,0:T(8,128)(2,1)S(1)}, u32[]{:S(2)}, u32[]{:S(2)}) %collective-permute-start.18) | collective-permute-done | bytes 69664 | tf_op jit(solution)/shard_map/ppermute | solution.py:517
  39.9 2.4 %collective-permute-start.21 = (f32[64,128]{1,0:T(8,128)S(1)}, f32[64,128]{1,0:T(8,128)S(1)}, u32[]{:S(2)}, u32[]{:S(2)}) collective-permute-start(f32[64,128]{1,0:T(8,128)S(1)} %get-tuple-element.34.refs_0_), channel_id=1, source_target_pairs={{0,7},{1,6},{2,5},{3,4},{4,3},{5,2},{6,1},{7,0},{8,15},{9,14},{10,... | collective-permute-start | bytes 98312 | tf_op jit(solution)/shard_map/ppermute | solution.py:527
  42.8 2.4 %collective-permute-done.20.refs_1_ = f32[64,128]{1,0:T(8,128)S(1)} collective-permute-done((f32[64,128]{1,0:T(8,128)S(1)}, f32[64,128]{1,0:T(8,128)S(1)}, u32[]{:S(2)}, u32[]{:S(2)}) %collective-permute-start.20) | collective-permute-done | bytes 32800 | tf_op jit(solution)/shard_map/ppermute | solution.py:527
  45.3 1.0 %collective-permute-done.22.refs_3_ = f32[64,128]{1,0:T(8,128)S(1)} collective-permute-done((f32[64,128]{1,0:T(8,128)S(1)}, f32[64,128]{1,0:T(8,128)S(1)}, u32[]{:S(2)}, u32[]{:S(2)}) %collective-permute-start.22) | collective-permute-done | bytes 32800 | tf_op jit(solution)/shard_map/ppermute | solution.py:527
  46.3 1.4 %collective-permute-start.23 = (f32[32,128]{1,0:T(8,128)S(1)}, f32[32,128]{1,0:T(8,128)S(1)}, u32[]{:S(2)}, u32[]{:S(2)}) collective-permute-start(f32[32,128]{1,0:T(8,128)S(1)} %get-tuple-element.36.refs_0_), channel_id=1, source_target_pairs={{0,28},{4,24},{8,20},{12,16},{16,12},{20,8},{24,4},{28,0},{1,29},{... | collective-permute-start | bytes 49160 | tf_op jit(solution)/shard_map/ppermute | solution.py:517
  47.7 1.3 %collective-permute-start.24 = (f32[32,128]{1,0:T(8,128)S(1)}, f32[32,128]{1,0:T(8,128)S(1)}, u32[]{:S(2)}, u32[]{:S(2)}) collective-permute-start(f32[32,128]{1,0:T(8,128)S(1)} %get-tuple-element.36.refs_0_), channel_id=1, source_target_pairs={{0,20},{4,16},{8,28},{12,24},{16,4},{20,0},{24,12},{28,8},{1,21},{... | collective-permute-start | bytes 49160 | tf_op jit(solution)/shard_map/ppermute | solution.py:517
  49.3 1.3 %first_factor.1.refs_4_.inverse_ref = f32[64,64]{1,0:T(8,128)S(1)} custom-call(f32[32,128]{1,0:T(8,128)S(1)} %get-tuple-element.35.gram_ref), custom_call_target="tpu_custom_call" | custom-call | tf_op jit(solution)/shard_map/first_factor/pallas_call | solution.py:37
  50.9 1.3 %collective-permute-done.25.refs_3_ = f32[32,128]{1,0:T(8,128)S(1)} collective-permute-done((f32[32,128]{1,0:T(8,128)S(1)}, f32[32,128]{1,0:T(8,128)S(1)}, u32[]{:S(2)}, u32[]{:S(2)}) %collective-permute-start.25) | collective-permute-done | bytes 16416 | tf_op jit(solution)/shard_map/ppermute | solution.py:517
  52.3 1.1 %collective-permute-done.26.refs_1_ = f32[32,128]{1,0:T(8,128)S(1)} collective-permute-done((f32[32,128]{1,0:T(8,128)S(1)}, f32[32,128]{1,0:T(8,128)S(1)}, u32[]{:S(2)}, u32[]{:S(2)}) %collective-permute-start.26) | collective-permute-done | bytes 16416 | tf_op jit(solution)/shard_map/ppermute | solution.py:517
  53.4 2.6 %finish.1 = f32[1,8,4096]{2,1,0:T(8,128)} custom-call(f32[256,128]{1,0:T(8,128)S(1)} %get-tuple-element.33.rows_ref, f32[64,64]{1,0:T(8,128)S(1)} %first_factor.1.refs_4_.inverse_ref, f32[32,128]{1,0:T(8,128)S(1)} %add_parts.1.refs_0_, f32[32,128]{1,0:T(8,128)S(1)} %collective-permute-done.26.refs_1_), custom_call_target="tpu_custom_call" | custom-call | tf_op jit(solution)/shard_map/finish/pallas_call | solution.py:37
  (52 shorter events, 11.4 us)
Async XLA Ops:
  1.0 6.7 %collective-permute-start = (bf16[256,128]{1,0:T(8,128)(2,1)S(1)}, bf16[256,128]{1,0:T(8,128)(2,1)S(1)}, u32[]{:S(2)}, u32[]{:S(2)}) collective-permute-start(bf16[256,128]{1,0:T(8,128)(2,1)S(1)} %start.1), channel_id=1, source_target_pairs={{0,28},{4,24},{8,20},{12,16},{16,12},{20,8},{24,4},{28,0},{1,29},{... | collective-permute-start | bytes 196616 | tf_op jit(solution)/shard_map/ppermute | solution.py:517
  4.4 3.9 %collective-permute-start.1 = (bf16[256,128]{1,0:T(8,128)(2,1)S(1)}, bf16[256,128]{1,0:T(8,128)(2,1)S(1)}, u32[]{:S(2)}, u32[]{:S(2)}) collective-permute-start(bf16[256,128]{1,0:T(8,128)(2,1)S(1)} %start.1), channel_id=1, source_target_pairs={{0,20},{4,16},{8,28},{12,24},{16,4},{20,0},{24,12},{28,8},{1,21},{... | collective-permute-start | bytes 196616 | tf_op jit(solution)/shard_map/ppermute | solution.py:517
  5.2 4.3 %collective-permute-start.2 = (bf16[256,128]{1,0:T(8,128)(2,1)S(1)}, bf16[256,128]{1,0:T(8,128)(2,1)S(1)}, u32[]{:S(2)}, u32[]{:S(2)}) collective-permute-start(bf16[256,128]{1,0:T(8,128)(2,1)S(1)} %start.1), channel_id=1, source_target_pairs={{0,12},{4,8},{8,4},{12,0},{16,28},{20,24},{24,20},{28,16},{1,13},{... | collective-permute-start | bytes 196616 | tf_op jit(solution)/shard_map/ppermute | solution.py:517
  5.3 4.4 %collective-permute-start.3 = (bf16[1,256,128]{2,1,0:T(8,128)(2,1)S(1)}, bf16[1,256,128]{2,1,0:T(8,128)(2,1)S(1)}, u32[]{:S(2)}, u32[]{:S(2)}) collective-permute-start(bf16[1,256,128]{2,1,0:T(8,128)(2,1)S(1)} %bitcast.27), channel_id=1, source_target_pairs={{0,4},{4,0},{8,12},{12,8},{16,20},{20,16},{24,28},{28,24},{1,5},{5... | collective-permute-start | bytes 196616 | tf_op jit(solution)/shard_map/ppermute | solution.py:517
  7.7 2.0 %collective-permute-start.4 = (bf16[1,256,128]{2,1,0:T(8,128)(2,1)S(1)}, bf16[1,256,128]{2,1,0:T(8,128)(2,1)S(1)}, u32[]{:S(2)}, u32[]{:S(2)}) collective-permute-start(bf16[1,256,128]{2,1,0:T(8,128)(2,1)S(1)} %stack.1.refs_1_), channel_id=1, source_target_pairs={{0,4},{4,0},{8,12},{12,8},{16,20},{20,16},{24,28},{28,24},{1,5},{5... | collective-permute-start | bytes 196616 | tf_op jit(solution)/shard_map/ppermute | solution.py:517
  8.2 1.7 %collective-permute-start.5 = (bf16[1,256,128]{2,1,0:T(8,128)(2,1)S(1)}, bf16[1,256,128]{2,1,0:T(8,128)(2,1)S(1)}, u32[]{:S(2)}, u32[]{:S(2)}) collective-permute-start(bf16[1,256,128]{2,1,0:T(8,128)(2,1)S(1)} %bitcast.30), channel_id=1, source_target_pairs={{0,4},{4,0},{8,12},{12,8},{16,20},{20,16},{24,28},{28,24},{1,5},{5... | collective-permute-start | bytes 196616 | tf_op jit(solution)/shard_map/ppermute | solution.py:517
  11.5 6.3 %collective-permute-start.7 = (bf16[256,128]{1,0:T(8,128)(2,1)S(1)}, bf16[256,128]{1,0:T(8,128)(2,1)S(1)}, u32[]{:S(2)}, u32[]{:S(2)}) collective-permute-start(bf16[256,128]{1,0:T(8,128)(2,1)S(1)} %get-tuple-element.25), channel_id=1, source_target_pairs={{0,3},{1,2},{2,1},{3,0},{4,7},{5,6},{6,5},{7,4},{8,11},{9,10},{10,... | collective-permute-start | bytes 196616 | tf_op jit(solution)/shard_map/ppermute | solution.py:517
  15.2 5.9 %collective-permute-start.8 = (bf16[256,128]{1,0:T(8,128)(2,1)S(1)}, bf16[256,128]{1,0:T(8,128)(2,1)S(1)}, u32[]{:S(2)}, u32[]{:S(2)}) collective-permute-start(bf16[256,128]{1,0:T(8,128)(2,1)S(1)} %get-tuple-element.26), channel_id=1, source_target_pairs={{0,2},{1,3},{2,0},{3,1},{4,6},{5,7},{6,4},{7,5},{8,10},{9,11},{10,... | collective-permute-start | bytes 196616 | tf_op jit(solution)/shard_map/ppermute | solution.py:517
  15.2 5.9 %collective-permute-start.9 = (bf16[256,128]{1,0:T(8,128)(2,1)S(1)}, bf16[256,128]{1,0:T(8,128)(2,1)S(1)}, u32[]{:S(2)}, u32[]{:S(2)}) collective-permute-start(bf16[256,128]{1,0:T(8,128)(2,1)S(1)} %get-tuple-element.27), channel_id=1, source_target_pairs={{0,1},{1,0},{2,3},{3,2},{4,5},{5,4},{6,7},{7,6},{8,9},{9,8},{10,11... | collective-permute-start | bytes 196616 | tf_op jit(solution)/shard_map/ppermute | solution.py:517
  21.1 5.4 %collective-permute-start.10 = (bf16[272,128]{1,0:T(8,128)(2,1)S(1)}, bf16[272,128]{1,0:T(8,128)(2,1)S(1)}, u32[]{:S(2)}, u32[]{:S(2)}) collective-permute-start(bf16[272,128]{1,0:T(8,128)(2,1)S(1)} %middle.1), channel_id=1, source_target_pairs={{0,28},{4,24},{8,20},{12,16},{16,12},{20,8},{24,4},{28,0},{1,29},{... | collective-permute-start | bytes 208904 | tf_op jit(solution)/shard_map/ppermute | solution.py:517
  22.2 5.7 %collective-permute-start.11 = (bf16[272,128]{1,0:T(8,128)(2,1)S(1)}, bf16[272,128]{1,0:T(8,128)(2,1)S(1)}, u32[]{:S(2)}, u32[]{:S(2)}) collective-permute-start(bf16[272,128]{1,0:T(8,128)(2,1)S(1)} %middle.1), channel_id=1, source_target_pairs={{0,20},{4,16},{8,28},{12,24},{16,4},{20,0},{24,12},{28,8},{1,21},{... | collective-permute-start | bytes 208904 | tf_op jit(solution)/shard_map/ppermute | solution.py:517
  23.7 4.4 %collective-permute-start.12 = (bf16[272,128]{1,0:T(8,128)(2,1)S(1)}, bf16[272,128]{1,0:T(8,128)(2,1)S(1)}, u32[]{:S(2)}, u32[]{:S(2)}) collective-permute-start(bf16[272,128]{1,0:T(8,128)(2,1)S(1)} %middle.1), channel_id=1, source_target_pairs={{0,12},{4,8},{8,4},{12,0},{16,28},{20,24},{24,20},{28,16},{1,13},{... | collective-permute-start | bytes 208904 | tf_op jit(solution)/shard_map/ppermute | solution.py:517
  24.0 4.4 %collective-permute-start.13 = (bf16[1,272,128]{2,1,0:T(8,128)(2,1)S(1)}, bf16[1,272,128]{2,1,0:T(8,128)(2,1)S(1)}, u32[]{:S(2)}, u32[]{:S(2)}) collective-permute-start(bf16[1,272,128]{2,1,0:T(8,128)(2,1)S(1)} %bitcast.11), channel_id=1, source_target_pairs={{0,4},{4,0},{8,12},{12,8},{16,20},{20,16},{24,28},{28,24},{1,5},{5... | collective-permute-start | bytes 208904 | tf_op jit(solution)/shard_map/ppermute | solution.py:517
  26.6 1.8 %collective-permute-start.14 = (bf16[1,272,128]{2,1,0:T(8,128)(2,1)S(1)}, bf16[1,272,128]{2,1,0:T(8,128)(2,1)S(1)}, u32[]{:S(2)}, u32[]{:S(2)}) collective-permute-start(bf16[1,272,128]{2,1,0:T(8,128)(2,1)S(1)} %bitcast.15), channel_id=1, source_target_pairs={{0,4},{4,0},{8,12},{12,8},{16,20},{20,16},{24,28},{28,24},{1,5},{5... | collective-permute-start | bytes 208904 | tf_op jit(solution)/shard_map/ppermute | solution.py:517
  27.9 1.3 %collective-permute-start.15 = (bf16[1,272,128]{2,1,0:T(8,128)(2,1)S(1)}, bf16[1,272,128]{2,1,0:T(8,128)(2,1)S(1)}, u32[]{:S(2)}, u32[]{:S(2)}) collective-permute-start(bf16[1,272,128]{2,1,0:T(8,128)(2,1)S(1)} %bitcast.19), channel_id=1, source_target_pairs={{0,4},{4,0},{8,12},{12,8},{16,20},{20,16},{24,28},{28,24},{1,5},{5... | collective-permute-start | bytes 208904 | tf_op jit(solution)/shard_map/ppermute | solution.py:517
  30.2 7.0 %collective-permute-start.17 = (bf16[272,128]{1,0:T(8,128)(2,1)S(1)}, bf16[272,128]{1,0:T(8,128)(2,1)S(1)}, u32[]{:S(2)}, u32[]{:S(2)}) collective-permute-start(bf16[272,128]{1,0:T(8,128)(2,1)S(1)} %get-tuple-element.30), channel_id=1, source_target_pairs={{0,3},{1,2},{2,1},{3,0},{4,7},{5,6},{6,5},{7,4},{8,11},{9,10},{10,... | collective-permute-start | bytes 208904 | tf_op jit(solution)/shard_map/ppermute | solution.py:517
  32.5 6.9 %collective-permute-start.18 = (bf16[272,128]{1,0:T(8,128)(2,1)S(1)}, bf16[272,128]{1,0:T(8,128)(2,1)S(1)}, u32[]{:S(2)}, u32[]{:S(2)}) collective-permute-start(bf16[272,128]{1,0:T(8,128)(2,1)S(1)} %get-tuple-element.31), channel_id=1, source_target_pairs={{0,2},{1,3},{2,0},{3,1},{4,6},{5,7},{6,4},{7,5},{8,10},{9,11},{10,... | collective-permute-start | bytes 208904 | tf_op jit(solution)/shard_map/ppermute | solution.py:517
  32.7 6.7 %collective-permute-start.19 = (bf16[272,128]{1,0:T(8,128)(2,1)S(1)}, bf16[272,128]{1,0:T(8,128)(2,1)S(1)}, u32[]{:S(2)}, u32[]{:S(2)}) collective-permute-start(bf16[272,128]{1,0:T(8,128)(2,1)S(1)} %get-tuple-element.32), channel_id=1, source_target_pairs={{0,1},{1,0},{2,3},{3,2},{4,5},{5,4},{6,7},{7,6},{8,9},{9,8},{10,11... | collective-permute-start | bytes 208904 | tf_op jit(solution)/shard_map/ppermute | solution.py:517
  39.9 5.4 %collective-permute-start.20 = (f32[64,128]{1,0:T(8,128)S(1)}, f32[64,128]{1,0:T(8,128)S(1)}, u32[]{:S(2)}, u32[]{:S(2)}) collective-permute-start(f32[64,128]{1,0:T(8,128)S(1)} %get-tuple-element.34.refs_0_), channel_id=1, source_target_pairs={{0,6},{1,7},{2,4},{3,5},{4,2},{5,3},{6,0},{7,1},{8,14},{9,15},{10,... | collective-permute-start | bytes 98312 | tf_op jit(solution)/shard_map/ppermute | solution.py:527
  39.9 5.4 %collective-permute-start.21 = (f32[64,128]{1,0:T(8,128)S(1)}, f32[64,128]{1,0:T(8,128)S(1)}, u32[]{:S(2)}, u32[]{:S(2)}) collective-permute-start(f32[64,128]{1,0:T(8,128)S(1)} %get-tuple-element.34.refs_0_), channel_id=1, source_target_pairs={{0,7},{1,6},{2,5},{3,4},{4,3},{5,2},{6,1},{7,0},{8,15},{9,14},{10,... | collective-permute-start | bytes 98312 | tf_op jit(solution)/shard_map/ppermute | solution.py:527
  42.3 4.0 %collective-permute-start.22 = (f32[64,128]{1,0:T(8,128)S(1)}, f32[64,128]{1,0:T(8,128)S(1)}, u32[]{:S(2)}, u32[]{:S(2)}) collective-permute-start(f32[64,128]{1,0:T(8,128)S(1)} %get-tuple-element.34.refs_0_), channel_id=1, source_target_pairs={{0,5},{1,4},{2,7},{3,6},{4,1},{5,0},{6,3},{7,2},{8,13},{9,12},{10,... | collective-permute-start | bytes 98312 | tf_op jit(solution)/shard_map/ppermute | solution.py:527
  46.3 4.3 %collective-permute-start.23 = (f32[32,128]{1,0:T(8,128)S(1)}, f32[32,128]{1,0:T(8,128)S(1)}, u32[]{:S(2)}, u32[]{:S(2)}) collective-permute-start(f32[32,128]{1,0:T(8,128)S(1)} %get-tuple-element.36.refs_0_), channel_id=1, source_target_pairs={{0,28},{4,24},{8,20},{12,16},{16,12},{20,8},{24,4},{28,0},{1,29},{... | collective-permute-start | bytes 49160 | tf_op jit(solution)/shard_map/ppermute | solution.py:517
  47.7 3.2 %collective-permute-start.24 = (f32[32,128]{1,0:T(8,128)S(1)}, f32[32,128]{1,0:T(8,128)S(1)}, u32[]{:S(2)}, u32[]{:S(2)}) collective-permute-start(f32[32,128]{1,0:T(8,128)S(1)} %get-tuple-element.36.refs_0_), channel_id=1, source_target_pairs={{0,20},{4,16},{8,28},{12,24},{16,4},{20,0},{24,12},{28,8},{1,21},{... | collective-permute-start | bytes 49160 | tf_op jit(solution)/shard_map/ppermute | solution.py:517
  49.1 3.2 %collective-permute-start.25 = (f32[32,128]{1,0:T(8,128)S(1)}, f32[32,128]{1,0:T(8,128)S(1)}, u32[]{:S(2)}, u32[]{:S(2)}) collective-permute-start(f32[32,128]{1,0:T(8,128)S(1)} %get-tuple-element.36.refs_0_), channel_id=1, source_target_pairs={{0,12},{4,8},{8,4},{12,0},{16,28},{20,24},{24,20},{28,16},{1,13},{... | collective-permute-start | bytes 49160 | tf_op jit(solution)/shard_map/ppermute | solution.py:517
  (5 other events, 12.3 us)
